TPU v7x, 32 devices: a whole 2x2x4 slice. The times are simulated.
32 devices in a mesh: dp: 8 (over z, y), seq: 4 (over x, core).
Axes of the slice: x: 2, y: 2, z: 4, core: 2. Of those that a mesh axis runs over, the one named last changes fastest.
Arguments:
- token_ids: int32 [32, 2, 512], P('dp', None, 'seq'), may hold values from 0 to 30719
- lengths: int32 [32, 2], P('dp'), may hold values from 64 to 512, as said below
- labeled: int32 [32], P('dp'), may hold values 0 or 1
- gold: float32 [32], P('dp'), may hold values from 0 to 1
- embed: float32 [30720, 768], P(('dp', 'seq')), may hold values from -0.3 to 0.3
- position: float32 [512, 768], P(None, ('dp', 'seq')), may hold values from -0.3 to 0.3
- attn_in: float32 [768, 2304], P(('dp', 'seq')), may hold values from -0.21875 to 0.21875
- attn_out: float32 [768, 768], P(('dp', 'seq')), may hold values from -0.875 to 0.875
- ff_in: float32 [768, 3072], P(('dp', 'seq')), may hold values from -0.21875 to 0.21875
- ff_out: float32 [3072, 768], P(('dp', 'seq')), may hold values from -0.109375 to 0.109375
- vectors: float32 [14, 768], P(None, ('dp', 'seq'))
- mom_embed: float32 [30720, 768], P(('dp', 'seq')), may hold values from -2.670288e-05 to 2.670288e-05
- mom_position: float32 [512, 768], P(None, ('dp', 'seq')), may hold values from -2.670288e-05 to 2.670288e-05
- mom_attn_in: float32 [768, 2304], P(('dp', 'seq')), may hold values from -2.670288e-05 to 2.670288e-05
- mom_attn_out: float32 [768, 768], P(('dp', 'seq')), may hold values from -2.670288e-05 to 2.670288e-05
- mom_ff_in: float32 [768, 3072], P(('dp', 'seq')), may hold values from -2.670288e-05 to 2.670288e-05
- mom_ff_out: float32 [3072, 768], P(('dp', 'seq')), may hold values from -2.670288e-05 to 2.670288e-05
- mom_vectors: float32 [14, 768], P(None, ('dp', 'seq')), may hold values from -0.00010681152 to 0.00010681152
- avg_embed: float32 [30720, 768], P(('dp', 'seq')), may hold values from -0.3 to 0.3
- avg_position: float32 [512, 768], P(None, ('dp', 'seq')), may hold values from -0.3 to 0.3
- avg_attn_in: float32 [768, 2304], P(('dp', 'seq')), may hold values from -0.21875 to 0.21875
- avg_attn_out: float32 [768, 768], P(('dp', 'seq')), may hold values from -0.875 to 0.875
- avg_ff_in: float32 [768, 3072], P(('dp', 'seq')), may hold values from -0.21875 to 0.21875
- avg_ff_out: float32 [3072, 768], P(('dp', 'seq')), may hold values from -0.109375 to 0.109375
- avg_vectors: float32 [14, 768], P(None, ('dp', 'seq')), may hold values from 0.5 to 1.5
Outputs:
- loss_sum: float32 [], replicated
- loss_count: float32 [], replicated
- grad_norm: float32 [], replicated
- new_embed: float32 [30720, 768], P(('dp', 'seq'))
- new_position: float32 [512, 768], P(None, ('dp', 'seq'))
- new_attn_in: float32 [768, 2304], P(('dp', 'seq'))
- new_attn_out: float32 [768, 768], P(('dp', 'seq'))
- new_ff_in: float32 [768, 3072], P(('dp', 'seq'))
- new_ff_out: float32 [3072, 768], P(('dp', 'seq'))
- new_vectors: float32 [14, 768], P(None, ('dp', 'seq'))
- next_mom_embed: float32 [30720, 768], P(('dp', 'seq'))
- next_mom_position: float32 [512, 768], P(None, ('dp', 'seq'))
- next_mom_attn_in: float32 [768, 2304], P(('dp', 'seq'))
- next_mom_attn_out: float32 [768, 768], P(('dp', 'seq'))
- next_mom_ff_in: float32 [768, 3072], P(('dp', 'seq'))
- next_mom_ff_out: float32 [3072, 768], P(('dp', 'seq'))
- next_mom_vectors: float32 [14, 768], P(None, ('dp', 'seq'))
- next_avg_embed: float32 [30720, 768], P(('dp', 'seq'))
- next_avg_position: float32 [512, 768], P(None, ('dp', 'seq'))
- next_avg_attn_in: float32 [768, 2304], P(('dp', 'seq'))
- next_avg_attn_out: float32 [768, 768], P(('dp', 'seq'))
- next_avg_ff_in: float32 [768, 3072], P(('dp', 'seq'))
- next_avg_ff_out: float32 [3072, 768], P(('dp', 'seq'))
- next_avg_vectors: float32 [14, 768], P(None, ('dp', 'seq'))
Inputs may be any that keep to these rules, and one draw needn't show every extreme that they name: `lengths`: each group of the 8 sentences of one index of dp holds at least one sentence of exactly 512 tokens, which one drawn.
All inputs are finite; a program needn't handle non-finite values. No bound on the sum of `labeled` on one device may be relied on, other than what follows from the above.
Results may differ from a plain program's by a relative error of at most 0.012.
Values may be sent and summed in bfloat16 or wider, within the bound.
No kernel may reach another device: no remote copies, remote signals or barrier semaphores. Data moves between devices by JAX's collectives and lax.ppermute only.
A program may use at most 320 MiB of HBM per device.

v0:
```python
import jax
import jax.numpy as jnp
from jax import lax
from jax.sharding import PartitionSpec as P

HEADS = 12
HEAD_DIM = 64
FF = 3072


EPS = 1e-06
RATE = 10000.0
MOMENT = 0.5
DECAY = 0.5
CLIP = 0.01


def shortened(x):
    return jax.tree.map(lambda a: a.astype(jnp.bfloat16) if a.dtype == jnp.float32 else a, x)


def layer_norm(v, gain, bias):
    center = v - jnp.mean(v, axis=-1, keepdims=True)
    spread = jnp.mean(center * center, axis=-1, keepdims=True)
    return center * lax.rsqrt(spread + EPS) * gain + bias


def exact_gelu(v):
    return jax.nn.gelu(v, approximate=False)


def scores(query, keys, lens):
    raw = jnp.einsum("sqhd,skhd->shqk", query, keys, preferred_element_type=jnp.float32) * 0.125
    live = jnp.arange(keys.shape[1])[None, :] < lens[:, None]
    return (raw, live[:, None, None, :])


def dot_left(left, right):
    return lax.dot_general(
        left, right, (((0,), (0,)), ((), ())), preferred_element_type=jnp.float32
    )


def dot_right(left, right):
    return lax.dot_general(
        left, right, (((1,), (1,)), ((), ())), preferred_element_type=jnp.float32
    )


def layer_forward(h0, weights, lens, sents, local):
    attn_in, attn_out, ff_in, ff_out, vec = weights
    width = h0.shape[1]
    hin = h0.astype(jnp.bfloat16)
    bias = jnp.concatenate([vec[2], jnp.zeros_like(vec[2]), vec[3]])
    proj = jnp.dot(hin, attn_in, preferred_element_type=jnp.float32) + bias
    shape = (sents, local, HEADS, HEAD_DIM)
    query = proj[:, :width].astype(jnp.bfloat16).reshape(shape)
    keys = proj[:, width : 2 * width].astype(jnp.bfloat16).reshape(shape)
    values = proj[:, 2 * width :].astype(jnp.bfloat16).reshape(shape)
    saved = {"hin": hin, "query": query, "keys": keys, "values": values}
    top = jnp.full((sents, HEADS, local), -1e30, jnp.float32)
    total = jnp.zeros((sents, HEADS, local), jnp.float32)
    raw, live = scores(
        query, jax.tree.map(lambda a: lax.all_gather(a, "seq", axis=1, tiled=True), keys), lens
    )
    new_top = jnp.maximum(top, jnp.max(jnp.where(live, raw, -1e30), axis=-1))
    total = total * jnp.exp(top - new_top) + jnp.sum(
        jnp.where(live, jnp.exp(raw - new_top[..., None]), 0.0), axis=-1
    )
    top, total = (new_top, total)
    lse = top + jnp.log(total)
    raw, live = scores(query, lax.all_gather(keys, "seq", axis=1, tiled=True), lens)
    prob = jnp.where(live, jnp.exp(raw - lse[..., None]), 0.0).astype(jnp.bfloat16)
    out = jnp.zeros(shape, jnp.float32) + jnp.einsum(
        "shqk,skhd->sqhd",
        prob,
        lax.all_gather(values, "seq", axis=1, tiled=True),
        preferred_element_type=jnp.float32,
    )
    saved["lse"] = lse
    out_b = out.reshape(sents * local, width).astype(jnp.bfloat16)
    saved["out"] = out_b
    branch = jnp.dot(out_b, attn_out, preferred_element_type=jnp.float32) + vec[4]
    h1, back_one = jax.vjp(layer_norm, h0 + branch, vec[5], vec[6])
    h1_b = h1.astype(jnp.bfloat16)
    hidden = jnp.dot(h1_b, ff_in, preferred_element_type=jnp.float32) + vec[
        7 : 7 + FF // width
    ].reshape(-1)
    act, back_act = jax.vjp(exact_gelu, hidden)
    act_b = act.astype(jnp.bfloat16)
    mixed = jnp.dot(act_b, ff_out, preferred_element_type=jnp.float32) + vec[7 + FF // width]
    h2, back_two = jax.vjp(layer_norm, h1 + mixed, vec[8 + FF // width], vec[9 + FF // width])
    saved.update(
        {"back_one": back_one, "h1": h1_b, "back_act": back_act, "act": act_b, "back_two": back_two}
    )
    return (h2, saved)


def layer_backward(d_h2, saved, weights, lens, sents, local):
    attn_in, attn_out, ff_in, ff_out, vec = weights
    width = d_h2.shape[1]
    d_r2, d_g2, d_b2n = saved["back_two"](d_h2)
    d_y = d_r2.astype(jnp.bfloat16)
    g_ff_out = dot_left(saved["act"], d_y)
    d_act = dot_right(d_y, ff_out)
    d_f = saved["back_act"](d_act)[0].astype(jnp.bfloat16)
    g_ff_in = dot_left(saved["h1"], d_f)
    d_h1 = d_r2 + dot_right(d_f, ff_in)
    d_r1, d_g1, d_b1 = saved["back_one"](d_h1)
    d_a = d_r1.astype(jnp.bfloat16)
    g_attn_out = dot_left(saved["out"], d_a)
    d_out = dot_right(d_a, attn_out).astype(jnp.bfloat16).reshape(sents, local, HEADS, HEAD_DIM)
    key_all, value_all = (
        lax.all_gather(shortened(saved["keys"]), "seq", axis=1, tiled=True),
        lax.all_gather(shortened(saved["values"]), "seq", axis=1, tiled=True),
    )
    query = saved["query"]
    raw, live = scores(query, key_all, lens)
    prob = jnp.where(live, jnp.exp(raw - saved["lse"][..., None]), 0.0)
    prob_b = prob.astype(jnp.bfloat16)
    d_value_all = jnp.einsum("shqk,sqhd->skhd", prob_b, d_out, preferred_element_type=jnp.float32)
    d_prob = jnp.einsum("sqhd,skhd->shqk", d_out, value_all, preferred_element_type=jnp.float32)
    d_score = (prob * (d_prob - jnp.sum(prob * d_prob, axis=-1, keepdims=True))).astype(
        jnp.bfloat16
    )
    d_query = (
        jnp.einsum("shqk,skhd->sqhd", d_score, key_all, preferred_element_type=jnp.float32) * 0.125
    )
    d_key_all = (
        jnp.einsum("shqk,sqhd->skhd", d_score, query, preferred_element_type=jnp.float32) * 0.125
    )
    d_key, d_value = (
        lax.psum_scatter(
            d_key_all.astype(jnp.bfloat16), "seq", scatter_dimension=1, tiled=True
        ).astype(jnp.float32),
        lax.psum_scatter(
            d_value_all.astype(jnp.bfloat16), "seq", scatter_dimension=1, tiled=True
        ).astype(jnp.float32),
    )
    rows = sents * local
    d_proj = jnp.concatenate(
        [d_query.reshape(rows, width), d_key.reshape(rows, width), d_value.reshape(rows, width)],
        axis=1,
    ).astype(jnp.bfloat16)
    g_attn_in = dot_left(saved["hin"], d_proj)
    d_h0 = d_r1 + dot_right(d_proj, attn_in)
    bias_sums = jnp.sum(d_proj.astype(jnp.float32), axis=0)
    d_hb = jnp.sum(d_f.astype(jnp.float32), axis=0).reshape(FF // width, width)
    rows_mid = jnp.stack(
        [
            bias_sums[:width],
            bias_sums[2 * width :],
            jnp.sum(d_a.astype(jnp.float32), axis=0),
            d_g1,
            d_b1,
        ]
    )
    rows_end = jnp.stack([jnp.sum(d_y.astype(jnp.float32), axis=0), d_g2, d_b2n])
    return (d_h0, (g_attn_in, g_attn_out, g_ff_in, g_ff_out), rows_mid, d_hb, rows_end)


def body(
    token_ids,
    lengths,
    labeled,
    gold,
    embed,
    position,
    attn_in,
    attn_out,
    ff_in,
    ff_out,
    vectors,
    mom_embed,
    mom_position,
    mom_attn_in,
    mom_attn_out,
    mom_ff_in,
    mom_ff_out,
    mom_vectors,
    avg_embed,
    avg_position,
    avg_attn_in,
    avg_attn_out,
    avg_ff_in,
    avg_ff_out,
    avg_vectors,
):
    bf = jnp.bfloat16
    full = (
        lax.all_gather(shortened(embed.astype(bf)), ("dp", "seq"), axis=0, tiled=True),
        lax.all_gather(shortened(position.astype(bf)), ("dp", "seq"), axis=1, tiled=True),
        lax.all_gather(shortened(attn_in.astype(bf)), ("dp", "seq"), axis=0, tiled=True),
        lax.all_gather(shortened(attn_out.astype(bf)), ("dp", "seq"), axis=0, tiled=True),
        lax.all_gather(shortened(ff_in.astype(bf)), ("dp", "seq"), axis=0, tiled=True),
        lax.all_gather(shortened(ff_out.astype(bf)), ("dp", "seq"), axis=0, tiled=True),
        lax.all_gather(shortened(vectors.astype(bf)), ("dp", "seq"), axis=1, tiled=True),
    )
    table, pos_table, w_qkv, w_out, w_in, w_back, vec_b = full
    vec = vec_b.astype(jnp.float32)
    pairs_here, _, local = token_ids.shape
    sents = 2 * pairs_here
    width = table.shape[1]
    rows = sents * local
    offset = lax.axis_index("seq") * local
    ids = token_ids.reshape(sents, local)
    lens = lengths.reshape(sents)
    lens_f = lens.astype(jnp.float32)
    pos_rows = lax.dynamic_slice_in_dim(pos_table, offset, local, 0).astype(jnp.float32)
    summed = jnp.take(table, ids, axis=0).astype(jnp.float32) + pos_rows[None]
    h0, back_embed = jax.vjp(layer_norm, summed, vec[0], vec[1])
    layer_weights = (w_qkv, w_out, w_in, w_back, vec)
    h2, saved = layer_forward(h0.reshape(rows, width), layer_weights, lens, sents, local)
    keep = ((offset + jnp.arange(local))[None, :] < lens[:, None]).astype(jnp.float32)
    partial_sum = jnp.sum(h2.reshape(sents, local, width) * keep[:, :, None], axis=1)
    pooled_sum = lax.psum(partial_sum, "seq")
    lab = labeled.astype(jnp.float32)

    def head(pooled_total):
        pooled = (pooled_total / lens_f[:, None]).reshape(pairs_here, 2, width)
        first, second = (pooled[:, 0], pooled[:, 1])
        cos = (
            jnp.sum(first * second, axis=-1)
            * lax.rsqrt(jnp.sum(first * first, axis=-1) + EPS)
            * lax.rsqrt(jnp.sum(second * second, axis=-1) + EPS)
        )
        miss = cos - gold
        return jnp.sum(lab * miss * miss)

    loss_here, back_head = jax.vjp(head, pooled_sum)
    loss_sum, count_all = lax.psum((loss_here, jnp.sum(lab)), "dp")
    count = jnp.maximum(count_all, 1.0)
    d_pooled = back_head(1.0 / count)[0]
    d_h2 = (keep[:, :, None] * d_pooled[:, None, :]).reshape(rows, width)
    d_h0, mats, rows_mid, d_hb, rows_end = layer_backward(
        d_h2, saved, layer_weights, lens, sents, local
    )
    d_x, d_ge, d_be = back_embed(d_h0.reshape(sents, local, width))
    g_embed = jnp.zeros(table.shape, jnp.float32).at[ids.reshape(-1)].add(d_x.reshape(rows, width))
    g_position = lax.dynamic_update_slice_in_dim(
        jnp.zeros(pos_table.shape, jnp.float32), jnp.sum(d_x, axis=0), offset, 0
    )
    g_vectors = jnp.concatenate([jnp.stack([d_ge, d_be]), rows_mid, d_hb, rows_end], axis=0)
    grads = (
        lax.psum_scatter(g_embed, ("dp", "seq"), scatter_dimension=0, tiled=True),
        lax.psum_scatter(g_position, ("dp", "seq"), scatter_dimension=1, tiled=True),
        lax.psum_scatter(mats[0], ("dp", "seq"), scatter_dimension=0, tiled=True),
        lax.psum_scatter(mats[1], ("dp", "seq"), scatter_dimension=0, tiled=True),
        lax.psum_scatter(mats[2], ("dp", "seq"), scatter_dimension=0, tiled=True),
        lax.psum_scatter(mats[3], ("dp", "seq"), scatter_dimension=0, tiled=True),
        lax.psum_scatter(g_vectors, ("dp", "seq"), scatter_dimension=1, tiled=True),
    )
    squares = sum((jnp.sum(g * g) for g in grads))
    norm = jnp.sqrt(lax.psum(squares, ("dp", "seq")))
    scale = jnp.minimum(1.0, CLIP / (norm + 1e-06))
    weights = (embed, position, attn_in, attn_out, ff_in, ff_out, vectors)
    moms = (mom_embed, mom_position, mom_attn_in, mom_attn_out, mom_ff_in, mom_ff_out, mom_vectors)
    avgs = (avg_embed, avg_position, avg_attn_in, avg_attn_out, avg_ff_in, avg_ff_out, avg_vectors)
    news, next_moms, next_avgs = ([], [], [])
    for weight, grad, mom, avg in zip(weights, grads, moms, avgs):
        clipped = grad * scale
        moment = MOMENT * mom + clipped
        fresh = weight - RATE * (clipped + MOMENT * moment)
        news.append(fresh)
        next_moms.append(moment)
        next_avgs.append(DECAY * avg + (1.0 - DECAY) * fresh)
    return (
        loss_sum,
        count,
        norm,
        news[0],
        news[1],
        news[2],
        news[3],
        news[4],
        news[5],
        news[6],
        next_moms[0],
        next_moms[1],
        next_moms[2],
        next_moms[3],
        next_moms[4],
        next_moms[5],
        next_moms[6],
        next_avgs[0],
        next_avgs[1],
        next_avgs[2],
        next_avgs[3],
        next_avgs[4],
        next_avgs[5],
        next_avgs[6],
    )


def solution(mesh):
    placed = (
        P("dp", None, "seq"),
        P("dp", None),
        P("dp"),
        P("dp"),
        P(("dp", "seq"), None),
        P(None, ("dp", "seq")),
        P(("dp", "seq"), None),
        P(("dp", "seq"), None),
        P(("dp", "seq"), None),
        P(("dp", "seq"), None),
        P(None, ("dp", "seq")),
        P(("dp", "seq"), None),
        P(None, ("dp", "seq")),
        P(("dp", "seq"), None),
        P(("dp", "seq"), None),
        P(("dp", "seq"), None),
        P(("dp", "seq"), None),
        P(None, ("dp", "seq")),
        P(("dp", "seq"), None),
        P(None, ("dp", "seq")),
        P(("dp", "seq"), None),
        P(("dp", "seq"), None),
        P(("dp", "seq"), None),
        P(("dp", "seq"), None),
        P(None, ("dp", "seq")),
    )
    return jax.shard_map(
        body,
        mesh=mesh,
        in_specs=placed,
        out_specs=(
            P(),
            P(),
            P(),
            P(("dp", "seq"), None),
            P(None, ("dp", "seq")),
            P(("dp", "seq"), None),
            P(("dp", "seq"), None),
            P(("dp", "seq"), None),
            P(("dp", "seq"), None),
            P(None, ("dp", "seq")),
            P(("dp", "seq"), None),
            P(None, ("dp", "seq")),
            P(("dp", "seq"), None),
            P(("dp", "seq"), None),
            P(("dp", "seq"), None),
            P(("dp", "seq"), None),
            P(None, ("dp", "seq")),
            P(("dp", "seq"), None),
            P(None, ("dp", "seq")),
            P(("dp", "seq"), None),
            P(("dp", "seq"), None),
            P(("dp", "seq"), None),
            P(("dp", "seq"), None),
            P(None, ("dp", "seq")),
        ),
        check_vma=False,
    )
```

profile of v0, /device:TPU:0, one launch (start us, length us, event | category | flops | bytes accessed | tf_op | source)
XLA Modules:
  0.0 2422.8 jit_solution(15125660576407082122)
XLA Ops:
  7.3 3.2 convert_element_type.125
  11.3 44.8 %all-gather = bf16[32,24,14]{1,2,0:T(8,128)(2,1)S(1)} all-gather(bf16[1,24,14]{1,2,0:T(8,128)(2,1)S(1)} %convert_bitcast_fusion.1), channel_id=1, replica_groups=mesh['dp'=8,'seq'=4] {'dp','seq'}, dimensions={0}, use_global_device_ids=true | all-gather | bytes 22176 | tf_op jit(solution)/shard_map/all_gather | solution.py:197
  56.5 42.2 %all_gather.31 = bf16[512,768]{0,1:T(8,128)(2,1)S(1)} all-gather(bf16[512,24]{0,1:T(8,128)(2,1)S(1)} %convert_element_type.127), channel_id=1, replica_groups=mesh['dp'=8,'seq'=4] {'dp','seq'}, dimensions={1}, use_global_device_ids=true | all-gather | bytes 811008 | tf_op jit(solution)/shard_map/all_gather | solution.py:192
  100.9 179.9 %all-gather.9.cloned.1.call-done = bf16[30720,768]{1,0:T(8,128)(2,1)} async-done(((bf16[960,768]{1,0:T(8,128)(2,1)}), bf16[30720,768]{1,0:T(8,128)(2,1)}) %all-gather.9.cloned.1.call-update) | async-done | bytes 47185936 | tf_op jit(solution)/shard_map/all_gather | solution.py:191
  280.7 14.1 gather_fusion
  298.3 44.2 %all-gather.11.cloned.1.call-done = bf16[768,2304]{1,0:T(8,128)(2,1)} async-done(((bf16[24,2304]{1,0:T(8,128)(2,1)}), bf16[768,2304]{1,0:T(8,128)(2,1)}) %all-gather.11.cloned.1.call-update) | async-done | bytes 3538960 | tf_op jit(solution)/shard_map/all_gather | solution.py:193
  342.5 6.0 add_convert_fusion.1
  348.5 2.0 fusion.61
  350.5 2.6 copy.99
  356.5 2.6 copy.95
  381.1 21.6 all-gather.15.cloned.1.call-done
  402.7 13.8 select_reduce_fusion.1
  416.5 11.6 select_reduce_fusion
  428.2 23.7 all-gather.13.cloned.1.call-done
  451.9 12.8 fusion.25
  465.9 43.4 %all-gather.17.cloned.1.call-done = bf16[768,768]{1,0:T(8,128)(2,1)} async-done(((bf16[24,768]{1,0:T(8,128)(2,1)}), bf16[768,768]{1,0:T(8,128)(2,1)}) %all-gather.17.cloned.1.call-update) | async-done | bytes 1179664 | tf_op jit(solution)/shard_map/all_gather | solution.py:194
  509.3 3.7 fusion.63
  515.3 59.9 %all-gather.19.cloned.1.call-done = bf16[768,3072]{1,0:T(8,128)(2,1)} async-done(((bf16[24,3072]{1,0:T(8,128)(2,1)}), bf16[768,3072]{1,0:T(8,128)(2,1)}) %all-gather.19.cloned.1.call-update) | async-done | bytes 4718608 | tf_op jit(solution)/shard_map/all_gather | solution.py:195
  575.3 38.7 %multiply_convert_fusion.2 = (bf16[1024,3072]{1,0:T(8,128)(2,1)}, f32[1024,3072]{1,0:T(8,128)}, f32[1024,3072]{1,0:T(8,128)}) fusion(f32[3072]{0:T(1024)S(1)} %copy-done.67, bf16[768,3072]{1,0:T(8,128)(2,1)} %all-gather.19.cloned.1.call-done, f32[1024,768]{1,0:T(8,128)} %copy-done.3, f32[768]{0:T(1024)S(1)} %copy-done.43, f32[768]{0:T(1024)S(1)} %copy-done.41, ...), kind=kOutput, calls=%fused_computation.13 | convolution fusion | flops 5043388416 | bytes 39348224 | tf_op jit(solution)/shard_map/dot_general | solution.py:86
  613.9 27.2 %all-gather.21.cloned.1.call-done = bf16[3072,768]{1,0:T(8,128)(2,1)} async-done(((bf16[96,768]{1,0:T(8,128)(2,1)}), bf16[3072,768]{1,0:T(8,128)(2,1)}) %all-gather.21.cloned.1.call-update) | async-done | bytes 4718608 | tf_op jit(solution)/shard_map/all_gather | solution.py:196
  641.2 8.8 fusion.64
  652.7 11.4 psum.28
  665.0 20.1 all-reduce.3
  686.0 3.5 fusion.15
  691.0 2.1 convert_reduce_fusion.2
  693.1 18.9 convert_reduce_fusion
  712.0 10.1 multiply_reduce_fusion.2
  727.3 2.6 convolution_convert_fusion
  729.9 2.6 copy.103
  735.5 13.0 convert_bitcast_fusion
  748.5 23.7 copy.113
  772.1 21.3 reshape.480
  793.5 23.2 multiply_reduce_fusion
  816.8 20.8 multiply_convert_fusion
  837.6 4.6 copy-done
  842.2 3.6 fusion.7
  845.8 23.7 copy.111
  869.5 21.3 reshape.478
  890.9 4.7 fusion.22
  895.6 11.6 fusion.53
  908.6 11.4 fusion.66
  920.0 10.9 fusion.26
  933.7 6.2 reshape.481
  940.0 7.5 copy.109
  947.6 6.2 reshape.479
  953.9 7.5 copy.107
  964.9 8.7 multiply_reduce_fusion.3
  975.5 2.3 fusion.9
  981.2 9.6 fusion.65
  991.5 1.9 broadcast_add_fusion
  993.5 30.5 %broadcast_in_dim.125 = f32[30720,768]{1,0:T(8,128)} broadcast(f32[]{:T(128)} %constant.53.clone.1), dimensions={} | broadcast | bytes 94371840 | tf_op jit(solution)/shard_map/broadcast_in_dim | solution.py:239
  1023.9 131.3 %scatter_fusion = f32[30720,768]{1,0:T(8,128)} fusion(f32[30720,768]{1,0:T(8,128)} %broadcast_in_dim.125, s32[1024]{0:T(1024)S(1)} %bitcast.201, f32[1024,768]{1,0:T(8,128)S(1)} %copy-done.13), kind=kCustom, calls=%fused_computation.1 | custom fusion | flops 786432 | bytes 9441280 | tf_op jit(solution)/shard_map/scatter-add | solution.py:239
  1157.9 3.0 convert_reduce_fusion.1
  1161.2 40.2 %all-reduce.2 = f32[14,768]{1,0:T(8,128)S(1)} all-reduce(f32[14,768]{1,0:T(8,128)S(1)} %concatenate.12), channel_id=10, replica_groups=mesh['dp'=8,'seq'=4] {'dp','seq'}, use_global_device_ids=true, to_apply=%region_50.51.clone | all-reduce | flops 10752 | bytes 86016
  1203.8 130.6 %reduce-scatter.24.cloned.1.call-done = f32[96,768]{1,0:T(8,128)} async-done(((f32[3072,768]{1,0:T(8,128)}), f32[96,768]{1,0:T(8,128)}) %reduce-scatter.24.cloned.1.call-update) | async-done | bytes 294928 | tf_op jit(solution)/shard_map/reduce_scatter | solution.py:250
  1336.1 101.0 %reduce-scatter.16.cloned.1.call-done = f32[512,24]{0,1:T(8,128)} async-done(((f32[512,768]{0,1:T(8,128)}), f32[512,24]{0,1:T(8,128)}) %reduce-scatter.16.cloned.1.call-update) | async-done | bytes 49168 | tf_op jit(solution)/shard_map/reduce_scatter | solution.py:246
  1438.5 123.3 %reduce-scatter.18.cloned.1.call-done = f32[24,2304]{1,0:T(8,128)} async-done(((f32[768,2304]{1,0:T(8,128)}), f32[24,2304]{1,0:T(8,128)}) %reduce-scatter.18.cloned.1.call-update) | async-done | bytes 221200 | tf_op jit(solution)/shard_map/reduce_scatter | solution.py:247
  1563.4 784.8 %reduce-scatter.14.cloned.1.call-done = f32[960,768]{1,0:T(8,128)} async-done(((f32[30720,768]{1,0:T(8,128)}), f32[960,768]{1,0:T(8,128)}) %reduce-scatter.14.cloned.1.call-update) | async-done | bytes 2949136 | tf_op jit(solution)/shard_map/reduce_scatter | solution.py:245
  2348.2 3.3 multiply_reduce_fusion.10
  2356.1 39.4 %psum.31 = f32[]{:T(128)} all-reduce(f32[]{:T(128)S(6)} %add.388), channel_id=1, replica_groups=mesh['dp'=8,'seq'=4] {'dp','seq'}, use_global_device_ids=true, to_apply=%region_52.53 | all-reduce | flops 1 | bytes 8 | tf_op jit(solution)/shard_map/psum | solution.py:254
  2401.1 2.3 add_multiply_fusion.3
  2403.3 2.1 add_multiply_fusion.2
  2405.5 2.0 add_multiply_fusion.1
  2407.5 6.1 add_multiply_fusion
  (288 shorter events, 77.4 us)
Async XLA Ops:
  7.2 4.1 copy-start.33
  7.2 4.1 copy-start.56
  7.2 273.5 %all-gather.9.cloned.1.call-start = ((), (), s32[]{:S(2)}) async-start(), calls=%async_computation.8 | async-start | bytes 48660480 | tf_op jit(solution)/shard_map/all_gather | solution.py:191
  10.4 89.8 %copy-start.47 = (s32[4,2,128]{2,1,0:T(2,128)S(1)}, s32[4,2,128]{2,1,0:T(2,128)}, u32[]{:S(2)}) copy-start(s32[4,2,128]{2,1,0:T(2,128)} %param.25) | copy-start | bytes 12292
  10.5 332.0 %all-gather.11.cloned.1.call-start = ((), (), s32[]{:S(2)}) async-start(), calls=%async_computation.9 | async-start | bytes 3649536 | tf_op jit(solution)/shard_map/all_gather | solution.py:193
  11.2 391.5 %all-gather.15.cloned.1.call-start = ((), (), s32[]{:S(2)}) async-start(), calls=%async_computation.11 | async-start | bytes 7864320 | tf_op jit(solution)/shard_map/all_gather | solution.py:72
  56.5 44.4 %copy-start.34 = (f32[768,14]{0,1:T(8,128)}, f32[768,14]{0,1:T(8,128)S(1)}, u32[]{:S(2)}) copy-start(f32[768,14]{0,1:T(8,128)S(1)} %reshape.477) | copy-start | bytes 129028
  98.9 410.4 %copy-start.9 = (f32[128,768]{1,0:T(8,128)}, f32[128,768]{1,0:T(8,128)S(1)}, u32[]{:S(2)}) copy-start(f32[128,768]{1,0:T(8,128)S(1)} %copy.92) | copy-start | bytes 1179652
  99.6 197.5 %copy-start.49 = (f32[768]{0:T(1024)}, f32[768]{0:T(1024)S(1)}, u32[]{:S(2)}) copy-start(f32[768]{0:T(1024)S(1)} %get-tuple-element.40) | copy-start | bytes 9220
  99.6 409.7 %copy-start.35 = (f32[768]{0:T(1024)}, f32[768]{0:T(1024)S(1)}, u32[]{:S(2)}) copy-start(f32[768]{0:T(1024)S(1)} %get-tuple-element.41) | copy-start | bytes 9220
  100.9 194.8 %copy-start.60 = (pred[8,128]{1,0:T(8,128)(4,1)}, pred[8,128]{1,0:T(8,128)(4,1)S(1)}, u32[]{:S(2)}) copy-start(pred[8,128]{1,0:T(8,128)(4,1)S(1)} %compare_and_fusion) | copy-start | bytes 3076
  294.9 214.4 %copy-start.1 = (bf16[1024,768]{1,0:T(8,128)(2,1)}, bf16[1024,768]{1,0:T(8,128)(2,1)S(1)}, u32[]{:S(2)}) copy-start(bf16[1024,768]{1,0:T(8,128)(2,1)S(1)} %gather_fusion) | copy-start | bytes 4718596
  295.6 213.7 %copy-start.37 = (f32[1024]{0:T(1024)}, f32[1024]{0:T(1024)S(1)}, u32[]{:S(2)}) copy-start(f32[1024]{0:T(1024)S(1)} %get-tuple-element.96) | copy-start | bytes 12292
  296.6 212.7 %copy-start.39 = (f32[1024]{0:T(1024)}, f32[1024]{0:T(1024)S(1)}, u32[]{:S(2)}) copy-start(f32[1024]{0:T(1024)S(1)} %bitcast_rsqrt_fusion) | copy-start | bytes 12292
  298.3 44.2 %copy-start.19 = (bf16[1024,768]{1,0:T(8,128)(2,1)}, bf16[1024,768]{1,0:T(8,128)(2,1)S(1)}, u32[]{:S(2)}) copy-start(bf16[1024,768]{1,0:T(8,128)(2,1)S(1)} %fusion.20) | copy-start | bytes 4718596
  356.5 95.4 %all-gather.13.cloned.1.call-start = ((), (), s32[]{:S(2)}) async-start(), calls=%async_computation.10 | async-start | bytes 7864320 | tf_op jit(solution)/shard_map/all_gather | solution.py:77
  361.0 7.4 copy-start.75
  362.6 146.7 %all-gather.17.cloned.1.call-start = ((), (), s32[]{:S(2)}) async-start(), calls=%async_computation.12 | async-start | bytes 1216512 | tf_op jit(solution)/shard_map/all_gather | solution.py:194
  364.2 211.1 %all-gather.19.cloned.1.call-start = ((), (), s32[]{:S(2)}) async-start(), calls=%async_computation.13 | async-start | bytes 4866048 | tf_op jit(solution)/shard_map/all_gather | solution.py:195
  365.9 275.3 %all-gather.21.cloned.1.call-start = ((), (), s32[]{:S(2)}) async-start(), calls=%async_computation.14 | async-start | bytes 4866048 | tf_op jit(solution)/shard_map/all_gather | solution.py:196
  367.6 566.1 %reduce-scatter.28.cloned.1.call-start = ((), (), s32[]{:S(2)}) async-start(), calls=%async_computation.22 | async-start | bytes 7864320
  371.6 80.3 %copy-start.29 = (pred[8,512]{1,0:T(8,128)(4,1)}, pred[8,512]{1,0:T(8,128)(4,1)S(1)}, u32[]{:S(2)}) copy-start(pred[8,512]{1,0:T(8,128)(4,1)S(1)} %iota_compare_fusion) | copy-start | bytes 12292
  381.1 35.4 %copy-start.11 = (bf16[96,8,8,128]{3,2,1,0:T(8,128)(2,1)}, bf16[96,8,8,128]{3,2,1,0:T(8,128)(2,1)S(1)}, u32[]{:S(2)}) copy-start(bf16[96,8,8,128]{3,2,1,0:T(8,128)(2,1)S(1)} %copy.120) | copy-start | bytes 4718596
  428.2 23.7 copy-start.27
  464.7 44.6 %copy-start.50 = (f32[768]{0:T(1024)S(1)}, f32[768]{0:T(1024)}, u32[]{:S(2)}) copy-start(f32[768]{0:T(1024)} %copy-done.49) | copy-start | bytes 9220
  465.9 47.1 %copy-start.16 = (bf16[8,128,12,64]{1,0,3,2:T(8,128)(2,1)}, bf16[8,128,12,64]{1,0,3,2:T(8,128)(2,1)S(1)}, u32[]{:S(2)}) copy-start(bf16[8,128,12,64]{1,0,3,2:T(8,128)(2,1)S(1)} %copy.102) | copy-start | bytes 4718596
  513.1 62.1 %copy-start.41 = (f32[768]{0:T(1024)S(1)}, f32[768]{0:T(1024)}, u32[]{:S(2)}) copy-start(f32[768]{0:T(1024)} %get-tuple-element.36) | copy-start | bytes 9220
  513.1 62.1 %copy-start.43 = (f32[768]{0:T(1024)S(1)}, f32[768]{0:T(1024)}, u32[]{:S(2)}) copy-start(f32[768]{0:T(1024)} %get-tuple-element.35) | copy-start | bytes 9220
  513.1 62.1 %copy-start.67 = (f32[3072]{0:T(1024)S(1)}, f32[3072]{0:T(1024)}, u32[]{:S(2)}) copy-start(f32[3072]{0:T(1024)} %add.364) | copy-start | bytes 36868
  575.2 65.9 %copy-start.4 = (f32[1024,768]{1,0:T(8,128)S(1)}, f32[1024,768]{1,0:T(8,128)}, u32[]{:S(2)}) copy-start(f32[1024,768]{1,0:T(8,128)} %copy-done.3) | copy-start | bytes 9437188
  575.2 65.9 %copy-start.70 = (f32[768]{0:T(1024)S(1)}, f32[768]{0:T(1024)}, u32[]{:S(2)}) copy-start(f32[768]{0:T(1024)} %get-tuple-element.34) | copy-start | bytes 9220
  650.1 14.0 copy-start.73
  650.1 14.3 copy-start.74
  650.1 14.3 copy-start.76
  650.1 35.9 %copy-start.51 = (f32[1024]{0:T(1024)S(1)}, f32[1024]{0:T(1024)}, u32[]{:S(2)}) copy-start(f32[1024]{0:T(1024)} %fusion.43) | copy-start | bytes 12292
  685.9 3.6 copy-start.6
  686.0 5.0 copy-start.31
  723.6 3.7 copy-start.22
  729.9 5.6 copy-start.28
  729.9 5.6 copy-start.30
  793.5 154.1 %reduce-scatter.26.cloned.1.call-start = ((), (), s32[]{:S(2)}) async-start(), calls=%async_computation.21 | async-start | bytes 7864320
  816.8 25.4 %copy-start.12 = (bf16[96,8,8,128]{3,2,1,0:T(8,128)(2,1)S(1)}, bf16[96,8,8,128]{3,2,1,0:T(8,128)(2,1)}, u32[]{:S(2)}) copy-start(bf16[96,8,8,128]{3,2,1,0:T(8,128)(2,1)} %copy-done.11) | copy-start | bytes 4718596
  837.6 4.6 copy-start
  890.8 265.6 %reduce-scatter.20.cloned.1.call-start = ((), (), s32[]{:S(2)}) async-start(), calls=%async_computation.18 | async-start | bytes 2433024 | tf_op jit(solution)/shard_map/reduce_scatter | solution.py:248
  895.6 306.5 %reduce-scatter.22.cloned.1.call-start = ((), (), s32[]{:S(2)}) async-start(), calls=%async_computation.19 | async-start | bytes 9732096 | tf_op jit(solution)/shard_map/reduce_scatter | solution.py:249
  907.2 427.2 %reduce-scatter.24.cloned.1.call-start = ((), (), s32[]{:S(2)}) async-start(), calls=%async_computation.20 | async-start | bytes 9732096 | tf_op jit(solution)/shard_map/reduce_scatter | solution.py:250
  920.0 517.1 %reduce-scatter.16.cloned.1.call-start = ((), (), s32[]{:S(2)}) async-start(), calls=%async_computation.16 | async-start | bytes 1622016 | tf_op jit(solution)/shard_map/reduce_scatter | solution.py:246
  961.4 3.4 copy-start.10
  961.4 3.4 copy-start.36
  961.4 3.4 copy-start.38
  961.5 3.4 copy-start.40
  964.9 8.7 copy-start.46
  981.2 580.7 %reduce-scatter.18.cloned.1.call-start = ((), (), s32[]{:S(2)}) async-start(), calls=%async_computation.17 | async-start | bytes 7299072 | tf_op jit(solution)/shard_map/reduce_scatter | solution.py:247
  990.8 1357.4 %reduce-scatter.14.cloned.1.call-start = ((), (), s32[]{:S(2)}) async-start(), calls=%async_computation.15 | async-start | bytes 97320960 | tf_op jit(solution)/shard_map/reduce_scatter | solution.py:245
  993.5 30.5 %copy-start.13 = (f32[1024,768]{1,0:T(8,128)S(1)}, f32[1024,768]{1,0:T(8,128)}, u32[]{:S(2)}) copy-start(f32[1024,768]{1,0:T(8,128)} %broadcast_add_fusion) | copy-start | bytes 9437188
  1161.0 1235.3 %copy-start.57 = (f32[14,24]{1,0:T(8,128)S(1)}, f32[14,24]{1,0:T(8,128)}, u32[]{:S(2)}) copy-start(f32[14,24]{1,0:T(8,128)} %param.35) | copy-start | bytes 4036
  1161.0 1235.3 %copy-start.68 = (f32[14,24]{1,0:T(8,128)S(1)}, f32[14,24]{1,0:T(8,128)}, u32[]{:S(2)}) copy-start(f32[14,24]{1,0:T(8,128)} %param.49) | copy-start | bytes 4036
  1201.4 362.0 %copy-start.42 = (f32[14,768]{1,0:T(8,128)}, f32[14,768]{1,0:T(8,128)S(1)}, u32[]{:S(2)}) copy-start(f32[14,768]{1,0:T(8,128)S(1)} %all-reduce.2) | copy-start | bytes 129028
  1202.1 1201.2 %copy-start.23 = (f32[24,3072]{1,0:T(8,128)S(1)}, f32[24,3072]{1,0:T(8,128)}, u32[]{:S(2)}) copy-start(f32[24,3072]{1,0:T(8,128)} %param.33) | copy-start | bytes 884740
  1563.4 842.0 %copy-start.24 = (f32[96,768]{1,0:T(8,128)S(1)}, f32[96,768]{1,0:T(8,128)}, u32[]{:S(2)}) copy-start(f32[96,768]{1,0:T(8,128)} %param.34) | copy-start | bytes 884740
  2348.2 59.3 %copy-start.18 = (f32[960,768]{1,0:T(8,128)S(1)}, f32[960,768]{1,0:T(8,128)}, u32[]{:S(2)}) copy-start(f32[960,768]{1,0:T(8,128)} %param.43) | copy-start | bytes 8847364
  2396.2 9.2 copy-start.25
  2399.2 8.3 copy-start.14
  2399.2 8.3 copy-start.15
  (28 other events, 43.6 us)
Sparse Core Ops, SparseCore 0:
  11.5 269.1 all-gather.8
  284.2 58.2 all-gather.10
  356.6 45.9 all-gather.14
  404.6 47.2 all-gather.12
  455.2 54.0 all-gather.16
  512.6 62.5 all-gather.18
  578.7 62.4 all-gather.20
  793.6 55.5 reduce-scatter.27
  891.0 56.6 reduce-scatter.25
  953.3 99.0 reduce-scatter.19
  1059.3 134.5 reduce-scatter.21
  1199.7 134.6 reduce-scatter.23
  1341.1 95.9 reduce-scatter.15
  1443.6 118.2 reduce-scatter.17
  1568.1 780.0 reduce-scatter.13
where the time goes:
time: 2440 us; the launch traced here: 2420 us
  waiting for transfers between devices  1540 us (63%)
  other arithmetic  232 us (10%)
  local copies, waits for them, and re-layouts  216 us (9%)
  matrix products  212 us (9%)
  blocking collectives  198 us (8%)
    reduce_scatter x1, waiting for transfers between devices, body(): lax.psum_scatter(g_embed, ('dp', 'seq'), scatter_dimension=0, tiled=True)  785 us
    all_gather x1, waiting for transfers between devices, body(): lax.all_gather(shortened(embed.astype(bf)), ('dp', 'seq'), axis=0, tiled=...  180 us
    scatter-add x1, other arithmetic, body(): jnp.zeros(table.shape, jnp.float32).at[ids.reshape(-1)]  131 us
    reduce_scatter x1, waiting for transfers between devices, body(): lax.psum_scatter(mats[3], ('dp', 'seq'), scatter_dimension=0, tiled=True)  131 us
    unnamed x167, local copies, waits for them, and re-layouts  129 us
    reduce_scatter x1, waiting for transfers between devices, body(): lax.psum_scatter(mats[0], ('dp', 'seq'), scatter_dimension=0, tiled=True)  123 us
    reduce_scatter x1, waiting for transfers between devices, body(): lax.psum_scatter(g_position, ('dp', 'seq'), scatter_dimension=1, tiled=True)  101 us
    all_gather x1, waiting for transfers between devices, body(): lax.all_gather(shortened(ff_in.astype(bf)), ('dp', 'seq'), axis=0, tiled=...  59.9 us
  transfers between devices with their start and end apart: 15, of which 12 were waited for; matrix products, arithmetic and copies ran while one was open for 20% of the time, Pallas kernels for 0%

commit v1 on v0

v1 whole, which is shorter than its diff:
```python
import jax
import jax.numpy as jnp
from jax import lax
from jax.sharding import PartitionSpec as P

HEADS = 12
HEAD_DIM = 64
EPS = 1e-06
RATE = 10000.0
MOMENT = 0.5
DECAY = 0.5
CLIP = 0.01
SLOTS = 32
AXES = ("dp", "seq")
bf = jnp.bfloat16
f32 = jnp.float32


def layer_norm(v, gain, bias):
    center = v - jnp.mean(v, axis=-1, keepdims=True)
    spread = jnp.mean(center * center, axis=-1, keepdims=True)
    return center * lax.rsqrt(spread + EPS) * gain + bias


def exact_gelu(v):
    return jax.nn.gelu(v, approximate=False)


def mm(left, right):
    return jnp.dot(left, right, preferred_element_type=f32)


def mm_left(left, right):
    return lax.dot_general(left, right, (((0,), (0,)), ((), ())), preferred_element_type=f32)


def mm_right(left, right):
    return lax.dot_general(left, right, (((1,), (1,)), ((), ())), preferred_element_type=f32)


def exchange(v):
    return lax.all_to_all(v, AXES, 0, 0, tiled=True)


def route(ids, valid, per_owner):
    count = ids.shape[0]
    spot = jnp.arange(count, dtype=jnp.int32)
    owner = ids // per_owner
    local = ids - owner * per_owner
    key = jnp.where(valid, ids, -1 - spot)
    alike = key[:, None] == key[None, :]
    first_at = jnp.min(jnp.where(alike, spot[None, :], count), axis=1)
    first = (first_at == spot) & valid
    before = (owner[:, None] == owner[None, :]) & first[None, :] & (spot[None, :] < first_at[:, None])
    rank = jnp.sum(before.astype(jnp.int32), axis=1)
    return owner, local, first, rank


def requests(owner, local, first, rank, start, devices):
    slot = jnp.where(first & (rank >= start) & (rank < start + SLOTS), owner * SLOTS + rank - start, -1)
    line = jnp.arange(devices * SLOTS, dtype=jnp.int32)
    hit = slot[None, :] == line[:, None]
    return jnp.max(jnp.where(hit, local[None, :], -1), axis=1)


def token_slots(owner, valid, rank, start):
    return jnp.where(valid & (rank >= start) & (rank < start + SLOTS), owner * SLOTS + rank - start, -1)


def one_hot(index, size):
    return (index[:, None] == jnp.arange(size, dtype=jnp.int32)[None, :]).astype(bf)


def forward_backward(summed, weights, vec, lens, labeled, gold, count):
    w_qkv, w_out, w_in, w_back = weights
    sents, length, width = summed.shape
    rows = sents * length
    hidden_rows = w_in.shape[1] // width
    h0, back_embed = jax.vjp(layer_norm, summed.reshape(rows, width), vec[0], vec[1])
    hin = h0.astype(bf)
    bias = jnp.concatenate([vec[2], jnp.zeros_like(vec[2]), vec[3]])
    proj = (mm(hin, w_qkv) + bias).astype(bf).reshape(sents, length, 3, HEADS, HEAD_DIM)
    query, keys, values = (proj[:, :, i].transpose(0, 2, 1, 3) for i in range(3))
    live = (jnp.arange(length)[None, :] < lens[:, None])
    mask = live[:, None, None, :]
    raw = jnp.einsum("shqd,shkd->shqk", query, keys, preferred_element_type=f32) * 0.125
    raw = jnp.where(mask, raw, -1e30)
    top = jnp.max(raw, axis=-1, keepdims=True)
    power = jnp.exp(raw - top)
    prob = power / jnp.sum(power, axis=-1, keepdims=True)
    prob_b = prob.astype(bf)
    out = jnp.einsum("shqk,shkd->shqd", prob_b, values, preferred_element_type=f32).astype(bf)
    out_b = out.transpose(0, 2, 1, 3).reshape(rows, width)
    branch = mm(out_b, w_out) + vec[4]
    h1, back_one = jax.vjp(layer_norm, h0 + branch, vec[5], vec[6])
    h1_b = h1.astype(bf)
    hidden = mm(h1_b, w_in) + vec[7 : 7 + hidden_rows].reshape(-1)
    act, back_act = jax.vjp(exact_gelu, hidden)
    act_b = act.astype(bf)
    mixed = mm(act_b, w_back) + vec[7 + hidden_rows]
    h2, back_two = jax.vjp(layer_norm, h1 + mixed, vec[8 + hidden_rows], vec[9 + hidden_rows])
    keep = live.astype(f32)
    pooled_sum = jnp.sum(h2.reshape(sents, length, width) * keep[:, :, None], axis=1)

    def head(total):
        pooled = (total / lens.astype(f32)[:, None]).reshape(sents // 2, 2, width)
        first, second = pooled[:, 0], pooled[:, 1]
        cos = (
            jnp.sum(first * second, axis=-1)
            * lax.rsqrt(jnp.sum(first * first, axis=-1) + EPS)
            * lax.rsqrt(jnp.sum(second * second, axis=-1) + EPS)
        )
        miss = cos - gold
        return jnp.sum(labeled * miss * miss)

    loss, back_head = jax.vjp(head, pooled_sum)
    d_pooled = back_head(1.0 / count)[0]
    d_h2 = (keep[:, :, None] * d_pooled[:, None, :]).reshape(rows, width)

    d_r2, d_g2, d_b2n = back_two(d_h2)
    d_y = d_r2.astype(bf)
    g_ff_out = mm_left(act_b, d_y)
    d_f = back_act(mm_right(d_y, w_back))[0].astype(bf)
    g_ff_in = mm_left(h1_b, d_f)
    d_r1, d_g1, d_b1 = back_one(d_r2 + mm_right(d_f, w_in))
    d_a = d_r1.astype(bf)
    g_attn_out = mm_left(out_b, d_a)
    d_out = mm_right(d_a, w_out).astype(bf).reshape(sents, length, HEADS, HEAD_DIM).transpose(0, 2, 1, 3)
    d_value = jnp.einsum("shqk,shqd->shkd", prob_b, d_out, preferred_element_type=f32)
    d_prob = jnp.einsum("shqd,shkd->shqk", d_out, values, preferred_element_type=f32)
    d_score = (prob * (d_prob - jnp.sum(prob * d_prob, axis=-1, keepdims=True))).astype(bf)
    d_query = jnp.einsum("shqk,shkd->shqd", d_score, keys, preferred_element_type=f32) * 0.125
    d_key = jnp.einsum("shqk,shqd->shkd", d_score, query, preferred_element_type=f32) * 0.125
    d_proj = jnp.concatenate(
        [d.astype(bf).transpose(0, 2, 1, 3).reshape(rows, width) for d in (d_query, d_key, d_value)], axis=1
    )
    g_attn_in = mm_left(hin, d_proj)
    d_h0 = d_r1 + mm_right(d_proj, w_qkv)
    bias_sums = jnp.sum(d_proj.astype(f32), axis=0)
    d_x, d_ge, d_be = back_embed(d_h0)
    g_vectors = jnp.concatenate(
        [
            jnp.stack([d_ge, d_be, bias_sums[:width], bias_sums[2 * width :], jnp.sum(d_a.astype(f32), axis=0), d_g1, d_b1]),
            jnp.sum(d_f.astype(f32), axis=0).reshape(hidden_rows, width),
            jnp.stack([jnp.sum(d_y.astype(f32), axis=0), d_g2, d_b2n]),
        ],
        axis=0,
    )
    return loss, (g_attn_in, g_attn_out, g_ff_in, g_ff_out), g_vectors, d_x


def body(
    token_ids, lengths, labeled, gold,
    embed, position, attn_in, attn_out, ff_in, ff_out, vectors,
    mom_embed, mom_position, mom_attn_in, mom_attn_out, mom_ff_in, mom_ff_out, mom_vectors,
    avg_embed, avg_position, avg_attn_in, avg_attn_out, avg_ff_in, avg_ff_out, avg_vectors,
):
    pairs_here, _, local = token_ids.shape
    seq = lax.axis_size("seq")
    devices = lax.axis_size("dp") * seq
    length = local * seq
    per_owner, width = embed.shape
    depth = attn_in.shape[0]
    hidden = ff_in.shape[1]
    nvec = vectors.shape[0]
    turns = ff_out.shape[0] // depth
    mine = pairs_here // seq
    sents = 2 * mine
    rows = sents * length
    spare = 128 - nvec

    shard = jnp.concatenate(
        [attn_in, attn_out, ff_in]
        + [ff_out[i * depth : (i + 1) * depth] for i in range(turns)]
        + [position.T, vectors.T, jnp.zeros((depth, spare), f32)],
        axis=1,
    ).astype(bf)
    full = lax.all_gather(shard, AXES, axis=0, tiled=True)

    ids = lax.all_to_all(token_ids, "seq", 0, 2, tiled=True).reshape(rows)
    turn = lax.axis_index("seq") * mine
    lens = lax.dynamic_slice_in_dim(lengths, turn, mine, 0).reshape(sents)
    lab = lax.dynamic_slice_in_dim(labeled, turn, mine, 0)
    goal = lax.dynamic_slice_in_dim(gold, turn, mine, 0)
    lab_f = lab.astype(f32)
    used = (jnp.arange(length)[None, :] < lens[:, None]) & (jnp.repeat(lab, 2) > 0)[:, None]
    used = used.reshape(rows)
    owner, place, first, rank = route(ids, used, per_owner)
    most = jnp.max(jnp.where(used, rank + 1, 0))
    asked = requests(owner, place, first, rank, 0, devices).reshape(devices, SLOTS)
    note = jnp.stack([most, jnp.sum(lab)])[None, :]
    note = jnp.broadcast_to(note, (devices, 2))
    got = exchange(jnp.concatenate([asked, note, jnp.zeros((devices, 126 - SLOTS), jnp.int32)], axis=1))
    rounds = (jnp.max(got[:, SLOTS]) + SLOTS - 1) // SLOTS
    count = jnp.maximum(jnp.sum(got[:, SLOTS + 1]).astype(f32), 1.0)

    table = embed.astype(bf)

    def fetch(wanted, start):
        picked = mm(one_hot(wanted, per_owner), table).astype(bf).reshape(devices, SLOTS, width)
        back = exchange(picked).reshape(devices * SLOTS, width)
        return mm(one_hot(token_slots(owner, used, rank, start), devices * SLOTS), back)

    wanted_first = got[:, :SLOTS].reshape(-1)
    found = fetch(wanted_first, 0)

    def more(state):
        step, total = state
        start = step * SLOTS
        wanted = exchange(requests(owner, place, first, rank, start, devices).reshape(devices, SLOTS)).reshape(-1)
        return step + 1, total + fetch(wanted, start)

    _, found = lax.while_loop(lambda state: state[0] < rounds, more, (jnp.int32(1), found))

    at = 3 * width
    w_qkv, w_out, w_in = full[:, :at], full[:, at : at + width], full[:, at + width : at + width + hidden]
    at = at + width + hidden
    w_back = (
        full[:, at : at + turns * width].reshape(devices, depth, turns, width).transpose(0, 2, 1, 3).reshape(hidden, width)
    )
    at = at + turns * width
    pos = full[:, at : at + length].T.astype(f32)
    vec = full[:, at + length : at + length + nvec].T.astype(f32)

    summed = found.reshape(sents, length, width) + pos[None]
    loss, mats, g_vec, d_x = forward_backward(summed, (w_qkv, w_out, w_in, w_back), vec, lens, lab_f, goal, count)

    scatter = lambda g: lax.psum_scatter(g.astype(bf), AXES, scatter_dimension=0, tiled=True).astype(f32)
    g_ff_out = scatter(mats[3])
    g_ff_in = scatter(mats[2])
    d_xb = d_x.astype(bf)
    g_rest = scatter(
        jnp.concatenate(
            [mats[0], mats[1], jnp.sum(d_x.reshape(sents, length, width), axis=0).T, g_vec.T, jnp.zeros((width, spare), f32)],
            axis=1,
        )
    )
    g_attn_in, g_attn_out = g_rest[:, : 3 * width], g_rest[:, 3 * width : 4 * width]
    g_position = g_rest[:, 4 * width : 4 * width + length].T
    g_vectors = g_rest[:, 4 * width + length : 4 * width + length + nvec].T

    def give(wanted, start):
        sums = mm_left(one_hot(token_slots(owner, used, rank, start), devices * SLOTS), d_xb).astype(bf)
        back = exchange(sums.reshape(devices, SLOTS, width)).reshape(devices * SLOTS, width)
        return mm_left(one_hot(wanted, per_owner), back)

    g_embed = give(wanted_first, 0)

    def more_back(state):
        step, total = state
        start = step * SLOTS
        wanted = exchange(requests(owner, place, first, rank, start, devices).reshape(devices, SLOTS)).reshape(-1)
        return step + 1, total + give(wanted, start)

    _, g_embed = lax.while_loop(lambda state: state[0] < rounds, more_back, (jnp.int32(1), g_embed))

    grads = (g_embed, g_position, g_attn_in, g_attn_out, g_ff_in, g_ff_out, g_vectors)
    squares = sum(jnp.sum(g * g) for g in grads)
    sums = exchange(jnp.broadcast_to(jnp.stack([squares, loss])[None, :], (devices, 2)))
    sums = jnp.sum(sums, axis=0)
    norm = jnp.sqrt(sums[0])
    loss_sum = sums[1]
    scale = jnp.minimum(1.0, CLIP / (norm + 1e-06))
    weights = (embed, position, attn_in, attn_out, ff_in, ff_out, vectors)
    moms = (mom_embed, mom_position, mom_attn_in, mom_attn_out, mom_ff_in, mom_ff_out, mom_vectors)
    avgs = (avg_embed, avg_position, avg_attn_in, avg_attn_out, avg_ff_in, avg_ff_out, avg_vectors)
    news, next_moms, next_avgs = [], [], []
    for weight, grad, mom, avg in zip(weights, grads, moms, avgs):
        clipped = grad * scale
        moment = MOMENT * mom + clipped
        fresh = weight - RATE * (clipped + MOMENT * moment)
        news.append(fresh)
        next_moms.append(moment)
        next_avgs.append(DECAY * avg + (1.0 - DECAY) * fresh)
    return (loss_sum, count, norm, *news, *next_moms, *next_avgs)


def solution(mesh):
    whole = (
        P(AXES, None),
        P(None, AXES),
        P(AXES, None),
        P(AXES, None),
        P(AXES, None),
        P(AXES, None),
        P(None, AXES),
    )
    return jax.shard_map(
        body,
        mesh=mesh,
        in_specs=(P("dp", None, "seq"), P("dp", None), P("dp"), P("dp")) + whole * 3,
        out_specs=(P(), P(), P()) + whole * 3,
        check_vma=False,
    )
```

time: 2440 us -> 719 us (0.29)
  waiting for transfers between devices: 1540 us -> 260 us
  blocking collectives: 198 us -> 0 us
  other arithmetic: 232 us -> 91 us
  local copies, waits for them, and re-layouts: 216 us -> 94.9 us
    reduce_scatter x6 -> x2, waiting for transfers between devices: 1140 us -> 27.7 us  [body(): lax.psum_scatter(g.astype(bf), AXES, scatter_dimension=0, tiled=True)]
    all_gather x7 -> x1, waiting for transfers between devices: 400 us -> 35.8 us  [body(): full = lax.all_gather(shard, AXES, axis=0, tiled=True)]
    scatter-add x1 -> x0, other arithmetic: 131 us -> none  [body(): jnp.zeros(table.shape, jnp.float32).at[ids.reshape(-1)]]
    unnamed x17 -> x5, waiting for transfers between devices: 0.4 us -> 111 us
    unnamed x167 -> x187, local copies, waits for them, and re-layouts: 129 us -> 23.4 us
    all_gather x2 -> x0, blocking collectives: 86.9 us -> none  [the longest x1 44.8 us: body(): lax.all_gather(shortened(vectors.astype(bf)), ('dp', 'seq'), axis=1, tile...]
    all_to_all x0 -> x5, waiting for transfers between devices: none -> 84.8 us  [the longest x4 81.8 us: exchange(): return lax.all_to_all(v, AXES, 0, 0, tiled=True)]
    psum x3 -> x0, blocking collectives: 70.9 us -> none  [the longest x1 39.4 us: body(): norm = jnp.sqrt(lax.psum(squares, ('dp', 'seq')))]
  transfers between devices with their start and end apart: 15 -> 9, of which waited for: 12 -> 8; matrix products, arithmetic and copies ran while one was open for 20% -> 26% of each run, Pallas kernels for 0% -> 0%
where the time goes in v1:
time: 719 us; the launch traced here: 710 us
  waiting for transfers between devices  260 us (36%)
  matrix products  215 us (30%)
  local copies, waits for them, and re-layouts  94.9 us (13%)
  other arithmetic  91 us (13%)
  between operations  29.2 us (4%)
  starting transfers between devices  19.7 us (3%)
    unnamed x5, waiting for transfers between devices  111 us
    all_to_all x4, waiting for transfers between devices, exchange(): return lax.all_to_all(v, AXES, 0, 0, tiled=True)  81.8 us
    dot_general x6, matrix products, mm(): return jnp.dot(left, right, preferred_element_type=f32)  63.4 us
    dot_general x4, matrix products, mm_right(): lax.dot_general(left, right, (((1,), (1,)), ((), ())), preferred_element_...  40.6 us
    dot_general x6, matrix products, mm_left(): lax.dot_general(left, right, (((0,), (0,)), ((), ())), preferred_element_...  38.7 us
    all_gather x1, waiting for transfers between devices, body(): full = lax.all_gather(shard, AXES, axis=0, tiled=True)  35.8 us
    reduce_scatter x2, waiting for transfers between devices, body(): lax.psum_scatter(g.astype(bf), AXES, scatter_dimension=0, tiled=True)  27.7 us
    unnamed x187, local copies, waits for them, and re-layouts  23.4 us
  transfers between devices with their start and end apart: 9, of which 8 were waited for; matrix products, arithmetic and copies ran while one was open for 26% of the time, Pallas kernels for 0%

profile of v1, /device:TPU:0, one launch (start us, length us, event | category | flops | bytes accessed | tf_op | source)
XLA Modules:
  0.0 709.6 jit_solution(15631229688977721369)
XLA Ops:
  15.2 4.2 all-to-all-start.4
  20.2 3.0 all-to-all-done.4
  29.0 5.4 all-to-all-start.5
  35.6 5.9 all-to-all-done.5
  41.6 4.5 fusion.63
  46.1 2.8 all-to-all-start.6
  53.5 54.1 %all-to-all-done.6 = bf16[32,32,768]{2,1,0:T(8,128)(2,1)S(1)} async-done(((bf16[32,32,768]{2,1,0:T(8,128)(2,1)}), bf16[32,32,768]{2,1,0:T(8,128)(2,1)S(1)}, u32[]{:S(2)}, u32[]{:S(2)}) %all-to-all-start.6) | async-done | bytes 1572896 | tf_op jit(solution)/shard_map/all_to_all | solution.py:42
  107.6 3.6 fusion.32
  111.2 35.8 %all-gather.2.cloned.1.call-done = bf16[768,9856]{1,0:T(8,128)(2,1)} async-done(((bf16[24,9856]{1,0:T(8,128)(2,1)}), bf16[768,9856]{1,0:T(8,128)(2,1)}) %all-gather.2.cloned.1.call-update) | async-done | bytes 15138832 | tf_op jit(solution)/shard_map/all_gather | solution.py:178
  148.0 2.6 slice_reduce_fusion.1
  153.8 2.8 fusion.52
  156.6 2.2 multiply_reduce_fusion.9
  159.6 8.2 %add_convert_fusion.1 = bf16[1024,2304]{1,0:T(8,128)(2,1)} fusion(f32[2304]{0:T(1024)S(1)} %pad_maximum_fusion, bf16[768,9856]{1,0:T(8,128)(2,1)} %all-gather.2.cloned.1.call-done, f32[1024,768]{1,0:T(8,128)S(1)} %get-tuple-element.420, f32[768]{0:T(1024)S(1)} %copy-done.74, f32[768]{0:T(1024)S(1)} %copy-done.60, f32[1024]{0:T(1024)S(1)} %fusion.101), kind=kOutput, calls=%fused_computation.61 | convolution fusion | flops 3631742976 | bytes 11422720 | tf_op jit(solution)/shard_map/dot_general | solution.py:30
  167.8 6.6 copy.202
  174.4 8.9 %reshape.667 = bf16[2,512,3,12,64]{1,0,4,3,2:T(2,128)(2,1)} reshape(bf16[1024,2304]{0,1:T(8,128)(2,1)} %copy.202) | data formatting | bytes 9437184 | tf_op jit(solution)/shard_map/reshape | solution.py:82
  183.3 6.4 fusion.126
  189.7 16.2 %fusion.130 = (f32[2,12,512]{2,1,0:T(8,128)}, f32[2,12,512,512]{2,3,1,0:T(8,128)}) fusion(pred[2,512]{1,0:T(4,128)(4,1)S(1)} %copy-done.81, bf16[2,512,1,12,64]{1,0,4,3,2:T(2,128)(2,1)} %get-tuple-element.422, bf16[2,512,1,12,64]{1,0,4,3,2:T(2,128)(2,1)} %get-tuple-element.421), kind=kOutput, calls=%fused_computation.270 | convolution fusion | flops 830472704 | bytes 28361728 | tf_op jit(solution)/shard_map/sub | solution.py:89
  206.0 10.9 %fusion.74 = bf16[2,512,12,64]{1,3,2,0:T(8,128)(2,1)S(1)} fusion(bf16[2,512,1,12,64]{1,0,4,3,2:T(2,128)(2,1)} %get-tuple-element.423, f32[2,12,512,512]{2,3,1,0:T(8,128)} %get-tuple-element.445, f32[2,12,512]{2,1,0:T(8,128)} %get-tuple-element.444), kind=kOutput, calls=%fused_computation.144 | convolution fusion | flops 818675712 | bytes 28360704 | tf_op jit(solution)/shard_map/shqk,shkd->shqd/dot_general | solution.py:92
  216.9 1.6 copy.207
  219.0 3.8 fusion.131
  222.8 1.7 copy-done.7
  225.2 4.8 slice.176
  230.0 9.8 %reshape.669 = bf16[32,24,4,768]{3,2,1,0:T(4,128)(2,1)} reshape(bf16[768,3072]{1,0:T(8,128)(2,1)} %slice.176) | data formatting | bytes 9437184 | tf_op jit(solution)/shard_map/reshape | solution.py:219
  239.7 3.4 copy.209
  243.2 37.8 %multiply_convert_fusion.1 = (bf16[1024,3072]{1,0:T(8,128)(2,1)S(1)}, f32[1024,3072]{1,0:T(8,128)}, f32[1024,3072]{1,0:T(8,128)}) fusion(f32[3072]{0:T(1024)S(1)} %add.347, bf16[768,9856]{1,0:T(8,128)(2,1)} %all-gather.2.cloned.1.call-done, f32[1024,768]{1,0:T(8,128)S(1)} %copy-done.8, f32[768]{0:T(1024)S(1)} %copy-done.77, f32[768]{0:T(1024)S(1)} %copy-done.64, ...), kind=kOutput, calls=%fused_computation.43 | convolution fusion | flops 5043388416 | bytes 39348224 | tf_op jit(solution)/shard_map/dot_general | solution.py:30
  281.1 5.5 fusion.132
  292.3 2.0 fusion.47
  294.3 1.6 fusion.123
  296.0 1.8 copy-done.5
  298.7 17.3 %fusion.133 = (bf16[3072]{0:T(1024)(128)(2,1)S(1)}, bf16[1024,3072]{1,0:T(8,128)(2,1)}) fusion(f32[1024,3072]{1,0:T(8,128)} %get-tuple-element.418, bf16[1024,768]{1,0:T(8,128)(2,1)S(1)} %get-tuple-element.408, bf16[3072,768]{1,0:T(8,128)(2,1)} %bitcast.214, f32[1024,3072]{1,0:T(8,128)} %get-tuple-element.448, f32[3072]{0:T(1024)S(1)} %add.347), kind=kOutput, calls=%fused_computation.273 | convolution fusion | flops 4882166784 | bytes 37767168 | tf_op jit(solution)/shard_map/dot_general | solution.py:38
  316.0 10.2 %convolution_convert_fusion.1 = bf16[768,3072]{1,0:T(8,128)(2,1)} fusion(bf16[1024,3072]{1,0:T(8,128)(2,1)} %get-tuple-element.456, f32[1024,768]{1,0:T(8,128)S(1)} %copy-done.9, f32[768]{0:T(1024)S(1)} %copy-done.77, f32[768]{0:T(1024)S(1)} %copy-done.64, f32[1024]{0:T(1024)S(1)} %fusion.102, f32[1024]{0:T(1024)S(1)} %broadcast_multiply_fusion.1), kind=kOutput, calls=%fused_computation.67 | convolution fusion | flops 4838129664 | bytes 14170112 | tf_op jit(solution)/shard_map/dot_general | solution.py:34
  326.3 1.8 copy-done.6
  328.1 11.5 %multiply_reduce_fusion.2 = (bf16[768]{0:T(1024)(128)(2,1)S(1)}, f32[1024]{0:T(1024)S(1)}, bf16[768]{0:T(1024)(128)(2,1)S(1)}, f32[1024,768]{1,0:T(8,128)S(1)}) fusion(f32[1024,768]{1,0:T(8,128)} %copy-done.7, f32[1024]{0:T(1024)S(1)} %fusion.102, f32[1024]{0:T(1024)S(1)} %broadcast_multiply_fusion.1, f32[768]{0:T(1024)S(1)} %copy-done.64, ...), kind=kOutput, calls=%fused_computation.98 | convolution fusion | flops 4839699456 | bytes 20469760 | tf_op jit(solution)/shard_map/dot_general | solution.py:38
  341.1 1.7 copy-done.11
  344.2 3.9 convolution_convert_fusion.3
  348.2 1.8 copy.210
  350.0 2.4 reshape.673
  352.5 17.9 %multiply_reduce_fusion = (f32[2,12,512]{2,1,0:T(8,128)S(1)}, f32[2,12,512,512]{2,3,1,0:T(8,128)}) fusion(f32[2,12,512,512]{2,3,1,0:T(8,128)} %get-tuple-element.445, f32[2,12,512]{2,1,0:T(8,128)S(1)} %copy-done.50, bf16[2,512,1,12,64]{1,0,4,3,2:T(2,128)(2,1)S(1)} %copy-done.23, bf16[2,12,512,64]{2,0,3,1:T(2,128)(2,1)} %bitcast.220), kind=kOutput, calls=%fused_computation.36 | convolution fusion | flops 824168448 | bytes 53575680 | tf_op jit(solution)/shard_map/shqd,shkd->shqk/dot_general | solution.py:130
  370.4 23.2 %multiply_convert_fusion = bf16[2,12,512,512]{2,3,1,0:T(8,128)(2,1)} fusion(f32[2,12,512,512]{2,3,1,0:T(8,128)} %get-tuple-element.453, f32[2,12,512]{2,1,0:T(8,128)S(1)} %get-tuple-element.452, f32[2,12,512,512]{2,3,1,0:T(8,128)} %get-tuple-element.445, f32[2,12,512]{2,1,0:T(8,128)S(1)} %copy-done.50), kind=kLoop, calls=%fused_computation.35 | loop fusion | flops 25165824 | bytes 63012864 | tf_op jit(solution)/shard_map/convert_element_type | solution.py:131
  393.6 8.5 %fusion.78 = bf16[2,512,12,64]{1,3,2,0:T(8,128)(2,1)S(1)} fusion(bf16[2,12,512,512]{2,3,1,0:T(8,128)(2,1)} %multiply_convert_fusion, bf16[2,512,1,12,64]{1,0,4,3,2:T(2,128)(2,1)S(1)} %copy-done.22), kind=kOutput, calls=%fused_computation.146 | convolution fusion | flops 806879232 | bytes 15728640 | tf_op jit(solution)/shard_map/shqk,shqd->shkd/dot_general | solution.py:133
  404.2 6.9 fusion.77
  414.5 7.0 convolution_convert_fusion
  421.5 11.8 %fusion.71 = bf16[2,512,12,64]{1,3,2,0:T(8,128)(2,1)} fusion(bf16[2,12,512,64]{2,0,3,1:T(2,128)(2,1)S(1)} %bitcast.221, f32[2,12,512,512]{2,3,1,0:T(8,128)} %get-tuple-element.445, f32[2,12,512]{2,1,0:T(8,128)S(1)} %copy-done.50), kind=kOutput, calls=%fused_computation.143 | convolution fusion | flops 818675712 | bytes 28360704 | tf_op jit(solution)/shard_map/shqk,shqd->shkd/dot_general | solution.py:129
  440.3 7.9 %fusion.112 = (bf16[768]{0:T(1024)(128)(2,1)S(1)}, f32[1024]{0:T(1024)S(1)}, f32[1024,768]{1,0:T(8,128)S(1)}) fusion(f32[1024,768]{1,0:T(8,128)S(1)} %copy-done.3, f32[768]{0:T(1024)S(1)} %copy-done.62, bf16[1024,2304]{0,1:T(8,128)(2,1)} %constant_dynamic-update-slice_fusion, bf16[768,9856]{1,0:T(8,128)(2,1)} %all-gather.2.cloned.1.call-done, ...), kind=kOutput, calls=%fused_computation.260 | convolution fusion | flops 3628595456 | bytes 17707520 | tf_op jit(solution)/shard_map/dot_general | solution.py:38
  448.2 1.6 multiply_reduce_fusion.3
  449.8 2.2 fusion.121
  452.0 3.5 fusion.64
  455.6 3.4 all-to-all-start.7
  459.1 3.2 reduce.16
  463.3 3.3 reduce_sum.434
  466.6 2.3 copy.220
  468.9 4.4 convolution_convert_fusion.4
  473.3 8.2 %convolution_convert_fusion.2 = bf16[768,2304]{1,0:T(8,128)(2,1)} fusion(bf16[1024,2304]{0,1:T(8,128)(2,1)} %constant_dynamic-update-slice_fusion, f32[1024,768]{1,0:T(8,128)S(1)} %copy-done.3, f32[768]{0:T(1024)S(1)} %copy-done.76, f32[768]{0:T(1024)S(1)} %copy-done.62, f32[1024]{0:T(1024)S(1)} %copy-done.59), kind=kOutput, calls=%fused_computation.68 | convolution fusion | flops 3628793856 | bytes 11413504 | tf_op jit(solution)/shard_map/dot_general | solution.py:34
  481.6 9.3 %concatenate.26 = bf16[768,3712]{1,0:T(8,128)(2,1)} concatenate(bf16[768,2304]{1,0:T(8,128)(2,1)} %convolution_convert_fusion.2, bf16[768,768]{1,0:T(8,128)(2,1)} %convolution_convert_fusion.4, bf16[768,512]{1,0:T(8,128)(2,1)} %bitcast.215, bf16[768,14]{1,0:T(8,128)(2,1)S(1)} %bitcast.222, bf16[768,114]{1,0:T(8,128)(2,1)S(1)} %broadcast_in_dim.197), dimensions={1} | concatenate | bytes 11403264 | tf_op jit(solution)/shard_map/concatenate | solution.py:233
  490.9 18.1 %all-to-all-done.7 = bf16[32,32,768]{2,1,0:T(8,128)(2,1)} async-done(((bf16[32,32,768]{2,1,0:T(8,128)(2,1)}), bf16[32,32,768]{2,1,0:T(8,128)(2,1)}, u32[]{:S(2)}, u32[]{:S(2)}) %all-to-all-start.7) | async-done | bytes 1572896 | tf_op jit(solution)/shard_map/all_to_all | solution.py:42
  509.1 5.4 fusion.33
  514.8 3.3 multiply_reduce_fusion.10
  519.7 27.7 %reduce-scatter.8.cloned.1.call-done = bf16[96,768]{1,0:T(8,128)(2,1)} async-done(((bf16[3072,768]{1,0:T(8,128)(2,1)}), bf16[96,768]{1,0:T(8,128)(2,1)}) %reduce-scatter.8.cloned.1.call-update) | async-done | bytes 147472 | tf_op jit(solution)/shard_map/reduce_scatter | solution.py:228
  549.0 111.1 %reduce-scatter.10.cloned.1.call-done = bf16[24,3712]{1,0:T(8,128)(2,1)} async-done(((bf16[768,3712]{1,0:T(8,128)(2,1)}), bf16[24,3712]{1,0:T(8,128)(2,1)}) %reduce-scatter.10.cloned.1.call-update) | async-done | bytes 178192
  668.8 3.7 all-to-all-start.8
  675.9 3.6 all-to-all-done.8
  685.0 1.7 add_multiply_fusion.4
  686.7 1.9 add_multiply_fusion.3
  690.2 8.1 %add_multiply_fusion = (f32[960,768]{1,0:T(8,128)}, f32[960,768]{1,0:T(8,128)}, f32[960,768]{1,0:T(8,128)}) fusion(f32[960,768]{1,0:T(8,128)} %param.47, f32[960,768]{1,0:T(8,128)S(1)} %copy-done.15, f32[960,768]{1,0:T(8,128)} %get-tuple-element.121, f32[]{:T(128)S(6)} %min.3, f32[960,768]{1,0:T(8,128)} %param.40), kind=kLoop, calls=%fused_computation.122 | loop fusion | flops 6635520 | bytes 20643844 | tf_op jit(solution)/shard_map/add | solution.py:274
  (292 shorter events, 62.4 us)
Async XLA Ops:
  7.2 7.2 %copy-start = (s32[4,2]{0,1:T(2,128)S(1)}, s32[4,2]{0,1:T(2,128)}, u32[]{:S(2)}) copy-start(s32[4,2]{0,1:T(2,128)} %param.30) | copy-start | bytes 100
  7.2 6.5 copy-start.82
  7.2 27.1 %copy-start.14 = (f32[960,768]{1,0:T(8,128)S(1)}, f32[960,768]{1,0:T(8,128)}, u32[]{:S(2)}) copy-start(f32[960,768]{1,0:T(8,128)} %param.33) | copy-start | bytes 8847364
  7.2 139.8 %all-gather.2.cloned.1.call-start = ((), (), s32[]{:S(2)}) async-start(), calls=%async_computation.12 | async-start | bytes 15611904 | tf_op jit(solution)/shard_map/all_gather | solution.py:178
  14.5 34.4 %copy-start.47 = (s32[2]{0:T(128)}, s32[2]{0:T(128)S(1)}, u32[]{:S(2)}) copy-start(s32[2]{0:T(128)S(1)} %dynamic-slice_reduce_fusion) | copy-start | bytes 28
  15.2 8.0 %all-to-all-start.4 = ((s32[4,2,128]{2,1,0:T(2,128)}), s32[4,2,128]{2,1,0:T(2,128)S(1)}, u32[]{:S(2)}, u32[]{:S(2)}) async-start(s32[4,2,128]{2,1,0:T(2,128)} %param.29), calls=%async_computation.4 | async-start | bytes 8192 | tf_op jit(solution)/shard_map/all_to_all | solution.py:180
  26.2 81.4 %copy-start.72 = (s32[1024]{0:T(1024)}, s32[1024]{0:T(1024)S(1)}, u32[]{:S(2)}) copy-start(s32[1024]{0:T(1024)S(1)} %get-tuple-element.428) | copy-start | bytes 12292
  29.0 12.6 %all-to-all-start.5 = ((s32[32,1,128]{2,1,0:T(1,128)}), s32[32,1,128]{2,1,0:T(1,128)S(1)}, u32[]{:S(2)}, u32[]{:S(2)}) async-start(s32[32,1,128]{2,1,0:T(1,128)} %bitcast.5), calls=%async_computation.5 | async-start | bytes 32768 | tf_op jit(solution)/shard_map/all_to_all | solution.py:42
  41.6 4.5 copy-start.70
  46.1 4.1 copy-start.83
  46.1 61.5 %all-to-all-start.6 = ((bf16[32,32,768]{2,1,0:T(8,128)(2,1)}), bf16[32,32,768]{2,1,0:T(8,128)(2,1)S(1)}, u32[]{:S(2)}, u32[]{:S(2)}) async-start(bf16[32,32,768]{2,1,0:T(8,128)(2,1)} %bitcast.7), calls=%async_computation.6 | async-start | bytes 3145728 | tf_op jit(solution)/shard_map/all_to_all | solution.py:42
  48.9 469.2 %reduce-scatter.6.cloned.1.call-start = ((), (), s32[]{:S(2)}) async-start(), calls=%async_computation.13 | async-start | bytes 4866048 | tf_op jit(solution)/shard_map/reduce_scatter | solution.py:228
  152.8 6.1 copy-start.18
  152.8 6.1 copy-start.20
  152.8 6.0 copy-start.37
  152.9 6.0 copy-start.43
  152.9 3.7 copy-start.13
  158.9 60.0 %copy-start.2 = (f32[1024,768]{1,0:T(8,128)}, f32[1024,768]{1,0:T(8,128)S(1)}, u32[]{:S(2)}) copy-start(f32[1024,768]{1,0:T(8,128)S(1)} %get-tuple-element.420) | copy-start | bytes 9437188
  159.5 59.4 %copy-start.58 = (f32[1024]{0:T(1024)}, f32[1024]{0:T(1024)S(1)}, u32[]{:S(2)}) copy-start(f32[1024]{0:T(1024)S(1)} %fusion.101) | copy-start | bytes 12292
  183.3 6.4 copy-start.81
  218.9 3.8 copy-start.27
  225.0 5.0 copy-start.56
  243.1 37.9 %copy-start.17 = (bf16[32,4,24,768]{3,2,1,0:T(8,128)(2,1)}, bf16[32,4,24,768]{3,2,1,0:T(8,128)(2,1)S(1)}, u32[]{:S(2)}) copy-start(bf16[32,4,24,768]{3,2,1,0:T(8,128)(2,1)S(1)} %copy.209) | copy-start | bytes 14155780
  243.2 37.9 %copy-start.78 = (f32[768]{0:T(1024)S(1)}, f32[768]{0:T(1024)}, u32[]{:S(2)}) copy-start(f32[768]{0:T(1024)} %get-tuple-element.327) | copy-start | bytes 9220
  281.0 5.5 copy-start.84
  286.6 5.7 copy-start.51
  292.3 3.7 copy-start.45
  298.7 17.3 %copy-start.25 = (bf16[1024,768]{1,0:T(8,128)(2,1)}, bf16[1024,768]{1,0:T(8,128)(2,1)S(1)}, u32[]{:S(2)}) copy-start(bf16[1024,768]{1,0:T(8,128)(2,1)S(1)} %get-tuple-element.408) | copy-start | bytes 4718596
  298.7 17.3 %copy-start.9 = (f32[1024,768]{1,0:T(8,128)S(1)}, f32[1024,768]{1,0:T(8,128)}, u32[]{:S(2)}) copy-start(f32[1024,768]{1,0:T(8,128)} %copy-done.7) | copy-start | bytes 9437188
  326.3 13.3 %copy-start.57 = (f32[1024]{0:T(1024)S(1)}, f32[1024]{0:T(1024)}, u32[]{:S(2)}) copy-start(f32[1024]{0:T(1024)} %copy-done.56) | copy-start | bytes 12292
  326.3 221.1 %reduce-scatter.8.cloned.1.call-start = ((), (), s32[]{:S(2)}) async-start(), calls=%async_computation.14 | async-start | bytes 4866048 | tf_op jit(solution)/shard_map/reduce_scatter | solution.py:228
  328.1 11.5 %copy-start.10 = (f32[1024,768]{1,0:T(8,128)S(1)}, f32[1024,768]{1,0:T(8,128)}, u32[]{:S(2)}) copy-start(f32[1024,768]{1,0:T(8,128)} %copy-done.7) | copy-start | bytes 9437188
  348.2 4.3 copy-start.23
  348.2 4.3 copy-start.50
  370.4 23.2 %copy-start.22 = (bf16[2,512,1,12,64]{1,0,4,3,2:T(2,128)(2,1)S(1)}, bf16[2,512,1,12,64]{1,0,4,3,2:T(2,128)(2,1)}, u32[]{:S(2)}) copy-start(bf16[2,512,1,12,64]{1,0,4,3,2:T(2,128)(2,1)} %get-tuple-element.422) | copy-start | bytes 4718596
  402.1 12.3 %slice-start = ((s8[6291456]{0:T(1024)(128)(4,1)}), s8[4194304]{0:T(1024)(128)(4,1)S(1)}, s32[]{:S(2)}) async-start(s8[6291456]{0:T(1024)(128)(4,1)} %bitcast.230), calls=%async_computation.16 | async-start | bytes 8388608
  404.2 10.3 %slice-start.1 = ((s8[6291456]{0:T(1024)(128)(4,1)}), s8[2097152]{0:T(1024)(128)(4,1)S(1)}, s32[]{:S(2)}) async-start(s8[6291456]{0:T(1024)(128)(4,1)} %bitcast.230), calls=%async_computation.17 | async-start | bytes 4194304
  414.5 7.0 copy-start.28
  433.3 5.3 copy-start.62
  440.3 7.9 %copy-start.55 = (f32[1024]{0:T(1024)S(1)}, f32[1024]{0:T(1024)}, u32[]{:S(2)}) copy-start(f32[1024]{0:T(1024)} %copy-done.54) | copy-start | bytes 12292
  440.3 7.9 %copy-start.59 = (f32[1024]{0:T(1024)S(1)}, f32[1024]{0:T(1024)}, u32[]{:S(2)}) copy-start(f32[1024]{0:T(1024)} %copy-done.58) | copy-start | bytes 12292
  455.6 53.4 %all-to-all-start.7 = ((bf16[32,32,768]{2,1,0:T(8,128)(2,1)}), bf16[32,32,768]{2,1,0:T(8,128)(2,1)}, u32[]{:S(2)}, u32[]{:S(2)}) async-start(bf16[32,32,768]{2,1,0:T(8,128)(2,1)} %bitcast.218), calls=%async_computation.7 | async-start | bytes 3145728 | tf_op jit(solution)/shard_map/all_to_all | solution.py:42
  459.1 201.1 %reduce-scatter.10.cloned.1.call-start = ((), (), s32[]{:S(2)}) async-start(), calls=%async_computation.15 | async-start | bytes 5879808
  468.9 4.4 copy-start.76
  490.9 18.2 %copy-start.71 = (s32[1024]{0:T(1024)S(1)}, s32[1024]{0:T(1024)}, u32[]{:S(2)}) copy-start(s32[1024]{0:T(1024)} %copy-done.70) | copy-start | bytes 12292
  509.0 5.4 copy-start.19
  509.0 5.4 copy-start.21
  509.0 5.4 copy-start.31
  509.0 5.4 copy-start.38
  509.0 5.4 copy-start.44
  509.0 5.4 copy-start.48
  514.7 157.7 %copy-start.63 = (f32[14,24]{1,0:T(8,128)S(1)}, f32[14,24]{1,0:T(8,128)}, u32[]{:S(2)}) copy-start(f32[14,24]{1,0:T(8,128)} %param.39) | copy-start | bytes 4036
  514.7 171.9 %copy-start.34 = (f32[24,2304]{1,0:T(8,128)S(1)}, f32[24,2304]{1,0:T(8,128)}, u32[]{:S(2)}) copy-start(f32[24,2304]{1,0:T(8,128)} %param.35) | copy-start | bytes 663556
  514.8 175.4 %copy-start.15 = (f32[960,768]{1,0:T(8,128)S(1)}, f32[960,768]{1,0:T(8,128)}, u32[]{:S(2)}) copy-start(f32[960,768]{1,0:T(8,128)} %param.33) | copy-start | bytes 8847364
  668.8 10.8 %all-to-all-start.8 = ((f32[32,1,2]{2,1,0:T(1,128)}), f32[32,1,2]{2,1,0:T(1,128)S(1)}, u32[]{:S(2)}, u32[]{:S(2)}) async-start(f32[32,1,2]{2,1,0:T(1,128)} %broadcast_in_dim.198), calls=%async_computation.10 | async-start | bytes 32768 | tf_op jit(solution)/shard_map/all_to_all | solution.py:42
  690.1 8.2 %copy-start.32 = (f32[96,768]{1,0:T(8,128)S(1)}, f32[96,768]{1,0:T(8,128)}, u32[]{:S(2)}) copy-start(f32[96,768]{1,0:T(8,128)} %param.38) | copy-start | bytes 884740
  690.1 8.2 %copy-start.36 = (bf16[96,768]{1,0:T(8,128)(2,1)S(1)}, bf16[96,768]{1,0:T(8,128)(2,1)}, u32[]{:S(2)}) copy-start(bf16[96,768]{1,0:T(8,128)(2,1)} %reduce-scatter.8.cloned.1.call-done) | copy-start | bytes 442372
  690.1 8.2 %copy-start.39 = (f32[96,768]{1,0:T(8,128)S(1)}, f32[96,768]{1,0:T(8,128)}, u32[]{:S(2)}) copy-start(f32[96,768]{1,0:T(8,128)} %param.52) | copy-start | bytes 884740
  690.1 8.2 %copy-start.40 = (f32[96,768]{1,0:T(8,128)S(1)}, f32[96,768]{1,0:T(8,128)}, u32[]{:S(2)}) copy-start(f32[96,768]{1,0:T(8,128)} %param.45) | copy-start | bytes 884740
  690.1 9.2 %copy-start.33 = (f32[24,3072]{1,0:T(8,128)S(1)}, f32[24,3072]{1,0:T(8,128)}, u32[]{:S(2)}) copy-start(f32[24,3072]{1,0:T(8,128)} %param.37) | copy-start | bytes 884740
  690.2 9.2 %copy-start.35 = (bf16[24,3072]{1,0:T(8,128)(2,1)S(1)}, bf16[24,3072]{1,0:T(8,128)(2,1)}, u32[]{:S(2)}) copy-start(bf16[24,3072]{1,0:T(8,128)(2,1)} %reduce-scatter.6.cloned.1.call-done) | copy-start | bytes 442372
  690.2 9.2 %copy-start.41 = (f32[24,3072]{1,0:T(8,128)S(1)}, f32[24,3072]{1,0:T(8,128)}, u32[]{:S(2)}) copy-start(f32[24,3072]{1,0:T(8,128)} %param.51) | copy-start | bytes 884740
  690.2 9.2 %copy-start.42 = (f32[24,3072]{1,0:T(8,128)S(1)}, f32[24,3072]{1,0:T(8,128)}, u32[]{:S(2)}) copy-start(f32[24,3072]{1,0:T(8,128)} %param.44) | copy-start | bytes 884740
  690.2 10.1 %copy-start.1 = (s32[4,2]{0,1:T(2,128)S(1)}, s32[4,2]{0,1:T(2,128)}, u32[]{:S(2)}) copy-start(s32[4,2]{0,1:T(2,128)} %param.30) | copy-start | bytes 100
  (32 other events, 73.1 us)
Sparse Core Ops, SparseCore 0:
  13.9 133.1 all-gather.1
  326.4 105.2 reduce-scatter.5
  438.1 109.2 reduce-scatter.7
  553.1 107.0 reduce-scatter.9

commit v2 on v1

v2 whole, which is shorter than its diff:
```python
import functools

import jax
import jax.numpy as jnp
from jax import lax
from jax.experimental import pallas as pl
from jax.experimental.pallas import tpu as pltpu
from jax.sharding import PartitionSpec as P

HEADS = 12
HEAD_DIM = 64
EPS = 1e-06
RATE = 10000.0
MOMENT = 0.5
DECAY = 0.5
CLIP = 0.01
SLOTS = 32
GROUP = 128
ROWS = 256
AXES = ("dp", "seq")
bf = jnp.bfloat16
f32 = jnp.float32


def mm(left, right):
    return jnp.dot(left, right, preferred_element_type=f32)


def mm_left(left, right):
    return lax.dot_general(left, right, (((0,), (0,)), ((), ())), preferred_element_type=f32)


def mm_right(left, right):
    return lax.dot_general(left, right, (((1,), (1,)), ((), ())), preferred_element_type=f32)


def exchange(v):
    return lax.all_to_all(v, AXES, 0, 0, tiled=True)


def route(ids, valid, per_owner):
    count = ids.shape[0]
    spot = jnp.arange(count, dtype=jnp.int32)
    owner = ids // per_owner
    local = ids - owner * per_owner
    key = jnp.where(valid, ids, -1 - spot)
    alike = key[:, None] == key[None, :]
    first_at = jnp.min(jnp.where(alike, spot[None, :], count), axis=1)
    first = (first_at == spot) & valid
    before = (owner[:, None] == owner[None, :]) & first[None, :] & (spot[None, :] < first_at[:, None])
    rank = jnp.sum(before.astype(jnp.int32), axis=1)
    return owner, local, first, rank


def requests(owner, local, first, rank, start, devices):
    slot = jnp.where(first & (rank >= start) & (rank < start + SLOTS), owner * SLOTS + rank - start, -1)
    line = jnp.arange(devices * SLOTS, dtype=jnp.int32)
    hit = slot[None, :] == line[:, None]
    return jnp.max(jnp.where(hit, local[None, :], -1), axis=1)


def token_slots(owner, valid, rank, start):
    return jnp.where(valid & (rank >= start) & (rank < start + SLOTS), owner * SLOTS + rank - start, -1)


def one_hot(index, size):
    return (index[:, None] == jnp.arange(size, dtype=jnp.int32)[None, :]).astype(bf)


NEAR = 0.3
TAIL = (
    0.11962924781130464, 0.12075473126046088, 0.09990870957740686, 0.12857719637511858,
    -0.05371263258867769, 0.2063844888355699, -0.15722075016774184, 0.03567893567949022,
)


def dot(left, right):
    return jnp.dot(left, right, preferred_element_type=f32)


def dot_nt(left, right):
    return lax.dot_general(left, right, (((1,), (1,)), ((), ())), preferred_element_type=f32)


def dot_tn(left, right):
    return lax.dot_general(left, right, (((0,), (0,)), ((), ())), preferred_element_type=f32)


def iota(shape, axis):
    return lax.broadcasted_iota(jnp.int32, shape, axis)


def normal(v):
    center = v - jnp.mean(v, axis=-1, keepdims=True)
    scale = lax.rsqrt(jnp.mean(center * center, axis=-1, keepdims=True) + EPS)
    return center * scale, scale


def normal_back(grad, unit, scale):
    inner = jnp.mean(grad * unit, axis=-1, keepdims=True)
    return scale * (grad - jnp.mean(grad, axis=-1, keepdims=True) - unit * inner)


def column_sums(v):
    return dot(jnp.full((8, v.shape[0]), 1.0, bf), v)[:1]


def gelu_pair(v):
    bell = jnp.exp(v * v * -0.5)
    t = 1.0 / (1.0 + NEAR * jnp.abs(v))
    poly = TAIL[-1]
    for c in TAIL[-2::-1]:
        poly = poly * t + c
    tail = poly * t * bell
    area = jnp.where(v < 0, tail, 1.0 - tail)
    return v * area, area + v * bell * 0.3989422804014327


def params(limit, **more):
    return pltpu.CompilerParams(vmem_limit_bytes=limit << 20, **more)


def fixed(shape, index):
    return pl.BlockSpec(shape, lambda *_: index, pipeline_mode=pl.Buffered(1))


def spread_kernel(depth, turns, width, src, out):
    tall = src[...].astype(f32)
    parts = []
    for e in range(2):
        for j in range(turns):
            parts.append(tall[e * depth : (e + 1) * depth, j * width : (j + 1) * width])
    out[...] = jnp.concatenate(parts, axis=0).astype(bf)


def first_kernel(slot, back, extra, w_qkv, pos_t, vec_t, x_out, hin_out, qkv_out, vec_out):
    rows, width = x_out.shape
    length = pos_t.shape[1]
    vec = dot_nt((iota((16, 128), 0) == iota((16, 128), 1)).astype(f32).astype(bf), vec_t[...])
    vec_out[...] = vec
    where = jnp.where(slot[...] == iota((rows, back.shape[0]), 1), 1.0, 0.0).astype(bf)
    begin = lax.rem(pl.program_id(0), length // rows) * rows
    line = jnp.where(iota((rows, length), 0) + begin == iota((rows, length), 1), 1.0, 0.0).astype(bf)
    x = dot(where, back[...]) + extra[...].astype(f32) + dot_nt(line, pos_t[...])
    x_out[...] = x
    unit, _ = normal(x)
    hin = (unit * vec[0:1] + vec[1:2]).astype(bf)
    hin_out[...] = hin
    qkv_out[:, :width] = (dot(hin, w_qkv[:, :width]) + vec[2:3]).astype(bf)
    qkv_out[:, width : 2 * width] = dot(hin, w_qkv[:, width : 2 * width]).astype(bf)
    qkv_out[:, 2 * width :] = (dot(hin, w_qkv[:, 2 * width :]) + vec[3:4]).astype(bf)


def head_parts(lens, query, keys, half):
    length = query.shape[0]
    lane = iota((length, GROUP), 1)
    inside = (lane // HEAD_DIM) == half
    spare = lane == (1 - half) * HEAD_DIM
    dead = iota((length, GROUP), 0) >= lens
    key = jnp.where(inside, keys.astype(f32), jnp.where(spare & dead, -1e30, 0.0)).astype(bf)
    ask = jnp.where(inside, query.astype(f32) * 0.125, jnp.where(spare, 1.0, 0.0)).astype(bf)
    return inside, ask, key


def attend_kernel(lens, query, keys, values, out):
    size = lens[pl.program_id(0)]
    total = None
    for half in range(2):
        inside, ask, key = head_parts(size, query[...], keys[...], half)
        score = dot_nt(ask, key)
        power = jnp.exp(score - jnp.max(score, axis=1, keepdims=True))
        prob = (power * (1.0 / jnp.sum(power, axis=1, keepdims=True))).astype(bf)
        part = dot(prob, jnp.where(inside, values[...].astype(f32), 0.0).astype(bf))
        total = part if total is None else total + part
    out[...] = total.astype(bf)


def attend_back_kernel(lens, query, keys, values, d_out, d_proj):
    size = lens[pl.program_id(0)]
    d_query, d_key, d_value = None, None, None
    add = lambda a, b: b if a is None else a + b
    for half in range(2):
        inside, ask, key = head_parts(size, query[...], keys[...], half)
        clean = lambda v: jnp.where(inside, v.astype(f32), 0.0).astype(bf)
        score = dot_nt(key, ask)
        power = jnp.exp(score - jnp.max(score, axis=0, keepdims=True))
        prob = power * (1.0 / jnp.sum(power, axis=0, keepdims=True))
        grad = clean(d_out[...])
        d_value = add(d_value, dot(prob.astype(bf), grad))
        d_prob = dot_nt(values[...], grad)
        inner = jnp.sum(prob * d_prob, axis=0, keepdims=True)
        d_score = (prob * (d_prob - inner)).astype(bf)
        d_key = add(d_key, dot(d_score, clean(ask)))
        d_query = add(d_query, dot_tn(d_score, clean(key)))
    d_proj[0] = (d_query * 0.125).astype(bf)
    d_proj[1] = d_key.astype(bf)
    d_proj[2] = d_value.astype(bf)


def middle_kernel(per_sent, lens, x, mixed, w_out, w_in, w_back, vec, vec_ff, z1_out, h1_out, act_out, slope_out, z2_out, pooled):
    rows, width = x.shape
    step = pl.program_id(0)
    unit, _ = normal(x[...])
    h0 = unit * vec[0:1] + vec[1:2]
    z1 = h0 + dot(mixed[...], w_out[...]) + vec[4:5]
    z1_out[...] = z1
    unit, _ = normal(z1)
    h1 = unit * vec[5:6] + vec[6:7]
    h1_b = h1.astype(bf)
    h1_out[...] = h1_b
    turns = w_in.shape[1] // width
    y = None
    for j in range(turns):
        at = slice(j * width, (j + 1) * width)
        hidden = dot(h1_b, w_in[:, at]) + vec_ff[:, at]
        act, slope = gelu_pair(hidden)
        act = act.astype(bf)
        act_out[:, at] = act
        slope_out[:, at] = slope.astype(bf)
        part = dot(act, w_back[at, :])
        y = part if y is None else y + part
    z2 = h1 + y + vec[7 + turns : 8 + turns]
    z2_out[...] = z2
    unit, _ = normal(z2)
    h2 = unit * vec[8 + turns : 9 + turns] + vec[9 + turns : 10 + turns]
    sent = step // per_sent
    begin = lax.rem(step, per_sent) * rows
    keep = iota((rows, width), 0) + begin < lens[sent]
    sums = jnp.sum(jnp.where(keep, h2, 0.0), axis=0, keepdims=True)

    @pl.when(step == 0)
    def _():
        pooled[...] = jnp.zeros_like(pooled)

    pooled[...] += jnp.where(iota(pooled.shape, 0) == sent, sums, 0.0)


def back_kernel(per_sent, lens, facts, pooled, z1, slope, z2, w_out, w_in, w_back, vec, d_y_out, d_f_out, d_r1_out, d_a_out, d_o_out, sums, sums_ff, loss):
    rows, width = z1.shape
    step = pl.program_id(0)
    sent = step // per_sent
    labeled, gold, count = facts[0], facts[1], facts[2]
    size = [lens[i].astype(f32) for i in range(2)]
    side = [pooled[i : i + 1] / size[i] for i in range(2)]
    total = lambda a, b: jnp.sum(a * b, axis=1, keepdims=True)
    cross = total(side[0], side[1])
    root = [lax.rsqrt(total(s, s) + EPS) for s in side]
    miss = cross * root[0] * root[1] - gold
    loss[...] = jnp.broadcast_to(labeled * miss * miss, loss.shape)
    push = 2.0 * labeled * miss / count
    grads = [
        push * (side[1 - i] * root[0] * root[1] - cross * root[i] * root[i] * root[i] * root[1 - i] * side[i]) / size[i]
        for i in range(2)
    ]
    d_pooled = jnp.where(sent == 0, grads[0], grads[1])
    begin = lax.rem(step, per_sent) * rows
    keep = iota((rows, width), 0) + begin < lens[sent]
    d_h2 = jnp.where(keep, d_pooled, 0.0)
    turns = w_in.shape[1] // width

    unit, scale = normal(z2[...])
    d_g2 = jnp.sum(d_h2 * unit, axis=0, keepdims=True)
    d_b2n = jnp.sum(d_h2, axis=0, keepdims=True)
    d_r2 = normal_back(d_h2 * vec[8 + turns : 9 + turns], unit, scale)
    d_y = d_r2.astype(bf)
    d_y_out[...] = d_y
    d_h1 = d_r2
    ff = []
    for j in range(turns):
        at = slice(j * width, (j + 1) * width)
        d_f = (dot_nt(d_y, w_back[at, :]) * slope[:, at].astype(f32)).astype(bf)
        d_f_out[:, at] = d_f
        ff.append(column_sums(d_f))
        d_h1 = d_h1 + dot_nt(d_f, w_in[:, at])
    unit, scale = normal(z1[...])
    d_g1 = jnp.sum(d_h1 * unit, axis=0, keepdims=True)
    d_b1 = jnp.sum(d_h1, axis=0, keepdims=True)
    d_r1 = normal_back(d_h1 * vec[5:6], unit, scale)
    d_r1_out[...] = d_r1
    d_a = d_r1.astype(bf)
    d_a_out[...] = d_a
    d_o_out[...] = dot_nt(d_a, w_out[...]).astype(bf)
    fresh = jnp.concatenate([column_sums(d_a), d_g1, d_b1, column_sums(d_y), d_g2, d_b2n, d_g2, d_b2n], axis=0)

    @pl.when(step == 0)
    def _():
        sums[...] = jnp.zeros_like(sums)
        sums_ff[...] = jnp.zeros_like(sums_ff)

    sums[...] += fresh
    sums_ff[...] += jnp.concatenate(ff, axis=0)


def last_kernel(slot, x, d_r1, d_proj, hin, w_qkv, vec, d_x_out, sums, rows_out, total):
    rows, width = x.shape
    step = pl.program_id(0)
    d_h0 = d_r1[...]
    for i in range(3):
        d_h0 = d_h0 + dot_nt(d_proj[i], w_qkv[:, i * width : (i + 1) * width])
    unit, scale = normal(x[...])
    d_ge = jnp.sum(d_h0 * unit, axis=0, keepdims=True)
    d_be = jnp.sum(d_h0, axis=0, keepdims=True)
    d_x = normal_back(d_h0 * vec[0:1], unit, scale)
    d_xb = d_x.astype(bf)
    d_x_out[...] = d_xb
    bias_q, bias_v = column_sums(d_proj[0]), column_sums(d_proj[2])
    fresh = jnp.concatenate([d_ge, d_be, bias_q, bias_v, d_ge, d_be, bias_q, bias_v], axis=0)
    hit = jnp.where(slot[...] == iota((rows_out.shape[0], rows), 0), 1.0, 0.0).astype(bf)

    @pl.when(step == 0)
    def _():
        sums[...] = jnp.zeros_like(sums)
        total[...] = jnp.zeros_like(total)

    sums[...] += fresh
    total[...] += dot(hit, d_xb)

    @pl.when(step == pl.num_programs(0) - 1)
    def _():
        rows_out[...] = total[...].astype(bf)


def blocks(v, depth):
    return v.reshape(v.shape[0] // depth, depth, v.shape[1])


def dense_grads_kernel(depth, turns, act, d_y, h1, d_f, mixed, d_a, out):
    width = d_y.shape[1]
    g = dot_tn(act[...], d_y[...])
    g = g.reshape(out.shape[0], turns, depth, width)
    for j in range(turns):
        out[:, j] = g[:, j].astype(bf)
    for j in range(turns):
        out[:, turns + j] = blocks(dot_tn(h1[...], d_f[:, j * width : (j + 1) * width]), depth).astype(bf)
    out[:, 2 * turns] = blocks(dot_tn(mixed[...], d_a[...]), depth).astype(bf)


def rest_grads_kernel(depth, length, core, hin, d_proj, d_x, sums_0, sums, sums_ff, keep, send):
    rows, width = d_proj.shape[1], d_proj.shape[2]
    part = hin.shape[1]
    mine = core[0]

    def put(kind, g):
        g = g.reshape(part // (2 * depth), 2, depth, width)
        even, odd = g[:, 0], g[:, 1]
        keep[:, kind] = jnp.where(mine == 0, even, odd).astype(bf)
        send[:, kind] = jnp.where(mine == 0, odd, even).astype(bf)

    for i in range(3):
        put(i, dot_tn(hin[...], d_proj[i]))
    g_pos = None
    for i in range(rows // length):
        line = jnp.where(iota((length, length), 0) == iota((length, length), 1), 1.0, 0.0).astype(bf)
        g = dot_tn(d_x[i * length : (i + 1) * length], line)
        g_pos = g if g_pos is None else g_pos + g
    turns = sums_ff.shape[0]
    vec = jnp.concatenate([sums_0[:4], sums[:3], sums_ff[...], sums[3:6]], axis=0)
    vec = jnp.concatenate([vec, jnp.zeros((128 - vec.shape[0], part), f32)], axis=0)
    put(3, jnp.concatenate([g_pos, vec.T, jnp.zeros((part, width - length - 128), f32)], axis=1))


def cost(flops, nbytes):
    return pl.CostEstimate(flops=int(flops), bytes_accessed=int(nbytes), transcendentals=0)


def run_forward_backward(full, back, extra, slots, lens, facts, core, devices, depth, length, hidden):
    width = back.shape[1]
    rows = slots.shape[0]
    sents = rows // length
    steps = rows // ROWS
    per_sent = length // ROWS
    turns = hidden // width
    pairs = width // GROUP
    shape = jax.ShapeDtypeStruct
    row = lambda cols, kind=None: pl.BlockSpec((ROWS, cols), lambda i, *_: (i, 0))
    column = lambda block: fixed((width, width), (0, block))
    at_back = 4 * width + hidden

    if depth % 8 == 0:
        w_back = pl.pallas_call(
            functools.partial(spread_kernel, depth, turns, width),
            grid=(devices // 2,),
            in_specs=[pl.BlockSpec((2 * depth, turns * width), lambda i: (i, at_back // (turns * width)))],
            out_specs=pl.BlockSpec((2 * depth * turns, width), lambda i: (i, 0)),
            out_shape=shape((hidden, width), bf),
            name="spread",
        )(full)
    else:
        w_back = full[:, at_back : at_back + turns * width].reshape(devices, depth, turns, width)
        w_back = w_back.transpose(0, 2, 1, 3).reshape(hidden, width)

    at_pos = at_back + turns * width
    at_vec = at_pos + length
    w_qkv_spec = fixed((width, 3 * width), (0, 0))
    w_out_spec = column(3)
    w_in_spec = fixed((width, hidden), (0, 4 * width // hidden))
    vec_spec = fixed((16, width), (0, 0))

    x, hin, qkv, vec = pl.pallas_call(
        first_kernel,
        grid=(steps,),
        in_specs=[
            pl.BlockSpec((ROWS, 1), lambda i: (i, 0)),
            fixed(back.shape, (0, 0)),
            row(width),
            w_qkv_spec,
            fixed((width, length), (0, at_pos // length)),
            fixed((width, 128), (0, at_vec // 128)),
        ],
        out_specs=[row(width), row(width), row(3 * width), pl.BlockSpec((16, width), lambda i: (0, 0))],
        out_shape=[shape((rows, width), f32), shape((rows, width), bf), shape((rows, 3 * width), bf), shape((16, width), f32)],
        compiler_params=params(56),
        name="first",
    )(slots[:, None], back, extra, full, full, full)

    block = lambda part: pl.BlockSpec((length, GROUP), lambda s, p, *_: (s, part * pairs + p))
    mixed = pl.pallas_call(
        attend_kernel,
        grid_spec=pltpu.PrefetchScalarGridSpec(
            num_scalar_prefetch=1,
            grid=(sents, pairs),
            in_specs=[block(0), block(1), block(2)],
            out_specs=block(0),
        ),
        out_shape=shape((rows, width), bf),
        compiler_params=params(56),
        name="attend",
    )(lens, qkv, qkv, qkv)

    vec_ff = vec[7 : 7 + turns].reshape(1, hidden)
    z1, h1, act, slope, z2, pooled = pl.pallas_call(
        functools.partial(middle_kernel, per_sent),
        grid_spec=pltpu.PrefetchScalarGridSpec(
            num_scalar_prefetch=1,
            grid=(steps,),
            in_specs=[
                row(width), row(width), w_out_spec, w_in_spec, fixed((hidden, width), (0, 0)), vec_spec, fixed((1, hidden), (0, 0)),
            ],
            out_specs=[row(width), row(width), row(hidden), row(hidden), row(width), pl.BlockSpec((8, width), lambda i, *_: (0, 0))],
        ),
        out_shape=[
            shape((rows, width), f32), shape((rows, width), bf), shape((rows, hidden), bf), shape((rows, hidden), bf),
            shape((rows, width), f32), shape((8, width), f32),
        ],
        compiler_params=params(60),
        name="middle",
    )(lens, x, mixed, full, full, w_back, vec, vec_ff)

    d_y, d_f, d_r1, d_a, d_o, sums, sums_ff, loss = pl.pallas_call(
        functools.partial(back_kernel, per_sent),
        grid_spec=pltpu.PrefetchScalarGridSpec(
            num_scalar_prefetch=2,
            grid=(steps,),
            in_specs=[
                fixed((8, width), (0, 0)), row(width), row(hidden), row(width), w_out_spec, w_in_spec, fixed((hidden, width), (0, 0)), vec_spec,
            ],
            out_specs=[
                row(width), row(hidden), row(width), row(width), row(width),
                pl.BlockSpec((8, width), lambda i, *_: (0, 0)),
                pl.BlockSpec((turns, width), lambda i, *_: (0, 0)),
                pl.BlockSpec((8, 128), lambda i, *_: (0, 0)),
            ],
        ),
        out_shape=[
            shape((rows, width), bf), shape((rows, hidden), bf), shape((rows, width), f32), shape((rows, width), bf), shape((rows, width), bf),
            shape((8, width), f32), shape((turns, width), f32), shape((8, 128), f32),
        ],
        compiler_params=params(60),
        name="back",
    )(lens, facts, pooled, z1, slope, z2, full, full, w_back, vec)

    tall = depth % 8 == 0
    half = devices // 2
    part = width // 2
    halves = lambda cols: pl.BlockSpec((rows, cols), lambda i, *_: (0, i))
    if tall:
        dense = pl.pallas_call(
            functools.partial(dense_grads_kernel, depth, turns),
            grid=(2,),
            in_specs=[
                halves(hidden // 2), fixed((rows, width), (0, 0)), halves(part), fixed((rows, hidden), (0, 0)), halves(part),
                fixed((rows, width), (0, 0)),
            ],
            out_specs=pl.BlockSpec((half, 2 * turns + 1, depth, width), lambda i: (i, 0, 0, 0)),
            out_shape=shape((devices, 2 * turns + 1, depth, width), bf),
            compiler_params=params(60),
            name="dense_grads",
        )(act, d_y, h1, d_f, mixed, d_a)
    else:
        cut = lambda g: g.astype(bf).reshape(devices, depth, -1, width).transpose(0, 2, 1, 3)
        g_out = dot_tn(act, d_y).astype(bf).reshape(devices, turns, depth, width)
        dense = jnp.concatenate([g_out, cut(dot_tn(h1, d_f)), cut(dot_tn(mixed, d_a))], axis=1)
    d_o, dense = lax.optimization_barrier((d_o, dense))

    d_proj = pl.pallas_call(
        attend_back_kernel,
        grid_spec=pltpu.PrefetchScalarGridSpec(
            num_scalar_prefetch=1,
            grid=(sents, pairs),
            in_specs=[block(0), block(1), block(2), block(0)],
            out_specs=pl.BlockSpec((3, length, GROUP), lambda s, p, *_: (0, s, p)),
        ),
        out_shape=shape((3, rows, width), bf),
        compiler_params=params(56),
        name="attend_back",
    )(lens, qkv, qkv, qkv, d_o)

    d_xb, sums_0, give_rows = pl.pallas_call(
        last_kernel,
        grid=(steps,),
        in_specs=[
            pl.BlockSpec((1, ROWS), lambda i: (0, i)), row(width), row(width),
            pl.BlockSpec((3, ROWS, width), lambda i: (0, i, 0)), row(width), w_qkv_spec, vec_spec,
        ],
        out_specs=[
            row(width), pl.BlockSpec((8, width), lambda i: (0, 0)),
            pl.BlockSpec(back.shape, lambda i: (0, 0)),
        ],
        out_shape=[shape((rows, width), bf), shape((8, width), f32), shape(back.shape, bf)],
        scratch_shapes=[pltpu.VMEM(back.shape, f32)],
        compiler_params=params(60),
        name="last",
    )(slots[None, :], x, d_r1, d_proj, hin, full, vec)

    if tall:
        quarter = pl.BlockSpec((half // 2, 4, depth, width), lambda i, *_: (i, 0, 0, 0))
        rest = pl.pallas_call(
            functools.partial(rest_grads_kernel, depth, length),
            grid_spec=pltpu.PrefetchScalarGridSpec(
                num_scalar_prefetch=1,
                grid=(2,),
                in_specs=[
                    halves(part), fixed((3, rows, width), (0, 0, 0)), halves(part),
                    pl.BlockSpec((8, part), lambda i, *_: (0, i)), pl.BlockSpec((8, part), lambda i, *_: (0, i)),
                    pl.BlockSpec((turns, part), lambda i, *_: (0, i)),
                ],
                out_specs=[quarter, quarter],
            ),
            out_shape=[shape((half, 4, depth, width), bf)] * 2,
            compiler_params=params(60),
            name="rest_grads",
        )(core, hin, d_proj, d_xb, sums_0, sums, sums_ff)
    else:
        g_vec = jnp.concatenate([sums_0[:4], sums[:3], sums_ff, sums[3:6]], axis=0)
        g_pos = jnp.sum(d_xb.astype(f32).reshape(sents, length, width), axis=0).T
        spare = jnp.zeros((width, width - length - g_vec.shape[0]), f32)
        rest = [dot_tn(hin, d_proj[i]) for i in range(3)] + [jnp.concatenate([g_pos, g_vec.T, spare], axis=1)]
        rest = jnp.stack([g.astype(bf).reshape(devices, depth, width) for g in rest], axis=1)
    return loss[0, 0], dense, rest, d_xb, give_rows


def swap(v, bit, devices):
    return lax.ppermute(v, AXES, [(i, i ^ bit) for i in range(devices)])


def add(a, b):
    return (a.astype(f32) + b.astype(f32)).astype(bf)


def gather_sums(keep, send):
    devices = 32
    x = lax.axis_index("seq") // 2
    y = lax.rem(lax.axis_index("dp"), 2)
    kinds = keep.shape[1]
    view = lambda v: v.reshape((4, 2, 2) + v.shape[1:])
    keep, send = view(keep), view(send)
    pick = lambda v, axis, index: lax.dynamic_index_in_dim(v, index, axis, keepdims=False)
    cut = kinds // 2
    one = add(keep[:, :, :, :cut], swap(send[:, :, :, :cut], 1, devices))
    two = add(keep[:, :, :, cut:], swap(send[:, :, :, cut:], 1, devices))
    one = add(pick(one, 2, x), swap(pick(one, 2, 1 - x), 2, devices))
    two = add(pick(two, 1, y), swap(pick(two, 1, 1 - y), 4, devices))
    one = add(pick(one, 1, y), swap(pick(one, 1, 1 - y), 4, devices))
    two = add(pick(two, 1, x), swap(pick(two, 1, 1 - x), 2, devices))
    both = jnp.concatenate([one, two], axis=1)
    groups = [[low + 8 * z for z in range(4)] for low in range(8)]
    both = lax.all_to_all(both, AXES, 0, 0, tiled=True, axis_index_groups=groups)
    return jnp.sum(both.astype(f32), axis=0)


def body(
    token_ids, lengths, labeled, gold,
    embed, position, attn_in, attn_out, ff_in, ff_out, vectors,
    mom_embed, mom_position, mom_attn_in, mom_attn_out, mom_ff_in, mom_ff_out, mom_vectors,
    avg_embed, avg_position, avg_attn_in, avg_attn_out, avg_ff_in, avg_ff_out, avg_vectors,
):
    pairs_here, _, local = token_ids.shape
    seq = lax.axis_size("seq")
    devices = lax.axis_size("dp") * seq
    length = local * seq
    per_owner, width = embed.shape
    depth = attn_in.shape[0]
    hidden = ff_in.shape[1]
    nvec = vectors.shape[0]
    turns = ff_out.shape[0] // depth
    mine = pairs_here // seq
    sents = 2 * mine
    rows = sents * length
    spare = 128 - nvec

    shard = jnp.concatenate(
        [attn_in, attn_out, ff_in]
        + [ff_out[i * depth : (i + 1) * depth] for i in range(turns)]
        + [position.T, vectors.T, jnp.zeros((depth, spare), f32)],
        axis=1,
    ).astype(bf)
    full = lax.all_gather(shard, AXES, axis=0, tiled=True)

    ids = lax.all_to_all(token_ids, "seq", 0, 2, tiled=True).reshape(rows)
    turn = lax.axis_index("seq") * mine
    lens = lax.dynamic_slice_in_dim(lengths, turn, mine, 0).reshape(sents)
    lab = lax.dynamic_slice_in_dim(labeled, turn, mine, 0)
    goal = lax.dynamic_slice_in_dim(gold, turn, mine, 0)
    lab_f = lab.astype(f32)
    used = (jnp.arange(length)[None, :] < lens[:, None]) & (jnp.repeat(lab, 2) > 0)[:, None]
    used = used.reshape(rows)
    owner, place, first, rank = route(ids, used, per_owner)
    most = jnp.max(jnp.where(used, rank + 1, 0))
    asked = requests(owner, place, first, rank, 0, devices).reshape(devices, SLOTS)
    note = jnp.stack([most, jnp.sum(lab)])[None, :]
    note = jnp.broadcast_to(note, (devices, 2))
    got = exchange(jnp.concatenate([asked, note, jnp.zeros((devices, 126 - SLOTS), jnp.int32)], axis=1))
    rounds = (jnp.max(got[:, SLOTS]) + SLOTS - 1) // SLOTS
    count = jnp.maximum(jnp.sum(got[:, SLOTS + 1]).astype(f32), 1.0)

    table = embed.astype(bf)
    slots = token_slots(owner, used, rank, 0)
    wanted_first = got[:, :SLOTS].reshape(-1)

    def pick(wanted):
        picked = mm(one_hot(wanted, per_owner), table).astype(bf).reshape(devices, SLOTS, width)
        return exchange(picked).reshape(devices * SLOTS, width)

    back = pick(wanted_first)

    def ask_again(start):
        return exchange(requests(owner, place, first, rank, start, devices).reshape(devices, SLOTS)).reshape(-1)

    def more(state):
        step, total = state
        start = step * SLOTS
        there = one_hot(token_slots(owner, used, rank, start), devices * SLOTS)
        return step + 1, total + mm(there, pick(ask_again(start))).astype(bf)

    _, extra = lax.while_loop(lambda state: state[0] < rounds, more, (jnp.int32(1), jnp.zeros((rows, width), bf)))
    facts = jnp.stack([lab_f[0], goal[0], count, count])
    core = lax.rem(lax.axis_index("seq"), 2)[None]
    loss, dense, rest, d_xb, give_rows = run_forward_backward(
        full, back, extra, slots, lens, facts, core, devices, depth, length, hidden
    )

    scatter = lambda g: lax.psum_scatter(g, AXES, scatter_dimension=0, tiled=True).astype(f32)[0]
    dense = scatter(dense)
    if not isinstance(rest, list | tuple):
        rest = scatter(rest)
    elif (seq, devices) == (4, 32):
        rest = gather_sums(*rest)
    else:
        keep, send = rest
        both = jnp.stack([jnp.where(core[0] == 0, keep, send), jnp.where(core[0] == 0, send, keep)], axis=1)
        rest = scatter(both.reshape((devices,) + keep.shape[1:]))
    beside = lambda v: jnp.concatenate(list(v), axis=1)
    g_ff_out = dense[:turns].reshape(turns * depth, width)
    g_ff_in = beside(dense[turns : 2 * turns])
    g_attn_out = dense[2 * turns]
    g_attn_in = beside(rest[:3])
    g_position = rest[3, :, :length].T
    g_vectors = rest[3, :, length : length + nvec].T

    def give(wanted, sums):
        there = exchange(sums.reshape(devices, SLOTS, width)).reshape(devices * SLOTS, width)
        return mm_left(one_hot(wanted, per_owner), there)

    def more_back(state):
        step, total = state
        start = step * SLOTS
        sums = mm_left(one_hot(token_slots(owner, used, rank, start), devices * SLOTS), d_xb).astype(bf)
        return step + 1, total + give(ask_again(start), sums)

    _, g_embed = lax.while_loop(lambda state: state[0] < rounds, more_back, (jnp.int32(1), give(wanted_first, give_rows)))

    grads = (g_embed, g_position, g_attn_in, g_attn_out, g_ff_in, g_ff_out, g_vectors)
    squares = sum(jnp.sum(g * g) for g in grads)
    sums = exchange(jnp.broadcast_to(jnp.stack([squares, loss])[None, :], (devices, 2)))
    sums = jnp.sum(sums, axis=0)
    norm = jnp.sqrt(sums[0])
    loss_sum = sums[1]
    scale = jnp.minimum(1.0, CLIP / (norm + 1e-06))
    weights = (embed, position, attn_in, attn_out, ff_in, ff_out, vectors)
    moms = (mom_embed, mom_position, mom_attn_in, mom_attn_out, mom_ff_in, mom_ff_out, mom_vectors)
    avgs = (avg_embed, avg_position, avg_attn_in, avg_attn_out, avg_ff_in, avg_ff_out, avg_vectors)
    news, next_moms, next_avgs = [], [], []
    for weight, grad, mom, avg in zip(weights, grads, moms, avgs):
        clipped = grad * scale
        moment = MOMENT * mom + clipped
        fresh = weight - RATE * (clipped + MOMENT * moment)
        news.append(fresh)
        next_moms.append(moment)
        next_avgs.append(DECAY * avg + (1.0 - DECAY) * fresh)
    return (loss_sum, count, norm, *news, *next_moms, *next_avgs)


def solution(mesh):
    whole = (
        P(AXES, None),
        P(None, AXES),
        P(AXES, None),
        P(AXES, None),
        P(AXES, None),
        P(AXES, None),
        P(None, AXES),
    )
    return jax.shard_map(
        body,
        mesh=mesh,
        in_specs=(P("dp", None, "seq"), P("dp", None), P("dp"), P("dp")) + whole * 3,
        out_specs=(P(), P(), P()) + whole * 3,
        check_vma=False,
    )
```

time: 719 us -> 562 us (0.78)
  matrix products: 215 us -> 8.35 us
  Pallas kernels: 0 us -> 178 us
  local copies, waits for them, and re-layouts: 94.9 us -> 21.5 us
  other arithmetic: 91 us -> 50.4 us
  waiting for transfers between devices: 260 us -> 228 us
  blocking collectives: 0 us -> 17.2 us
    pallas_call x0 -> x9, Pallas kernels: none -> 178 us  [the longest x1 32.3 us: run_forward_backward(): pl.pallas_call(functools.partial(middle_kernel, per_sent), grid_spec=pltp...]
    unnamed x5 -> x2, waiting for transfers between devices: 111 us -> 0.03 us
    dot_general x9 -> x0, matrix products: 96.5 us -> none  [the longest x4 40.6 us: mm_right(): lax.dot_general(left, right, (((1,), (1,)), ((), ())), preferred_element_...]
    dot_general x6 -> x1, matrix products: 63.4 us -> 4.5 us  [mm(): return jnp.dot(left, right, preferred_element_type=f32)]
    all_to_all x4, waiting for transfers between devices: 81.8 us -> 123 us  [exchange(): return lax.all_to_all(v, AXES, 0, 0, tiled=True)]
    dot_general x6 -> x1, matrix products: 38.7 us -> 3.85 us  [mm_left(): lax.dot_general(left, right, (((0,), (0,)), ((), ())), preferred_element_...]
    reduce_sum x16 -> x1, other arithmetic: 22.9 us -> 0.08 us  [gather_sums(): return jnp.sum(both.astype(f32), axis=0)]
    convert_element_type x6 -> x7, other arithmetic: 29.2 us -> 7.13 us  [the longest x6 6.11 us: add(): return (a.astype(f32) + b.astype(f32)).astype(bf)]
  transfers between devices with their start and end apart: 9 -> 13, of which waited for: 8 -> 11; matrix products, arithmetic and copies ran while one was open for 26% -> 7% of each run, Pallas kernels for 0% -> 0%
where the time goes in v2:
time: 562 us; the launch traced here: 553 us
  waiting for transfers between devices  228 us (41%)
  Pallas kernels  178 us (32%)
  other arithmetic  50.4 us (9%)
  between operations  24.9 us (4%)
  starting transfers between devices  23.5 us (4%)
  local copies, waits for them, and re-layouts  21.5 us (4%)
  blocking collectives  17.2 us (3%)
  matrix products  8.35 us (1%)
    all_to_all x4, waiting for transfers between devices, exchange(): return lax.all_to_all(v, AXES, 0, 0, tiled=True)  123 us
    reduce_scatter x1, waiting for transfers between devices, body(): lax.psum_scatter(g, AXES, scatter_dimension=0, tiled=True).astype(f32)[0]  45.6 us
    all_gather x1, waiting for transfers between devices, body(): full = lax.all_gather(shard, AXES, axis=0, tiled=True)  36.7 us
    pallas_call x1, Pallas kernels, run_forward_backward(): pl.pallas_call(functools.partial(middle_kernel, per_sent), grid_spec=pltp...  32.3 us
    pallas_call x1, Pallas kernels, run_forward_backward(): pl.pallas_call(attend_back_kernel, grid_spec=pltpu.PrefetchScalarGridSpec...  30.3 us
    pallas_call x1, Pallas kernels, run_forward_backward(): pl.pallas_call(functools.partial(back_kernel, per_sent), grid_spec=pltpu....  28.1 us
    pallas_call x1, Pallas kernels, run_forward_backward(): pl.pallas_call(attend_kernel, grid_spec=pltpu.PrefetchScalarGridSpec(num_...  21 us
    pallas_call x1, Pallas kernels, run_forward_backward(): pl.pallas_call(functools.partial(dense_grads_kernel, depth, turns), grid=...  19.2 us
  transfers between devices with their start and end apart: 13, of which 11 were waited for; matrix products, arithmetic and copies ran while one was open for 7% of the time, Pallas kernels for 0%

profile of v2, /device:TPU:0, one launch (start us, length us, event | category | flops | bytes accessed | tf_op | source)
XLA Modules:
  0.0 552.6 jit_solution(17851281348303952850)
XLA Ops:
  7.3 1.1 convert.36
  8.4 1.0 convert.35
  9.4 1.0 convert.33
  10.4 0.9 convert.34
  12.9 0.9 concatenate.17
  15.2 4.2 all-to-all-start.4
  19.6 3.6 all-to-all-done.4
  24.0 1.5 convert_reduce_fusion
  26.9 1.4 pad_add_fusion
  29.0 5.4 all-to-all-start.5
  34.4 1.3 convert_element_type.104
  35.6 5.8 %all-to-all-done.5 = s32[32,1,128]{2,1,0:T(1,128)S(1)} async-done(((s32[32,1,128]{2,1,0:T(1,128)}), s32[32,1,128]{2,1,0:T(1,128)S(1)}, u32[]{:S(2)}, u32[]{:S(2)}) %all-to-all-start.5) | async-done | bytes 16416 | tf_op jit(solution)/shard_map/all_to_all | solution.py:38
  42.9 4.5 fusion.22
  47.5 2.7 all-to-all-start.6
  52.5 1.0 copy.187
  53.5 1.0 copy.191
  55.2 2.3 fusion.29.slot
  58.1 1.2 pad_maximum_fusion.3.facts
  59.3 50.7 %all-to-all-done.6 = bf16[32,32,768]{2,1,0:T(8,128)(2,1)S(1)} async-done(((bf16[32,32,768]{2,1,0:T(8,128)(2,1)}), bf16[32,32,768]{2,1,0:T(8,128)(2,1)S(1)}, u32[]{:S(2)}, u32[]{:S(2)}) %all-to-all-start.6) | async-done | bytes 1572896 | tf_op jit(solution)/shard_map/all_to_all | solution.py:38
  110.0 36.7 %all-gather.2.cloned.1.call-done.w_qkv.pos_t.vec_t.src.w_out.w_in = bf16[768,9856]{1,0:T(8,128)(2,1)} async-done(((bf16[24,9856]{1,0:T(8,128)(2,1)}), bf16[768,9856]{1,0:T(8,128)(2,1)}) %all-gather.2.cloned.1.call-update) | async-done | bytes 15138832 | tf_op jit(solution)/shard_map/all_gather | solution.py:607
  146.6 13.2 %first.1 = (f32[1024,768]{1,0:T(8,128)}, bf16[1024,768]{1,0:T(8,128)(2,1)}, bf16[1024,2304]{1,0:T(8,128)(2,1)}, f32[16,768]{1,0:T(8,128)}) custom-call(s32[1024,1]{1,0:T(8,128)} %fusion.29.slot, bf16[1024,768]{1,0:T(8,128)(2,1)} %bitcast.159, bf16[1024,768]{1,0:T(8,128)(2,1)S(1)} %get-tuple-element.145.extra, ...), custom_call_target="tpu_custom_call" | custom-call | tf_op jit(solution)/shard_map/first/pallas_call | solution.py:399
  159.9 21.0 %attend.1.mixed = bf16[1024,768]{1,0:T(8,128)(2,1)} custom-call(s32[2]{0:T(128)S(1)} %get-tuple-element.723, bf16[1024,2304]{1,0:T(8,128)(2,1)} %get-tuple-element.147.query.keys.values, bf16[1024,2304]{1,0:T(8,128)(2,1)} %get-tuple-element.147.query.keys.values, bf16[1024,2304]{1,0:T(8,128)(2,1)} %get-tuple-element.147.query.keys.values), custom_call_target="tpu_custom_call" | custom-call | tf_op jit(solution)/shard_map/attend/pallas_call | solution.py:417
  182.2 10.3 %spread.1.w_back = bf16[3072,768]{1,0:T(8,128)(2,1)} custom-call(bf16[768,9856]{1,0:T(8,128)(2,1)} %all-gather.2.cloned.1.call-done.w_qkv.pos_t.vec_t.src.w_out.w_in), custom_call_target="tpu_custom_call" | custom-call | tf_op jit(solution)/shard_map/spread/pallas_call | solution.py:380
  192.6 32.3 %middle.1 = (f32[1024,768]{1,0:T(8,128)}, bf16[1024,768]{1,0:T(8,128)(2,1)}, bf16[1024,3072]{1,0:T(8,128)(2,1)}, bf16[1024,3072]{1,0:T(8,128)(2,1)}, f32[1024,768]{1,0:T(8,128)}, /*index=5*/f32[8,768]{1,0:T(8,128)}) custom-call(s32[2]{0:T(128)S(1)} %get-tuple-element.723, f32[1024,768]{1,0:T(8,128)} %get-tuple-element.146.x, bf16[1024,768]{1,0:T(8,128)(2,1)} %attend.1.mixed, ...), custom_call_target="tpu_custom_call" | custom-call | tf_op jit(solution)/shard_map/middle/pallas_call | solution.py:431
  224.9 28.1 %back.1 = (bf16[1024,768]{1,0:T(8,128)(2,1)}, bf16[1024,3072]{1,0:T(8,128)(2,1)}, f32[1024,768]{1,0:T(8,128)}, bf16[1024,768]{1,0:T(8,128)(2,1)}, bf16[1024,768]...) custom-call(s32[2]{0:T(128)S(1)} %get-tuple-element.723, f32[4]{0:T(128)} %pad_maximum_fusion.3.facts, ...), custom_call_target="tpu_custom_call" | custom-call | tf_op jit(solution)/shard_map/back/pallas_call | solution.py:449
  253.0 19.2 %dense_grads.1 = bf16[32,9,24,768]{3,2,1,0:T(8,128)(2,1)} custom-call(bf16[1024,3072]{1,0:T(8,128)(2,1)} %get-tuple-element.155.act, bf16[1024,768]{1,0:T(8,128)(2,1)} %get-tuple-element.156.d_y, bf16[1024,768]{1,0:T(8,128)(2,1)} %get-tuple-element.157.h1, bf16[1024,3072]{1,0:T(8,128)(2,1)} %get-tuple-element.158.d_f, bf16[1024,768]{1,0:T(8,128)(2,1)} %attend.1.mixed, ...), custom_call_target="tpu_custom_call" | custom-call | tf_op jit(solution)/shard_map/dense_grads/pallas_call | solution.py:477
  272.2 30.3 %attend_back.1.d_proj = bf16[3,1024,768]{2,1,0:T(8,128)(2,1)} custom-call(s32[2]{0:T(128)S(1)} %get-tuple-element.723, bf16[1024,2304]{1,0:T(8,128)(2,1)} %get-tuple-element.147.query.keys.values, bf16[1024,2304]{1,0:T(8,128)(2,1)} %get-tuple-element.147.query.keys.values, bf16[1024,2304]{1,0:T(8,128)(2,1)} %get-tuple-element.147.query.keys.values, ...), custom_call_target="tpu_custom_call" | custom-call | tf_op jit(solution)/shard_map/attend_back/pallas_call | solution.py:495
  302.5 14.2 %last.1 = (bf16[1024,768]{1,0:T(8,128)(2,1)S(1)}, f32[8,768]{1,0:T(8,128)}, bf16[1024,768]{1,0:T(8,128)(2,1)}) custom-call(s32[1,1024]{1,0:T(1,128)} %and_select_fusion.4.slot, f32[1024,768]{1,0:T(8,128)} %get-tuple-element.146.x, f32[1024,768]{1,0:T(8,128)} %get-tuple-element.153.d_r1, bf16[3,1024,768]{2,1,0:T(8,128)(2,1)} %attend_back.1.d_proj, ...), custom_call_target="tpu_custom_call" | custom-call | tf_op jit(solution)/shard_map/last/pallas_call | solution.py:508
  316.7 9.6 %rest_grads.1 = (bf16[16,4,24,768]{3,2,1,0:T(8,128)(2,1)}, bf16[16,4,24,768]{3,2,1,0:T(8,128)(2,1)}) custom-call(s32[1]{0:T(128)} %bitcast.20.core, bf16[1024,768]{1,0:T(8,128)(2,1)} %get-tuple-element.161.hin, bf16[3,1024,768]{2,1,0:T(8,128)(2,1)} %attend_back.1.d_proj, bf16[1024,768]{1,0:T(8,128)(2,1)S(1)} %get-tuple-element.666.d_x, ...), custom_call_target="tpu_custom_call" | custom-call | tf_op jit(solution)/shard_map/rest_grads/pallas_call | solution.py:527
  326.3 1.8 fusion.53
  328.1 1.1 copy.209
  329.5 1.1 copy.211
  330.9 1.6 copy-done.6
  332.8 1.6 add_convert_fusion.1
  334.5 1.0 collective-permute-start.1
  335.5 1.7 add_convert_fusion
  338.1 1.0 collective-permute-start.4
  339.1 11.0 %collective-permute-done.1 = bf16[4,2,2,24,768]{4,3,2,0,1:T(8,128)(2,1)} collective-permute-done((bf16[4,2,2,24,768]{4,3,2,0,1:T(8,128)(2,1)S(1)}, bf16[4,2,2,24,768]{4,3,2,0,1:T(8,128)(2,1)}, u32[]{:S(2)}, u32[]{:S(2)}) %collective-permute-start.1) | collective-permute-done | bytes 589856 | tf_op jit(solution)/shard_map/ppermute | solution.py:553
  350.2 1.3 fusion.24
  351.5 1.0 collective-permute-start.2
  352.5 1.1 collective-permute-done.4
  353.6 1.3 fusion.23
  355.0 1.0 collective-permute-start.5
  356.0 3.9 collective-permute-done.2
  360.0 3.1 collective-permute-done.5
  363.2 17.2 %all_to_all.88 = bf16[4,4,24,768]{3,2,1,0:T(8,128)(2,1)S(1)} all-to-all(bf16[4,4,24,768]{3,2,1,0:T(8,128)(2,1)S(1)} %pad_maximum_fusion), channel_id=1, replica_groups={{0,8,16,24},{1,9,17,25},{2,10,18,26},{3,11,19,27},{4,12,20,28},{5,13,21..., dimensions={0} | all-to-all | bytes 1179648 | tf_op jit(solution)/shard_map/all_to_all | solution.py:577
  380.4 2.7 all-to-all-start.7
  383.1 1.2 slice.93
  386.3 60.7 %all-to-all-done.7 = bf16[32,32,768]{2,1,0:T(8,128)(2,1)S(1)} async-done(((bf16[32,32,768]{2,1,0:T(8,128)(2,1)}), bf16[32,32,768]{2,1,0:T(8,128)(2,1)S(1)}, u32[]{:S(2)}, u32[]{:S(2)}) %all-to-all-start.7) | async-done | bytes 1572896 | tf_op jit(solution)/shard_map/all_to_all | solution.py:38
  447.0 3.9 fusion.17
  451.1 3.3 multiply_reduce_fusion
  456.4 45.6 %reduce-scatter.2.cloned.1.call-done = bf16[1,9,24,768]{3,2,1,0:T(8,128)(2,1)} async-done(((bf16[32,9,24,768]{3,2,1,0:T(8,128)(2,1)}), bf16[1,9,24,768]{3,2,1,0:T(8,128)(2,1)}) %reduce-scatter.2.cloned.1.call-update) | async-done | bytes 331792 | tf_op jit(solution)/shard_map/reduce_scatter | solution.py:652
  502.0 1.0 convert_element_type.131
  509.0 3.7 all-to-all-start.9
  513.6 6.2 %all-to-all-done.9 = f32[32,1,2]{2,1,0:T(1,128)S(1)} async-done(((f32[32,1,2]{2,1,0:T(1,128)}), f32[32,1,2]{2,1,0:T(1,128)S(1)}, u32[]{:S(2)}, u32[]{:S(2)}) %all-to-all-start.9) | async-done | bytes 288 | tf_op jit(solution)/shard_map/all_to_all | solution.py:38
  522.0 1.5 add_multiply_fusion.6
  523.4 1.4 copy.204
  524.8 1.4 copy.205
  526.2 1.4 copy.206
  527.6 2.2 add_multiply_fusion.2
  529.8 1.7 add_multiply_fusion.4
  531.5 2.0 add_multiply_fusion.3
  534.2 8.1 %add_multiply_fusion = (f32[960,768]{1,0:T(8,128)}, f32[960,768]{1,0:T(8,128)}, f32[960,768]{1,0:T(8,128)}) fusion(f32[960,768]{1,0:T(8,128)} %param.47, f32[960,768]{1,0:T(8,128)S(1)} %copy-done.3, f32[960,768]{1,0:T(8,128)} %get-tuple-element.164, f32[]{:T(128)S(6)} %min.3, f32[960,768]{1,0:T(8,128)} %param.40), kind=kLoop, calls=%fused_computation.44 | loop fusion | flops 6635520 | bytes 20643844 | tf_op jit(solution)/shard_map/add | solution.py:699
  542.3 1.0 add_multiply_fusion.1
  (115 shorter events, 20.5 us)
Async XLA Ops:
  7.2 6.6 %copy-start = (s32[4,2]{0,1:T(2,128)S(1)}, s32[4,2]{0,1:T(2,128)}, u32[]{:S(2)}) copy-start(s32[4,2]{0,1:T(2,128)} %param.30) | copy-start | bytes 100
  7.2 6.7 %copy-start.22 = (s32[4]{0:T(128)S(1)}, s32[4]{0:T(128)}, u32[]{:S(2)}) copy-start(s32[4]{0:T(128)} %param.31) | copy-start | bytes 52
  7.2 27.1 %copy-start.2 = (f32[960,768]{1,0:T(8,128)S(1)}, f32[960,768]{1,0:T(8,128)}, u32[]{:S(2)}) copy-start(f32[960,768]{1,0:T(8,128)} %param.33) | copy-start | bytes 8847364
  7.2 139.4 %all-gather.2.cloned.1.call-start = ((), (), s32[]{:S(2)}) async-start(), calls=%async_computation.11 | async-start | bytes 15611904 | tf_op jit(solution)/shard_map/all_gather | solution.py:607
  15.2 8.0 %all-to-all-start.4 = ((s32[4,2,128]{2,1,0:T(2,128)}), s32[4,2,128]{2,1,0:T(2,128)S(1)}, u32[]{:S(2)}, u32[]{:S(2)}) async-start(s32[4,2,128]{2,1,0:T(2,128)} %param.29), calls=%async_computation.4 | async-start | bytes 8192 | tf_op jit(solution)/shard_map/all_to_all | solution.py:609
  29.0 12.5 %all-to-all-start.5 = ((s32[32,1,128]{2,1,0:T(1,128)}), s32[32,1,128]{2,1,0:T(1,128)S(1)}, u32[]{:S(2)}, u32[]{:S(2)}) async-start(s32[32,1,128]{2,1,0:T(1,128)} %bitcast.7), calls=%async_computation.5 | async-start | bytes 32768 | tf_op jit(solution)/shard_map/all_to_all | solution.py:38
  47.5 3.9 copy-start.23
  47.5 62.5 %all-to-all-start.6 = ((bf16[32,32,768]{2,1,0:T(8,128)(2,1)}), bf16[32,32,768]{2,1,0:T(8,128)(2,1)S(1)}, u32[]{:S(2)}, u32[]{:S(2)}) async-start(bf16[32,32,768]{2,1,0:T(8,128)(2,1)} %bitcast.164), calls=%async_computation.6 | async-start | bytes 3145728 | tf_op jit(solution)/shard_map/all_to_all | solution.py:38
  50.2 451.8 %reduce-scatter.2.cloned.1.call-start = ((), (), s32[]{:S(2)}) async-start(), calls=%async_computation.12 | async-start | bytes 10948608 | tf_op jit(solution)/shard_map/reduce_scatter | solution.py:652
  110.0 36.7 %copy-start.4 = (bf16[32,32,768]{2,1,0:T(8,128)(2,1)}, bf16[32,32,768]{2,1,0:T(8,128)(2,1)S(1)}, u32[]{:S(2)}) copy-start(bf16[32,32,768]{2,1,0:T(8,128)(2,1)S(1)} %all-to-all-done.6) | copy-start | bytes 4718596
  316.7 9.6 %copy-start.7 = (bf16[1024,768]{1,0:T(8,128)(2,1)}, bf16[1024,768]{1,0:T(8,128)(2,1)S(1)}, u32[]{:S(2)}) copy-start(bf16[1024,768]{1,0:T(8,128)(2,1)S(1)} %get-tuple-element.666.d_x) | copy-start | bytes 4718596
  329.2 3.6 collective-permute-start
  330.6 4.9 collective-permute-start.3
  330.8 1.7 copy-start.6
  334.5 15.7 %collective-permute-start.1 = (bf16[4,2,2,24,768]{4,3,2,0,1:T(8,128)(2,1)S(1)}, bf16[4,2,2,24,768]{4,3,2,0,1:T(8,128)(2,1)}, u32[]{:S(2)}, u32[]{:S(2)}) collective-permute-start(bf16[4,2,2,24,768]{4,3,2,0,1:T(8,128)(2,1)S(1)} %dynamic-slice_bitcast_fusion.1), channel_id=1, source_target_pairs={{0,2},{1,3},{2,0},{3,1},{4,6},{5,7},{6,4},{7,5},{8,10},{9,11},{10,... | collective-permute-start | bytes 1769480 | tf_op jit(solution)/shard_map/ppermute | solution.py:553
  338.1 15.5 %collective-permute-start.4 = (bf16[4,2,2,24,768]{4,3,2,0,1:T(8,128)(2,1)}, bf16[4,2,2,24,768]{4,3,2,0,1:T(8,128)(2,1)}, u32[]{:S(2)}, u32[]{:S(2)}) collective-permute-start(bf16[4,2,2,24,768]{4,3,2,0,1:T(8,128)(2,1)} %dynamic-slice_bitcast_fusion), channel_id=1, source_target_pairs={{0,4},{1,5},{2,6},{3,7},{4,0},{5,1},{6,2},{7,3},{8,12},{9,13},{10,... | collective-permute-start | bytes 1769480 | tf_op jit(solution)/shard_map/ppermute | solution.py:553
  351.5 8.4 %collective-permute-start.2 = (bf16[4,2,24,768]{3,2,1,0:T(8,128)(2,1)S(1)}, bf16[4,2,24,768]{3,2,1,0:T(8,128)(2,1)S(1)}, u32[]{:S(2)}, u32[]{:S(2)}) collective-permute-start(bf16[4,2,24,768]{3,2,1,0:T(8,128)(2,1)S(1)} %dynamic-slice_bitcast_fusion.3), channel_id=1, source_target_pairs={{0,4},{1,5},{2,6},{3,7},{4,0},{5,1},{6,2},{7,3},{8,12},{9,13},{10,... | collective-permute-start | bytes 884744 | tf_op jit(solution)/shard_map/ppermute | solution.py:553
  355.0 8.1 %collective-permute-start.5 = (bf16[4,2,24,768]{3,2,1,0:T(8,128)(2,1)S(1)}, bf16[4,2,24,768]{3,2,1,0:T(8,128)(2,1)S(1)}, u32[]{:S(2)}, u32[]{:S(2)}) collective-permute-start(bf16[4,2,24,768]{3,2,1,0:T(8,128)(2,1)S(1)} %dynamic-slice_bitcast_fusion.2), channel_id=1, source_target_pairs={{0,2},{1,3},{2,0},{3,1},{4,6},{5,7},{6,4},{7,5},{8,10},{9,11},{10,... | collective-permute-start | bytes 884744 | tf_op jit(solution)/shard_map/ppermute | solution.py:553
  380.4 66.6 %all-to-all-start.7 = ((bf16[32,32,768]{2,1,0:T(8,128)(2,1)}), bf16[32,32,768]{2,1,0:T(8,128)(2,1)S(1)}, u32[]{:S(2)}, u32[]{:S(2)}) async-start(bf16[32,32,768]{2,1,0:T(8,128)(2,1)} %bitcast.18), calls=%async_computation.7 | async-start | bytes 3145728 | tf_op jit(solution)/shard_map/all_to_all | solution.py:38
  451.1 61.6 %copy-start.19 = (f32[14,24]{1,0:T(8,128)S(1)}, f32[14,24]{1,0:T(8,128)}, u32[]{:S(2)}) copy-start(f32[14,24]{1,0:T(8,128)} %param.39) | copy-start | bytes 4036
  451.1 61.7 %copy-start.20 = (f32[14,24]{1,0:T(8,128)S(1)}, f32[14,24]{1,0:T(8,128)}, u32[]{:S(2)}) copy-start(f32[14,24]{1,0:T(8,128)} %param.46) | copy-start | bytes 4036
  451.1 61.8 %copy-start.21 = (f32[14,24]{1,0:T(8,128)S(1)}, f32[14,24]{1,0:T(8,128)}, u32[]{:S(2)}) copy-start(f32[14,24]{1,0:T(8,128)} %param.53) | copy-start | bytes 4036
  503.0 18.1 %copy-start.5 = (f32[1,9,24,768]{3,2,1,0:T(8,128)}, f32[1,9,24,768]{3,2,1,0:T(8,128)S(1)}, u32[]{:S(2)}) copy-start(f32[1,9,24,768]{3,2,1,0:T(8,128)S(1)} %convert_element_type.131) | copy-start | bytes 1990660
  503.7 17.4 %copy-start.10 = (f32[24,768]{1,0:T(8,128)}, f32[24,768]{1,0:T(8,128)S(1)}, u32[]{:S(2)}) copy-start(f32[24,768]{1,0:T(8,128)S(1)} %get-tuple-element.463) | copy-start | bytes 221188
  503.7 17.4 %copy-start.11 = (f32[24,768]{1,0:T(8,128)}, f32[24,768]{1,0:T(8,128)S(1)}, u32[]{:S(2)}) copy-start(f32[24,768]{1,0:T(8,128)S(1)} %get-tuple-element.464) | copy-start | bytes 221188
  503.8 17.4 %copy-start.12 = (f32[24,768]{1,0:T(8,128)}, f32[24,768]{1,0:T(8,128)S(1)}, u32[]{:S(2)}) copy-start(f32[24,768]{1,0:T(8,128)S(1)} %get-tuple-element.465) | copy-start | bytes 221188
  503.8 17.4 %copy-start.13 = (f32[24,768]{1,0:T(8,128)}, f32[24,768]{1,0:T(8,128)S(1)}, u32[]{:S(2)}) copy-start(f32[24,768]{1,0:T(8,128)S(1)} %get-tuple-element.466) | copy-start | bytes 221188
  509.0 10.7 %all-to-all-start.9 = ((f32[32,1,2]{2,1,0:T(1,128)}), f32[32,1,2]{2,1,0:T(1,128)S(1)}, u32[]{:S(2)}, u32[]{:S(2)}) async-start(f32[32,1,2]{2,1,0:T(1,128)} %broadcast_in_dim.119), calls=%async_computation.10 | async-start | bytes 32768 | tf_op jit(solution)/shard_map/all_to_all | solution.py:38
  521.2 12.3 %copy-start.16 = (f32[512,24]{0,1:T(8,128)S(1)}, f32[512,24]{0,1:T(8,128)}, u32[]{:S(2)}) copy-start(f32[512,24]{0,1:T(8,128)} %param.34) | copy-start | bytes 147460
  521.9 12.2 %copy-start.3 = (f32[960,768]{1,0:T(8,128)S(1)}, f32[960,768]{1,0:T(8,128)}, u32[]{:S(2)}) copy-start(f32[960,768]{1,0:T(8,128)} %param.33) | copy-start | bytes 8847364
  527.6 6.0 %copy-start.17 = (f32[512,24]{0,1:T(8,128)S(1)}, f32[512,24]{0,1:T(8,128)}, u32[]{:S(2)}) copy-start(f32[512,24]{0,1:T(8,128)} %param.48) | copy-start | bytes 147460
  527.6 6.0 %copy-start.18 = (f32[512,24]{0,1:T(8,128)S(1)}, f32[512,24]{0,1:T(8,128)}, u32[]{:S(2)}) copy-start(f32[512,24]{0,1:T(8,128)} %param.41) | copy-start | bytes 147460
  534.2 8.1 %copy-start.8 = (f32[96,768]{1,0:T(8,128)S(1)}, f32[96,768]{1,0:T(8,128)}, u32[]{:S(2)}) copy-start(f32[96,768]{1,0:T(8,128)} %param.38) | copy-start | bytes 884740
  534.2 8.1 %copy-start.9 = (f32[1,4,24,768]{3,2,1,0:T(8,128)S(1)}, f32[1,4,24,768]{3,2,1,0:T(8,128)}, u32[]{:S(2)}) copy-start(f32[1,4,24,768]{3,2,1,0:T(8,128)} %slice_multiply_fusion) | copy-start | bytes 884740
  534.2 8.1 %copy-start.14 = (f32[96,768]{1,0:T(8,128)S(1)}, f32[96,768]{1,0:T(8,128)}, u32[]{:S(2)}) copy-start(f32[96,768]{1,0:T(8,128)} %param.52) | copy-start | bytes 884740
  534.2 8.1 %copy-start.15 = (f32[96,768]{1,0:T(8,128)S(1)}, f32[96,768]{1,0:T(8,128)}, u32[]{:S(2)}) copy-start(f32[96,768]{1,0:T(8,128)} %param.45) | copy-start | bytes 884740
  534.2 9.1 %copy-start.1 = (s32[4,2]{0,1:T(2,128)S(1)}, s32[4,2]{0,1:T(2,128)}, u32[]{:S(2)}) copy-start(s32[4,2]{0,1:T(2,128)} %param.30) | copy-start | bytes 100
Sparse Core Ops, SparseCore 0:
  13.9 132.7 all-gather.1
  331.0 170.9 reduce-scatter.1

commit v3 on v2

--- a/solution.py
+++ b/solution.py
@@ -175,8 +175,9 @@
     out[...] = total.astype(bf)
 
 
-def attend_back_kernel(lens, query, keys, values, d_out, d_proj):
-    size = lens[pl.program_id(0)]
+def attend_back_kernel(sent, lens, query, keys, values, d_out, *more):
+    size = lens[sent]
+    d_proj = more[-1]
     d_query, d_key, d_value = None, None, None
     add = lambda a, b: b if a is None else a + b
     for half in range(2):
@@ -324,15 +325,23 @@
     return v.reshape(v.shape[0] // depth, depth, v.shape[1])
 
 
-def dense_grads_kernel(depth, turns, act, d_y, h1, d_f, mixed, d_a, out):
+def put_split(keep, send, kind, g, mine):
+    g = g.reshape((g.shape[0] // 2, 2) + g.shape[1:])
+    even, odd = g[:, 0], g[:, 1]
+    keep[:, kind] = jnp.where(mine == 0, even, odd).astype(bf)
+    send[:, kind] = jnp.where(mine == 0, odd, even).astype(bf)
+
+
+def dense_grads_kernel(depth, turns, core, act, d_y, h1, d_f, mixed, d_a, keep, send):
     width = d_y.shape[1]
+    mine = core[0]
     g = dot_tn(act[...], d_y[...])
-    g = g.reshape(out.shape[0], turns, depth, width)
+    g = g.reshape(2 * keep.shape[0], turns, depth, width)
     for j in range(turns):
-        out[:, j] = g[:, j].astype(bf)
+        put_split(keep, send, j, g[:, j], mine)
     for j in range(turns):
-        out[:, turns + j] = blocks(dot_tn(h1[...], d_f[:, j * width : (j + 1) * width]), depth).astype(bf)
-    out[:, 2 * turns] = blocks(dot_tn(mixed[...], d_a[...]), depth).astype(bf)
+        put_split(keep, send, turns + j, blocks(dot_tn(h1[...], d_f[:, j * width : (j + 1) * width]), depth), mine)
+    put_split(keep, send, 2 * turns, blocks(dot_tn(mixed[...], d_a[...]), depth), mine)
 
 
 def rest_grads_kernel(depth, length, core, hin, d_proj, d_x, sums_0, sums, sums_ff, keep, send):
@@ -341,10 +350,7 @@
     mine = core[0]
 
     def put(kind, g):
-        g = g.reshape(part // (2 * depth), 2, depth, width)
-        even, odd = g[:, 0], g[:, 1]
-        keep[:, kind] = jnp.where(mine == 0, even, odd).astype(bf)
-        send[:, kind] = jnp.where(mine == 0, odd, even).astype(bf)
+        put_split(keep, send, kind, blocks(g, depth), mine)
 
     for i in range(3):
         put(i, dot_tn(hin[...], d_proj[i]))
@@ -363,7 +369,7 @@
     return pl.CostEstimate(flops=int(flops), bytes_accessed=int(nbytes), transcendentals=0)
 
 
-def run_forward_backward(full, back, extra, slots, lens, facts, core, devices, depth, length, hidden):
+def run_forward_backward(full, back, extra, slots, lens, facts, core, staged, devices, depth, length, hidden):
     width = back.shape[1]
     rows = slots.shape[0]
     sents = rows // length
@@ -474,36 +480,55 @@
     part = width // 2
     halves = lambda cols: pl.BlockSpec((rows, cols), lambda i, *_: (0, i))
     if tall:
+        quarter = pl.BlockSpec((half // 2, 2 * turns + 1, depth, width), lambda i, *_: (i, 0, 0, 0))
         dense = pl.pallas_call(
             functools.partial(dense_grads_kernel, depth, turns),
-            grid=(2,),
-            in_specs=[
-                halves(hidden // 2), fixed((rows, width), (0, 0)), halves(part), fixed((rows, hidden), (0, 0)), halves(part),
-                fixed((rows, width), (0, 0)),
-            ],
-            out_specs=pl.BlockSpec((half, 2 * turns + 1, depth, width), lambda i: (i, 0, 0, 0)),
-            out_shape=shape((devices, 2 * turns + 1, depth, width), bf),
+            grid_spec=pltpu.PrefetchScalarGridSpec(
+                num_scalar_prefetch=1,
+                grid=(2,),
+                in_specs=[
+                    halves(hidden // 2), fixed((rows, width), (0, 0)), halves(part), fixed((rows, hidden), (0, 0)), halves(part),
+                    fixed((rows, width), (0, 0)),
+                ],
+                out_specs=[quarter, quarter],
+            ),
+            out_shape=[shape((half, 2 * turns + 1, depth, width), bf)] * 2,
             compiler_params=params(60),
             name="dense_grads",
-        )(act, d_y, h1, d_f, mixed, d_a)
+        )(core, act, d_y, h1, d_f, mixed, d_a)
     else:
         cut = lambda g: g.astype(bf).reshape(devices, depth, -1, width).transpose(0, 2, 1, 3)
         g_out = dot_tn(act, d_y).astype(bf).reshape(devices, turns, depth, width)
         dense = jnp.concatenate([g_out, cut(dot_tn(h1, d_f)), cut(dot_tn(mixed, d_a))], axis=1)
-    d_o, dense = lax.optimization_barrier((d_o, dense))
-
-    d_proj = pl.pallas_call(
-        attend_back_kernel,
-        grid_spec=pltpu.PrefetchScalarGridSpec(
-            num_scalar_prefetch=1,
-            grid=(sents, pairs),
-            in_specs=[block(0), block(1), block(2), block(0)],
-            out_specs=pl.BlockSpec((3, length, GROUP), lambda s, p, *_: (0, s, p)),
-        ),
-        out_shape=shape((3, rows, width), bf),
-        compiler_params=params(56),
-        name="attend_back",
-    )(lens, qkv, qkv, qkv, d_o)
+    if staged:
+        dense = over_cores(*dense)
+    else:
+        d_o, dense = lax.optimization_barrier((d_o, dense))
+
+    def attend_back(sent, total):
+        part = lambda kind: pl.BlockSpec((length, GROUP), lambda p, *_: (sent, kind * pairs + p))
+        more = () if total is None else (total,)
+        return pl.pallas_call(
+            functools.partial(attend_back_kernel, sent),
+            grid_spec=pltpu.PrefetchScalarGridSpec(
+                num_scalar_prefetch=1,
+                grid=(pairs,),
+                in_specs=[part(0), part(1), part(2), part(0)] + [pl.BlockSpec(memory_space=pl.ANY)] * len(more),
+                out_specs=pl.BlockSpec((3, length, GROUP), lambda p, *_: (0, sent, p)),
+            ),
+            out_shape=shape((3, rows, width), bf),
+            input_output_aliases={5: 0} if more else {},
+            compiler_params=params(56),
+            cost_estimate=cost(10 * length * length * GROUP * pairs, 8 * length * width * 2),
+            name="attend_back",
+        )(lens, qkv, qkv, qkv, d_o, *more)
+
+    d_proj = None
+    for sent in range(sents):
+        d_proj = attend_back(sent, d_proj)
+        if staged and sent == 0:
+            d_proj, dense = lax.optimization_barrier((d_proj, dense))
+            dense = over_wide(*dense)
 
     d_xb, sums_0, give_rows = pl.pallas_call(
         last_kernel,
@@ -522,6 +547,8 @@
         name="last",
     )(slots[None, :], x, d_r1, d_proj, hin, full, vec)
 
+    if staged:
+        d_xb, dense = lax.optimization_barrier((d_xb, dense))
     if tall:
         quarter = pl.BlockSpec((half // 2, 4, depth, width), lambda i, *_: (i, 0, 0, 0))
         rest = pl.pallas_call(
@@ -557,25 +584,41 @@
     return (a.astype(f32) + b.astype(f32)).astype(bf)
 
 
-def gather_sums(keep, send):
-    devices = 32
-    x = lax.axis_index("seq") // 2
-    y = lax.rem(lax.axis_index("dp"), 2)
-    kinds = keep.shape[1]
+def spot(v, axis, index):
+    return lax.dynamic_index_in_dim(v, index, axis, keepdims=False)
+
+
+def place_in_slice():
+    row = lax.axis_index("dp")
+    return row // 2, lax.rem(row, 2), lax.axis_index("seq") // 2
+
+
+def over_cores(keep, send):
     view = lambda v: v.reshape((4, 2, 2) + v.shape[1:])
     keep, send = view(keep), view(send)
-    pick = lambda v, axis, index: lax.dynamic_index_in_dim(v, index, axis, keepdims=False)
-    cut = kinds // 2
-    one = add(keep[:, :, :, :cut], swap(send[:, :, :, :cut], 1, devices))
-    two = add(keep[:, :, :, cut:], swap(send[:, :, :, cut:], 1, devices))
-    one = add(pick(one, 2, x), swap(pick(one, 2, 1 - x), 2, devices))
-    two = add(pick(two, 1, y), swap(pick(two, 1, 1 - y), 4, devices))
-    one = add(pick(one, 1, y), swap(pick(one, 1, 1 - y), 4, devices))
-    two = add(pick(two, 1, x), swap(pick(two, 1, 1 - x), 2, devices))
+    cut = keep.shape[3] // 2
+    one = add(keep[:, :, :, :cut], swap(send[:, :, :, :cut], 1, 32))
+    two = add(keep[:, :, :, cut:], swap(send[:, :, :, cut:], 1, 32))
+    return one, two
+
+
+def over_wide(one, two):
+    _, y, x = place_in_slice()
+    return add(spot(one, 2, x), swap(spot(one, 2, 1 - x), 2, 32)), add(spot(two, 1, y), swap(spot(two, 1, 1 - y), 4, 32))
+
+
+def over_other(one, two):
+    _, y, x = place_in_slice()
+    return add(spot(one, 1, y), swap(spot(one, 1, 1 - y), 4, 32)), add(spot(two, 1, x), swap(spot(two, 1, 1 - x), 2, 32))
+
+
+def over_long(one, two):
+    z, _, _ = place_in_slice()
     both = jnp.concatenate([one, two], axis=1)
-    groups = [[low + 8 * z for z in range(4)] for low in range(8)]
-    both = lax.all_to_all(both, AXES, 0, 0, tiled=True, axis_index_groups=groups)
-    return jnp.sum(both.astype(f32), axis=0)
+    total = spot(both, 0, z).astype(f32)
+    for step in range(1, 4):
+        total = total + swap(spot(both, 0, z ^ step), 8 * step, 32).astype(f32)
+    return total
 
 
 def body(
@@ -645,20 +688,26 @@
     _, extra = lax.while_loop(lambda state: state[0] < rounds, more, (jnp.int32(1), jnp.zeros((rows, width), bf)))
     facts = jnp.stack([lab_f[0], goal[0], count, count])
     core = lax.rem(lax.axis_index("seq"), 2)[None]
+    staged = (seq, devices) == (4, 32) and depth % 8 == 0
     loss, dense, rest, d_xb, give_rows = run_forward_backward(
-        full, back, extra, slots, lens, facts, core, devices, depth, length, hidden
+        full, back, extra, slots, lens, facts, core, staged, devices, depth, length, hidden
     )
 
-    scatter = lambda g: lax.psum_scatter(g, AXES, scatter_dimension=0, tiled=True).astype(f32)[0]
-    dense = scatter(dense)
-    if not isinstance(rest, list | tuple):
-        rest = scatter(rest)
-    elif (seq, devices) == (4, 32):
-        rest = gather_sums(*rest)
+    def sum_up(parts):
+        if isinstance(parts, list | tuple):
+            keep, send = parts
+            both = jnp.stack([jnp.where(core[0] == 0, keep, send), jnp.where(core[0] == 0, send, keep)], axis=1)
+            parts = both.reshape((devices,) + keep.shape[1:])
+        return lax.psum_scatter(parts, AXES, scatter_dimension=0, tiled=True).astype(f32)[0]
+
+    give_rows = exchange(give_rows.reshape(devices, SLOTS, width))
+    if staged:
+        dense = over_long(*over_other(*dense))
+        rest = over_other(*over_wide(*over_cores(*rest)))
+        rest, give_rows = lax.optimization_barrier((rest, give_rows))
+        rest = over_long(*rest)
     else:
-        keep, send = rest
-        both = jnp.stack([jnp.where(core[0] == 0, keep, send), jnp.where(core[0] == 0, send, keep)], axis=1)
-        rest = scatter(both.reshape((devices,) + keep.shape[1:]))
+        dense, rest = sum_up(dense), sum_up(rest)
     beside = lambda v: jnp.concatenate(list(v), axis=1)
     g_ff_out = dense[:turns].reshape(turns * depth, width)
     g_ff_in = beside(dense[turns : 2 * turns])
@@ -667,15 +716,14 @@
     g_position = rest[3, :, :length].T
     g_vectors = rest[3, :, length : length + nvec].T
 
-    def give(wanted, sums):
-        there = exchange(sums.reshape(devices, SLOTS, width)).reshape(devices * SLOTS, width)
-        return mm_left(one_hot(wanted, per_owner), there)
+    def give(wanted, there):
+        return mm_left(one_hot(wanted, per_owner), there.reshape(devices * SLOTS, width))
 
     def more_back(state):
         step, total = state
         start = step * SLOTS
         sums = mm_left(one_hot(token_slots(owner, used, rank, start), devices * SLOTS), d_xb).astype(bf)
-        return step + 1, total + give(ask_again(start), sums)
+        return step + 1, total + give(ask_again(start), exchange(sums.reshape(devices, SLOTS, width)))
 
     _, g_embed = lax.while_loop(lambda state: state[0] < rounds, more_back, (jnp.int32(1), give(wanted_first, give_rows)))
 

time: 562 us -> 531 us (0.945)
  waiting for transfers between devices: 228 us -> 169 us
  starting transfers between devices: 23.5 us -> 44.6 us
  blocking collectives: 17.2 us -> 0 us
  other arithmetic: 50.4 us -> 62.4 us
  local copies, waits for them, and re-layouts: 21.5 us -> 29.7 us
    all_to_all x4, waiting for transfers between devices: 123 us -> 65.3 us  [exchange(): return lax.all_to_all(v, AXES, 0, 0, tiled=True)]
    ppermute x6 -> x18, waiting for transfers between devices: 19.1 us -> 66.7 us  [swap(): return lax.ppermute(v, AXES, [(i, i ^ bit) for i in range(devices)])]
    reduce_scatter x1 -> x0, waiting for transfers between devices: 45.6 us -> none  [body(): lax.psum_scatter(g, AXES, scatter_dimension=0, tiled=True).astype(f32)[0]]
    ppermute x6 -> x18, starting transfers between devices: 4.6 us -> 23.5 us  [swap(): return lax.ppermute(v, AXES, [(i, i ^ bit) for i in range(devices)])]
    all_to_all x1 -> x0, blocking collectives: 17.2 us -> none  [gather_sums(): lax.all_to_all(both, AXES, 0, 0, tiled=True, axis_index_groups=groups)]
    convert_element_type x6 -> x11, other arithmetic: 6.11 us -> 18 us  [add(): return (a.astype(f32) + b.astype(f32)).astype(bf)]
    pallas_call x2 -> x3, Pallas kernels: 49.5 us -> 52 us  [the longest x2 32.9 us: attend_back(): pl.pallas_call(functools.partial(attend_back_kernel, sent), grid_spec=plt...]
  transfers between devices with their start and end apart: 13 -> 24, of which waited for: 11 -> 12; matrix products, arithmetic and copies ran while one was open for 7% -> 10% of each run, Pallas kernels for 0% -> 11%
where the time goes in v3:
time: 531 us; the launch traced here: 522 us
  Pallas kernels  181 us (34%)
  waiting for transfers between devices  169 us (32%)
  other arithmetic  62.4 us (12%)
  starting transfers between devices  44.6 us (8%)
  local copies, waits for them, and re-layouts  29.7 us (6%)
  between operations  25.3 us (5%)
  matrix products  9.73 us (2%)
    ppermute x18, waiting for transfers between devices, swap(): return lax.ppermute(v, AXES, [(i, i ^ bit) for i in range(devices)])  66.7 us
    all_to_all x4, waiting for transfers between devices, exchange(): return lax.all_to_all(v, AXES, 0, 0, tiled=True)  65.3 us
    all_gather x1, waiting for transfers between devices, body(): full = lax.all_gather(shard, AXES, axis=0, tiled=True)  33.1 us
    pallas_call x2, Pallas kernels, attend_back(): pl.pallas_call(functools.partial(attend_back_kernel, sent), grid_spec=plt...  32.9 us
    pallas_call x1, Pallas kernels, run_forward_backward(): pl.pallas_call(functools.partial(middle_kernel, per_sent), grid_spec=pltp...  32.3 us
    pallas_call x1, Pallas kernels, run_forward_backward(): pl.pallas_call(functools.partial(back_kernel, per_sent), grid_spec=pltpu....  28.1 us
    ppermute x18, starting transfers between devices, swap(): return lax.ppermute(v, AXES, [(i, i ^ bit) for i in range(devices)])  23.5 us
    pallas_call x1, Pallas kernels, run_forward_backward(): pl.pallas_call(attend_kernel, grid_spec=pltpu.PrefetchScalarGridSpec(num_...  21 us
  transfers between devices with their start and end apart: 24, of which 12 were waited for; matrix products, arithmetic and copies ran while one was open for 10% of the time, Pallas kernels for 11%

profile of v3, /device:TPU:0, one launch (start us, length us, event | category | flops | bytes accessed | tf_op | source)
XLA Modules:
  0.0 521.8 jit_solution(6352138908922328728)
XLA Ops:
  7.3 1.1 convert.42
  15.2 4.2 all-to-all-start.4
  19.6 3.6 all-to-all-done.4
  24.0 1.5 convert_reduce_fusion
  26.9 1.4 pad_add_fusion
  29.0 5.4 %all-to-all-start.5 = ((s32[32,1,128]{2,1,0:T(1,128)}), s32[32,1,128]{2,1,0:T(1,128)S(1)}, u32[]{:S(2)}, u32[]{:S(2)}) async-start(s32[32,1,128]{2,1,0:T(1,128)} %bitcast.7), calls=%async_computation.5 | async-start | bytes 32768 | tf_op jit(solution)/shard_map/all_to_all | solution.py:38
  34.4 1.3 convert_element_type.194
  35.6 5.8 %all-to-all-done.5 = s32[32,1,128]{2,1,0:T(1,128)S(1)} async-done(((s32[32,1,128]{2,1,0:T(1,128)}), s32[32,1,128]{2,1,0:T(1,128)S(1)}, u32[]{:S(2)}, u32[]{:S(2)}) %all-to-all-start.5) | async-done | bytes 16416 | tf_op jit(solution)/shard_map/all_to_all | solution.py:38
  42.9 4.5 fusion.24
  47.5 2.9 all-to-all-start.6
  54.5 2.3 fusion.35.slot
  57.5 1.2 pad_maximum_fusion.2.facts
  58.7 53.9 %all-to-all-done.6 = bf16[32,32,768]{2,1,0:T(8,128)(2,1)S(1)} async-done(((bf16[32,32,768]{2,1,0:T(8,128)(2,1)}), bf16[32,32,768]{2,1,0:T(8,128)(2,1)S(1)}, u32[]{:S(2)}, u32[]{:S(2)}) %all-to-all-start.6) | async-done | bytes 1572896 | tf_op jit(solution)/shard_map/all_to_all | solution.py:38
  112.6 33.1 %all-gather.2.cloned.1.call-done.w_qkv.pos_t.vec_t.src.w_out.w_in = bf16[768,9856]{1,0:T(8,128)(2,1)} async-done(((bf16[24,9856]{1,0:T(8,128)(2,1)}), bf16[768,9856]{1,0:T(8,128)(2,1)}) %all-gather.2.cloned.1.call-update) | async-done | bytes 15138832 | tf_op jit(solution)/shard_map/all_gather | solution.py:650
  145.7 13.2 %first.1 = (f32[1024,768]{1,0:T(8,128)}, bf16[1024,768]{1,0:T(8,128)(2,1)}, bf16[1024,2304]{1,0:T(8,128)(2,1)}, f32[16,768]{1,0:T(8,128)}) custom-call(s32[1024,1]{1,0:T(8,128)} %fusion.35.slot, bf16[1024,768]{1,0:T(8,128)(2,1)} %bitcast.201, bf16[1024,768]{1,0:T(8,128)(2,1)S(1)} %get-tuple-element.154.extra, ...), custom_call_target="tpu_custom_call" | custom-call | tf_op jit(solution)/shard_map/first/pallas_call | solution.py:405
  158.9 21.0 %attend.1.mixed = bf16[1024,768]{1,0:T(8,128)(2,1)} custom-call(s32[2]{0:T(128)S(1)} %get-tuple-element.753, bf16[1024,2304]{1,0:T(8,128)(2,1)} %get-tuple-element.156.query.keys.values, bf16[1024,2304]{1,0:T(8,128)(2,1)} %get-tuple-element.156.query.keys.values, bf16[1024,2304]{1,0:T(8,128)(2,1)} %get-tuple-element.156.query.keys.values), custom_call_target="tpu_custom_call" | custom-call | tf_op jit(solution)/shard_map/attend/pallas_call | solution.py:423
  181.3 10.3 %spread.1.w_back = bf16[3072,768]{1,0:T(8,128)(2,1)} custom-call(bf16[768,9856]{1,0:T(8,128)(2,1)} %all-gather.2.cloned.1.call-done.w_qkv.pos_t.vec_t.src.w_out.w_in), custom_call_target="tpu_custom_call" | custom-call | tf_op jit(solution)/shard_map/spread/pallas_call | solution.py:386
  191.7 32.3 %middle.1 = (f32[1024,768]{1,0:T(8,128)}, bf16[1024,768]{1,0:T(8,128)(2,1)}, bf16[1024,3072]{1,0:T(8,128)(2,1)}, bf16[1024,3072]{1,0:T(8,128)(2,1)}, f32[1024,768]{1,0:T(8,128)}, /*index=5*/f32[8,768]{1,0:T(8,128)}) custom-call(s32[2]{0:T(128)S(1)} %get-tuple-element.753, f32[1024,768]{1,0:T(8,128)} %get-tuple-element.157.x, bf16[1024,768]{1,0:T(8,128)(2,1)} %attend.1.mixed, ...), custom_call_target="tpu_custom_call" | custom-call | tf_op jit(solution)/shard_map/middle/pallas_call | solution.py:437
  223.9 28.1 %back.1 = (bf16[1024,768]{1,0:T(8,128)(2,1)}, bf16[1024,3072]{1,0:T(8,128)(2,1)}, f32[1024,768]{1,0:T(8,128)}, bf16[1024,768]{1,0:T(8,128)(2,1)}, bf16[1024,768]...) custom-call(s32[2]{0:T(128)S(1)} %get-tuple-element.753, f32[4]{0:T(128)} %pad_maximum_fusion.2.facts, ...), custom_call_target="tpu_custom_call" | custom-call | tf_op jit(solution)/shard_map/back/pallas_call | solution.py:455
  252.0 19.2 %dense_grads.1 = (bf16[16,9,24,768]{3,2,1,0:T(8,128)(2,1)}, bf16[16,9,24,768]{3,2,1,0:T(8,128)(2,1)}) custom-call(s32[1]{0:T(128)} %bitcast.9.core, bf16[1024,3072]{1,0:T(8,128)(2,1)} %get-tuple-element.164.act, bf16[1024,768]{1,0:T(8,128)(2,1)} %get-tuple-element.165.d_y, bf16[1024,768]{1,0:T(8,128)(2,1)} %get-tuple-element.166.h1, ...), custom_call_target="tpu_custom_call" | custom-call | tf_op jit(solution)/shard_map/dense_grads/pallas_call | solution.py:484
  271.2 2.0 slice.115
  273.8 1.9 slice.113
  275.7 1.6 copy.222
  277.5 16.5 %attend_back.2.more_0_ = bf16[3,1024,768]{2,1,0:T(8,128)(2,1)} custom-call(s32[2]{0:T(128)S(1)} %get-tuple-element.753, bf16[1024,2304]{1,0:T(8,128)(2,1)} %get-tuple-element.156.query.keys.values, bf16[1024,2304]{1,0:T(8,128)(2,1)} %get-tuple-element.156.query.keys.values, bf16[1024,2304]{1,0:T(8,128)(2,1)} %get-tuple-element.156.query.keys.values, ...), custom_call_target="tpu_custom_call" | custom-call | flops 2013265920 | bytes 6291456 | tf_op jit(solution)/shard_map/attend_back/pallas_call | solution.py:511
  294.0 3.1 add_convert_fusion.1
  297.1 4.3 add_convert_fusion
  301.3 1.2 dynamic-slice_bitcast_fusion
  302.6 1.3 collective-permute-start.3
  303.8 1.2 dynamic-slice_bitcast_fusion.1
  305.0 1.6 collective-permute-start.2
  307.2 16.4 %attend_back.3.d_proj = bf16[3,1024,768]{2,1,0:T(8,128)(2,1)} custom-call(s32[2]{0:T(128)S(1)} %get-tuple-element.753, bf16[1024,2304]{1,0:T(8,128)(2,1)} %get-tuple-element.156.query.keys.values, bf16[1024,2304]{1,0:T(8,128)(2,1)} %get-tuple-element.156.query.keys.values, ...), custom_call_target="tpu_custom_call", output_to_operand_aliasing={{}: (5, {})} | custom-call | flops 2013265920 | bytes 6291456 | tf_op jit(solution)/shard_map/attend_back/pallas_call | solution.py:511
  323.5 14.2 %last.1 = (bf16[1024,768]{1,0:T(8,128)(2,1)}, f32[8,768]{1,0:T(8,128)}, bf16[1024,768]{1,0:T(8,128)(2,1)}) custom-call(s32[1,1024]{1,0:T(1,128)} %and_select_fusion.4.slot, f32[1024,768]{1,0:T(8,128)} %get-tuple-element.157.x, f32[1024,768]{1,0:T(8,128)} %get-tuple-element.172.d_r1, bf16[3,1024,768]{2,1,0:T(8,128)(2,1)} %attend_back.3.d_proj, ...), custom_call_target="tpu_custom_call" | custom-call | tf_op jit(solution)/shard_map/last/pallas_call | solution.py:533
  337.8 1.9 fusion.21
  339.7 3.3 fusion.20
  344.4 9.9 %rest_grads.1 = (bf16[16,4,24,768]{3,2,1,0:T(8,128)(2,1)}, bf16[16,4,24,768]{3,2,1,0:T(8,128)(2,1)}) custom-call(s32[1]{0:T(128)} %bitcast.9.core, bf16[1024,768]{1,0:T(8,128)(2,1)} %get-tuple-element.155.hin, bf16[3,1024,768]{2,1,0:T(8,128)(2,1)} %attend_back.3.d_proj, bf16[1024,768]{1,0:T(8,128)(2,1)} %get-tuple-element.690.d_x, ...), custom_call_target="tpu_custom_call" | custom-call | tf_op jit(solution)/shard_map/rest_grads/pallas_call | solution.py:554
  354.4 3.3 fusion.68
  359.8 1.2 slice.102
  361.0 3.5 all-to-all-start.7
  364.5 1.2 fusion.26
  365.8 23.5 %collective-permute-done.14 = bf16[4,5,24,768]{3,2,1,0:T(8,128)(2,1)} collective-permute-done((bf16[4,5,24,768]{3,2,1,0:T(8,128)(2,1)}, bf16[4,5,24,768]{3,2,1,0:T(8,128)(2,1)}, u32[]{:S(2)}, u32[]{:S(2)}) %collective-permute-start.14) | collective-permute-done | bytes 737312 | tf_op jit(solution)/shard_map/ppermute | solution.py:580
  389.3 1.3 fusion.25
  390.9 4.3 collective-permute-start.17
  395.2 2.4 add_convert_fusion.2
  398.7 4.4 collective-permute-done.15
  403.1 20.9 %collective-permute-done.16 = bf16[9,24,768]{2,1,0:T(8,128)(2,1)S(1)} collective-permute-done((bf16[9,24,768]{2,1,0:T(8,128)(2,1)S(1)}, bf16[9,24,768]{2,1,0:T(8,128)(2,1)S(1)}, u32[]{:S(2)}, u32[]{:S(2)}) %collective-permute-start.16) | collective-permute-done | bytes 331808 | tf_op jit(solution)/shard_map/ppermute | solution.py:580
  424.3 1.1 collective-permute-start.5
  427.3 13.3 %collective-permute-done.5 = bf16[4,2,2,24,768]{4,3,2,1,0:T(8,128)(2,1)S(1)} collective-permute-done((bf16[4,2,2,24,768]{4,3,2,1,0:T(8,128)(2,1)S(1)}, bf16[4,2,2,24,768]{4,3,2,1,0:T(8,128)(2,1)S(1)}, u32[]{:S(2)}, u32[]{:S(2)}) %collective-permute-start.5) | collective-permute-done | bytes 589856 | tf_op jit(solution)/shard_map/ppermute | solution.py:580
  440.8 1.2 collective-permute-start.6
  443.4 1.7 collective-permute-done.9
  445.2 2.5 collective-permute-done.6
  448.6 7.2 %collective-permute-start.10 = (bf16[4,24,768]{2,1,0:T(8,128)(2,1)}, bf16[4,24,768]{2,1,0:T(8,128)(2,1)S(1)}, u32[]{:S(2)}, u32[]{:S(2)}) collective-permute-start(bf16[4,24,768]{2,1,0:T(8,128)(2,1)} %get-tuple-element.489), channel_id=1, source_target_pairs={{0,8},{1,9},{2,10},{3,11},{4,12},{5,13},{6,14},{7,15},{8,0},{9,1},... | collective-permute-start | bytes 442376 | tf_op jit(solution)/shard_map/ppermute | solution.py:580
  456.2 1.9 collective-permute-start.12
  458.1 5.2 %fusion.17 = f32[960,768]{1,0:T(8,128)} fusion(bf16[1024,768]{1,0:T(8,128)(2,1)} %bitcast.36, s32[1024]{0:T(1024)S(1)} %copy-done.31), kind=kOutput, calls=%fused_computation.38 | convolution fusion | flops 1510932480 | bytes 4526080 | tf_op jit(solution)/shard_map/dot_general | solution.py:30
  463.6 3.2 multiply_reduce_fusion
  476.5 5.1 all-to-all-start.8
  483.0 5.6 %all-to-all-done.8 = f32[32,1,2]{2,1,0:T(1,128)S(1)} async-done(((f32[32,1,2]{2,1,0:T(1,128)}), f32[32,1,2]{2,1,0:T(1,128)S(1)}, u32[]{:S(2)}, u32[]{:S(2)}) %all-to-all-start.8) | async-done | bytes 288 | tf_op jit(solution)/shard_map/all_to_all | solution.py:38
  490.8 1.5 add_multiply_fusion.6
  492.3 1.4 copy.217
  493.7 1.4 copy.218
  495.1 1.4 copy.219
  496.5 2.2 add_multiply_fusion.2
  498.7 1.7 add_multiply_fusion.4
  500.4 2.1 add_multiply_fusion.3
  503.2 8.1 %add_multiply_fusion = (f32[960,768]{1,0:T(8,128)}, f32[960,768]{1,0:T(8,128)}, f32[960,768]{1,0:T(8,128)}) fusion(f32[960,768]{1,0:T(8,128)} %param.47, f32[960,768]{1,0:T(8,128)S(1)} %copy-done.3, f32[960,768]{1,0:T(8,128)} %get-tuple-element.184, f32[]{:T(128)S(6)} %min.3, f32[960,768]{1,0:T(8,128)} %param.40), kind=kLoop, calls=%fused_computation.48 | loop fusion | flops 6635520 | bytes 20643844 | tf_op jit(solution)/shard_map/add | solution.py:747
  (169 shorter events, 36.0 us)
Async XLA Ops:
  7.2 6.6 %copy-start = (s32[4,2]{0,1:T(2,128)S(1)}, s32[4,2]{0,1:T(2,128)}, u32[]{:S(2)}) copy-start(s32[4,2]{0,1:T(2,128)} %param.30) | copy-start | bytes 100
  7.2 6.8 %copy-start.32 = (s32[4]{0:T(128)S(1)}, s32[4]{0:T(128)}, u32[]{:S(2)}) copy-start(s32[4]{0:T(128)} %param.31) | copy-start | bytes 52
  7.2 27.1 %copy-start.2 = (f32[960,768]{1,0:T(8,128)S(1)}, f32[960,768]{1,0:T(8,128)}, u32[]{:S(2)}) copy-start(f32[960,768]{1,0:T(8,128)} %param.33) | copy-start | bytes 8847364
  7.2 138.5 %all-gather.2.cloned.1.call-start = ((), (), s32[]{:S(2)}) async-start(), calls=%async_computation.9 | async-start | bytes 15611904 | tf_op jit(solution)/shard_map/all_gather | solution.py:650
  15.2 8.0 %all-to-all-start.4 = ((s32[4,2,128]{2,1,0:T(2,128)}), s32[4,2,128]{2,1,0:T(2,128)S(1)}, u32[]{:S(2)}, u32[]{:S(2)}) async-start(s32[4,2,128]{2,1,0:T(2,128)} %param.29), calls=%async_computation.4 | async-start | bytes 8192 | tf_op jit(solution)/shard_map/all_to_all | solution.py:652
  29.0 12.5 %all-to-all-start.5 = ((s32[32,1,128]{2,1,0:T(1,128)}), s32[32,1,128]{2,1,0:T(1,128)S(1)}, u32[]{:S(2)}, u32[]{:S(2)}) async-start(s32[32,1,128]{2,1,0:T(1,128)} %bitcast.7), calls=%async_computation.5 | async-start | bytes 32768 | tf_op jit(solution)/shard_map/all_to_all | solution.py:38
  42.9 4.5 copy-start.30
  47.5 3.9 copy-start.33
  47.5 65.0 %all-to-all-start.6 = ((bf16[32,32,768]{2,1,0:T(8,128)(2,1)}), bf16[32,32,768]{2,1,0:T(8,128)(2,1)S(1)}, u32[]{:S(2)}, u32[]{:S(2)}) async-start(bf16[32,32,768]{2,1,0:T(8,128)(2,1)} %bitcast.211), calls=%async_computation.6 | async-start | bytes 3145728 | tf_op jit(solution)/shard_map/all_to_all | solution.py:38
  112.6 33.2 %copy-start.5 = (bf16[32,32,768]{2,1,0:T(8,128)(2,1)}, bf16[32,32,768]{2,1,0:T(8,128)(2,1)S(1)}, u32[]{:S(2)}) copy-start(bf16[32,32,768]{2,1,0:T(8,128)(2,1)S(1)} %all-to-all-done.6) | copy-start | bytes 4718596
  273.5 23.6 %collective-permute-start.1 = (bf16[4,2,2,5,24,768]{5,4,3,0,2,1:T(8,128)(2,1)S(1)}, bf16[4,2,2,5,24,768]{5,4,3,0,2,1:T(8,128)(2,1)}, u32[]{:S(2)}, u32[]{:S(2)}) collective-permute-start(bf16[4,2,2,5,24,768]{5,4,3,0,2,1:T(8,128)(2,1)S(1)} %copy.224), channel_id=1, source_target_pairs={{0,1},{1,0},{2,3},{3,2},{4,5},{5,4},{6,7},{7,6},{8,9},{9,8},{10,11... | collective-permute-start | bytes 8847368 | tf_op jit(solution)/shard_map/ppermute | solution.py:580
  277.2 16.7 %collective-permute-start = (bf16[4,2,2,4,24,768]{5,4,3,0,1,2:T(8,128)(2,1)}, bf16[4,2,2,4,24,768]{5,4,3,0,1,2:T(8,128)(2,1)}, u32[]{:S(2)}, u32[]{:S(2)}) collective-permute-start(bf16[4,2,2,4,24,768]{5,4,3,0,1,2:T(8,128)(2,1)} %copy.222), channel_id=1, source_target_pairs={{0,1},{1,0},{2,3},{3,2},{4,5},{5,4},{6,7},{7,6},{8,9},{9,8},{10,11... | collective-permute-start | bytes 7077896 | tf_op jit(solution)/shard_map/ppermute | solution.py:580
  297.1 6.8 %copy-start.4 = (bf16[4,2,2,4,24,768]{5,4,3,0,1,2:T(8,128)(2,1)}, bf16[4,2,2,4,24,768]{5,4,3,0,1,2:T(8,128)(2,1)S(1)}, u32[]{:S(2)}) copy-start(bf16[4,2,2,4,24,768]{5,4,3,0,1,2:T(8,128)(2,1)S(1)} %add_convert_fusion.1) | copy-start | bytes 7077892
  302.6 37.1 %collective-permute-start.3 = (bf16[4,2,5,24,768]{4,3,2,0,1:T(8,128)(2,1)}, bf16[4,2,5,24,768]{4,3,2,0,1:T(8,128)(2,1)}, u32[]{:S(2)}, u32[]{:S(2)}) collective-permute-start(bf16[4,2,5,24,768]{4,3,2,0,1:T(8,128)(2,1)} %dynamic-slice_bitcast_fusion), channel_id=1, source_target_pairs={{0,4},{1,5},{2,6},{3,7},{4,0},{5,1},{6,2},{7,3},{8,12},{9,13},{10,... | collective-permute-start | bytes 4423688 | tf_op jit(solution)/shard_map/ppermute | solution.py:580
  305.0 32.8 %collective-permute-start.2 = (bf16[4,2,4,24,768]{4,3,2,0,1:T(8,128)(2,1)}, bf16[4,2,4,24,768]{4,3,2,0,1:T(8,128)(2,1)}, u32[]{:S(2)}, u32[]{:S(2)}) collective-permute-start(bf16[4,2,4,24,768]{4,3,2,0,1:T(8,128)(2,1)} %dynamic-slice_bitcast_fusion.1), channel_id=1, source_target_pairs={{0,2},{1,3},{2,0},{3,1},{4,6},{5,7},{6,4},{7,5},{8,10},{9,11},{10,... | collective-permute-start | bytes 3538952 | tf_op jit(solution)/shard_map/ppermute | solution.py:580
  339.7 4.2 copy-start.7
  343.9 20.6 %collective-permute-start.13 = (bf16[4,4,24,768]{3,2,1,0:T(8,128)(2,1)}, bf16[4,4,24,768]{3,2,1,0:T(8,128)(2,1)}, u32[]{:S(2)}, u32[]{:S(2)}) collective-permute-start(bf16[4,4,24,768]{3,2,1,0:T(8,128)(2,1)} %dynamic-slice_bitcast_fusion.3), channel_id=1, source_target_pairs={{0,4},{1,5},{2,6},{3,7},{4,0},{5,1},{6,2},{7,3},{8,12},{9,13},{10,... | collective-permute-start | bytes 1769480 | tf_op jit(solution)/shard_map/ppermute | solution.py:580
  354.4 3.8 copy-start.6
  357.7 6.8 %copy-start.8 = (bf16[4,2,4,24,768]{4,3,2,0,1:T(8,128)(2,1)S(1)}, bf16[4,2,4,24,768]{4,3,2,0,1:T(8,128)(2,1)}, u32[]{:S(2)}) copy-start(bf16[4,2,4,24,768]{4,3,2,0,1:T(8,128)(2,1)} %copy-done.7) | copy-start | bytes 3538948
  357.7 37.5 %collective-permute-start.4 = (bf16[4,2,2,2,24,768]{5,4,3,2,1,0:T(8,128)(2,1)}, bf16[4,2,2,2,24,768]{5,4,3,2,1,0:T(8,128)(2,1)}, u32[]{:S(2)}, u32[]{:S(2)}) collective-permute-start(bf16[4,2,2,2,24,768]{5,4,3,2,1,0:T(8,128)(2,1)} %get-tuple-element.480), channel_id=1, source_target_pairs={{0,1},{1,0},{2,3},{3,2},{4,5},{5,4},{6,7},{7,6},{8,9},{9,8},{10,11... | collective-permute-start | bytes 3538952 | tf_op jit(solution)/shard_map/ppermute | solution.py:580
  357.7 37.5 %collective-permute-start.7 = (bf16[4,2,2,2,24,768]{5,4,3,2,1,0:T(8,128)(2,1)}, bf16[4,2,2,2,24,768]{5,4,3,2,1,0:T(8,128)(2,1)}, u32[]{:S(2)}, u32[]{:S(2)}) collective-permute-start(bf16[4,2,2,2,24,768]{5,4,3,2,1,0:T(8,128)(2,1)} %get-tuple-element.479), channel_id=1, source_target_pairs={{0,1},{1,0},{2,3},{3,2},{4,5},{5,4},{6,7},{7,6},{8,9},{9,8},{10,11... | collective-permute-start | bytes 3538952 | tf_op jit(solution)/shard_map/ppermute | solution.py:580
  359.1 30.2 %collective-permute-start.14 = (bf16[4,5,24,768]{3,2,1,0:T(8,128)(2,1)}, bf16[4,5,24,768]{3,2,1,0:T(8,128)(2,1)}, u32[]{:S(2)}, u32[]{:S(2)}) collective-permute-start(bf16[4,5,24,768]{3,2,1,0:T(8,128)(2,1)} %dynamic-slice_bitcast_fusion.2), channel_id=1, source_target_pairs={{0,2},{1,3},{2,0},{3,1},{4,6},{5,7},{6,4},{7,5},{8,10},{9,11},{10,... | collective-permute-start | bytes 2211848 | tf_op jit(solution)/shard_map/ppermute | solution.py:580
  361.0 86.7 %all-to-all-start.7 = ((bf16[32,32,768]{2,1,0:T(8,128)(2,1)}), bf16[32,32,768]{2,1,0:T(8,128)(2,1)}, u32[]{:S(2)}, u32[]{:S(2)}) async-start(bf16[32,32,768]{2,1,0:T(8,128)(2,1)} %bitcast.210), calls=%async_computation.7 | async-start | bytes 3145728 | tf_op jit(solution)/shard_map/all_to_all | solution.py:38
  365.8 29.4 %copy-start.10 = (bf16[16,4,24,768]{3,2,1,0:T(8,128)(2,1)S(1)}, bf16[16,4,24,768]{3,2,1,0:T(8,128)(2,1)}, u32[]{:S(2)}) copy-start(bf16[16,4,24,768]{3,2,1,0:T(8,128)(2,1)} %get-tuple-element.180) | copy-start | bytes 7077892
  390.7 12.4 %collective-permute-start.15 = (bf16[9,24,768]{2,1,0:T(8,128)(2,1)S(1)}, bf16[9,24,768]{2,1,0:T(8,128)(2,1)S(1)}, u32[]{:S(2)}, u32[]{:S(2)}) collective-permute-start(bf16[9,24,768]{2,1,0:T(8,128)(2,1)S(1)} %get-tuple-element.481), channel_id=1, source_target_pairs={{0,8},{1,9},{2,10},{3,11},{4,12},{5,13},{6,14},{7,15},{8,0},{9,1},... | collective-permute-start | bytes 995336 | tf_op jit(solution)/shard_map/ppermute | solution.py:580
  390.8 33.2 %collective-permute-start.16 = (bf16[9,24,768]{2,1,0:T(8,128)(2,1)S(1)}, bf16[9,24,768]{2,1,0:T(8,128)(2,1)S(1)}, u32[]{:S(2)}, u32[]{:S(2)}) collective-permute-start(bf16[9,24,768]{2,1,0:T(8,128)(2,1)S(1)} %get-tuple-element.482), channel_id=1, source_target_pairs={{0,16},{1,17},{2,18},{3,19},{4,20},{5,21},{6,22},{7,23},{8,24},{9,... | collective-permute-start | bytes 995336 | tf_op jit(solution)/shard_map/ppermute | solution.py:580
  390.9 33.2 %collective-permute-start.17 = (bf16[9,24,768]{2,1,0:T(8,128)(2,1)S(1)}, bf16[9,24,768]{2,1,0:T(8,128)(2,1)S(1)}, u32[]{:S(2)}, u32[]{:S(2)}) collective-permute-start(bf16[9,24,768]{2,1,0:T(8,128)(2,1)S(1)} %get-tuple-element.483), channel_id=1, source_target_pairs={{0,24},{1,25},{2,26},{3,27},{4,28},{5,29},{6,30},{7,31},{8,16},{9,... | collective-permute-start | bytes 995336 | tf_op jit(solution)/shard_map/ppermute | solution.py:580
  397.7 28.4 %collective-permute-start.8 = (bf16[4,2,2,24,768]{4,3,2,1,0:T(8,128)(2,1)S(1)}, bf16[4,2,2,24,768]{4,3,2,1,0:T(8,128)(2,1)S(1)}, u32[]{:S(2)}, u32[]{:S(2)}) collective-permute-start(bf16[4,2,2,24,768]{4,3,2,1,0:T(8,128)(2,1)S(1)} %dynamic-slice_bitcast_fusion.4), channel_id=1, source_target_pairs={{0,4},{1,5},{2,6},{3,7},{4,0},{5,1},{6,2},{7,3},{8,12},{9,13},{10,... | collective-permute-start | bytes 1769480 | tf_op jit(solution)/shard_map/ppermute | solution.py:580
  424.2 65.8 %copy-start.9 = (f32[9,24,768]{2,1,0:T(8,128)}, f32[9,24,768]{2,1,0:T(8,128)S(1)}, u32[]{:S(2)}) copy-start(f32[9,24,768]{2,1,0:T(8,128)S(1)} %fusion.30) | copy-start | bytes 1990660
  424.3 16.3 %collective-permute-start.5 = (bf16[4,2,2,24,768]{4,3,2,1,0:T(8,128)(2,1)S(1)}, bf16[4,2,2,24,768]{4,3,2,1,0:T(8,128)(2,1)S(1)}, u32[]{:S(2)}, u32[]{:S(2)}) collective-permute-start(bf16[4,2,2,24,768]{4,3,2,1,0:T(8,128)(2,1)S(1)} %dynamic-slice_bitcast_fusion.5), channel_id=1, source_target_pairs={{0,2},{1,3},{2,0},{3,1},{4,6},{5,7},{6,4},{7,5},{8,10},{9,11},{10,... | collective-permute-start | bytes 1769480 | tf_op jit(solution)/shard_map/ppermute | solution.py:580
  426.1 16.6 %copy-start.14 = (f32[24,768]{1,0:T(8,128)}, f32[24,768]{1,0:T(8,128)S(1)}, u32[]{:S(2)}) copy-start(f32[24,768]{1,0:T(8,128)S(1)} %get-tuple-element.484) | copy-start | bytes 221188
  426.1 16.6 %copy-start.15 = (f32[24,768]{1,0:T(8,128)}, f32[24,768]{1,0:T(8,128)S(1)}, u32[]{:S(2)}) copy-start(f32[24,768]{1,0:T(8,128)S(1)} %get-tuple-element.485) | copy-start | bytes 221188
  426.1 16.6 %copy-start.16 = (f32[24,768]{1,0:T(8,128)}, f32[24,768]{1,0:T(8,128)S(1)}, u32[]{:S(2)}) copy-start(f32[24,768]{1,0:T(8,128)S(1)} %get-tuple-element.486) | copy-start | bytes 221188
  426.1 16.6 %copy-start.17 = (f32[24,768]{1,0:T(8,128)}, f32[24,768]{1,0:T(8,128)S(1)}, u32[]{:S(2)}) copy-start(f32[24,768]{1,0:T(8,128)S(1)} %get-tuple-element.487) | copy-start | bytes 221188
  426.3 18.8 %collective-permute-start.9 = (bf16[4,2,24,768]{3,2,1,0:T(8,128)(2,1)S(1)}, bf16[4,2,24,768]{3,2,1,0:T(8,128)(2,1)S(1)}, u32[]{:S(2)}, u32[]{:S(2)}) collective-permute-start(bf16[4,2,24,768]{3,2,1,0:T(8,128)(2,1)S(1)} %dynamic-slice_bitcast_fusion.6), channel_id=1, source_target_pairs={{0,2},{1,3},{2,0},{3,1},{4,6},{5,7},{6,4},{7,5},{8,10},{9,11},{10,... | collective-permute-start | bytes 884744 | tf_op jit(solution)/shard_map/ppermute | solution.py:580
  440.8 17.3 %copy-start.31 = (s32[1024]{0:T(1024)S(1)}, s32[1024]{0:T(1024)}, u32[]{:S(2)}) copy-start(s32[1024]{0:T(1024)} %copy-done.30) | copy-start | bytes 12292
  440.8 6.8 %collective-permute-start.6 = (bf16[4,2,24,768]{3,2,1,0:T(8,128)(2,1)S(1)}, bf16[4,2,24,768]{3,2,1,0:T(8,128)(2,1)S(1)}, u32[]{:S(2)}, u32[]{:S(2)}) collective-permute-start(bf16[4,2,24,768]{3,2,1,0:T(8,128)(2,1)S(1)} %dynamic-slice_bitcast_fusion.7), channel_id=1, source_target_pairs={{0,4},{1,5},{2,6},{3,7},{4,0},{5,1},{6,2},{7,3},{8,12},{9,13},{10,... | collective-permute-start | bytes 884744 | tf_op jit(solution)/shard_map/ppermute | solution.py:580
  448.6 18.3 %collective-permute-start.10 = (bf16[4,24,768]{2,1,0:T(8,128)(2,1)}, bf16[4,24,768]{2,1,0:T(8,128)(2,1)S(1)}, u32[]{:S(2)}, u32[]{:S(2)}) collective-permute-start(bf16[4,24,768]{2,1,0:T(8,128)(2,1)} %get-tuple-element.489), channel_id=1, source_target_pairs={{0,8},{1,9},{2,10},{3,11},{4,12},{5,13},{6,14},{7,15},{8,0},{9,1},... | collective-permute-start | bytes 442376 | tf_op jit(solution)/shard_map/ppermute | solution.py:580
  455.7 11.4 %collective-permute-start.11 = (bf16[4,24,768]{2,1,0:T(8,128)(2,1)}, bf16[4,24,768]{2,1,0:T(8,128)(2,1)}, u32[]{:S(2)}, u32[]{:S(2)}) collective-permute-start(bf16[4,24,768]{2,1,0:T(8,128)(2,1)} %get-tuple-element.491), channel_id=1, source_target_pairs={{0,16},{1,17},{2,18},{3,19},{4,20},{5,21},{6,22},{7,23},{8,24},{9,... | collective-permute-start | bytes 442376 | tf_op jit(solution)/shard_map/ppermute | solution.py:580
  456.2 11.4 %collective-permute-start.12 = (bf16[4,24,768]{2,1,0:T(8,128)(2,1)}, bf16[4,24,768]{2,1,0:T(8,128)(2,1)}, u32[]{:S(2)}, u32[]{:S(2)}) collective-permute-start(bf16[4,24,768]{2,1,0:T(8,128)(2,1)} %get-tuple-element.490), channel_id=1, source_target_pairs={{0,24},{1,25},{2,26},{3,27},{4,28},{5,29},{6,30},{7,31},{8,16},{9,... | collective-permute-start | bytes 442376 | tf_op jit(solution)/shard_map/ppermute | solution.py:580
  463.6 18.0 %copy-start.27 = (f32[14,24]{1,0:T(8,128)S(1)}, f32[14,24]{1,0:T(8,128)}, u32[]{:S(2)}) copy-start(f32[14,24]{1,0:T(8,128)} %param.39) | copy-start | bytes 4036
  463.6 18.1 %copy-start.28 = (f32[14,24]{1,0:T(8,128)S(1)}, f32[14,24]{1,0:T(8,128)}, u32[]{:S(2)}) copy-start(f32[14,24]{1,0:T(8,128)} %param.46) | copy-start | bytes 4036
  463.6 18.8 %copy-start.29 = (f32[14,24]{1,0:T(8,128)S(1)}, f32[14,24]{1,0:T(8,128)}, u32[]{:S(2)}) copy-start(f32[14,24]{1,0:T(8,128)} %param.53) | copy-start | bytes 4036
  463.6 32.8 %copy-start.11 = (f32[24,3072]{1,0:T(8,128)S(1)}, f32[24,3072]{1,0:T(8,128)}, u32[]{:S(2)}) copy-start(f32[24,3072]{1,0:T(8,128)} %param.37) | copy-start | bytes 884740
  466.9 0.7 copy-start.24
  468.7 21.3 %copy-start.18 = (f32[24,768]{1,0:T(8,128)}, f32[24,768]{1,0:T(8,128)S(1)}, u32[]{:S(2)}) copy-start(f32[24,768]{1,0:T(8,128)S(1)} %get-tuple-element.492) | copy-start | bytes 221188
  468.7 21.3 %copy-start.19 = (f32[24,768]{1,0:T(8,128)}, f32[24,768]{1,0:T(8,128)S(1)}, u32[]{:S(2)}) copy-start(f32[24,768]{1,0:T(8,128)S(1)} %get-tuple-element.493) | copy-start | bytes 221188
  468.7 21.3 %copy-start.20 = (f32[24,768]{1,0:T(8,128)}, f32[24,768]{1,0:T(8,128)S(1)}, u32[]{:S(2)}) copy-start(f32[24,768]{1,0:T(8,128)S(1)} %get-tuple-element.494) | copy-start | bytes 221188
  476.5 12.2 %all-to-all-start.8 = ((f32[32,1,2]{2,1,0:T(1,128)}), f32[32,1,2]{2,1,0:T(1,128)S(1)}, u32[]{:S(2)}, u32[]{:S(2)}) async-start(f32[32,1,2]{2,1,0:T(1,128)} %broadcast_in_dim.119), calls=%async_computation.8 | async-start | bytes 32768 | tf_op jit(solution)/shard_map/all_to_all | solution.py:38
  490.8 12.4 %copy-start.3 = (f32[960,768]{1,0:T(8,128)S(1)}, f32[960,768]{1,0:T(8,128)}, u32[]{:S(2)}) copy-start(f32[960,768]{1,0:T(8,128)} %param.33) | copy-start | bytes 8847364
  496.4 6.0 %copy-start.23 = (f32[512,24]{0,1:T(8,128)S(1)}, f32[512,24]{0,1:T(8,128)}, u32[]{:S(2)}) copy-start(f32[512,24]{0,1:T(8,128)} %param.34) | copy-start | bytes 147460
  496.4 6.0 %copy-start.25 = (f32[512,24]{0,1:T(8,128)S(1)}, f32[512,24]{0,1:T(8,128)}, u32[]{:S(2)}) copy-start(f32[512,24]{0,1:T(8,128)} %param.48) | copy-start | bytes 147460
  496.4 6.0 %copy-start.26 = (f32[512,24]{0,1:T(8,128)S(1)}, f32[512,24]{0,1:T(8,128)}, u32[]{:S(2)}) copy-start(f32[512,24]{0,1:T(8,128)} %param.41) | copy-start | bytes 147460
  503.2 8.1 %copy-start.12 = (f32[96,768]{1,0:T(8,128)S(1)}, f32[96,768]{1,0:T(8,128)}, u32[]{:S(2)}) copy-start(f32[96,768]{1,0:T(8,128)} %param.38) | copy-start | bytes 884740
  503.2 8.1 %copy-start.13 = (f32[4,24,768]{2,1,0:T(8,128)S(1)}, f32[4,24,768]{2,1,0:T(8,128)}, u32[]{:S(2)}) copy-start(f32[4,24,768]{2,1,0:T(8,128)} %slice_multiply_fusion) | copy-start | bytes 884740
  503.2 8.1 %copy-start.21 = (f32[96,768]{1,0:T(8,128)S(1)}, f32[96,768]{1,0:T(8,128)}, u32[]{:S(2)}) copy-start(f32[96,768]{1,0:T(8,128)} %param.52) | copy-start | bytes 884740
  503.2 8.1 %copy-start.22 = (f32[96,768]{1,0:T(8,128)S(1)}, f32[96,768]{1,0:T(8,128)}, u32[]{:S(2)}) copy-start(f32[96,768]{1,0:T(8,128)} %param.45) | copy-start | bytes 884740
  503.2 9.1 %copy-start.1 = (s32[4,2]{0,1:T(2,128)S(1)}, s32[4,2]{0,1:T(2,128)}, u32[]{:S(2)}) copy-start(s32[4,2]{0,1:T(2,128)} %param.30) | copy-start | bytes 100
Sparse Core Ops, SparseCore 0:
  13.9 131.7 all-gather.1

commit v4 on v3

v4 whole, which is shorter than its diff:
```python
import functools

import jax
import jax.numpy as jnp
from jax import lax
from jax.experimental import pallas as pl
from jax.experimental.pallas import tpu as pltpu
from jax.sharding import PartitionSpec as P

HEADS = 12
HEAD_DIM = 64
EPS = 1e-06
RATE = 10000.0
MOMENT = 0.5
DECAY = 0.5
CLIP = 0.01
SLOTS = 1024
GROUP = 128
ROWS = 288
BLOCKS = 4
SIZES = (128, 256, 384, 512)
AXES = ("dp", "seq")
bf = jnp.bfloat16
f32 = jnp.float32


def mm(left, right):
    return jnp.dot(left, right, preferred_element_type=f32)


def mm_left(left, right):
    return lax.dot_general(left, right, (((0,), (0,)), ((), ())), preferred_element_type=f32)


def mm_right(left, right):
    return lax.dot_general(left, right, (((1,), (1,)), ((), ())), preferred_element_type=f32)


def exchange(v):
    return lax.all_to_all(v, AXES, 0, 0, tiled=True)


def slots_of(devices):
    return max(16, SLOTS // devices)


def route(ids, valid, per_owner):
    count = ids.shape[0]
    spot = jnp.arange(count, dtype=jnp.int32)
    owner = ids // per_owner
    local = ids - owner * per_owner
    key = jnp.where(valid, ids, -1 - spot)
    alike = key[:, None] == key[None, :]
    first_at = jnp.min(jnp.where(alike, spot[None, :], count), axis=1)
    first = (first_at == spot) & valid
    before = (owner[:, None] == owner[None, :]) & first[None, :] & (spot[None, :] < first_at[:, None])
    rank = jnp.sum(before.astype(jnp.int32), axis=1)
    return owner, local, first, rank


def requests(owner, local, first, rank, start, devices):
    room = slots_of(devices)
    slot = jnp.where(first & (rank >= start) & (rank < start + room), owner * room + rank - start, -1)
    line = jnp.arange(devices * room, dtype=jnp.int32)
    hit = slot[None, :] == line[:, None]
    return jnp.max(jnp.where(hit, local[None, :], -1), axis=1)


def token_slots(owner, valid, rank, start, room):
    return jnp.where(valid & (rank >= start) & (rank < start + room), owner * room + rank - start, -1)


def one_hot(index, size):
    return (index[:, None] == jnp.arange(size, dtype=jnp.int32)[None, :]).astype(bf)


NEAR = 0.3
TAIL = (
    0.11962924781130464, 0.12075473126046088, 0.09990870957740686, 0.12857719637511858,
    -0.05371263258867769, 0.2063844888355699, -0.15722075016774184, 0.03567893567949022,
)


def dot(left, right):
    return jnp.dot(left, right, preferred_element_type=f32)


def dot_nt(left, right):
    return lax.dot_general(left, right, (((1,), (1,)), ((), ())), preferred_element_type=f32)


def dot_tn(left, right):
    return lax.dot_general(left, right, (((0,), (0,)), ((), ())), preferred_element_type=f32)


def iota(shape, axis):
    return lax.broadcasted_iota(jnp.int32, shape, axis)


def normal(v):
    center = v - jnp.mean(v, axis=-1, keepdims=True)
    scale = lax.rsqrt(jnp.mean(center * center, axis=-1, keepdims=True) + EPS)
    return center * scale, scale


def normal_back(grad, unit, scale):
    inner = jnp.mean(grad * unit, axis=-1, keepdims=True)
    return scale * (grad - jnp.mean(grad, axis=-1, keepdims=True) - unit * inner)


def column_sums(v):
    return dot(jnp.full((8, v.shape[0]), 1.0, bf), v)[:1]


def gelu_pair(v):
    bell = jnp.exp(v * v * -0.5)
    t = 1.0 / (1.0 + NEAR * jnp.abs(v))
    poly = TAIL[-1]
    for c in TAIL[-2::-1]:
        poly = poly * t + c
    tail = poly * t * bell
    area = jnp.where(v < 0, tail, 1.0 - tail)
    return v * area, area + v * bell * 0.3989422804014327


def params(limit, **more):
    return pltpu.CompilerParams(vmem_limit_bytes=limit << 20, **more)


def fixed(shape, index):
    return pl.BlockSpec(shape, lambda *_: index, pipeline_mode=pl.Buffered(1))


def spread_kernel(depth, turns, width, src, out):
    tall = src[...].astype(f32)
    parts = []
    for e in range(2):
        for j in range(turns):
            parts.append(tall[e * depth : (e + 1) * depth, j * width : (j + 1) * width])
    out[...] = jnp.concatenate(parts, axis=0).astype(bf)


def live_rows(plan, shape):
    row = iota(shape, 0) + pl.program_id(0) * shape[0]
    return row < plan[0], (row >= plan[2]) & (row < plan[2] + plan[1])


def when_live(kernel):
    def run(*refs):
        pl.when(pl.program_id(0) < refs[0][3])(lambda: kernel(*refs))

    return run


def first_kernel(plan, slot, spot_in, back, extra, w_qkv, pos_t, vec_t, x_out, hin_out, qkv_out, vec_out):
    rows, width = x_out.shape
    length = pos_t.shape[1]
    vec = dot_nt((iota((16, 128), 0) == iota((16, 128), 1)).astype(f32).astype(bf), vec_t[...])
    vec_out[...] = vec
    where = jnp.where(slot[...] == iota((rows, back.shape[0]), 1), 1.0, 0.0).astype(bf)
    line = jnp.where(spot_in[...] == iota((rows, length), 1), 1.0, 0.0).astype(bf)
    x = dot(where, back[...]) + extra[...].astype(f32) + dot_nt(line, pos_t[...])
    x_out[...] = x
    unit, _ = normal(x)
    hin = (unit * vec[0:1] + vec[1:2]).astype(bf)
    hin_out[...] = hin
    qkv_out[:, :width] = (dot(hin, w_qkv[:, :width]) + vec[2:3]).astype(bf)
    qkv_out[:, width : 2 * width] = dot(hin, w_qkv[:, width : 2 * width]).astype(bf)
    qkv_out[:, 2 * width :] = (dot(hin, w_qkv[:, 2 * width :]) + vec[3:4]).astype(bf)


def head_parts(size, query, keys, half):
    shape = query.shape
    lane = iota(shape, 1)
    live = iota(shape, 0) < size
    inside = ((lane // HEAD_DIM) == half) & live
    spare = lane == (1 - half) * HEAD_DIM
    key = jnp.where(inside, keys.astype(f32), jnp.where(spare & ~live, -1e30, 0.0)).astype(bf)
    ask = jnp.where(inside, query.astype(f32) * 0.125, jnp.where(spare, 1.0, 0.0)).astype(bf)
    return inside, ask, key


def each_sentence(plan, run):
    def one(index, carry):
        size = jnp.where(index == 0, plan[0], plan[1])
        start = pl.multiple_of(jnp.where(index == 0, 0, plan[2]), 16)
        under = 0
        for count in SIZES:
            pl.when((size > under) & (size <= count))(functools.partial(run, pl.ds(start, count), size))
            under = count
        return carry

    lax.fori_loop(0, 2, one, 0)


def attend_kernel(plan, query, keys, values, out):
    out[...] = jnp.zeros_like(out)

    def run(rows, size):
        total = None
        for half in range(2):
            inside, ask, key = head_parts(size, query[rows, :], keys[rows, :], half)
            score = dot_nt(ask, key)
            power = jnp.exp(score - jnp.max(score, axis=1, keepdims=True))
            prob = (power * (1.0 / jnp.sum(power, axis=1, keepdims=True))).astype(bf)
            part = dot(prob, jnp.where(inside, values[rows, :].astype(f32), 0.0).astype(bf))
            total = part if total is None else total + part
        out[rows, :] = total.astype(bf)

    each_sentence(plan, run)


def attend_back_kernel(plan, query, keys, values, d_out, *more):
    d_proj = more[-1]
    d_proj[...] = jnp.zeros_like(d_proj)
    plus = lambda a, b: b if a is None else a + b

    def run(rows, size):
        d_query, d_key, d_value = None, None, None
        for half in range(2):
            inside, ask, key = head_parts(size, query[rows, :], keys[rows, :], half)
            clean = lambda v: jnp.where(inside, v.astype(f32), 0.0).astype(bf)
            score = dot_nt(key, ask)
            power = jnp.exp(score - jnp.max(score, axis=0, keepdims=True))
            prob = power * (1.0 / jnp.sum(power, axis=0, keepdims=True))
            grad = clean(d_out[rows, :])
            d_value = plus(d_value, dot(prob.astype(bf), grad))
            d_prob = dot_nt(clean(values[rows, :]), grad)
            inner = jnp.sum(prob * d_prob, axis=0, keepdims=True)
            d_score = (prob * (d_prob - inner)).astype(bf)
            d_key = plus(d_key, dot(d_score, clean(ask)))
            d_query = plus(d_query, dot_tn(d_score, clean(key)))
        d_proj[0, rows, :] = (d_query * 0.125).astype(bf)
        d_proj[1, rows, :] = d_key.astype(bf)
        d_proj[2, rows, :] = d_value.astype(bf)

    each_sentence(plan, run)


def middle_kernel(plan, x, mixed, w_out, w_in, w_back, vec, vec_ff, z1_out, h1_out, act_out, slope_out, z2_out, pooled):
    rows, width = x.shape
    unit, _ = normal(x[...])
    h0 = unit * vec[0:1] + vec[1:2]
    z1 = h0 + dot(mixed[...], w_out[...]) + vec[4:5]
    z1_out[...] = z1
    unit, _ = normal(z1)
    h1 = unit * vec[5:6] + vec[6:7]
    h1_b = h1.astype(bf)
    h1_out[...] = h1_b
    turns = w_in.shape[1] // width
    y = None
    for j in range(turns):
        at = slice(j * width, (j + 1) * width)
        hidden = dot(h1_b, w_in[:, at]) + vec_ff[:, at]
        act, slope = gelu_pair(hidden)
        act = act.astype(bf)
        act_out[:, at] = act
        slope_out[:, at] = slope.astype(bf)
        part = dot(act, w_back[at, :])
        y = part if y is None else y + part
    z2 = h1 + y + vec[7 + turns : 8 + turns]
    z2_out[...] = z2
    unit, _ = normal(z2)
    h2 = unit * vec[8 + turns : 9 + turns] + vec[9 + turns : 10 + turns]
    sums = [jnp.sum(jnp.where(keep, h2, 0.0), axis=0, keepdims=True) for keep in live_rows(plan, (rows, width))]

    @pl.when(pl.program_id(0) == 0)
    def _():
        pooled[...] = jnp.zeros_like(pooled)

    line = iota(pooled.shape, 0)
    pooled[...] += jnp.where(line == 0, sums[0], jnp.where(line == 1, sums[1], 0.0))


def back_kernel(plan, facts, pooled, partner, z1, slope, z2, w_out, w_in, w_back, vec, d_y_out, d_f_out, d_r1_out, d_a_out, d_o_out, sums, sums_ff, loss):
    rows, width = z1.shape
    step = pl.program_id(0)
    total = lambda a, b: jnp.sum(a * b, axis=1, keepdims=True)
    count = facts[10]
    grads, losses = [], []
    for i in range(2):
        labeled, gold, size, other_size, counts = (facts[5 * i + j] for j in range(5))
        own, other = pooled[i : i + 1] / size, partner[i : i + 1] / other_size
        cross = total(own, other)
        root, other_root = lax.rsqrt(total(own, own) + EPS), lax.rsqrt(total(other, other) + EPS)
        miss = cross * root * other_root - gold
        losses.append(counts * miss * miss)
        push = 2.0 * labeled * miss / count
        grads.append(push * (other * root * other_root - cross * root * root * root * other_root * own) / size)
    loss[...] = jnp.broadcast_to(losses[0] + losses[1], loss.shape)
    keep = live_rows(plan, (rows, width))
    d_h2 = jnp.where(keep[0], grads[0], jnp.where(keep[1], grads[1], 0.0))
    turns = w_in.shape[1] // width

    unit, scale = normal(z2[...])
    d_g2 = jnp.sum(d_h2 * unit, axis=0, keepdims=True)
    d_b2n = jnp.sum(d_h2, axis=0, keepdims=True)
    d_r2 = normal_back(d_h2 * vec[8 + turns : 9 + turns], unit, scale)
    d_y = d_r2.astype(bf)
    d_y_out[...] = d_y
    d_h1 = d_r2
    ff = []
    for j in range(turns):
        at = slice(j * width, (j + 1) * width)
        d_f = (dot_nt(d_y, w_back[at, :]) * slope[:, at].astype(f32)).astype(bf)
        d_f_out[:, at] = d_f
        ff.append(column_sums(d_f))
        d_h1 = d_h1 + dot_nt(d_f, w_in[:, at])
    unit, scale = normal(z1[...])
    d_g1 = jnp.sum(d_h1 * unit, axis=0, keepdims=True)
    d_b1 = jnp.sum(d_h1, axis=0, keepdims=True)
    d_r1 = normal_back(d_h1 * vec[5:6], unit, scale)
    d_r1_out[...] = d_r1
    d_a = d_r1.astype(bf)
    d_a_out[...] = d_a
    d_o_out[...] = dot_nt(d_a, w_out[...]).astype(bf)
    fresh = jnp.concatenate([column_sums(d_a), d_g1, d_b1, column_sums(d_y), d_g2, d_b2n, d_g2, d_b2n], axis=0)

    @pl.when(step == 0)
    def _():
        sums[...] = jnp.zeros_like(sums)
        sums_ff[...] = jnp.zeros_like(sums_ff)

    sums[...] += fresh
    sums_ff[...] += jnp.concatenate(ff, axis=0)


def last_kernel(plan, slot, x, d_r1, d_proj, w_qkv, vec, d_x_out, sums, rows_out, total):
    rows, width = x.shape
    step = pl.program_id(0)
    d_h0 = d_r1[...]
    for i in range(3):
        d_h0 = d_h0 + dot_nt(d_proj[i], w_qkv[:, i * width : (i + 1) * width])
    unit, scale = normal(x[...])
    d_ge = jnp.sum(d_h0 * unit, axis=0, keepdims=True)
    d_be = jnp.sum(d_h0, axis=0, keepdims=True)
    d_x = normal_back(d_h0 * vec[0:1], unit, scale)
    d_xb = d_x.astype(bf)
    d_x_out[...] = d_xb
    bias_q, bias_v = column_sums(d_proj[0]), column_sums(d_proj[2])
    fresh = jnp.concatenate([d_ge, d_be, bias_q, bias_v, d_ge, d_be, bias_q, bias_v], axis=0)
    hit = jnp.where(slot[...] == iota((rows, rows_out.shape[0]), 1), 1.0, 0.0).astype(bf)

    @pl.when(step == 0)
    def _():
        sums[...] = jnp.zeros_like(sums)
        total[...] = jnp.zeros_like(total)

    sums[...] += fresh
    total[...] += dot_tn(hit, d_xb)

    @pl.when(step == plan[3] - 1)
    def _():
        rows_out[...] = total[...].astype(bf)


def blocks(v, depth):
    return v.reshape(v.shape[0] // depth, depth, v.shape[1])


def put_split(keep, send, kind, g, mine):
    g = g.reshape((g.shape[0] // 2, 2) + g.shape[1:])
    even, odd = g[:, 0], g[:, 1]
    keep[:, kind] = jnp.where(mine == 0, even, odd).astype(bf)
    send[:, kind] = jnp.where(mine == 0, odd, even).astype(bf)


def by_blocks(plan, run):
    for count in range(2, BLOCKS + 1):
        pl.when(plan[3] == count)(functools.partial(run, count * ROWS))


def dense_grads_kernel(depth, turns, plan, act, d_y, h1, d_f, mixed, d_a, keep, send):
    width = d_y.shape[1]
    mine = plan[4]

    def run(rows):
        g = dot_tn(act[:rows], d_y[:rows])
        g = g.reshape(2 * keep.shape[0], turns, depth, width)
        for j in range(turns):
            put_split(keep, send, j, g[:, j], mine)
        for j in range(turns):
            put_split(keep, send, turns + j, blocks(dot_tn(h1[:rows], d_f[:rows, j * width : (j + 1) * width]), depth), mine)
        put_split(keep, send, 2 * turns, blocks(dot_tn(mixed[:rows], d_a[:rows]), depth), mine)

    by_blocks(plan, run)


def rest_grads_kernel(depth, length, plan, spot_in, hin, d_proj, d_x, sums_0, sums, sums_ff, keep, send):
    width = d_proj.shape[2]
    part = hin.shape[1]
    mine = plan[4]

    def run(rows):
        for i in range(3):
            put_split(keep, send, i, blocks(dot_tn(hin[:rows], d_proj[i, :rows]), depth), mine)
        line = jnp.where(spot_in[:rows] == iota((rows, length), 1), 1.0, 0.0).astype(bf)
        g_pos = dot_tn(d_x[:rows], line)
        vec = jnp.concatenate([sums_0[:4], sums[:3], sums_ff[...], sums[3:6]], axis=0)
        vec = jnp.concatenate([vec, jnp.zeros((128 - vec.shape[0], part), f32)], axis=0)
        put_split(keep, send, 3, blocks(jnp.concatenate([g_pos, vec.T, jnp.zeros((part, width - length - 128), f32)], axis=1), depth), mine)

    by_blocks(plan, run)


def cost(flops, nbytes):
    return pl.CostEstimate(flops=int(flops), bytes_accessed=int(nbytes), transcendentals=0)


def run_forward_backward(full, back, extra, slots, spots, plan, meet, staged, devices, depth, length, hidden):
    width = back.shape[1]
    rows = slots.shape[0]
    turns = hidden // width
    pairs = width // GROUP
    shape = jax.ShapeDtypeStruct
    at_row = lambda i, plan: jnp.minimum(i, plan[3] - 1)
    row = lambda cols: pl.BlockSpec((ROWS, cols), lambda i, plan, *_: (at_row(i, plan), 0))
    column = lambda block: fixed((width, width), (0, block))
    at_back = 4 * width + hidden
    whole_out = lambda *dims: pl.BlockSpec(dims, lambda *_: (0,) * len(dims))

    def call(kernel, prefetch, grid, in_specs, out_specs, out_shape, name, scratch=(), **more):
        return pl.pallas_call(
            kernel,
            grid_spec=pltpu.PrefetchScalarGridSpec(
                num_scalar_prefetch=prefetch, grid=grid, in_specs=in_specs, out_specs=out_specs, scratch_shapes=list(scratch)
            ),
            out_shape=out_shape,
            compiler_params=params(60),
            name=name,
            **more,
        )

    if depth % 8 == 0:
        w_back = pl.pallas_call(
            functools.partial(spread_kernel, depth, turns, width),
            grid=(devices // 2,),
            in_specs=[pl.BlockSpec((2 * depth, turns * width), lambda i: (i, at_back // (turns * width)))],
            out_specs=pl.BlockSpec((2 * depth * turns, width), lambda i: (i, 0)),
            out_shape=shape((hidden, width), bf),
            name="spread",
        )(full)
    else:
        w_back = full[:, at_back : at_back + turns * width].reshape(devices, depth, turns, width)
        w_back = w_back.transpose(0, 2, 1, 3).reshape(hidden, width)

    at_pos = at_back + turns * width
    at_vec = at_pos + length
    w_qkv_spec = fixed((width, 3 * width), (0, 0))
    w_out_spec = column(3)
    w_in_spec = fixed((width, hidden), (0, 4 * width // hidden))
    w_back_spec = fixed((hidden, width), (0, 0))
    vec_spec = fixed((16, width), (0, 0))

    x, hin, qkv, vec = call(
        when_live(first_kernel), 1, (BLOCKS,),
        [
            row(1), row(1), fixed(back.shape, (0, 0)), row(width), w_qkv_spec,
            fixed((width, length), (0, at_pos // length)), fixed((width, 128), (0, at_vec // 128)),
        ],
        [row(width), row(width), row(3 * width), whole_out(16, width)],
        [shape((rows, width), f32), shape((rows, width), bf), shape((rows, 3 * width), bf), shape((16, width), f32)],
        "first",
    )(plan, slots[:, None], spots[:, None], back, extra, full, full, full)

    block = lambda part, start=0: pl.BlockSpec((rows, GROUP), lambda p, *_: (0, part * pairs + start + p))
    mixed = call(
        attend_kernel, 1, (pairs,), [block(0), block(1), block(2)], block(0), shape((rows, width), bf), "attend"
    )(plan, qkv, qkv, qkv)

    vec_ff = vec[7 : 7 + turns].reshape(1, hidden)
    z1, h1, act, slope, z2, pooled = call(
        when_live(middle_kernel), 1, (BLOCKS,),
        [row(width), row(width), w_out_spec, w_in_spec, w_back_spec, vec_spec, fixed((1, hidden), (0, 0))],
        [row(width), row(width), row(hidden), row(hidden), row(width), whole_out(8, width)],
        [
            shape((rows, width), f32), shape((rows, width), bf), shape((rows, hidden), bf), shape((rows, hidden), bf),
            shape((rows, width), f32), shape((8, width), f32),
        ],
        "middle",
    )(plan, x, mixed, full, full, w_back, vec, vec_ff)

    partner, facts = meet(pooled)
    d_y, d_f, d_r1, d_a, d_o, sums, sums_ff, loss = call(
        when_live(back_kernel), 2, (BLOCKS,),
        [
            fixed((8, width), (0, 0)), fixed((2, width), (0, 0)), row(width), row(hidden), row(width), w_out_spec, w_in_spec,
            w_back_spec, vec_spec,
        ],
        [
            row(width), row(hidden), row(width), row(width), row(width), whole_out(8, width), whole_out(turns, width),
            whole_out(8, 128),
        ],
        [
            shape((rows, width), bf), shape((rows, hidden), bf), shape((rows, width), f32), shape((rows, width), bf), shape((rows, width), bf),
            shape((8, width), f32), shape((turns, width), f32), shape((8, 128), f32),
        ],
        "back",
    )(plan, facts, pooled, partner, z1, slope, z2, full, full, w_back, vec)

    tall = depth % 8 == 0
    half = devices // 2
    part = width // 2
    halves = lambda cols: pl.BlockSpec((rows, cols), lambda i, *_: (0, i))
    live = (jnp.arange(rows) < plan[3] * ROWS)[:, None]
    clean = lambda v: jnp.where(live, v, 0)
    if tall:
        quarter = pl.BlockSpec((half // 2, 2 * turns + 1, depth, width), lambda i, *_: (i, 0, 0, 0))
        dense = call(
            functools.partial(dense_grads_kernel, depth, turns), 1, (2,),
            [
                halves(hidden // 2), fixed((rows, width), (0, 0)), halves(part), fixed((rows, hidden), (0, 0)), halves(part),
                fixed((rows, width), (0, 0)),
            ],
            [quarter, quarter],
            [shape((half, 2 * turns + 1, depth, width), bf)] * 2,
            "dense_grads",
        )(plan, act, d_y, h1, d_f, mixed, d_a)
    else:
        cut = lambda g: g.astype(bf).reshape(devices, depth, -1, width).transpose(0, 2, 1, 3)
        g_out = dot_tn(clean(act), clean(d_y)).astype(bf).reshape(devices, turns, depth, width)
        g_in, g_mix = dot_tn(clean(h1), clean(d_f)), dot_tn(clean(mixed), clean(d_a))
        dense = jnp.concatenate([g_out, cut(g_in), cut(g_mix)], axis=1)
    if staged:
        dense = over_cores(*dense)
    else:
        d_o, dense = lax.optimization_barrier((d_o, dense))

    def attend_back(start, count, total):
        more = () if total is None else (total,)
        return call(
            attend_back_kernel, 1, (count,),
            [block(0, start), block(1, start), block(2, start), block(0, start)] + [pl.BlockSpec(memory_space=pl.ANY)] * len(more),
            pl.BlockSpec((3, rows, GROUP), lambda p, *_: (0, 0, start + p)),
            shape((3, rows, width), bf),
            "attend_back",
            input_output_aliases={5: 0} if more else {},
            cost_estimate=cost(10 * length * length * GROUP * count, 8 * rows * GROUP * count * 2),
        )(plan, qkv, qkv, qkv, d_o, *more)

    d_proj = attend_back(0, pairs // 2, None)
    if staged:
        d_proj, dense = lax.optimization_barrier((d_proj, dense))
        dense = over_wide(*dense)
    d_proj = attend_back(pairs // 2, pairs - pairs // 2, d_proj)

    d_xb, sums_0, give_rows = call(
        when_live(last_kernel), 1, (BLOCKS,),
        [
            row(1), row(width), row(width), pl.BlockSpec((3, ROWS, width), lambda i, plan: (0, at_row(i, plan), 0)), w_qkv_spec, vec_spec,
        ],
        [row(width), whole_out(8, width), whole_out(*back.shape)],
        [shape((rows, width), bf), shape((8, width), f32), shape(back.shape, bf)],
        "last",
        scratch=[pltpu.VMEM(back.shape, f32)],
    )(plan, slots[:, None], x, d_r1, d_proj, full, vec)

    if staged:
        d_xb, dense = lax.optimization_barrier((d_xb, dense))
    if tall:
        quarter = pl.BlockSpec((half // 2, 4, depth, width), lambda i, *_: (i, 0, 0, 0))
        cols = lambda count: pl.BlockSpec((count, part), lambda i, *_: (0, i))
        rest = call(
            functools.partial(rest_grads_kernel, depth, length), 1, (2,),
            [fixed((rows, 1), (0, 0)), halves(part), fixed((3, rows, width), (0, 0, 0)), halves(part), cols(8), cols(8), cols(turns)],
            [quarter, quarter],
            [shape((half, 4, depth, width), bf)] * 2,
            "rest_grads",
        )(plan, spots[:, None], hin, d_proj, d_xb, sums_0, sums, sums_ff)
    else:
        g_vec = jnp.concatenate([sums_0[:4], sums[:3], sums_ff, sums[3:6]], axis=0)
        g_pos = dot_tn(clean(d_xb), one_hot(spots, length))
        spare = jnp.zeros((width, width - length - g_vec.shape[0]), f32)
        rest = [dot_tn(clean(hin), clean(d_proj[i])) for i in range(3)] + [jnp.concatenate([g_pos, g_vec.T, spare], axis=1)]
        rest = jnp.stack([g.astype(bf).reshape(devices, depth, width) for g in rest], axis=1)
    return loss[0, 0], dense, rest, clean(d_xb), give_rows


def swap(v, bit, devices):
    return lax.ppermute(v, AXES, [(i, i ^ bit) for i in range(devices)])


def add(a, b):
    return (a.astype(f32) + b.astype(f32)).astype(bf)


def spot(v, axis, index):
    return lax.dynamic_index_in_dim(v, index, axis, keepdims=False)


def place_in_slice():
    row = lax.axis_index("dp")
    return row // 2, lax.rem(row, 2), lax.axis_index("seq") // 2


def over_cores(keep, send):
    view = lambda v: v.reshape((4, 2, 2) + v.shape[1:])
    keep, send = view(keep), view(send)
    cut = keep.shape[3] // 2
    one = add(keep[:, :, :, :cut], swap(send[:, :, :, :cut], 1, 32))
    two = add(keep[:, :, :, cut:], swap(send[:, :, :, cut:], 1, 32))
    return one, two


def over_wide(one, two):
    _, y, x = place_in_slice()
    return add(spot(one, 2, x), swap(spot(one, 2, 1 - x), 2, 32)), add(spot(two, 1, y), swap(spot(two, 1, 1 - y), 4, 32))


def over_other(one, two):
    _, y, x = place_in_slice()
    return add(spot(one, 1, y), swap(spot(one, 1, 1 - y), 4, 32)), add(spot(two, 1, x), swap(spot(two, 1, 1 - x), 2, 32))


def over_long(one, two):
    z, _, _ = place_in_slice()
    both = jnp.concatenate([one, two], axis=1)
    total = spot(both, 0, z).astype(f32)
    for step in range(1, 4):
        total = total + swap(spot(both, 0, z ^ step), 8 * step, 32).astype(f32)
    return total


def body(
    token_ids, lengths, labeled, gold,
    embed, position, attn_in, attn_out, ff_in, ff_out, vectors,
    mom_embed, mom_position, mom_attn_in, mom_attn_out, mom_ff_in, mom_ff_out, mom_vectors,
    avg_embed, avg_position, avg_attn_in, avg_attn_out, avg_ff_in, avg_ff_out, avg_vectors,
):
    pairs_here, _, local = token_ids.shape
    seq = lax.axis_size("seq")
    devices = lax.axis_size("dp") * seq
    length = local * seq
    per_owner, width = embed.shape
    depth = attn_in.shape[0]
    hidden = ff_in.shape[1]
    nvec = vectors.shape[0]
    turns = ff_out.shape[0] // depth
    rows = BLOCKS * ROWS
    room = slots_of(devices)
    spare = 128 - nvec

    shard = jnp.concatenate(
        [attn_in, attn_out, ff_in]
        + [ff_out[i * depth : (i + 1) * depth] for i in range(turns)]
        + [position.T, vectors.T, jnp.zeros((depth, spare), f32)],
        axis=1,
    ).astype(bf)
    full = lax.all_gather(shard, AXES, axis=0, tiled=True)

    group = 2 * pairs_here
    info = jnp.concatenate([lengths.reshape(1, group), labeled.reshape(1, pairs_here)], axis=1)
    info = jnp.pad(info, ((0, 0), (0, local - group - pairs_here)))
    news = jnp.concatenate([token_ids.reshape(group, local), info], axis=0)
    news = exchange(jnp.broadcast_to(news[None], (devices,) + news.shape)).reshape(devices // seq, seq, group + 1, local)
    lens = news[:, 0, group, :group].reshape(2 * devices)
    lab = news[:, 0, group, group : group + pairs_here].reshape(devices)
    live = jnp.where(jnp.repeat(lab, 2) > 0, lens, 0)
    index = jnp.arange(2 * devices, dtype=jnp.int32)
    ahead = (live[None, :] > live[:, None]) | ((live[None, :] == live[:, None]) & (index[None, :] < index[:, None]))
    order = jnp.sum(ahead.astype(jnp.int32), axis=1)
    me = lax.axis_index("dp") * seq + lax.axis_index("seq")
    take = lambda values, i: jnp.sum(jnp.where(index[: values.shape[0]] == i, values, 0))
    chosen = [jnp.sum(jnp.where(order == rank, index, 0)) for rank in (me, 2 * devices - 1 - me)]
    count = jnp.maximum(jnp.sum(lab).astype(f32), 1.0)
    size = [take(live, i) for i in chosen]
    start = (size[0] + 15) // 16 * 16
    two_ids = [
        lax.dynamic_slice(news, (i // group, 0, lax.rem(i, group), 0), (1, seq, 1, local)).reshape(length) for i in chosen
    ]
    ids = lax.dynamic_update_slice(jnp.pad(two_ids[0], (0, rows - length)), two_ids[1], (start,))
    line = jnp.arange(rows, dtype=jnp.int32)
    in_first, in_second = line < size[0], (line >= start) & (line < start + size[1])
    used = in_first | in_second
    spots = jnp.where(in_first, line, jnp.where(in_second, line - start, -1))
    total = jnp.where(size[1] > 0, start + size[1], size[0])
    core = lax.rem(lax.axis_index("seq"), 2)
    plan = jnp.stack([size[0], size[1], start, jnp.clip((total + ROWS - 1) // ROWS, 2, BLOCKS), core])
    owner, place, first, rank = route(ids, used, per_owner)
    most = jnp.max(jnp.where(used, rank + 1, 0))
    asked = requests(owner, place, first, rank, 0, devices).reshape(devices, room)
    note = jnp.broadcast_to(most, (devices, 1))
    got = exchange(jnp.concatenate([asked, note, jnp.zeros((devices, 127 - room), jnp.int32)], axis=1))
    rounds = (jnp.max(got[:, room]) + room - 1) // room

    table = embed.astype(bf)
    slots = token_slots(owner, used, rank, 0, room)
    wanted_first = got[:, :room].reshape(-1)

    def pick(wanted):
        picked = mm(one_hot(wanted, per_owner), table).astype(bf).reshape(devices, room, width)
        return exchange(picked).reshape(devices * room, width)

    back = pick(wanted_first)

    def ask_again(start):
        return exchange(requests(owner, place, first, rank, start, devices).reshape(devices, room)).reshape(-1)

    def more(state):
        step, total = state
        start = step * room
        there = one_hot(token_slots(owner, used, rank, start, room), devices * room)
        return step + 1, total + mm(there, pick(ask_again(start))).astype(bf)

    _, extra = lax.while_loop(lambda state: state[0] < rounds, more, (jnp.int32(1), jnp.zeros((rows, width), bf)))

    def meet(pooled):
        goal = jnp.pad(gold[None, :], ((0, 0), (0, width - pairs_here)))
        all_pooled = jnp.concatenate([pooled[:2], goal], axis=0)
        all_pooled = exchange(jnp.broadcast_to(all_pooled[None], (devices, 3, width)))
        vectors_of, facts = [], []
        for i in chosen:
            other = i ^ 1
            rank = take(order, other)
            holder = jnp.where(rank < devices, rank, 2 * devices - 1 - rank)
            vectors_of.append(lax.dynamic_slice(all_pooled, (holder, (rank >= devices).astype(jnp.int32), 0), (1, 1, width))[0])
            pair = i // 2
            goal = lax.dynamic_slice(all_pooled, (pair // pairs_here * seq, 2, lax.rem(pair, pairs_here)), (1, 1, 1))[0, 0, 0]
            weight = take(lab, pair).astype(f32)
            own = jnp.where(lax.rem(i, 2) == 0, weight, 0.0)
            facts += [weight, goal, take(lens, i).astype(f32), take(lens, other).astype(f32), own]
        return jnp.concatenate(vectors_of, axis=0), jnp.stack(facts + [count])

    staged = (seq, devices) == (4, 32) and depth % 8 == 0
    loss, dense, rest, d_xb, give_rows = run_forward_backward(
        full, back, extra, slots, spots, plan, meet, staged, devices, depth, length, hidden
    )

    def sum_up(parts):
        if isinstance(parts, list | tuple):
            keep, send = parts
            both = jnp.stack([jnp.where(core == 0, keep, send), jnp.where(core == 0, send, keep)], axis=1)
            parts = both.reshape((devices,) + keep.shape[1:])
        return lax.psum_scatter(parts, AXES, scatter_dimension=0, tiled=True).astype(f32)[0]

    give_rows = exchange(give_rows.reshape(devices, room, width))
    if staged:
        dense = over_long(*over_other(*dense))
        rest = over_other(*over_wide(*over_cores(*rest)))
        rest, give_rows = lax.optimization_barrier((rest, give_rows))
        rest = over_long(*rest)
    else:
        dense, rest = sum_up(dense), sum_up(rest)
    beside = lambda v: jnp.concatenate(list(v), axis=1)
    g_ff_out = dense[:turns].reshape(turns * depth, width)
    g_ff_in = beside(dense[turns : 2 * turns])
    g_attn_out = dense[2 * turns]
    g_attn_in = beside(rest[:3])
    g_position = rest[3, :, :length].T
    g_vectors = rest[3, :, length : length + nvec].T

    def give(wanted, there):
        return mm_left(one_hot(wanted, per_owner), there.reshape(devices * room, width))

    def more_back(state):
        step, total = state
        start = step * room
        sums = mm_left(one_hot(token_slots(owner, used, rank, start, room), devices * room), d_xb).astype(bf)
        return step + 1, total + give(ask_again(start), exchange(sums.reshape(devices, room, width)))

    _, g_embed = lax.while_loop(lambda state: state[0] < rounds, more_back, (jnp.int32(1), give(wanted_first, give_rows)))

    grads = (g_embed, g_position, g_attn_in, g_attn_out, g_ff_in, g_ff_out, g_vectors)
    squares = sum(jnp.sum(g * g) for g in grads)
    sums = exchange(jnp.broadcast_to(jnp.stack([squares, loss])[None, :], (devices, 2)))
    sums = jnp.sum(sums, axis=0)
    norm = jnp.sqrt(sums[0])
    loss_sum = sums[1]
    scale = jnp.minimum(1.0, CLIP / (norm + 1e-06))
    weights = (embed, position, attn_in, attn_out, ff_in, ff_out, vectors)
    moms = (mom_embed, mom_position, mom_attn_in, mom_attn_out, mom_ff_in, mom_ff_out, mom_vectors)
    avgs = (avg_embed, avg_position, avg_attn_in, avg_attn_out, avg_ff_in, avg_ff_out, avg_vectors)
    news, next_moms, next_avgs = [], [], []
    for weight, grad, mom, avg in zip(weights, grads, moms, avgs):
        clipped = grad * scale
        moment = MOMENT * mom + clipped
        fresh = weight - RATE * (clipped + MOMENT * moment)
        news.append(fresh)
        next_moms.append(moment)
        next_avgs.append(DECAY * avg + (1.0 - DECAY) * fresh)
    return (loss_sum, count, norm, *news, *next_moms, *next_avgs)


def solution(mesh):
    whole = (
        P(AXES, None),
        P(None, AXES),
        P(AXES, None),
        P(AXES, None),
        P(AXES, None),
        P(AXES, None),
        P(None, AXES),
    )
    return jax.shard_map(
        body,
        mesh=mesh,
        in_specs=(P("dp", None, "seq"), P("dp", None), P("dp"), P("dp")) + whole * 3,
        out_specs=(P(), P(), P()) + whole * 3,
        check_vma=False,
    )
```

time: 531 us -> 519 us (0.977)
  Pallas kernels: 181 us -> 137 us
  between operations: 25.3 us -> 42.2 us
  starting transfers between devices: 44.6 us -> 50.3 us
    pallas_call x9, Pallas kernels: 171 us -> 127 us  [the longest x1 22.6 us: run_forward_backward(): call(when_live(middle_kernel), 1, (BLOCKS,), [row(width), row(width), w_o...]
    all_to_all x4 -> x6, waiting for transfers between devices: 65.3 us -> 92.1 us  [exchange(): return lax.all_to_all(v, AXES, 0, 0, tiled=True)]
    all_gather x1, waiting for transfers between devices: 33.1 us -> 7.93 us  [body(): full = lax.all_gather(shard, AXES, axis=0, tiled=True)]
    all_to_all x4 -> x6, starting transfers between devices: 16.9 us -> 25.8 us  [exchange(): return lax.all_to_all(v, AXES, 0, 0, tiled=True)]
  transfers between devices with their start and end apart: 24 -> 25, of which waited for: 12 -> 14; matrix products, arithmetic and copies ran while one was open for 10% -> 12% of each run, Pallas kernels for 11% -> 8%
where the time goes in v4:
time: 519 us; the launch traced here: 512 us
  waiting for transfers between devices  171 us (33%)
  Pallas kernels  137 us (26%)
  other arithmetic  66.2 us (13%)
  starting transfers between devices  50.3 us (10%)
  between operations  42.2 us (8%)
  local copies, waits for them, and re-layouts  34.6 us (7%)
  matrix products  9.74 us (2%)
    all_to_all x6, waiting for transfers between devices, exchange(): return lax.all_to_all(v, AXES, 0, 0, tiled=True)  92.1 us
    ppermute x18, waiting for transfers between devices, swap(): return lax.ppermute(v, AXES, [(i, i ^ bit) for i in range(devices)])  71.1 us
    all_to_all x6, starting transfers between devices, exchange(): return lax.all_to_all(v, AXES, 0, 0, tiled=True)  25.8 us
    ppermute x18, starting transfers between devices, swap(): return lax.ppermute(v, AXES, [(i, i ^ bit) for i in range(devices)])  24.5 us
    pallas_call x1, Pallas kernels, run_forward_backward(): call(when_live(middle_kernel), 1, (BLOCKS,), [row(width), row(width), w_o...  22.6 us
    pallas_call x2, Pallas kernels, attend_back(): call(attend_back_kernel, 1, (count,), [block(0, start), block(1, start),...  21.6 us
    pallas_call x1, Pallas kernels, run_forward_backward(): call(when_live(back_kernel), 2, (BLOCKS,), [fixed((8, width), (0, 0)), fi...  19.7 us
    pallas_call x1, Pallas kernels, run_forward_backward(): call(functools.partial(dense_grads_kernel, depth, turns), 1, (2,), [halve...  18.1 us
  transfers between devices with their start and end apart: 25, of which 14 were waited for; matrix products, arithmetic and copies ran while one was open for 12% of the time, Pallas kernels for 8%

profile of v4, /device:TPU:0, one launch (start us, length us, event | category | flops | bytes accessed | tf_op | source)
XLA Modules:
  0.0 511.5 jit_solution(6325094680506443093)
XLA Ops:
  14.8 7.3 %all-to-all-start.4 = ((s32[32,9,128]{2,1,0:T(8,128)}), s32[32,9,128]{2,1,0:T(8,128)S(1)}, u32[]{:S(2)}, u32[]{:S(2)}) async-start(s32[32,9,128]{2,1,0:T(8,128)} %broadcast_in_dim.161), calls=%async_computation.4 | async-start | bytes 524288 | tf_op jit(solution)/shard_map/all_to_all | solution.py:40
  22.2 12.6 %all-to-all-done.4 = s32[32,9,128]{2,1,0:T(8,128)S(1)} async-done(((s32[32,9,128]{2,1,0:T(8,128)}), s32[32,9,128]{2,1,0:T(8,128)S(1)}, u32[]{:S(2)}, u32[]{:S(2)}) %all-to-all-start.4) | async-done | bytes 147488 | tf_op jit(solution)/shard_map/all_to_all | solution.py:40
  40.3 2.0 fusion.75
  48.7 1.7 convert_reduce_fusion
  50.4 1.3 and_select_fusion.3
  53.8 4.2 all-to-all-start.5
  59.3 5.9 %all-to-all-done.5 = s32[32,1,128]{2,1,0:T(1,128)S(1)} async-done(((s32[32,1,128]{2,1,0:T(1,128)}), s32[32,1,128]{2,1,0:T(1,128)S(1)}, u32[]{:S(2)}, u32[]{:S(2)}) %all-to-all-start.5) | async-done | bytes 16416 | tf_op jit(solution)/shard_map/all_to_all | solution.py:40
  66.7 4.5 fusion.34
  71.5 2.7 all-to-all-start.6
  77.2 1.9 stack.59.refs_0_.plan
  79.2 1.6 select_select_fusion.refs_2_.spot_in
  80.8 66.0 %all-to-all-done.6 = bf16[32,32,768]{2,1,0:T(8,128)(2,1)S(1)} async-done(((bf16[32,32,768]{2,1,0:T(8,128)(2,1)}), bf16[32,32,768]{2,1,0:T(8,128)(2,1)S(1)}, u32[]{:S(2)}, u32[]{:S(2)}) %all-to-all-start.6) | async-done | bytes 1572896 | tf_op jit(solution)/shard_map/all_to_all | solution.py:40
  146.8 7.9 %all-gather.2.cloned.1.call-done.refs_5_.refs_6_.refs_7_.src.refs_3_.refs_4_.refs_8_ = bf16[768,9856]{1,0:T(8,128)(2,1)} async-done(((bf16[24,9856]{1,0:T(8,128)(2,1)}), bf16[768,9856]{1,0:T(8,128)(2,1)}) %all-gather.2.cloned.1.call-update) | async-done | bytes 15138832 | tf_op jit(solution)/shard_map/all_gather | solution.py:649
  154.7 10.4 %first.1 = (f32[1152,768]{1,0:T(8,128)}, bf16[1152,768]{1,0:T(8,128)(2,1)}, bf16[1152,2304]{1,0:T(8,128)(2,1)}, f32[16,768]{1,0:T(8,128)}) custom-call(s32[5]{0:T(128)} %stack.59.refs_0_.plan, s32[1152,1]{1,0:T(8,128)} %broadcast_in_dim.184.refs_1_, s32[1152,1]{1,0:T(8,128)} %select_select_fusion.refs_2_.spot_in, bf16[1024,768]{1,0:T(8,128)(2,1)} %bitcast.198, ...), custom_call_target="tpu_custom_call" | custom-call | tf_op jit(solution)/shard_map/first/pallas_call | solution.py:455
  165.1 12.6 %attend.1.refs_2_.mixed = bf16[1152,768]{1,0:T(8,128)(2,1)} custom-call(s32[5]{0:T(128)} %stack.59.refs_0_.plan, bf16[1152,2304]{1,0:T(8,128)(2,1)} %get-tuple-element.156.query.keys.values, bf16[1152,2304]{1,0:T(8,128)(2,1)} %get-tuple-element.156.query.keys.values, bf16[1152,2304]{1,0:T(8,128)(2,1)} %get-tuple-element.156.query.keys.values), custom_call_target="tpu_custom_call" | custom-call | tf_op jit(solution)/shard_map/attend/pallas_call | solution.py:467
  179.1 10.3 %spread.1.refs_5_.refs_9_ = bf16[3072,768]{1,0:T(8,128)(2,1)} custom-call(bf16[768,9856]{1,0:T(8,128)(2,1)} %all-gather.2.cloned.1.call-done.refs_5_.refs_6_.refs_7_.src.refs_3_.refs_4_.refs_8_), custom_call_target="tpu_custom_call" | custom-call | tf_op jit(solution)/shard_map/spread/pallas_call | solution.py:435
  189.5 22.6 %middle.1 = (f32[1152,768]{1,0:T(8,128)}, bf16[1152,768]{1,0:T(8,128)(2,1)}, bf16[1152,3072]{1,0:T(8,128)(2,1)}, bf16[1152,3072]{1,0:T(8,128)(2,1)}, f32[1152,768]{1,0:T(8,128)}, /*index=5*/f32[8,768]{1,0:T(8,128)}) custom-call(s32[5]{0:T(128)} %stack.59.refs_0_.plan, f32[1152,768]{1,0:T(8,128)} %get-tuple-element.157.refs_1_.refs_2_, ...), custom_call_target="tpu_custom_call" | custom-call | tf_op jit(solution)/shard_map/middle/pallas_call | solution.py:472
  213.7 2.8 all-to-all-start.7
  227.8 1.9 all-to-all-done.7
  230.9 2.0 stack.69.refs_1_
  232.8 19.7 %back.1 = (bf16[1152,768]{1,0:T(8,128)(2,1)}, bf16[1152,3072]{1,0:T(8,128)(2,1)}, f32[1152,768]{1,0:T(8,128)}, bf16[1152,768]{1,0:T(8,128)(2,1)}, bf16[1152,768]...) custom-call(s32[5]{0:T(128)} %stack.59.refs_0_.plan, f32[11]{0:T(128)} %stack.69.refs_1_, ...), custom_call_target="tpu_custom_call" | custom-call | tf_op jit(solution)/shard_map/back/pallas_call | solution.py:484
  252.6 18.1 %dense_grads.1 = (bf16[16,9,24,768]{3,2,1,0:T(8,128)(2,1)}, bf16[16,9,24,768]{3,2,1,0:T(8,128)(2,1)}) custom-call(s32[5]{0:T(128)} %stack.59.refs_0_.plan, bf16[1152,3072]{1,0:T(8,128)(2,1)} %get-tuple-element.164.act, bf16[1152,768]{1,0:T(8,128)(2,1)} %get-tuple-element.165.d_y, bf16[1152,768]{1,0:T(8,128)(2,1)} %get-tuple-element.166.h1, ...), custom_call_target="tpu_custom_call" | custom-call | tf_op jit(solution)/shard_map/dense_grads/pallas_call | solution.py:509
  270.6 2.0 slice.147
  273.0 1.9 slice.145
  274.8 1.6 copy.172
  276.9 10.6 %attend_back.2.more_0_ = bf16[3,1152,768]{2,1,0:T(8,128)(2,1)} custom-call(s32[5]{0:T(128)} %stack.59.refs_0_.plan, bf16[1152,2304]{1,0:T(8,128)(2,1)} %get-tuple-element.156.query.keys.values, bf16[1152,2304]{1,0:T(8,128)(2,1)} %get-tuple-element.156.query.keys.values, bf16[1152,2304]{1,0:T(8,128)(2,1)} %get-tuple-element.156.query.keys.values, ...), custom_call_target="tpu_custom_call" | custom-call | flops 1006632960 | bytes 7077888 | tf_op jit(solution)/shard_map/attend_back/pallas_call | solution.py:531
  287.5 3.1 add_convert_fusion.1
  290.6 4.3 add_convert_fusion
  300.4 11.0 %attend_back.3.refs_4_.d_proj = bf16[3,1152,768]{2,1,0:T(8,128)(2,1)} custom-call(s32[5]{0:T(128)} %stack.59.refs_0_.plan, bf16[1152,2304]{1,0:T(8,128)(2,1)} %get-tuple-element.156.query.keys.values, bf16[1152,2304]{1,0:T(8,128)(2,1)} %get-tuple-element.156.query.keys.values, ...), custom_call_target="tpu_custom_call", output_to_operand_aliasing={{}: (5, {})} | custom-call | flops 1006632960 | bytes 7077888 | tf_op jit(solution)/shard_map/attend_back/pallas_call | solution.py:531
  311.4 11.9 %last.1 = (bf16[1152,768]{1,0:T(8,128)(2,1)}, f32[8,768]{1,0:T(8,128)}, bf16[1024,768]{1,0:T(8,128)(2,1)}) custom-call(s32[5]{0:T(128)} %stack.59.refs_0_.plan, s32[1152,1]{1,0:T(8,128)} %broadcast_in_dim.184.refs_1_, f32[1152,768]{1,0:T(8,128)} %get-tuple-element.157.refs_1_.refs_2_, f32[1152,768]{1,0:T(8,128)} %get-tuple-element.172.refs_3_, ...), custom_call_target="tpu_custom_call" | custom-call | tf_op jit(solution)/shard_map/last/pallas_call | solution.py:547
  323.3 2.9 collective-permute-done.2
  326.2 1.9 fusion.31
  328.1 2.6 collective-permute-done.3
  330.6 1.7 fusion.30
  335.5 9.9 %rest_grads.1 = (bf16[16,4,24,768]{3,2,1,0:T(8,128)(2,1)}, bf16[16,4,24,768]{3,2,1,0:T(8,128)(2,1)}) custom-call(s32[5]{0:T(128)} %stack.59.refs_0_.plan, s32[1152,1]{1,0:T(8,128)} %select_select_fusion.refs_2_.spot_in, bf16[1152,768]{1,0:T(8,128)(2,1)} %get-tuple-element.155.hin, bf16[3,1152,768]{2,1,0:T(8,128)(2,1)} %attend_back.3.refs_4_.d_proj, ...), custom_call_target="tpu_custom_call" | custom-call | tf_op jit(solution)/shard_map/rest_grads/pallas_call | solution.py:563
  345.4 3.3 fusion.90
  349.2 1.4 broadcast_select_fusion
  350.7 4.1 all-to-all-start.8
  356.0 1.4 fusion.35
  357.6 1.9 collective-permute-start.15
  359.5 2.4 collective-permute-start.16
  362.1 2.3 add_convert_fusion.2
  364.4 1.9 collective-permute-start.8
  366.4 22.1 %collective-permute-done.15 = bf16[9,24,768]{2,1,0:T(8,128)(2,1)S(1)} collective-permute-done((bf16[9,24,768]{2,1,0:T(8,128)(2,1)S(1)}, bf16[9,24,768]{2,1,0:T(8,128)(2,1)S(1)}, u32[]{:S(2)}, u32[]{:S(2)}) %collective-permute-start.15) | collective-permute-done | bytes 331808 | tf_op jit(solution)/shard_map/ppermute | solution.py:580
  388.5 25.7 %collective-permute-done.16 = bf16[9,24,768]{2,1,0:T(8,128)(2,1)S(1)} collective-permute-done((bf16[9,24,768]{2,1,0:T(8,128)(2,1)S(1)}, bf16[9,24,768]{2,1,0:T(8,128)(2,1)S(1)}, u32[]{:S(2)}, u32[]{:S(2)}) %collective-permute-start.16) | collective-permute-done | bytes 331808 | tf_op jit(solution)/shard_map/ppermute | solution.py:580
  414.5 1.3 collective-permute-start.5
  417.4 13.3 %collective-permute-done.5 = bf16[4,2,2,24,768]{4,3,2,1,0:T(8,128)(2,1)S(1)} collective-permute-done((bf16[4,2,2,24,768]{4,3,2,1,0:T(8,128)(2,1)S(1)}, bf16[4,2,2,24,768]{4,3,2,1,0:T(8,128)(2,1)S(1)}, u32[]{:S(2)}, u32[]{:S(2)}) %collective-permute-start.5) | collective-permute-done | bytes 589856 | tf_op jit(solution)/shard_map/ppermute | solution.py:580
  431.0 1.3 collective-permute-start.6
  433.6 1.6 collective-permute-done.9
  435.3 2.4 collective-permute-done.6
  438.7 7.2 %collective-permute-start.10 = (bf16[4,24,768]{2,1,0:T(8,128)(2,1)}, bf16[4,24,768]{2,1,0:T(8,128)(2,1)S(1)}, u32[]{:S(2)}, u32[]{:S(2)}) collective-permute-start(bf16[4,24,768]{2,1,0:T(8,128)(2,1)} %get-tuple-element.492), channel_id=1, source_target_pairs={{0,8},{1,9},{2,10},{3,11},{4,12},{5,13},{6,14},{7,15},{8,0},{9,1},... | collective-permute-start | bytes 442376 | tf_op jit(solution)/shard_map/ppermute | solution.py:580
  446.3 1.9 collective-permute-start.12
  448.2 5.2 %fusion.28 = f32[960,768]{1,0:T(8,128)} fusion(bf16[1024,768]{1,0:T(8,128)(2,1)} %bitcast.48, s32[1024]{0:T(1024)S(1)} %copy-done.33), kind=kOutput, calls=%fused_computation.56 | convolution fusion | flops 1510932480 | bytes 4526080 | tf_op jit(solution)/shard_map/dot_general | solution.py:32
  453.5 3.2 multiply_reduce_fusion
  467.0 4.6 all-to-all-start.9
  473.1 5.6 %all-to-all-done.9 = f32[32,1,2]{2,1,0:T(1,128)S(1)} async-done(((f32[32,1,2]{2,1,0:T(1,128)}), f32[32,1,2]{2,1,0:T(1,128)S(1)}, u32[]{:S(2)}, u32[]{:S(2)}) %all-to-all-start.9) | async-done | bytes 288 | tf_op jit(solution)/shard_map/all_to_all | solution.py:40
  480.9 1.5 add_multiply_fusion.6
  482.4 1.4 copy.167
  483.7 1.4 copy.168
  485.1 1.4 copy.169
  486.5 2.2 add_multiply_fusion.2
  488.7 1.7 add_multiply_fusion.4
  490.4 2.1 add_multiply_fusion.3
  493.2 8.0 %add_multiply_fusion = (f32[960,768]{1,0:T(8,128)}, f32[960,768]{1,0:T(8,128)}, f32[960,768]{1,0:T(8,128)}) fusion(f32[960,768]{1,0:T(8,128)} %param.47, f32[960,768]{1,0:T(8,128)S(1)} %copy-done.1, f32[960,768]{1,0:T(8,128)} %get-tuple-element.184, f32[]{:T(128)S(6)} %min.8, f32[960,768]{1,0:T(8,128)} %param.40), kind=kLoop, calls=%fused_computation.60 | loop fusion | flops 6635520 | bytes 20643844 | tf_op jit(solution)/shard_map/add | solution.py:780
  (197 shorter events, 49.8 us)
Async XLA Ops:
  7.2 6.6 %copy-start.34 = (s32[4,2]{0,1:T(2,128)S(1)}, s32[4,2]{0,1:T(2,128)}, u32[]{:S(2)}) copy-start(s32[4,2]{0,1:T(2,128)} %param.30) | copy-start | bytes 100
  7.2 6.8 %copy-start.36 = (s32[4]{0:T(128)S(1)}, s32[4]{0:T(128)}, u32[]{:S(2)}) copy-start(s32[4]{0:T(128)} %param.31) | copy-start | bytes 52
  7.2 6.8 %copy-start.31 = (s32[4,2,128]{2,1,0:T(2,128)S(1)}, s32[4,2,128]{2,1,0:T(2,128)}, u32[]{:S(2)}) copy-start(s32[4,2,128]{2,1,0:T(2,128)} %param.29) | copy-start | bytes 12292
  7.2 50.8 %copy-start = (f32[960,768]{1,0:T(8,128)S(1)}, f32[960,768]{1,0:T(8,128)}, u32[]{:S(2)}) copy-start(f32[960,768]{1,0:T(8,128)} %param.33) | copy-start | bytes 8847364
  7.2 147.5 %all-gather.2.cloned.1.call-start = ((), (), s32[]{:S(2)}) async-start(), calls=%async_computation.10 | async-start | bytes 15611904 | tf_op jit(solution)/shard_map/all_gather | solution.py:649
  14.8 20.0 %all-to-all-start.4 = ((s32[32,9,128]{2,1,0:T(8,128)}), s32[32,9,128]{2,1,0:T(8,128)S(1)}, u32[]{:S(2)}, u32[]{:S(2)}) async-start(s32[32,9,128]{2,1,0:T(8,128)} %broadcast_in_dim.161), calls=%async_computation.4 | async-start | bytes 524288 | tf_op jit(solution)/shard_map/all_to_all | solution.py:40
  53.8 11.4 %all-to-all-start.5 = ((s32[32,1,128]{2,1,0:T(1,128)}), s32[32,1,128]{2,1,0:T(1,128)S(1)}, u32[]{:S(2)}, u32[]{:S(2)}) async-start(s32[32,1,128]{2,1,0:T(1,128)} %bitcast.6), calls=%async_computation.5 | async-start | bytes 32768 | tf_op jit(solution)/shard_map/all_to_all | solution.py:40
  66.7 4.5 copy-start.32
  71.5 75.3 %all-to-all-start.6 = ((bf16[32,32,768]{2,1,0:T(8,128)(2,1)}), bf16[32,32,768]{2,1,0:T(8,128)(2,1)S(1)}, u32[]{:S(2)}, u32[]{:S(2)}) async-start(bf16[32,32,768]{2,1,0:T(8,128)(2,1)} %bitcast.206), calls=%async_computation.6 | async-start | bytes 3145728 | tf_op jit(solution)/shard_map/all_to_all | solution.py:40
  146.8 7.9 %copy-start.4 = (bf16[32,32,768]{2,1,0:T(8,128)(2,1)}, bf16[32,32,768]{2,1,0:T(8,128)(2,1)S(1)}, u32[]{:S(2)}) copy-start(bf16[32,32,768]{2,1,0:T(8,128)(2,1)S(1)} %all-to-all-done.6) | copy-start | bytes 4718596
  189.5 23.4 %copy-start.35 = (f32[4]{0:T(128)S(1)}, f32[4]{0:T(128)}, u32[]{:S(2)}) copy-start(f32[4]{0:T(128)} %param.32) | copy-start | bytes 52
  213.7 16.0 %all-to-all-start.7 = ((f32[32,3,768]{2,1,0:T(4,128)}), f32[32,3,768]{2,1,0:T(4,128)S(1)}, u32[]{:S(2)}, u32[]{:S(2)}) async-start(f32[32,3,768]{2,1,0:T(4,128)} %broadcast_in_dim.175), calls=%async_computation.7 | async-start | bytes 786432 | tf_op jit(solution)/shard_map/all_to_all | solution.py:40
  272.9 17.8 %collective-permute-start.1 = (bf16[4,2,2,5,24,768]{5,4,3,0,2,1:T(8,128)(2,1)S(1)}, bf16[4,2,2,5,24,768]{5,4,3,0,2,1:T(8,128)(2,1)}, u32[]{:S(2)}, u32[]{:S(2)}) collective-permute-start(bf16[4,2,2,5,24,768]{5,4,3,0,2,1:T(8,128)(2,1)S(1)} %copy.174), channel_id=1, source_target_pairs={{0,1},{1,0},{2,3},{3,2},{4,5},{5,4},{6,7},{7,6},{8,9},{9,8},{10,11... | collective-permute-start | bytes 8847368 | tf_op jit(solution)/shard_map/ppermute | solution.py:580
  276.4 11.1 %collective-permute-start = (bf16[4,2,2,4,24,768]{5,4,3,0,1,2:T(8,128)(2,1)}, bf16[4,2,2,4,24,768]{5,4,3,0,1,2:T(8,128)(2,1)}, u32[]{:S(2)}, u32[]{:S(2)}) collective-permute-start(bf16[4,2,2,4,24,768]{5,4,3,0,1,2:T(8,128)(2,1)} %copy.172), channel_id=1, source_target_pairs={{0,1},{1,0},{2,3},{3,2},{4,5},{5,4},{6,7},{7,6},{8,9},{9,8},{10,11... | collective-permute-start | bytes 7077896 | tf_op jit(solution)/shard_map/ppermute | solution.py:580
  290.6 6.5 %copy-start.2 = (bf16[4,2,2,4,24,768]{5,4,3,0,1,2:T(8,128)(2,1)}, bf16[4,2,2,4,24,768]{5,4,3,0,1,2:T(8,128)(2,1)S(1)}, u32[]{:S(2)}) copy-start(bf16[4,2,2,4,24,768]{5,4,3,0,1,2:T(8,128)(2,1)S(1)} %add_convert_fusion.1) | copy-start | bytes 7077892
  296.1 34.5 %collective-permute-start.3 = (bf16[4,2,5,24,768]{4,3,2,0,1:T(8,128)(2,1)}, bf16[4,2,5,24,768]{4,3,2,0,1:T(8,128)(2,1)}, u32[]{:S(2)}, u32[]{:S(2)}) collective-permute-start(bf16[4,2,5,24,768]{4,3,2,0,1:T(8,128)(2,1)} %dynamic-slice_bitcast_fusion), channel_id=1, source_target_pairs={{0,4},{1,5},{2,6},{3,7},{4,0},{5,1},{6,2},{7,3},{8,12},{9,13},{10,... | collective-permute-start | bytes 4423688 | tf_op jit(solution)/shard_map/ppermute | solution.py:580
  298.2 27.9 %collective-permute-start.2 = (bf16[4,2,4,24,768]{4,3,2,0,1:T(8,128)(2,1)}, bf16[4,2,4,24,768]{4,3,2,0,1:T(8,128)(2,1)}, u32[]{:S(2)}, u32[]{:S(2)}) collective-permute-start(bf16[4,2,4,24,768]{4,3,2,0,1:T(8,128)(2,1)} %dynamic-slice_bitcast_fusion.1), channel_id=1, source_target_pairs={{0,2},{1,3},{2,0},{3,1},{4,6},{5,7},{6,4},{7,5},{8,10},{9,11},{10,... | collective-permute-start | bytes 3538952 | tf_op jit(solution)/shard_map/ppermute | solution.py:580
  328.1 4.4 copy-start.7
  332.4 1.1 copy-start.5
  332.4 22.3 %collective-permute-start.13 = (bf16[4,4,24,768]{3,2,1,0:T(8,128)(2,1)S(1)}, bf16[4,4,24,768]{3,2,1,0:T(8,128)(2,1)}, u32[]{:S(2)}, u32[]{:S(2)}) collective-permute-start(bf16[4,4,24,768]{3,2,1,0:T(8,128)(2,1)S(1)} %dynamic-slice_bitcast_fusion.3), channel_id=1, source_target_pairs={{0,4},{1,5},{2,6},{3,7},{4,0},{5,1},{6,2},{7,3},{8,12},{9,13},{10,... | collective-permute-start | bytes 1769480 | tf_op jit(solution)/shard_map/ppermute | solution.py:580
  334.5 21.5 %collective-permute-start.14 = (bf16[4,5,24,768]{3,2,1,0:T(8,128)(2,1)}, bf16[4,5,24,768]{3,2,1,0:T(8,128)(2,1)}, u32[]{:S(2)}, u32[]{:S(2)}) collective-permute-start(bf16[4,5,24,768]{3,2,1,0:T(8,128)(2,1)} %dynamic-slice_bitcast_fusion.2), channel_id=1, source_target_pairs={{0,2},{1,3},{2,0},{3,1},{4,6},{5,7},{6,4},{7,5},{8,10},{9,11},{10,... | collective-permute-start | bytes 2211848 | tf_op jit(solution)/shard_map/ppermute | solution.py:580
  345.4 3.9 copy-start.3
  348.7 13.3 %collective-permute-start.4 = (bf16[4,2,2,2,24,768]{5,4,3,2,1,0:T(8,128)(2,1)}, bf16[4,2,2,2,24,768]{5,4,3,2,1,0:T(8,128)(2,1)}, u32[]{:S(2)}, u32[]{:S(2)}) collective-permute-start(bf16[4,2,2,2,24,768]{5,4,3,2,1,0:T(8,128)(2,1)} %get-tuple-element.483), channel_id=1, source_target_pairs={{0,1},{1,0},{2,3},{3,2},{4,5},{5,4},{6,7},{7,6},{8,9},{9,8},{10,11... | collective-permute-start | bytes 3538952 | tf_op jit(solution)/shard_map/ppermute | solution.py:580
  348.7 13.3 %collective-permute-start.7 = (bf16[4,2,2,2,24,768]{5,4,3,2,1,0:T(8,128)(2,1)}, bf16[4,2,2,2,24,768]{5,4,3,2,1,0:T(8,128)(2,1)}, u32[]{:S(2)}, u32[]{:S(2)}) collective-permute-start(bf16[4,2,2,2,24,768]{5,4,3,2,1,0:T(8,128)(2,1)} %get-tuple-element.482), channel_id=1, source_target_pairs={{0,1},{1,0},{2,3},{3,2},{4,5},{5,4},{6,7},{7,6},{8,9},{9,8},{10,11... | collective-permute-start | bytes 3538952 | tf_op jit(solution)/shard_map/ppermute | solution.py:580
  350.7 4.1 copy-start.8
  350.7 5.3 %copy-start.6 = (bf16[4,2,5,24,768]{4,3,2,0,1:T(8,128)(2,1)S(1)}, bf16[4,2,5,24,768]{4,3,2,0,1:T(8,128)(2,1)}, u32[]{:S(2)}) copy-start(bf16[4,2,5,24,768]{4,3,2,0,1:T(8,128)(2,1)} %copy-done.5) | copy-start | bytes 4423684
  350.7 87.2 %all-to-all-start.8 = ((bf16[32,32,768]{2,1,0:T(8,128)(2,1)}), bf16[32,32,768]{2,1,0:T(8,128)(2,1)}, u32[]{:S(2)}, u32[]{:S(2)}) async-start(bf16[32,32,768]{2,1,0:T(8,128)(2,1)} %bitcast.205), calls=%async_computation.8 | async-start | bytes 3145728 | tf_op jit(solution)/shard_map/all_to_all | solution.py:40
  356.0 6.1 %copy-start.10 = (bf16[16,4,24,768]{3,2,1,0:T(8,128)(2,1)S(1)}, bf16[16,4,24,768]{3,2,1,0:T(8,128)(2,1)}, u32[]{:S(2)}) copy-start(bf16[16,4,24,768]{3,2,1,0:T(8,128)(2,1)} %get-tuple-element.180) | copy-start | bytes 7077892
  357.6 30.9 %collective-permute-start.15 = (bf16[9,24,768]{2,1,0:T(8,128)(2,1)S(1)}, bf16[9,24,768]{2,1,0:T(8,128)(2,1)S(1)}, u32[]{:S(2)}, u32[]{:S(2)}) collective-permute-start(bf16[9,24,768]{2,1,0:T(8,128)(2,1)S(1)} %get-tuple-element.484), channel_id=1, source_target_pairs={{0,8},{1,9},{2,10},{3,11},{4,12},{5,13},{6,14},{7,15},{8,0},{9,1},... | collective-permute-start | bytes 995336 | tf_op jit(solution)/shard_map/ppermute | solution.py:580
  359.5 54.7 %collective-permute-start.16 = (bf16[9,24,768]{2,1,0:T(8,128)(2,1)S(1)}, bf16[9,24,768]{2,1,0:T(8,128)(2,1)S(1)}, u32[]{:S(2)}, u32[]{:S(2)}) collective-permute-start(bf16[9,24,768]{2,1,0:T(8,128)(2,1)S(1)} %get-tuple-element.485), channel_id=1, source_target_pairs={{0,16},{1,17},{2,18},{3,19},{4,20},{5,21},{6,22},{7,23},{8,24},{9,... | collective-permute-start | bytes 995336 | tf_op jit(solution)/shard_map/ppermute | solution.py:580
  361.9 52.3 %collective-permute-start.17 = (bf16[9,24,768]{2,1,0:T(8,128)(2,1)S(1)}, bf16[9,24,768]{2,1,0:T(8,128)(2,1)S(1)}, u32[]{:S(2)}, u32[]{:S(2)}) collective-permute-start(bf16[9,24,768]{2,1,0:T(8,128)(2,1)S(1)} %get-tuple-element.486), channel_id=1, source_target_pairs={{0,24},{1,25},{2,26},{3,27},{4,28},{5,29},{6,30},{7,31},{8,16},{9,... | collective-permute-start | bytes 995336 | tf_op jit(solution)/shard_map/ppermute | solution.py:580
  364.4 51.9 %collective-permute-start.8 = (bf16[4,2,2,24,768]{4,3,2,1,0:T(8,128)(2,1)S(1)}, bf16[4,2,2,24,768]{4,3,2,1,0:T(8,128)(2,1)S(1)}, u32[]{:S(2)}, u32[]{:S(2)}) collective-permute-start(bf16[4,2,2,24,768]{4,3,2,1,0:T(8,128)(2,1)S(1)} %dynamic-slice_bitcast_fusion.4), channel_id=1, source_target_pairs={{0,4},{1,5},{2,6},{3,7},{4,0},{5,1},{6,2},{7,3},{8,12},{9,13},{10,... | collective-permute-start | bytes 1769480 | tf_op jit(solution)/shard_map/ppermute | solution.py:580
  414.4 65.7 %copy-start.9 = (f32[9,24,768]{2,1,0:T(8,128)}, f32[9,24,768]{2,1,0:T(8,128)S(1)}, u32[]{:S(2)}) copy-start(f32[9,24,768]{2,1,0:T(8,128)S(1)} %fusion.40) | copy-start | bytes 1990660
  414.5 16.3 %collective-permute-start.5 = (bf16[4,2,2,24,768]{4,3,2,1,0:T(8,128)(2,1)S(1)}, bf16[4,2,2,24,768]{4,3,2,1,0:T(8,128)(2,1)S(1)}, u32[]{:S(2)}, u32[]{:S(2)}) collective-permute-start(bf16[4,2,2,24,768]{4,3,2,1,0:T(8,128)(2,1)S(1)} %dynamic-slice_bitcast_fusion.5), channel_id=1, source_target_pairs={{0,2},{1,3},{2,0},{3,1},{4,6},{5,7},{6,4},{7,5},{8,10},{9,11},{10,... | collective-permute-start | bytes 1769480 | tf_op jit(solution)/shard_map/ppermute | solution.py:580
  416.3 16.6 %copy-start.14 = (f32[24,768]{1,0:T(8,128)}, f32[24,768]{1,0:T(8,128)S(1)}, u32[]{:S(2)}) copy-start(f32[24,768]{1,0:T(8,128)S(1)} %get-tuple-element.487) | copy-start | bytes 221188
  416.3 16.6 %copy-start.15 = (f32[24,768]{1,0:T(8,128)}, f32[24,768]{1,0:T(8,128)S(1)}, u32[]{:S(2)}) copy-start(f32[24,768]{1,0:T(8,128)S(1)} %get-tuple-element.488) | copy-start | bytes 221188
  416.3 16.6 %copy-start.16 = (f32[24,768]{1,0:T(8,128)}, f32[24,768]{1,0:T(8,128)S(1)}, u32[]{:S(2)}) copy-start(f32[24,768]{1,0:T(8,128)S(1)} %get-tuple-element.489) | copy-start | bytes 221188
  416.3 16.6 %copy-start.17 = (f32[24,768]{1,0:T(8,128)}, f32[24,768]{1,0:T(8,128)S(1)}, u32[]{:S(2)}) copy-start(f32[24,768]{1,0:T(8,128)S(1)} %get-tuple-element.490) | copy-start | bytes 221188
  416.5 18.7 %collective-permute-start.9 = (bf16[4,2,24,768]{3,2,1,0:T(8,128)(2,1)S(1)}, bf16[4,2,24,768]{3,2,1,0:T(8,128)(2,1)S(1)}, u32[]{:S(2)}, u32[]{:S(2)}) collective-permute-start(bf16[4,2,24,768]{3,2,1,0:T(8,128)(2,1)S(1)} %dynamic-slice_bitcast_fusion.6), channel_id=1, source_target_pairs={{0,2},{1,3},{2,0},{3,1},{4,6},{5,7},{6,4},{7,5},{8,10},{9,11},{10,... | collective-permute-start | bytes 884744 | tf_op jit(solution)/shard_map/ppermute | solution.py:580
  431.0 17.3 %copy-start.33 = (s32[1024]{0:T(1024)S(1)}, s32[1024]{0:T(1024)}, u32[]{:S(2)}) copy-start(s32[1024]{0:T(1024)} %copy-done.32) | copy-start | bytes 12292
  431.0 6.8 %collective-permute-start.6 = (bf16[4,2,24,768]{3,2,1,0:T(8,128)(2,1)S(1)}, bf16[4,2,24,768]{3,2,1,0:T(8,128)(2,1)S(1)}, u32[]{:S(2)}, u32[]{:S(2)}) collective-permute-start(bf16[4,2,24,768]{3,2,1,0:T(8,128)(2,1)S(1)} %dynamic-slice_bitcast_fusion.7), channel_id=1, source_target_pairs={{0,4},{1,5},{2,6},{3,7},{4,0},{5,1},{6,2},{7,3},{8,12},{9,13},{10,... | collective-permute-start | bytes 884744 | tf_op jit(solution)/shard_map/ppermute | solution.py:580
  438.7 18.0 %collective-permute-start.10 = (bf16[4,24,768]{2,1,0:T(8,128)(2,1)}, bf16[4,24,768]{2,1,0:T(8,128)(2,1)S(1)}, u32[]{:S(2)}, u32[]{:S(2)}) collective-permute-start(bf16[4,24,768]{2,1,0:T(8,128)(2,1)} %get-tuple-element.492), channel_id=1, source_target_pairs={{0,8},{1,9},{2,10},{3,11},{4,12},{5,13},{6,14},{7,15},{8,0},{9,1},... | collective-permute-start | bytes 442376 | tf_op jit(solution)/shard_map/ppermute | solution.py:580
  445.9 11.3 %collective-permute-start.11 = (bf16[4,24,768]{2,1,0:T(8,128)(2,1)}, bf16[4,24,768]{2,1,0:T(8,128)(2,1)S(1)}, u32[]{:S(2)}, u32[]{:S(2)}) collective-permute-start(bf16[4,24,768]{2,1,0:T(8,128)(2,1)} %get-tuple-element.494), channel_id=1, source_target_pairs={{0,16},{1,17},{2,18},{3,19},{4,20},{5,21},{6,22},{7,23},{8,24},{9,... | collective-permute-start | bytes 442376 | tf_op jit(solution)/shard_map/ppermute | solution.py:580
  446.3 11.7 %collective-permute-start.12 = (bf16[4,24,768]{2,1,0:T(8,128)(2,1)}, bf16[4,24,768]{2,1,0:T(8,128)(2,1)}, u32[]{:S(2)}, u32[]{:S(2)}) collective-permute-start(bf16[4,24,768]{2,1,0:T(8,128)(2,1)} %get-tuple-element.493), channel_id=1, source_target_pairs={{0,24},{1,25},{2,26},{3,27},{4,28},{5,29},{6,30},{7,31},{8,16},{9,... | collective-permute-start | bytes 442376 | tf_op jit(solution)/shard_map/ppermute | solution.py:580
  453.5 18.2 %copy-start.28 = (f32[14,24]{1,0:T(8,128)S(1)}, f32[14,24]{1,0:T(8,128)}, u32[]{:S(2)}) copy-start(f32[14,24]{1,0:T(8,128)} %param.39) | copy-start | bytes 4036
  453.5 18.3 %copy-start.29 = (f32[14,24]{1,0:T(8,128)S(1)}, f32[14,24]{1,0:T(8,128)}, u32[]{:S(2)}) copy-start(f32[14,24]{1,0:T(8,128)} %param.46) | copy-start | bytes 4036
  453.5 18.9 %copy-start.30 = (f32[14,24]{1,0:T(8,128)S(1)}, f32[14,24]{1,0:T(8,128)}, u32[]{:S(2)}) copy-start(f32[14,24]{1,0:T(8,128)} %param.53) | copy-start | bytes 4036
  453.5 33.0 %copy-start.11 = (f32[24,3072]{1,0:T(8,128)S(1)}, f32[24,3072]{1,0:T(8,128)}, u32[]{:S(2)}) copy-start(f32[24,3072]{1,0:T(8,128)} %param.37) | copy-start | bytes 884740
  456.7 0.7 copy-start.24
  457.4 0.7 copy-start.25
  459.2 20.9 %copy-start.18 = (f32[24,768]{1,0:T(8,128)}, f32[24,768]{1,0:T(8,128)S(1)}, u32[]{:S(2)}) copy-start(f32[24,768]{1,0:T(8,128)S(1)} %get-tuple-element.499) | copy-start | bytes 221188
  459.2 20.9 %copy-start.19 = (f32[24,768]{1,0:T(8,128)}, f32[24,768]{1,0:T(8,128)S(1)}, u32[]{:S(2)}) copy-start(f32[24,768]{1,0:T(8,128)S(1)} %get-tuple-element.500) | copy-start | bytes 221188
  459.2 20.9 %copy-start.20 = (f32[24,768]{1,0:T(8,128)}, f32[24,768]{1,0:T(8,128)S(1)}, u32[]{:S(2)}) copy-start(f32[24,768]{1,0:T(8,128)S(1)} %get-tuple-element.501) | copy-start | bytes 221188
  467.0 11.7 %all-to-all-start.9 = ((f32[32,1,2]{2,1,0:T(1,128)}), f32[32,1,2]{2,1,0:T(1,128)S(1)}, u32[]{:S(2)}, u32[]{:S(2)}) async-start(f32[32,1,2]{2,1,0:T(1,128)} %broadcast_in_dim.177), calls=%async_computation.9 | async-start | bytes 32768 | tf_op jit(solution)/shard_map/all_to_all | solution.py:40
  480.9 12.4 %copy-start.1 = (f32[960,768]{1,0:T(8,128)S(1)}, f32[960,768]{1,0:T(8,128)}, u32[]{:S(2)}) copy-start(f32[960,768]{1,0:T(8,128)} %param.33) | copy-start | bytes 8847364
  486.5 6.0 %copy-start.23 = (f32[512,24]{0,1:T(8,128)S(1)}, f32[512,24]{0,1:T(8,128)}, u32[]{:S(2)}) copy-start(f32[512,24]{0,1:T(8,128)} %param.34) | copy-start | bytes 147460
  486.5 6.0 %copy-start.26 = (f32[512,24]{0,1:T(8,128)S(1)}, f32[512,24]{0,1:T(8,128)}, u32[]{:S(2)}) copy-start(f32[512,24]{0,1:T(8,128)} %param.48) | copy-start | bytes 147460
  486.5 6.0 %copy-start.27 = (f32[512,24]{0,1:T(8,128)S(1)}, f32[512,24]{0,1:T(8,128)}, u32[]{:S(2)}) copy-start(f32[512,24]{0,1:T(8,128)} %param.41) | copy-start | bytes 147460
  493.2 8.0 %copy-start.12 = (f32[96,768]{1,0:T(8,128)S(1)}, f32[96,768]{1,0:T(8,128)}, u32[]{:S(2)}) copy-start(f32[96,768]{1,0:T(8,128)} %param.38) | copy-start | bytes 884740
  493.2 8.0 %copy-start.13 = (f32[4,24,768]{2,1,0:T(8,128)S(1)}, f32[4,24,768]{2,1,0:T(8,128)}, u32[]{:S(2)}) copy-start(f32[4,24,768]{2,1,0:T(8,128)} %slice_multiply_fusion) | copy-start | bytes 884740
  493.2 8.0 %copy-start.21 = (f32[96,768]{1,0:T(8,128)S(1)}, f32[96,768]{1,0:T(8,128)}, u32[]{:S(2)}) copy-start(f32[96,768]{1,0:T(8,128)} %param.52) | copy-start | bytes 884740
  493.2 8.0 %copy-start.22 = (f32[96,768]{1,0:T(8,128)S(1)}, f32[96,768]{1,0:T(8,128)}, u32[]{:S(2)}) copy-start(f32[96,768]{1,0:T(8,128)} %param.45) | copy-start | bytes 884740
Sparse Core Ops, SparseCore 0:
  13.9 140.7 all-gather.1

commit v5 on v4

--- a/solution.py
+++ b/solution.py
@@ -131,13 +131,23 @@
     return pl.BlockSpec(shape, lambda *_: index, pipeline_mode=pl.Buffered(1))
 
 
-def spread_kernel(depth, turns, width, src, out):
-    tall = src[...].astype(f32)
-    parts = []
-    for e in range(2):
-        for j in range(turns):
-            parts.append(tall[e * depth : (e + 1) * depth, j * width : (j + 1) * width])
-    out[...] = jnp.concatenate(parts, axis=0).astype(bf)
+def spread(depth, turns, src, out):
+    width = out.shape[1]
+    if depth % 8:
+        out[...] = src[...]
+        return
+
+    def pair(index, carry):
+        tall = src[pl.ds(pl.multiple_of(index * 2 * depth, 16), 2 * depth), :].astype(f32)
+        parts = []
+        for e in range(2):
+            for j in range(turns):
+                parts.append(tall[e * depth : (e + 1) * depth, j * width : (j + 1) * width])
+        to = pl.multiple_of(index * 2 * depth * turns, 16)
+        out[pl.ds(to, 2 * depth * turns), :] = jnp.concatenate(parts, axis=0).astype(bf)
+        return carry
+
+    lax.fori_loop(0, src.shape[0] // (2 * depth), pair, 0)
 
 
 def live_rows(plan, shape):
@@ -237,8 +247,9 @@
     each_sentence(plan, run)
 
 
-def middle_kernel(plan, x, mixed, w_out, w_in, w_back, vec, vec_ff, z1_out, h1_out, act_out, slope_out, z2_out, pooled):
+def middle_kernel(depth, turns, plan, x, mixed, w_out, w_in, w_src, vec, vec_ff, z1_out, h1_out, act_out, slope_out, z2_out, pooled, w_back):
     rows, width = x.shape
+    pl.when(pl.program_id(0) == 0)(lambda: spread(depth, turns, w_src, w_back))
     unit, _ = normal(x[...])
     h0 = unit * vec[0:1] + vec[1:2]
     z1 = h0 + dot(mixed[...], w_out[...]) + vec[4:5]
@@ -247,7 +258,6 @@
     h1 = unit * vec[5:6] + vec[6:7]
     h1_b = h1.astype(bf)
     h1_out[...] = h1_b
-    turns = w_in.shape[1] // width
     y = None
     for j in range(turns):
         at = slice(j * width, (j + 1) * width)
@@ -272,7 +282,7 @@
     pooled[...] += jnp.where(line == 0, sums[0], jnp.where(line == 1, sums[1], 0.0))
 
 
-def back_kernel(plan, facts, pooled, partner, z1, slope, z2, w_out, w_in, w_back, vec, d_y_out, d_f_out, d_r1_out, d_a_out, d_o_out, sums, sums_ff, loss):
+def back_kernel(plan, facts, holders, pooled, all_pooled, z1, slope, z2, w_out, w_in, w_back, vec, d_y_out, d_f_out, d_r1_out, d_a_out, d_o_out, sums, sums_ff, loss):
     rows, width = z1.shape
     step = pl.program_id(0)
     total = lambda a, b: jnp.sum(a * b, axis=1, keepdims=True)
@@ -280,7 +290,7 @@
     grads, losses = [], []
     for i in range(2):
         labeled, gold, size, other_size, counts = (facts[5 * i + j] for j in range(5))
-        own, other = pooled[i : i + 1] / size, partner[i : i + 1] / other_size
+        own, other = pooled[i : i + 1] / size, all_pooled[pl.ds(holders[i], 1), :] / other_size
         cross = total(own, other)
         root, other_root = lax.rsqrt(total(own, own) + EPS), lax.rsqrt(total(other, other) + EPS)
         miss = cross * root * other_root - gold
@@ -358,11 +368,14 @@
     return v.reshape(v.shape[0] // depth, depth, v.shape[1])
 
 
-def put_split(keep, send, kind, g, mine):
+def put_split(outs, kind, g, mine):
     g = g.reshape((g.shape[0] // 2, 2) + g.shape[1:])
     even, odd = g[:, 0], g[:, 1]
-    keep[:, kind] = jnp.where(mine == 0, even, odd).astype(bf)
-    send[:, kind] = jnp.where(mine == 0, odd, even).astype(bf)
+    cut = outs[0].shape[1]
+    keep, send = outs[:2] if kind < cut else outs[2:]
+    at = kind if kind < cut else kind - cut
+    keep[:, at] = jnp.where(mine == 0, even, odd).astype(bf)
+    send[:, at] = jnp.where(mine == 0, odd, even).astype(bf)
 
 
 def by_blocks(plan, run):
@@ -370,35 +383,35 @@
         pl.when(plan[3] == count)(functools.partial(run, count * ROWS))
 
 
-def dense_grads_kernel(depth, turns, plan, act, d_y, h1, d_f, mixed, d_a, keep, send):
+def dense_grads_kernel(depth, turns, plan, act, d_y, h1, d_f, mixed, d_a, *outs):
     width = d_y.shape[1]
     mine = plan[4]
 
     def run(rows):
         g = dot_tn(act[:rows], d_y[:rows])
-        g = g.reshape(2 * keep.shape[0], turns, depth, width)
+        g = g.reshape(2 * outs[0].shape[0], turns, depth, width)
         for j in range(turns):
-            put_split(keep, send, j, g[:, j], mine)
+            put_split(outs, j, g[:, j], mine)
         for j in range(turns):
-            put_split(keep, send, turns + j, blocks(dot_tn(h1[:rows], d_f[:rows, j * width : (j + 1) * width]), depth), mine)
-        put_split(keep, send, 2 * turns, blocks(dot_tn(mixed[:rows], d_a[:rows]), depth), mine)
+            put_split(outs, turns + j, blocks(dot_tn(h1[:rows], d_f[:rows, j * width : (j + 1) * width]), depth), mine)
+        put_split(outs, 2 * turns, blocks(dot_tn(mixed[:rows], d_a[:rows]), depth), mine)
 
     by_blocks(plan, run)
 
 
-def rest_grads_kernel(depth, length, plan, spot_in, hin, d_proj, d_x, sums_0, sums, sums_ff, keep, send):
+def rest_grads_kernel(depth, length, plan, spot_in, hin, d_proj, d_x, sums_0, sums, sums_ff, *outs):
     width = d_proj.shape[2]
     part = hin.shape[1]
     mine = plan[4]
 
     def run(rows):
         for i in range(3):
-            put_split(keep, send, i, blocks(dot_tn(hin[:rows], d_proj[i, :rows]), depth), mine)
+            put_split(outs, i, blocks(dot_tn(hin[:rows], d_proj[i, :rows]), depth), mine)
         line = jnp.where(spot_in[:rows] == iota((rows, length), 1), 1.0, 0.0).astype(bf)
         g_pos = dot_tn(d_x[:rows], line)
         vec = jnp.concatenate([sums_0[:4], sums[:3], sums_ff[...], sums[3:6]], axis=0)
         vec = jnp.concatenate([vec, jnp.zeros((128 - vec.shape[0], part), f32)], axis=0)
-        put_split(keep, send, 3, blocks(jnp.concatenate([g_pos, vec.T, jnp.zeros((part, width - length - 128), f32)], axis=1), depth), mine)
+        put_split(outs, 3, blocks(jnp.concatenate([g_pos, vec.T, jnp.zeros((part, width - length - 128), f32)], axis=1), depth), mine)
 
     by_blocks(plan, run)
 
@@ -431,18 +444,11 @@
             **more,
         )
 
-    if depth % 8 == 0:
-        w_back = pl.pallas_call(
-            functools.partial(spread_kernel, depth, turns, width),
-            grid=(devices // 2,),
-            in_specs=[pl.BlockSpec((2 * depth, turns * width), lambda i: (i, at_back // (turns * width)))],
-            out_specs=pl.BlockSpec((2 * depth * turns, width), lambda i: (i, 0)),
-            out_shape=shape((hidden, width), bf),
-            name="spread",
-        )(full)
-    else:
-        w_back = full[:, at_back : at_back + turns * width].reshape(devices, depth, turns, width)
-        w_back = w_back.transpose(0, 2, 1, 3).reshape(hidden, width)
+    tall = depth % 8 == 0
+    w_src, w_src_spec = full, fixed((width, turns * width), (0, at_back // (turns * width)))
+    if not tall:
+        w_src = full[:, at_back : at_back + turns * width].reshape(devices, depth, turns, width)
+        w_src, w_src_spec = w_src.transpose(0, 2, 1, 3).reshape(hidden, width), fixed((hidden, width), (0, 0))
 
     at_pos = at_back + turns * width
     at_vec = at_pos + length
@@ -469,22 +475,23 @@
     )(plan, qkv, qkv, qkv)
 
     vec_ff = vec[7 : 7 + turns].reshape(1, hidden)
-    z1, h1, act, slope, z2, pooled = call(
-        when_live(middle_kernel), 1, (BLOCKS,),
-        [row(width), row(width), w_out_spec, w_in_spec, w_back_spec, vec_spec, fixed((1, hidden), (0, 0))],
-        [row(width), row(width), row(hidden), row(hidden), row(width), whole_out(8, width)],
+    z1, h1, act, slope, z2, pooled, w_back = call(
+        when_live(functools.partial(middle_kernel, depth, turns)), 1, (BLOCKS,),
+        [row(width), row(width), w_out_spec, w_in_spec, w_src_spec, vec_spec, fixed((1, hidden), (0, 0))],
+        [row(width), row(width), row(hidden), row(hidden), row(width), whole_out(8, width), whole_out(hidden, width)],
         [
             shape((rows, width), f32), shape((rows, width), bf), shape((rows, hidden), bf), shape((rows, hidden), bf),
-            shape((rows, width), f32), shape((8, width), f32),
+            shape((rows, width), f32), shape((8, width), f32), shape((hidden, width), bf),
         ],
         "middle",
-    )(plan, x, mixed, full, full, w_back, vec, vec_ff)
-
-    partner, facts = meet(pooled)
+    )(plan, x, mixed, full, full, w_src, vec, vec_ff)
+
+    all_pooled = exchange(jnp.broadcast_to(pooled[None, :2], (devices, 2, width))).reshape(2 * devices, width)
+    holders, facts = meet
     d_y, d_f, d_r1, d_a, d_o, sums, sums_ff, loss = call(
-        when_live(back_kernel), 2, (BLOCKS,),
+        when_live(back_kernel), 3, (BLOCKS,),
         [
-            fixed((8, width), (0, 0)), fixed((2, width), (0, 0)), row(width), row(hidden), row(width), w_out_spec, w_in_spec,
+            fixed((8, width), (0, 0)), fixed((2 * devices, width), (0, 0)), row(width), row(hidden), row(width), w_out_spec, w_in_spec,
             w_back_spec, vec_spec,
         ],
         [
@@ -496,24 +503,23 @@
             shape((8, width), f32), shape((turns, width), f32), shape((8, 128), f32),
         ],
         "back",
-    )(plan, facts, pooled, partner, z1, slope, z2, full, full, w_back, vec)
-
-    tall = depth % 8 == 0
+    )(plan, facts, holders, pooled, all_pooled, z1, slope, z2, full, full, w_back, vec)
+
     half = devices // 2
     part = width // 2
+    quarter = lambda kinds: pl.BlockSpec((half // 2, kinds, depth, width), lambda i, *_: (i, 0, 0, 0))
     halves = lambda cols: pl.BlockSpec((rows, cols), lambda i, *_: (0, i))
     live = (jnp.arange(rows) < plan[3] * ROWS)[:, None]
     clean = lambda v: jnp.where(live, v, 0)
     if tall:
-        quarter = pl.BlockSpec((half // 2, 2 * turns + 1, depth, width), lambda i, *_: (i, 0, 0, 0))
         dense = call(
             functools.partial(dense_grads_kernel, depth, turns), 1, (2,),
             [
                 halves(hidden // 2), fixed((rows, width), (0, 0)), halves(part), fixed((rows, hidden), (0, 0)), halves(part),
                 fixed((rows, width), (0, 0)),
             ],
-            [quarter, quarter],
-            [shape((half, 2 * turns + 1, depth, width), bf)] * 2,
+            [quarter(turns)] * 2 + [quarter(turns + 1)] * 2,
+            [shape((half, turns, depth, width), bf)] * 2 + [shape((half, turns + 1, depth, width), bf)] * 2,
             "dense_grads",
         )(plan, act, d_y, h1, d_f, mixed, d_a)
     else:
@@ -558,13 +564,12 @@
     if staged:
         d_xb, dense = lax.optimization_barrier((d_xb, dense))
     if tall:
-        quarter = pl.BlockSpec((half // 2, 4, depth, width), lambda i, *_: (i, 0, 0, 0))
         cols = lambda count: pl.BlockSpec((count, part), lambda i, *_: (0, i))
         rest = call(
             functools.partial(rest_grads_kernel, depth, length), 1, (2,),
             [fixed((rows, 1), (0, 0)), halves(part), fixed((3, rows, width), (0, 0, 0)), halves(part), cols(8), cols(8), cols(turns)],
-            [quarter, quarter],
-            [shape((half, 4, depth, width), bf)] * 2,
+            [quarter(2)] * 4,
+            [shape((half, 2, depth, width), bf)] * 4,
             "rest_grads",
         )(plan, spots[:, None], hin, d_proj, d_xb, sums_0, sums, sums_ff)
     else:
@@ -593,32 +598,37 @@
     return row // 2, lax.rem(row, 2), lax.axis_index("seq") // 2
 
 
-def over_cores(keep, send):
+def over_cores(keep_one, send_one, keep_two, send_two):
     view = lambda v: v.reshape((4, 2, 2) + v.shape[1:])
-    keep, send = view(keep), view(send)
-    cut = keep.shape[3] // 2
-    one = add(keep[:, :, :, :cut], swap(send[:, :, :, :cut], 1, 32))
-    two = add(keep[:, :, :, cut:], swap(send[:, :, :, cut:], 1, 32))
-    return one, two
+    return (view(keep_one), swap(view(send_one), 1, 32)), (view(keep_two), swap(view(send_two), 1, 32))
+
+
+def part_sum(pair, axis, index):
+    return add(spot(pair[0], axis, index), spot(pair[1], axis, index))
+
+
+def halve(pair, axis, index, bit):
+    return part_sum(pair, axis, index), swap(part_sum(pair, axis, 1 - index), bit, 32)
 
 
 def over_wide(one, two):
     _, y, x = place_in_slice()
-    return add(spot(one, 2, x), swap(spot(one, 2, 1 - x), 2, 32)), add(spot(two, 1, y), swap(spot(two, 1, 1 - y), 4, 32))
+    return halve(one, 2, x, 2), halve(two, 1, y, 4)
 
 
 def over_other(one, two):
     _, y, x = place_in_slice()
-    return add(spot(one, 1, y), swap(spot(one, 1, 1 - y), 4, 32)), add(spot(two, 1, x), swap(spot(two, 1, 1 - x), 2, 32))
+    return halve(one, 1, y, 4), halve(two, 1, x, 2)
 
 
 def over_long(one, two):
     z, _, _ = place_in_slice()
-    both = jnp.concatenate([one, two], axis=1)
-    total = spot(both, 0, z).astype(f32)
-    for step in range(1, 4):
-        total = total + swap(spot(both, 0, z ^ step), 8 * step, 32).astype(f32)
-    return total
+    part = lambda step: jnp.concatenate([part_sum(one, 0, z ^ step), part_sum(two, 0, z ^ step)], axis=0)
+    return [part(0)] + [swap(part(step), 8 * step, 32) for step in range(1, 4)]
+
+
+def total_of(parts):
+    return sum(p.astype(f32) for p in parts)
 
 
 def body(
@@ -704,22 +714,17 @@
 
     _, extra = lax.while_loop(lambda state: state[0] < rounds, more, (jnp.int32(1), jnp.zeros((rows, width), bf)))
 
-    def meet(pooled):
-        goal = jnp.pad(gold[None, :], ((0, 0), (0, width - pairs_here)))
-        all_pooled = jnp.concatenate([pooled[:2], goal], axis=0)
-        all_pooled = exchange(jnp.broadcast_to(all_pooled[None], (devices, 3, width)))
-        vectors_of, facts = [], []
-        for i in chosen:
-            other = i ^ 1
-            rank = take(order, other)
-            holder = jnp.where(rank < devices, rank, 2 * devices - 1 - rank)
-            vectors_of.append(lax.dynamic_slice(all_pooled, (holder, (rank >= devices).astype(jnp.int32), 0), (1, 1, width))[0])
-            pair = i // 2
-            goal = lax.dynamic_slice(all_pooled, (pair // pairs_here * seq, 2, lax.rem(pair, pairs_here)), (1, 1, 1))[0, 0, 0]
-            weight = take(lab, pair).astype(f32)
-            own = jnp.where(lax.rem(i, 2) == 0, weight, 0.0)
-            facts += [weight, goal, take(lens, i).astype(f32), take(lens, other).astype(f32), own]
-        return jnp.concatenate(vectors_of, axis=0), jnp.stack(facts + [count])
+    all_gold = exchange(jnp.broadcast_to(gold[None], (devices, pairs_here))).reshape(devices // seq, seq, pairs_here)[:, 0]
+    all_gold = all_gold.reshape(devices)
+    holders, facts = [], []
+    for i in chosen:
+        other, pair = i ^ 1, i // 2
+        rank = take(order, other)
+        holders.append(jnp.where(rank < devices, 2 * rank, 2 * (2 * devices - 1 - rank) + 1))
+        weight = take(lab, pair).astype(f32)
+        own = jnp.where(lax.rem(i, 2) == 0, weight, 0.0)
+        facts += [weight, take(all_gold, pair), take(lens, i).astype(f32), take(lens, other).astype(f32), own]
+    meet = jnp.stack(holders), jnp.stack(facts + [count])
 
     staged = (seq, devices) == (4, 32) and depth % 8 == 0
     loss, dense, rest, d_xb, give_rows = run_forward_backward(
@@ -728,17 +733,21 @@
 
     def sum_up(parts):
         if isinstance(parts, list | tuple):
-            keep, send = parts
+            keep, send = (jnp.concatenate([parts[i], parts[i + 2]], axis=1) for i in range(2))
             both = jnp.stack([jnp.where(core == 0, keep, send), jnp.where(core == 0, send, keep)], axis=1)
             parts = both.reshape((devices,) + keep.shape[1:])
         return lax.psum_scatter(parts, AXES, scatter_dimension=0, tiled=True).astype(f32)[0]
 
     give_rows = exchange(give_rows.reshape(devices, room, width))
     if staged:
-        dense = over_long(*over_other(*dense))
-        rest = over_other(*over_wide(*over_cores(*rest)))
-        rest, give_rows = lax.optimization_barrier((rest, give_rows))
+        dense = over_other(*dense)
+        rest = over_wide(*over_cores(*rest))
+        dense, give_rows = lax.optimization_barrier((dense, give_rows))
+        dense = over_long(*dense)
+        rest = over_other(*rest)
+        dense, rest = lax.optimization_barrier((dense, rest))
         rest = over_long(*rest)
+        dense, rest = total_of(dense), total_of(rest)
     else:
         dense, rest = sum_up(dense), sum_up(rest)
     beside = lambda v: jnp.concatenate(list(v), axis=1)
@@ -761,7 +770,7 @@
     _, g_embed = lax.while_loop(lambda state: state[0] < rounds, more_back, (jnp.int32(1), give(wanted_first, give_rows)))
 
     grads = (g_embed, g_position, g_attn_in, g_attn_out, g_ff_in, g_ff_out, g_vectors)
-    squares = sum(jnp.sum(g * g) for g in grads)
+    squares = sum(jnp.sum(g * g) for g in (g_embed, dense, rest))
     sums = exchange(jnp.broadcast_to(jnp.stack([squares, loss])[None, :], (devices, 2)))
     sums = jnp.sum(sums, axis=0)
     norm = jnp.sqrt(sums[0])

time: 519 us -> 501 us (0.965)
  waiting for transfers between devices: 171 us -> 161 us
  Pallas kernels: 137 us -> 129 us
  other arithmetic: 66.2 us -> 73.9 us
    ppermute x18, waiting for transfers between devices: 71.1 us -> 61.9 us  [swap(): return lax.ppermute(v, AXES, [(i, i ^ bit) for i in range(devices)])]
    pallas_call x3 -> x2, Pallas kernels: 52.7 us -> 44.1 us  [the longest x1 24.3 us: run_forward_backward(): call(when_live(functools.partial(middle_kernel, depth, turns)), 1, (BLOCK...]
    slice x4 -> x2, local copies, waits for them, and re-layouts: 7.99 us -> 0.75 us  [the longest x1 0.74 us: run_forward_backward(): pooled[None, :2]]
    reshape x0 -> x3, local copies, waits for them, and re-layouts: none -> 6.17 us  [the longest x2 5.36 us: over_cores(): view = lambda v: v.reshape((4, 2, 2) + v.shape[1:])]
    all_to_all x6 -> x7, starting transfers between devices: 25.8 us -> 31.3 us  [exchange(): return lax.all_to_all(v, AXES, 0, 0, tiled=True)]
    convert_element_type x11, other arithmetic: 16.4 us -> 21.9 us  [add(): return (a.astype(f32) + b.astype(f32)).astype(bf)]
    ppermute x18, starting transfers between devices: 24.5 us -> 19.3 us  [swap(): return lax.ppermute(v, AXES, [(i, i ^ bit) for i in range(devices)])]
    all_to_all x6 -> x7, waiting for transfers between devices: 92.1 us -> 95.8 us  [exchange(): return lax.all_to_all(v, AXES, 0, 0, tiled=True)]
  transfers between devices with their start and end apart: 25 -> 26, of which waited for: 14 -> 12; matrix products, arithmetic and copies ran while one was open for 12% -> 15% of each run, Pallas kernels for 8% -> 4%
where the time goes in v5:
time: 501 us; the launch traced here: 494 us
  waiting for transfers between devices  161 us (32%)
  Pallas kernels  129 us (26%)
  other arithmetic  73.9 us (15%)
  starting transfers between devices  50.6 us (10%)
  between operations  38.2 us (8%)
  local copies, waits for them, and re-layouts  31.5 us (6%)
  matrix products  9.75 us (2%)
    all_to_all x7, waiting for transfers between devices, exchange(): return lax.all_to_all(v, AXES, 0, 0, tiled=True)  95.8 us
    ppermute x18, waiting for transfers between devices, swap(): return lax.ppermute(v, AXES, [(i, i ^ bit) for i in range(devices)])  61.9 us
    all_to_all x7, starting transfers between devices, exchange(): return lax.all_to_all(v, AXES, 0, 0, tiled=True)  31.3 us
    pallas_call x1, Pallas kernels, run_forward_backward(): call(when_live(functools.partial(middle_kernel, depth, turns)), 1, (BLOCK...  24.3 us
    convert_element_type x11, other arithmetic, add(): return (a.astype(f32) + b.astype(f32)).astype(bf)  21.9 us
    pallas_call x2, Pallas kernels, attend_back(): call(attend_back_kernel, 1, (count,), [block(0, start), block(1, start),...  21.6 us
    pallas_call x1, Pallas kernels, run_forward_backward(): call(when_live(back_kernel), 3, (BLOCKS,), [fixed((8, width), (0, 0)), fi...  19.8 us
    ppermute x18, starting transfers between devices, swap(): return lax.ppermute(v, AXES, [(i, i ^ bit) for i in range(devices)])  19.3 us
  transfers between devices with their start and end apart: 26, of which 12 were waited for; matrix products, arithmetic and copies ran while one was open for 15% of the time, Pallas kernels for 4%

profile of v5, /device:TPU:0, one launch (start us, length us, event | category | flops | bytes accessed | tf_op | source)
XLA Modules:
  0.0 494.2 jit_solution(7795629602434140624)
XLA Ops:
  14.8 7.3 %all-to-all-start.4 = ((s32[32,9,128]{2,1,0:T(8,128)}), s32[32,9,128]{2,1,0:T(8,128)S(1)}, u32[]{:S(2)}, u32[]{:S(2)}) async-start(s32[32,9,128]{2,1,0:T(8,128)} %broadcast_in_dim.169), calls=%async_computation.4 | async-start | bytes 524288 | tf_op jit(solution)/shard_map/all_to_all | solution.py:40
  22.2 12.6 %all-to-all-done.4 = s32[32,9,128]{2,1,0:T(8,128)S(1)} async-done(((s32[32,9,128]{2,1,0:T(8,128)}), s32[32,9,128]{2,1,0:T(8,128)S(1)}, u32[]{:S(2)}, u32[]{:S(2)}) %all-to-all-start.4) | async-done | bytes 147488 | tf_op jit(solution)/shard_map/all_to_all | solution.py:40
  40.3 2.0 fusion.88
  48.8 1.7 convert_reduce_fusion
  53.8 4.2 all-to-all-start.5
  59.3 5.9 %all-to-all-done.5 = s32[32,1,128]{2,1,0:T(1,128)S(1)} async-done(((s32[32,1,128]{2,1,0:T(1,128)}), s32[32,1,128]{2,1,0:T(1,128)S(1)}, u32[]{:S(2)}, u32[]{:S(2)}) %all-to-all-start.5) | async-done | bytes 16416 | tf_op jit(solution)/shard_map/all_to_all | solution.py:40
  65.4 4.5 fusion.32
  70.5 2.5 all-to-all-start.7
  74.4 5.7 %all-to-all-done.7 = f32[32,1,4]{2,1,0:T(1,128)S(1)} async-done(((f32[32,1,4]{2,1,0:T(1,128)}), f32[32,1,4]{2,1,0:T(1,128)S(1)}, u32[]{:S(2)}, u32[]{:S(2)}) %all-to-all-start.7) | async-done | bytes 544 | tf_op jit(solution)/shard_map/all_to_all | solution.py:40
  80.4 2.7 all-to-all-start.6
  86.3 1.9 stack.74.refs_0_.plan
  88.2 1.6 select_select_fusion.refs_2_.spot_in
  89.8 65.1 %all-to-all-done.6 = bf16[32,32,768]{2,1,0:T(8,128)(2,1)S(1)} async-done(((bf16[32,32,768]{2,1,0:T(8,128)(2,1)}), bf16[32,32,768]{2,1,0:T(8,128)(2,1)S(1)}, u32[]{:S(2)}, u32[]{:S(2)}) %all-to-all-start.6) | async-done | bytes 1572896 | tf_op jit(solution)/shard_map/all_to_all | solution.py:40
  155.0 3.2 all-gather.2.cloned.1.call-done.refs_5_.refs_6_.refs_7_.refs_3_.refs_4_.refs_8_.refs_9_
  158.2 10.4 %first.1 = (f32[1152,768]{1,0:T(8,128)}, bf16[1152,768]{1,0:T(8,128)(2,1)}, bf16[1152,2304]{1,0:T(8,128)(2,1)}, f32[16,768]{1,0:T(8,128)}) custom-call(s32[5]{0:T(128)} %stack.74.refs_0_.plan, s32[1152,1]{1,0:T(8,128)} %broadcast_in_dim.193.refs_1_, s32[1152,1]{1,0:T(8,128)} %select_select_fusion.refs_2_.spot_in, bf16[1024,768]{1,0:T(8,128)(2,1)} %bitcast.217, ...), custom_call_target="tpu_custom_call" | custom-call | tf_op jit(solution)/shard_map/first/pallas_call | solution.py:461
  168.6 12.6 %attend.1.refs_2_.mixed = bf16[1152,768]{1,0:T(8,128)(2,1)} custom-call(s32[5]{0:T(128)} %stack.74.refs_0_.plan, bf16[1152,2304]{1,0:T(8,128)(2,1)} %get-tuple-element.175.query.keys.values, bf16[1152,2304]{1,0:T(8,128)(2,1)} %get-tuple-element.175.query.keys.values, bf16[1152,2304]{1,0:T(8,128)(2,1)} %get-tuple-element.175.query.keys.values), custom_call_target="tpu_custom_call" | custom-call | tf_op jit(solution)/shard_map/attend/pallas_call | solution.py:473
  182.6 24.3 %middle.1 = (f32[1152,768]{1,0:T(8,128)}, bf16[1152,768]{1,0:T(8,128)(2,1)}, bf16[1152,3072]{1,0:T(8,128)(2,1)}, bf16[1152,3072]{1,0:T(8,128)(2,1)}, f32[1152,76...) custom-call(s32[5]{0:T(128)} %stack.74.refs_0_.plan, f32[1152,768]{1,0:T(8,128)} %get-tuple-element.174.refs_1_.refs_2_, ...), custom_call_target="tpu_custom_call" | custom-call | tf_op jit(solution)/shard_map/middle/pallas_call | solution.py:478
  208.4 3.2 all-to-all-start.8
  216.1 1.5 slice_reduce_fusion.1
  222.7 1.9 stack.86.refs_1_
  226.0 19.8 %back.1 = (bf16[1152,768]{1,0:T(8,128)(2,1)}, bf16[1152,3072]{1,0:T(8,128)(2,1)}, f32[1152,768]{1,0:T(8,128)}, bf16[1152,768]{1,0:T(8,128)(2,1)}, bf16[1152,768]...) custom-call(s32[5]{0:T(128)} %stack.74.refs_0_.plan, f32[11]{0:T(128)} %stack.86.refs_1_, ...), custom_call_target="tpu_custom_call" | custom-call | tf_op jit(solution)/shard_map/back/pallas_call | solution.py:491
  245.8 18.3 %dense_grads.1 = (bf16[16,4,24,768]{3,2,1,0:T(8,128)(2,1)}, bf16[16,4,24,768]{3,2,1,0:T(8,128)(2,1)}, bf16[16,5,24,768]{3,2,1,0:T(8,128)(2,1)}, bf16[16,5,24,768]{3,2,1,0:T(8,128)(2,1)}) custom-call(s32[5]{0:T(128)} %stack.74.refs_0_.plan, bf16[1152,3072]{1,0:T(8,128)(2,1)} %get-tuple-element.184.act, bf16[1152,768]{1,0:T(8,128)(2,1)} %get-tuple-element.185.d_y, ...), custom_call_target="tpu_custom_call" | custom-call | tf_op jit(solution)/shard_map/dense_grads/pallas_call | solution.py:515
  264.1 3.8 copy.189
  268.1 1.6 copy.188
  270.0 10.6 %attend_back.2.more_0_ = bf16[3,1152,768]{2,1,0:T(8,128)(2,1)} custom-call(s32[5]{0:T(128)} %stack.74.refs_0_.plan, bf16[1152,2304]{1,0:T(8,128)(2,1)} %get-tuple-element.175.query.keys.values, bf16[1152,2304]{1,0:T(8,128)(2,1)} %get-tuple-element.175.query.keys.values, bf16[1152,2304]{1,0:T(8,128)(2,1)} %get-tuple-element.175.query.keys.values, ...), custom_call_target="tpu_custom_call" | custom-call | flops 1006632960 | bytes 7077888 | tf_op jit(solution)/shard_map/attend_back/pallas_call | solution.py:537
  280.6 10.9 %attend_back.3.refs_4_.d_proj = bf16[3,1152,768]{2,1,0:T(8,128)(2,1)} custom-call(s32[5]{0:T(128)} %stack.74.refs_0_.plan, bf16[1152,2304]{1,0:T(8,128)(2,1)} %get-tuple-element.175.query.keys.values, bf16[1152,2304]{1,0:T(8,128)(2,1)} %get-tuple-element.175.query.keys.values, ...), custom_call_target="tpu_custom_call", output_to_operand_aliasing={{}: (5, {})} | custom-call | flops 1006632960 | bytes 7077888 | tf_op jit(solution)/shard_map/attend_back/pallas_call | solution.py:537
  291.5 12.0 %last.1 = (bf16[1152,768]{1,0:T(8,128)(2,1)}, f32[8,768]{1,0:T(8,128)}, bf16[1024,768]{1,0:T(8,128)(2,1)}) custom-call(s32[5]{0:T(128)} %stack.74.refs_0_.plan, s32[1152,1]{1,0:T(8,128)} %broadcast_in_dim.193.refs_1_, f32[1152,768]{1,0:T(8,128)} %get-tuple-element.174.refs_1_.refs_2_, f32[1152,768]{1,0:T(8,128)} %get-tuple-element.182.refs_3_, ...), custom_call_target="tpu_custom_call" | custom-call | tf_op jit(solution)/shard_map/last/pallas_call | solution.py:553
  303.6 7.9 %all-to-all-start.9 = ((bf16[32,32,768]{2,1,0:T(8,128)(2,1)}), bf16[32,32,768]{2,1,0:T(8,128)(2,1)}, u32[]{:S(2)}, u32[]{:S(2)}) async-start(bf16[32,32,768]{2,1,0:T(8,128)(2,1)} %bitcast.222), calls=%async_computation.9 | async-start | bytes 3145728 | tf_op jit(solution)/shard_map/all_to_all | solution.py:40
  311.5 3.6 fusion.34
  315.1 1.8 collective-permute-start.3
  316.9 2.4 fusion.36
  319.2 1.5 collective-permute-start.2
  320.8 36.1 %collective-permute-done.2 = bf16[4,2,4,24,768]{4,3,2,0,1:T(8,128)(2,1)S(1)} collective-permute-done((bf16[4,2,4,24,768]{4,3,2,0,1:T(8,128)(2,1)S(1)}, bf16[4,2,4,24,768]{4,3,2,0,1:T(8,128)(2,1)S(1)}, u32[]{:S(2)}, u32[]{:S(2)}) %collective-permute-start.2) | collective-permute-done | bytes 1179680 | tf_op jit(solution)/shard_map/ppermute | solution.py:585
  356.9 5.9 %collective-permute-done.3 = bf16[4,2,5,24,768]{4,3,2,0,1:T(8,128)(2,1)S(1)} collective-permute-done((bf16[4,2,5,24,768]{4,3,2,0,1:T(8,128)(2,1)S(1)}, bf16[4,2,5,24,768]{4,3,2,0,1:T(8,128)(2,1)S(1)}, u32[]{:S(2)}, u32[]{:S(2)}) %collective-permute-start.3) | collective-permute-done | bytes 1474592 | tf_op jit(solution)/shard_map/ppermute | solution.py:585
  363.8 10.1 %rest_grads.1 = (bf16[16,2,24,768]{3,2,1,0:T(8,128)(2,1)}, bf16[16,2,24,768]{3,2,1,0:T(8,128)(2,1)}, bf16[16,2,24,768]{3,2,1,0:T(8,128)(2,1)}, bf16[16,2,24,768]{3,2,1,0:T(8,128)(2,1)}) custom-call(s32[5]{0:T(128)} %stack.74.refs_0_.plan, s32[1152,1]{1,0:T(8,128)} %select_select_fusion.refs_2_.spot_in, bf16[1152,768]{1,0:T(8,128)(2,1)} %get-tuple-element.211.hin, ...), custom_call_target="tpu_custom_call" | custom-call | tf_op jit(solution)/shard_map/rest_grads/pallas_call | solution.py:568
  377.2 1.8 fusion.38
  379.0 1.5 collective-permute-start.5
  382.0 1.4 broadcast_select_fusion
  383.4 2.5 add_convert_fusion.7
  385.9 1.7 collective-permute-start.13
  387.6 2.4 add_convert_fusion.9
  390.6 7.4 %collective-permute-done.4 = bf16[4,4,24,768]{3,2,1,0:T(8,128)(2,1)} collective-permute-done((bf16[4,4,24,768]{3,2,1,0:T(8,128)(2,1)S(1)}, bf16[4,4,24,768]{3,2,1,0:T(8,128)(2,1)}, u32[]{:S(2)}, u32[]{:S(2)}) %collective-permute-start.4) | collective-permute-done | bytes 589856 | tf_op jit(solution)/shard_map/ppermute | solution.py:585
  399.7 1.4 fusion.57
  401.9 3.3 collective-permute-start.8
  408.6 5.2 %fusion.28 = f32[960,768]{1,0:T(8,128)} fusion(bf16[1024,768]{1,0:T(8,128)(2,1)} %bitcast.44, s32[1024]{0:T(1024)S(1)} %copy-done.40), kind=kOutput, calls=%fused_computation.52 | convolution fusion | flops 1510932480 | bytes 4526080 | tf_op jit(solution)/shard_map/dot_general | solution.py:32
  414.7 2.1 fusion.51
  416.8 1.5 collective-permute-start.14
  418.3 2.0 fusion.49
  420.9 3.3 multiply_reduce_fusion
  424.2 8.6 %collective-permute-done.7 = bf16[9,24,768]{2,1,0:T(8,128)(2,1)} collective-permute-done((bf16[9,24,768]{2,1,0:T(8,128)(2,1)}, bf16[9,24,768]{2,1,0:T(8,128)(2,1)}, u32[]{:S(2)}, u32[]{:S(2)}) %collective-permute-start.7) | collective-permute-done | bytes 331808 | tf_op jit(solution)/shard_map/ppermute | solution.py:585
  434.2 2.8 collective-permute-start.16
  437.0 1.7 collective-permute-start.17
  438.7 2.8 multiply_reduce_fusion.1
  442.8 1.8 slice_bitcast_fusion.3
  444.7 3.4 collective-permute-done.16
  448.1 1.8 multiply_reduce_fusion.2
  451.8 3.3 all-to-all-start.10
  455.9 6.4 %all-to-all-done.10 = f32[32,1,2]{2,1,0:T(1,128)S(1)} async-done(((f32[32,1,2]{2,1,0:T(1,128)}), f32[32,1,2]{2,1,0:T(1,128)S(1)}, u32[]{:S(2)}, u32[]{:S(2)}) %all-to-all-start.10) | async-done | bytes 288 | tf_op jit(solution)/shard_map/all_to_all | solution.py:40
  465.9 1.4 copy.203
  467.3 1.4 copy.204
  468.7 1.4 copy.205
  470.1 1.7 add_multiply_fusion.4
  471.8 1.5 add_multiply_fusion.5
  473.3 7.9 %add_multiply_fusion = (f32[960,768]{1,0:T(8,128)}, f32[960,768]{1,0:T(8,128)}, f32[960,768]{1,0:T(8,128)}) fusion(f32[960,768]{1,0:T(8,128)} %param.47, f32[960,768]{1,0:T(8,128)S(1)} %copy-done.1, f32[960,768]{1,0:T(8,128)} %get-tuple-element.206, f32[]{:T(128)S(6)} %min.8, f32[960,768]{1,0:T(8,128)} %param.40), kind=kLoop, calls=%fused_computation.54 | loop fusion | flops 6635520 | bytes 20643844 | tf_op jit(solution)/shard_map/add | solution.py:789
  (201 shorter events, 49.5 us)
Async XLA Ops:
  7.2 6.6 %copy-start.41 = (s32[4,2]{0,1:T(2,128)S(1)}, s32[4,2]{0,1:T(2,128)}, u32[]{:S(2)}) copy-start(s32[4,2]{0,1:T(2,128)} %param.30) | copy-start | bytes 100
  7.2 6.8 %copy-start.43 = (s32[4]{0:T(128)S(1)}, s32[4]{0:T(128)}, u32[]{:S(2)}) copy-start(s32[4]{0:T(128)} %param.31) | copy-start | bytes 52
  7.2 6.8 %copy-start.38 = (s32[4,2,128]{2,1,0:T(2,128)S(1)}, s32[4,2,128]{2,1,0:T(2,128)}, u32[]{:S(2)}) copy-start(s32[4,2,128]{2,1,0:T(2,128)} %param.29) | copy-start | bytes 12292
  7.2 150.9 %all-gather.2.cloned.1.call-start = ((), (), s32[]{:S(2)}) async-start(), calls=%async_computation.11 | async-start | bytes 15611904 | tf_op jit(solution)/shard_map/all_gather | solution.py:659
  10.2 47.9 %copy-start = (f32[960,768]{1,0:T(8,128)S(1)}, f32[960,768]{1,0:T(8,128)}, u32[]{:S(2)}) copy-start(f32[960,768]{1,0:T(8,128)} %param.33) | copy-start | bytes 8847364
  14.8 20.0 %all-to-all-start.4 = ((s32[32,9,128]{2,1,0:T(8,128)}), s32[32,9,128]{2,1,0:T(8,128)S(1)}, u32[]{:S(2)}, u32[]{:S(2)}) async-start(s32[32,9,128]{2,1,0:T(8,128)} %broadcast_in_dim.169), calls=%async_computation.4 | async-start | bytes 524288 | tf_op jit(solution)/shard_map/all_to_all | solution.py:40
  34.8 13.9 %copy-start.34 = (s32[32,9,128]{2,0,1:T(8,128)}, s32[32,9,128]{2,0,1:T(8,128)S(1)}, u32[]{:S(2)}) copy-start(s32[32,9,128]{2,0,1:T(8,128)S(1)} %copy.182) | copy-start | bytes 442372
  53.8 11.4 %all-to-all-start.5 = ((s32[32,1,128]{2,1,0:T(1,128)}), s32[32,1,128]{2,1,0:T(1,128)S(1)}, u32[]{:S(2)}, u32[]{:S(2)}) async-start(s32[32,1,128]{2,1,0:T(1,128)} %bitcast.6), calls=%async_computation.5 | async-start | bytes 32768 | tf_op jit(solution)/shard_map/all_to_all | solution.py:40
  65.4 4.5 copy-start.39
  65.4 4.5 copy-start.42
  70.5 9.6 %all-to-all-start.7 = ((f32[32,1,4]{2,1,0:T(1,128)}), f32[32,1,4]{2,1,0:T(1,128)S(1)}, u32[]{:S(2)}, u32[]{:S(2)}) async-start(f32[32,1,4]{2,1,0:T(1,128)} %broadcast_in_dim.182), calls=%async_computation.7 | async-start | bytes 32768 | tf_op jit(solution)/shard_map/all_to_all | solution.py:40
  80.4 74.5 %all-to-all-start.6 = ((bf16[32,32,768]{2,1,0:T(8,128)(2,1)}), bf16[32,32,768]{2,1,0:T(8,128)(2,1)S(1)}, u32[]{:S(2)}, u32[]{:S(2)}) async-start(bf16[32,32,768]{2,1,0:T(8,128)(2,1)} %bitcast.223), calls=%async_computation.6 | async-start | bytes 3145728 | tf_op jit(solution)/shard_map/all_to_all | solution.py:40
  155.0 3.2 copy-start.3
  208.4 16.8 %all-to-all-start.8 = ((f32[32,2,768]{2,1,0:T(2,128)}), f32[32,2,768]{2,1,0:T(2,128)S(1)}, u32[]{:S(2)}, u32[]{:S(2)}) async-start(f32[32,2,768]{2,1,0:T(2,128)} %broadcast_in_dim.184), calls=%async_computation.8 | async-start | bytes 393216 | tf_op jit(solution)/shard_map/all_to_all | solution.py:40
  264.1 4.0 copy-start.5
  267.9 12.7 %collective-permute-start.1 = (bf16[4,2,2,5,24,768]{5,4,3,0,2,1:T(8,128)(2,1)}, bf16[4,2,2,5,24,768]{5,4,3,0,2,1:T(8,128)(2,1)S(1)}, u32[]{:S(2)}, u32[]{:S(2)}) collective-permute-start(bf16[4,2,2,5,24,768]{5,4,3,0,2,1:T(8,128)(2,1)} %copy.189), channel_id=1, source_target_pairs={{0,1},{1,0},{2,3},{3,2},{4,5},{5,4},{6,7},{7,6},{8,9},{9,8},{10,11... | collective-permute-start | bytes 8847368 | tf_op jit(solution)/shard_map/ppermute | solution.py:585
  269.7 10.9 %collective-permute-start = (bf16[4,2,2,4,24,768]{5,4,3,0,1,2:T(8,128)(2,1)}, bf16[4,2,2,4,24,768]{5,4,3,0,1,2:T(8,128)(2,1)}, u32[]{:S(2)}, u32[]{:S(2)}) collective-permute-start(bf16[4,2,2,4,24,768]{5,4,3,0,1,2:T(8,128)(2,1)} %copy.188), channel_id=1, source_target_pairs={{0,1},{1,0},{2,3},{3,2},{4,5},{5,4},{6,7},{7,6},{8,9},{9,8},{10,11... | collective-permute-start | bytes 7077896 | tf_op jit(solution)/shard_map/ppermute | solution.py:585
  280.6 10.9 %copy-start.4 = (bf16[4,2,2,5,24,768]{5,4,3,0,2,1:T(8,128)(2,1)}, bf16[4,2,2,5,24,768]{5,4,3,0,2,1:T(8,128)(2,1)S(1)}, u32[]{:S(2)}) copy-start(bf16[4,2,2,5,24,768]{5,4,3,0,2,1:T(8,128)(2,1)S(1)} %collective-permute-done.1) | copy-start | bytes 8847364
  303.6 94.9 %all-to-all-start.9 = ((bf16[32,32,768]{2,1,0:T(8,128)(2,1)}), bf16[32,32,768]{2,1,0:T(8,128)(2,1)}, u32[]{:S(2)}, u32[]{:S(2)}) async-start(bf16[32,32,768]{2,1,0:T(8,128)(2,1)} %bitcast.222), calls=%async_computation.9 | async-start | bytes 3145728 | tf_op jit(solution)/shard_map/all_to_all | solution.py:40
  311.5 5.4 %copy-start.6 = (bf16[16,4,24,768]{3,2,1,0:T(8,128)(2,1)S(1)}, bf16[16,4,24,768]{3,2,1,0:T(8,128)(2,1)}, u32[]{:S(2)}) copy-start(bf16[16,4,24,768]{3,2,1,0:T(8,128)(2,1)} %get-tuple-element.189) | copy-start | bytes 7077892
  315.1 47.6 %collective-permute-start.3 = (bf16[4,2,5,24,768]{4,3,2,0,1:T(8,128)(2,1)S(1)}, bf16[4,2,5,24,768]{4,3,2,0,1:T(8,128)(2,1)S(1)}, u32[]{:S(2)}, u32[]{:S(2)}) collective-permute-start(bf16[4,2,5,24,768]{4,3,2,0,1:T(8,128)(2,1)S(1)} %get-tuple-element.523), channel_id=1, source_target_pairs={{0,4},{1,5},{2,6},{3,7},{4,0},{5,1},{6,2},{7,3},{8,12},{9,13},{10,... | collective-permute-start | bytes 4423688 | tf_op jit(solution)/shard_map/ppermute | solution.py:585
  319.2 37.6 %collective-permute-start.2 = (bf16[4,2,4,24,768]{4,3,2,0,1:T(8,128)(2,1)S(1)}, bf16[4,2,4,24,768]{4,3,2,0,1:T(8,128)(2,1)S(1)}, u32[]{:S(2)}, u32[]{:S(2)}) collective-permute-start(bf16[4,2,4,24,768]{4,3,2,0,1:T(8,128)(2,1)S(1)} %get-tuple-element.525), channel_id=1, source_target_pairs={{0,2},{1,3},{2,0},{3,1},{4,6},{5,7},{6,4},{7,5},{8,10},{9,11},{10,... | collective-permute-start | bytes 3538952 | tf_op jit(solution)/shard_map/ppermute | solution.py:585
  356.9 7.0 %copy-start.15 = (bf16[4,2,4,24,768]{4,3,2,0,1:T(8,128)(2,1)}, bf16[4,2,4,24,768]{4,3,2,0,1:T(8,128)(2,1)S(1)}, u32[]{:S(2)}) copy-start(bf16[4,2,4,24,768]{4,3,2,0,1:T(8,128)(2,1)S(1)} %collective-permute-done.2) | copy-start | bytes 3538948
  363.8 10.7 %copy-start.35 = (f32[14,24]{1,0:T(8,128)S(1)}, f32[14,24]{1,0:T(8,128)}, u32[]{:S(2)}) copy-start(f32[14,24]{1,0:T(8,128)} %param.39) | copy-start | bytes 4036
  363.8 10.8 %copy-start.36 = (f32[14,24]{1,0:T(8,128)S(1)}, f32[14,24]{1,0:T(8,128)}, u32[]{:S(2)}) copy-start(f32[14,24]{1,0:T(8,128)} %param.46) | copy-start | bytes 4036
  363.8 11.4 %copy-start.37 = (f32[14,24]{1,0:T(8,128)S(1)}, f32[14,24]{1,0:T(8,128)}, u32[]{:S(2)}) copy-start(f32[14,24]{1,0:T(8,128)} %param.53) | copy-start | bytes 4036
  373.9 9.5 %collective-permute-start.12 = (bf16[4,2,2,2,24,768]{5,4,3,2,1,0:T(8,128)(2,1)}, bf16[4,2,2,2,24,768]{5,4,3,2,1,0:T(8,128)(2,1)}, u32[]{:S(2)}, u32[]{:S(2)}) collective-permute-start(bf16[4,2,2,2,24,768]{5,4,3,2,1,0:T(8,128)(2,1)} %bitcast.240), channel_id=1, source_target_pairs={{0,1},{1,0},{2,3},{3,2},{4,5},{5,4},{6,7},{7,6},{8,9},{9,8},{10,11... | collective-permute-start | bytes 3538952 | tf_op jit(solution)/shard_map/ppermute | solution.py:585
  374.0 13.5 %collective-permute-start.9 = (bf16[4,2,2,2,24,768]{5,4,3,2,1,0:T(8,128)(2,1)}, bf16[4,2,2,2,24,768]{5,4,3,2,1,0:T(8,128)(2,1)}, u32[]{:S(2)}, u32[]{:S(2)}) collective-permute-start(bf16[4,2,2,2,24,768]{5,4,3,2,1,0:T(8,128)(2,1)} %bitcast.239), channel_id=1, source_target_pairs={{0,1},{1,0},{2,3},{3,2},{4,5},{5,4},{6,7},{7,6},{8,9},{9,8},{10,11... | collective-permute-start | bytes 3538952 | tf_op jit(solution)/shard_map/ppermute | solution.py:585
  377.2 3.3 copy-start.16
  378.9 3.0 copy-start.2
  379.0 19.5 %collective-permute-start.5 = (bf16[4,5,24,768]{3,2,1,0:T(8,128)(2,1)S(1)}, bf16[4,5,24,768]{3,2,1,0:T(8,128)(2,1)}, u32[]{:S(2)}, u32[]{:S(2)}) collective-permute-start(bf16[4,5,24,768]{3,2,1,0:T(8,128)(2,1)S(1)} %get-tuple-element.527), channel_id=1, source_target_pairs={{0,2},{1,3},{2,0},{3,1},{4,6},{5,7},{6,4},{7,5},{8,10},{9,11},{10,... | collective-permute-start | bytes 2211848 | tf_op jit(solution)/shard_map/ppermute | solution.py:585
  381.6 1.8 copy-start.14
  381.6 16.3 %collective-permute-start.4 = (bf16[4,4,24,768]{3,2,1,0:T(8,128)(2,1)S(1)}, bf16[4,4,24,768]{3,2,1,0:T(8,128)(2,1)}, u32[]{:S(2)}, u32[]{:S(2)}) collective-permute-start(bf16[4,4,24,768]{3,2,1,0:T(8,128)(2,1)S(1)} %get-tuple-element.533), channel_id=1, source_target_pairs={{0,4},{1,5},{2,6},{3,7},{4,0},{5,1},{6,2},{7,3},{8,12},{9,13},{10,... | collective-permute-start | bytes 1769480 | tf_op jit(solution)/shard_map/ppermute | solution.py:585
  383.4 4.1 copy-start.13
  385.9 27.9 %collective-permute-start.13 = (bf16[4,2,2,24,768]{4,3,2,1,0:T(8,128)(2,1)}, bf16[4,2,2,24,768]{4,3,2,1,0:T(8,128)(2,1)S(1)}, u32[]{:S(2)}, u32[]{:S(2)}) collective-permute-start(bf16[4,2,2,24,768]{4,3,2,1,0:T(8,128)(2,1)} %get-tuple-element.530), channel_id=1, source_target_pairs={{0,4},{1,5},{2,6},{3,7},{4,0},{5,1},{6,2},{7,3},{8,12},{9,13},{10,... | collective-permute-start | bytes 1769480 | tf_op jit(solution)/shard_map/ppermute | solution.py:585
  387.6 10.9 %copy-start.7 = (bf16[4,4,24,768]{3,2,1,0:T(8,128)(2,1)S(1)}, bf16[4,4,24,768]{3,2,1,0:T(8,128)(2,1)}, u32[]{:S(2)}) copy-start(bf16[4,4,24,768]{3,2,1,0:T(8,128)(2,1)} %get-tuple-element.207) | copy-start | bytes 1769476
  390.0 28.2 %collective-permute-start.10 = (bf16[4,2,2,24,768]{4,3,2,1,0:T(8,128)(2,1)}, bf16[4,2,2,24,768]{4,3,2,1,0:T(8,128)(2,1)}, u32[]{:S(2)}, u32[]{:S(2)}) collective-permute-start(bf16[4,2,2,24,768]{4,3,2,1,0:T(8,128)(2,1)} %get-tuple-element.532), channel_id=1, source_target_pairs={{0,2},{1,3},{2,0},{3,1},{4,6},{5,7},{6,4},{7,5},{8,10},{9,11},{10,... | collective-permute-start | bytes 1769480 | tf_op jit(solution)/shard_map/ppermute | solution.py:585
  401.2 7.4 %copy-start.40 = (s32[1024]{0:T(1024)S(1)}, s32[1024]{0:T(1024)}, u32[]{:S(2)}) copy-start(s32[1024]{0:T(1024)} %copy-done.39) | copy-start | bytes 12292
  401.9 22.2 %collective-permute-start.8 = (bf16[9,24,768]{2,1,0:T(8,128)(2,1)}, bf16[9,24,768]{2,1,0:T(8,128)(2,1)}, u32[]{:S(2)}, u32[]{:S(2)}) collective-permute-start(bf16[9,24,768]{2,1,0:T(8,128)(2,1)} %pad_maximum_fusion.3), channel_id=1, source_target_pairs={{0,24},{1,25},{2,26},{3,27},{4,28},{5,29},{6,30},{7,31},{8,16},{9,... | collective-permute-start | bytes 995336 | tf_op jit(solution)/shard_map/ppermute | solution.py:585
  406.0 26.7 %collective-permute-start.7 = (bf16[9,24,768]{2,1,0:T(8,128)(2,1)}, bf16[9,24,768]{2,1,0:T(8,128)(2,1)}, u32[]{:S(2)}, u32[]{:S(2)}) collective-permute-start(bf16[9,24,768]{2,1,0:T(8,128)(2,1)} %pad_maximum_fusion.2), channel_id=1, source_target_pairs={{0,16},{1,17},{2,18},{3,19},{4,20},{5,21},{6,22},{7,23},{8,24},{9,... | collective-permute-start | bytes 995336 | tf_op jit(solution)/shard_map/ppermute | solution.py:585
  406.8 26.0 %collective-permute-start.6 = (bf16[9,24,768]{2,1,0:T(8,128)(2,1)}, bf16[9,24,768]{2,1,0:T(8,128)(2,1)}, u32[]{:S(2)}, u32[]{:S(2)}) collective-permute-start(bf16[9,24,768]{2,1,0:T(8,128)(2,1)} %pad_maximum_fusion.1), channel_id=1, source_target_pairs={{0,8},{1,9},{2,10},{3,11},{4,12},{5,13},{6,14},{7,15},{8,0},{9,1},... | collective-permute-start | bytes 995336 | tf_op jit(solution)/shard_map/ppermute | solution.py:585
  414.6 6.0 %copy-start.8 = (bf16[1152,768]{1,0:T(8,128)(2,1)S(1)}, bf16[1152,768]{1,0:T(8,128)(2,1)}, u32[]{:S(2)}) copy-start(bf16[1152,768]{1,0:T(8,128)(2,1)} %broadcast_select_fusion) | copy-start | bytes 5308420
  416.8 15.9 %collective-permute-start.14 = (bf16[4,2,24,768]{3,2,1,0:T(8,128)(2,1)}, bf16[4,2,24,768]{3,2,1,0:T(8,128)(2,1)}, u32[]{:S(2)}, u32[]{:S(2)}) collective-permute-start(bf16[4,2,24,768]{3,2,1,0:T(8,128)(2,1)} %get-tuple-element.539), channel_id=1, source_target_pairs={{0,2},{1,3},{2,0},{3,1},{4,6},{5,7},{6,4},{7,5},{8,10},{9,11},{10,... | collective-permute-start | bytes 884744 | tf_op jit(solution)/shard_map/ppermute | solution.py:585
  420.3 12.5 %collective-permute-start.11 = (bf16[4,2,24,768]{3,2,1,0:T(8,128)(2,1)}, bf16[4,2,24,768]{3,2,1,0:T(8,128)(2,1)}, u32[]{:S(2)}, u32[]{:S(2)}) collective-permute-start(bf16[4,2,24,768]{3,2,1,0:T(8,128)(2,1)} %get-tuple-element.541), channel_id=1, source_target_pairs={{0,4},{1,5},{2,6},{3,7},{4,0},{5,1},{6,2},{7,3},{8,12},{9,13},{10,... | collective-permute-start | bytes 884744 | tf_op jit(solution)/shard_map/ppermute | solution.py:585
  420.9 11.9 %copy-start.17 = (bf16[4,2,24,768]{3,2,1,0:T(8,128)(2,1)S(1)}, bf16[4,2,24,768]{3,2,1,0:T(8,128)(2,1)}, u32[]{:S(2)}) copy-start(bf16[4,2,24,768]{3,2,1,0:T(8,128)(2,1)} %get-tuple-element.225) | copy-start | bytes 884740
  420.9 11.9 %copy-start.18 = (bf16[4,2,24,768]{3,2,1,0:T(8,128)(2,1)S(1)}, bf16[4,2,24,768]{3,2,1,0:T(8,128)(2,1)}, u32[]{:S(2)}) copy-start(bf16[4,2,24,768]{3,2,1,0:T(8,128)(2,1)} %get-tuple-element.223) | copy-start | bytes 884740
  424.1 14.6 %copy-start.10 = (bf16[9,24,768]{2,1,0:T(8,128)(2,1)S(1)}, bf16[9,24,768]{2,1,0:T(8,128)(2,1)}, u32[]{:S(2)}) copy-start(bf16[9,24,768]{2,1,0:T(8,128)(2,1)} %pad_maximum_fusion) | copy-start | bytes 995332
  434.1 10.6 %collective-permute-start.15 = (bf16[4,24,768]{2,1,0:T(8,128)(2,1)S(1)}, bf16[4,24,768]{2,1,0:T(8,128)(2,1)}, u32[]{:S(2)}, u32[]{:S(2)}) collective-permute-start(bf16[4,24,768]{2,1,0:T(8,128)(2,1)S(1)} %pad_maximum_fusion.4), channel_id=1, source_target_pairs={{0,8},{1,9},{2,10},{3,11},{4,12},{5,13},{6,14},{7,15},{8,0},{9,1},... | collective-permute-start | bytes 442376 | tf_op jit(solution)/shard_map/ppermute | solution.py:585
  434.2 13.9 %collective-permute-start.16 = (bf16[4,24,768]{2,1,0:T(8,128)(2,1)S(1)}, bf16[4,24,768]{2,1,0:T(8,128)(2,1)}, u32[]{:S(2)}, u32[]{:S(2)}) collective-permute-start(bf16[4,24,768]{2,1,0:T(8,128)(2,1)S(1)} %pad_maximum_fusion.5), channel_id=1, source_target_pairs={{0,16},{1,17},{2,18},{3,19},{4,20},{5,21},{6,22},{7,23},{8,24},{9,... | collective-permute-start | bytes 442376 | tf_op jit(solution)/shard_map/ppermute | solution.py:585
  437.0 11.1 %collective-permute-start.17 = (bf16[4,24,768]{2,1,0:T(8,128)(2,1)S(1)}, bf16[4,24,768]{2,1,0:T(8,128)(2,1)}, u32[]{:S(2)}, u32[]{:S(2)}) collective-permute-start(bf16[4,24,768]{2,1,0:T(8,128)(2,1)S(1)} %pad_maximum_fusion.6), channel_id=1, source_target_pairs={{0,24},{1,25},{2,26},{3,27},{4,28},{5,29},{6,30},{7,31},{8,16},{9,... | collective-permute-start | bytes 442376 | tf_op jit(solution)/shard_map/ppermute | solution.py:585
  442.8 30.5 %copy-start.1 = (f32[960,768]{1,0:T(8,128)S(1)}, f32[960,768]{1,0:T(8,128)}, u32[]{:S(2)}) copy-start(f32[960,768]{1,0:T(8,128)} %param.33) | copy-start | bytes 8847364
  451.8 10.4 %all-to-all-start.10 = ((f32[32,1,2]{2,1,0:T(1,128)}), f32[32,1,2]{2,1,0:T(1,128)S(1)}, u32[]{:S(2)}, u32[]{:S(2)}) async-start(f32[32,1,2]{2,1,0:T(1,128)} %broadcast_in_dim.186), calls=%async_computation.10 | async-start | bytes 32768 | tf_op jit(solution)/shard_map/all_to_all | solution.py:40
  473.3 8.0 %copy-start.12 = (f32[96,768]{1,0:T(8,128)S(1)}, f32[96,768]{1,0:T(8,128)}, u32[]{:S(2)}) copy-start(f32[96,768]{1,0:T(8,128)} %param.38) | copy-start | bytes 884740
  473.3 8.0 %copy-start.30 = (f32[96,768]{1,0:T(8,128)S(1)}, f32[96,768]{1,0:T(8,128)}, u32[]{:S(2)}) copy-start(f32[96,768]{1,0:T(8,128)} %param.52) | copy-start | bytes 884740
  473.3 8.0 %copy-start.31 = (f32[96,768]{1,0:T(8,128)S(1)}, f32[96,768]{1,0:T(8,128)}, u32[]{:S(2)}) copy-start(f32[96,768]{1,0:T(8,128)} %param.45) | copy-start | bytes 884740
  481.3 1.3 copy-start.32
  481.3 1.5 copy-start.33
  481.3 2.4 copy-start.11
  481.3 2.4 copy-start.21
  481.4 2.4 copy-start.22
  481.4 2.4 copy-start.23
  481.4 2.4 copy-start.24
  481.4 2.4 copy-start.25
  481.4 2.4 copy-start.26
  (6 other events, 6.4 us)
Sparse Core Ops, SparseCore 0:
  13.9 144.2 all-gather.1

commit v6 on v5

--- a/solution.py
+++ b/solution.py
@@ -131,9 +131,9 @@
     return pl.BlockSpec(shape, lambda *_: index, pipeline_mode=pl.Buffered(1))
 
 
-def spread(depth, turns, src, out):
+def spread(staged, depth, turns, src, out):
     width = out.shape[1]
-    if depth % 8:
+    if not staged:
         out[...] = src[...]
         return
 
@@ -247,9 +247,9 @@
     each_sentence(plan, run)
 
 
-def middle_kernel(depth, turns, plan, x, mixed, w_out, w_in, w_src, vec, vec_ff, z1_out, h1_out, act_out, slope_out, z2_out, pooled, w_back):
+def middle_kernel(staged, depth, turns, plan, x, mixed, w_out, w_in, w_src, vec, vec_ff, z1_out, h1_out, act_out, slope_out, z2_out, pooled, w_back):
     rows, width = x.shape
-    pl.when(pl.program_id(0) == 0)(lambda: spread(depth, turns, w_src, w_back))
+    pl.when(pl.program_id(0) == 0)(lambda: spread(staged, depth, turns, w_src, w_back))
     unit, _ = normal(x[...])
     h0 = unit * vec[0:1] + vec[1:2]
     z1 = h0 + dot(mixed[...], w_out[...]) + vec[4:5]
@@ -368,14 +368,16 @@
     return v.reshape(v.shape[0] // depth, depth, v.shape[1])
 
 
-def put_split(outs, kind, g, mine):
-    g = g.reshape((g.shape[0] // 2, 2) + g.shape[1:])
-    even, odd = g[:, 0], g[:, 1]
-    cut = outs[0].shape[1]
-    keep, send = outs[:2] if kind < cut else outs[2:]
-    at = kind if kind < cut else kind - cut
-    keep[:, at] = jnp.where(mine == 0, even, odd).astype(bf)
-    send[:, at] = jnp.where(mine == 0, odd, even).astype(bf)
+def put_split(outs, order, kind, g, mine):
+    keep, send = outs
+    for z in range(2):
+        for y in range(2):
+            for x in range(2):
+                owner = 2 * (4 * z + 2 * y + x)
+                at = tuple({"z": z, "y": y, "x": x}[axis] for axis in order) + (kind,)
+                even, odd = g[owner], g[owner + 1]
+                keep[at] = jnp.where(mine == 0, even, odd).astype(bf)
+                send[at] = jnp.where(mine == 0, odd, even).astype(bf)
 
 
 def by_blocks(plan, run):
@@ -383,18 +385,27 @@
         pl.when(plan[3] == count)(functools.partial(run, count * ROWS))
 
 
-def dense_grads_kernel(depth, turns, plan, act, d_y, h1, d_f, mixed, d_a, *outs):
-    width = d_y.shape[1]
-    mine = plan[4]
-
+def out_grads_kernel(depth, turns, plan, act, d_y, *outs):
     def run(rows):
         g = dot_tn(act[:rows], d_y[:rows])
-        g = g.reshape(2 * outs[0].shape[0], turns, depth, width)
+        g = g.reshape(16, turns, depth, g.shape[1])
         for j in range(turns):
-            put_split(outs, j, g[:, j], mine)
+            put_split(outs, "zxy", j, g[:, j], plan[4])
+
+    by_blocks(plan, run)
+
+
+def in_grads_kernel(depth, turns, plan, h1, d_f, mixed, d_a, *outs):
+    width = d_a.shape[1]
+
+    def run(rows):
         for j in range(turns):
-            put_split(outs, turns + j, blocks(dot_tn(h1[:rows], d_f[:rows, j * width : (j + 1) * width]), depth), mine)
-        put_split(outs, 2 * turns, blocks(dot_tn(mixed[:rows], d_a[:rows]), depth), mine)
+            g = blocks(dot_tn(h1[:rows], d_f[:rows, j * width : (j + 1) * width]), depth)
+            if j < 2:
+                put_split(outs[:2], "xyz", j, g, plan[4])
+            else:
+                put_split(outs[2:], "yxz", j - 2, g, plan[4])
+        put_split(outs[2:], "yxz", turns - 2, blocks(dot_tn(mixed[:rows], d_a[:rows]), depth), plan[4])
 
     by_blocks(plan, run)
 
@@ -402,18 +413,49 @@
 def rest_grads_kernel(depth, length, plan, spot_in, hin, d_proj, d_x, sums_0, sums, sums_ff, *outs):
     width = d_proj.shape[2]
     part = hin.shape[1]
-    mine = plan[4]
+
+    def put(kind, g):
+        put_split(outs[:2] if kind < 2 else outs[2:], "xyz" if kind < 2 else "yxz", kind % 2, blocks(g, depth), plan[4])
 
     def run(rows):
         for i in range(3):
-            put_split(outs, i, blocks(dot_tn(hin[:rows], d_proj[i, :rows]), depth), mine)
+            put(i, dot_tn(hin[:rows], d_proj[i, :rows]))
         line = jnp.where(spot_in[:rows] == iota((rows, length), 1), 1.0, 0.0).astype(bf)
         g_pos = dot_tn(d_x[:rows], line)
         vec = jnp.concatenate([sums_0[:4], sums[:3], sums_ff[...], sums[3:6]], axis=0)
         vec = jnp.concatenate([vec, jnp.zeros((128 - vec.shape[0], part), f32)], axis=0)
-        put_split(outs, 3, blocks(jnp.concatenate([g_pos, vec.T, jnp.zeros((part, width - length - 128), f32)], axis=1), depth), mine)
+        put(3, jnp.concatenate([g_pos, vec.T, jnp.zeros((part, width - length - 128), f32)], axis=1))
 
     by_blocks(plan, run)
+
+
+def update_kernel(turns, scale, g_embed, dense_out, dense_in, rest, g_position, g_vectors, *refs):
+    factor = scale[0]
+    weights, moms, avgs, news, next_moms, next_avgs = (refs[7 * i : 7 * i + 7] for i in range(6))
+
+    def one(index, at, grad):
+        clipped = grad * factor
+        moment = MOMENT * moms[index][at] + clipped
+        fresh = weights[index][at] - RATE * (clipped + MOMENT * moment)
+        next_moms[index][at] = moment
+        news[index][at] = fresh
+        next_avgs[index][at] = DECAY * avgs[index][at] + (1.0 - DECAY) * fresh
+
+    every = (slice(None), slice(None))
+    one(0, every, g_embed[...])
+
+    @pl.when(pl.program_id(0) == 0)
+    def _():
+        depth, width = rest.shape[1:]
+        cols = lambda j: (slice(None), slice(j * width, (j + 1) * width))
+        one(1, every, g_position[...])
+        for j in range(3):
+            one(2, cols(j), rest[j])
+        one(3, every, dense_in[turns])
+        for j in range(turns):
+            one(4, cols(j), dense_in[j])
+            one(5, (slice(j * depth, (j + 1) * depth), slice(None)), dense_out[j])
+        one(6, every, g_vectors[...])
 
 
 def cost(flops, nbytes):
@@ -444,9 +486,8 @@
             **more,
         )
 
-    tall = depth % 8 == 0
     w_src, w_src_spec = full, fixed((width, turns * width), (0, at_back // (turns * width)))
-    if not tall:
+    if not staged:
         w_src = full[:, at_back : at_back + turns * width].reshape(devices, depth, turns, width)
         w_src, w_src_spec = w_src.transpose(0, 2, 1, 3).reshape(hidden, width), fixed((hidden, width), (0, 0))
 
@@ -476,7 +517,7 @@
 
     vec_ff = vec[7 : 7 + turns].reshape(1, hidden)
     z1, h1, act, slope, z2, pooled, w_back = call(
-        when_live(functools.partial(middle_kernel, depth, turns)), 1, (BLOCKS,),
+        when_live(functools.partial(middle_kernel, staged, depth, turns)), 1, (BLOCKS,),
         [row(width), row(width), w_out_spec, w_in_spec, w_src_spec, vec_spec, fixed((1, hidden), (0, 0))],
         [row(width), row(width), row(hidden), row(hidden), row(width), whole_out(8, width), whole_out(hidden, width)],
         [
@@ -505,32 +546,39 @@
         "back",
     )(plan, facts, holders, pooled, all_pooled, z1, slope, z2, full, full, w_back, vec)
 
-    half = devices // 2
     part = width // 2
-    quarter = lambda kinds: pl.BlockSpec((half // 2, kinds, depth, width), lambda i, *_: (i, 0, 0, 0))
     halves = lambda cols: pl.BlockSpec((rows, cols), lambda i, *_: (0, i))
     live = (jnp.arange(rows) < plan[3] * ROWS)[:, None]
     clean = lambda v: jnp.where(live, v, 0)
-    if tall:
-        dense = call(
-            functools.partial(dense_grads_kernel, depth, turns), 1, (2,),
-            [
-                halves(hidden // 2), fixed((rows, width), (0, 0)), halves(part), fixed((rows, hidden), (0, 0)), halves(part),
-                fixed((rows, width), (0, 0)),
-            ],
-            [quarter(turns)] * 2 + [quarter(turns + 1)] * 2,
-            [shape((half, turns, depth, width), bf)] * 2 + [shape((half, turns + 1, depth, width), bf)] * 2,
-            "dense_grads",
-        )(plan, act, d_y, h1, d_f, mixed, d_a)
+
+    def split_call(kernel, in_specs, streams, name):
+        specs, shapes = [], []
+        for order, kinds in streams:
+            at = order.index("z")
+            dims = tuple(4 if axis == "z" else 2 for axis in order) + (kinds, depth, width)
+            index = lambda i, *_, at=at: tuple(i if axis == at else 0 for axis in range(6))
+            specs += [pl.BlockSpec((2, 2, 2, kinds, depth, width), index)] * 2
+            shapes += [shape(dims, bf)] * 2
+        return call(kernel, 1, (2,), in_specs, specs, shapes, name)
+
+    if staged:
+        z, y, x_at = place_in_slice()
+        dense_out = split_call(
+            functools.partial(out_grads_kernel, depth, turns), [halves(hidden // 2), fixed((rows, width), (0, 0))], [("zxy", turns)], "out_grads"
+        )(plan, act, d_y)
+        dense_out = over_cores(*dense_out)
+        dense_in = split_call(
+            functools.partial(in_grads_kernel, depth, turns),
+            [halves(part), fixed((rows, hidden), (0, 0)), halves(part), fixed((rows, width), (0, 0))],
+            [("xyz", 2), ("yxz", turns - 1)],
+            "in_grads",
+        )(plan, h1, d_f, mixed, d_a)
+        d_o, dense_out, dense_in = lax.optimization_barrier((d_o, dense_out, dense_in))
+        dense_in = over_cores(*dense_in[:2]), over_cores(*dense_in[2:])
+        dense_out = over_long(dense_out, z)
     else:
-        cut = lambda g: g.astype(bf).reshape(devices, depth, -1, width).transpose(0, 2, 1, 3)
-        g_out = dot_tn(clean(act), clean(d_y)).astype(bf).reshape(devices, turns, depth, width)
-        g_in, g_mix = dot_tn(clean(h1), clean(d_f)), dot_tn(clean(mixed), clean(d_a))
-        dense = jnp.concatenate([g_out, cut(g_in), cut(g_mix)], axis=1)
-    if staged:
-        dense = over_cores(*dense)
-    else:
-        d_o, dense = lax.optimization_barrier((d_o, dense))
+        dense_out = dot_tn(clean(act), clean(d_y)).astype(bf)
+        dense_in = jnp.concatenate([dot_tn(clean(h1), clean(d_f)), dot_tn(clean(mixed), clean(d_a))], axis=1).astype(bf)
 
     def attend_back(start, count, total):
         more = () if total is None else (total,)
@@ -546,9 +594,11 @@
 
     d_proj = attend_back(0, pairs // 2, None)
     if staged:
-        d_proj, dense = lax.optimization_barrier((d_proj, dense))
-        dense = over_wide(*dense)
+        d_proj, dense_in = lax.optimization_barrier((d_proj, dense_in))
+        dense_in = halve(dense_in[0], x_at, 2), halve(dense_in[1], y, 4)
     d_proj = attend_back(pairs // 2, pairs - pairs // 2, d_proj)
+    if staged:
+        d_proj, dense_in = lax.optimization_barrier((d_proj, dense_in))
 
     d_xb, sums_0, give_rows = call(
         when_live(last_kernel), 1, (BLOCKS,),
@@ -562,14 +612,12 @@
     )(plan, slots[:, None], x, d_r1, d_proj, full, vec)
 
     if staged:
-        d_xb, dense = lax.optimization_barrier((d_xb, dense))
-    if tall:
+        give_rows, dense_out = lax.optimization_barrier((give_rows, dense_out))
         cols = lambda count: pl.BlockSpec((count, part), lambda i, *_: (0, i))
-        rest = call(
-            functools.partial(rest_grads_kernel, depth, length), 1, (2,),
+        rest = split_call(
+            functools.partial(rest_grads_kernel, depth, length),
             [fixed((rows, 1), (0, 0)), halves(part), fixed((3, rows, width), (0, 0, 0)), halves(part), cols(8), cols(8), cols(turns)],
-            [quarter(2)] * 4,
-            [shape((half, 2, depth, width), bf)] * 4,
+            [("xyz", 2), ("yxz", 2)],
             "rest_grads",
         )(plan, spots[:, None], hin, d_proj, d_xb, sums_0, sums, sums_ff)
     else:
@@ -577,8 +625,8 @@
         g_pos = dot_tn(clean(d_xb), one_hot(spots, length))
         spare = jnp.zeros((width, width - length - g_vec.shape[0]), f32)
         rest = [dot_tn(clean(hin), clean(d_proj[i])) for i in range(3)] + [jnp.concatenate([g_pos, g_vec.T, spare], axis=1)]
-        rest = jnp.stack([g.astype(bf).reshape(devices, depth, width) for g in rest], axis=1)
-    return loss[0, 0], dense, rest, clean(d_xb), give_rows
+        rest = jnp.concatenate(rest, axis=1).astype(bf)
+    return loss[0, 0], dense_out, dense_in, rest, clean(d_xb), give_rows
 
 
 def swap(v, bit, devices):
@@ -598,32 +646,24 @@
     return row // 2, lax.rem(row, 2), lax.axis_index("seq") // 2
 
 
-def over_cores(keep_one, send_one, keep_two, send_two):
-    view = lambda v: v.reshape((4, 2, 2) + v.shape[1:])
-    return (view(keep_one), swap(view(send_one), 1, 32)), (view(keep_two), swap(view(send_two), 1, 32))
-
-
-def part_sum(pair, axis, index):
-    return add(spot(pair[0], axis, index), spot(pair[1], axis, index))
-
-
-def halve(pair, axis, index, bit):
-    return part_sum(pair, axis, index), swap(part_sum(pair, axis, 1 - index), bit, 32)
-
-
-def over_wide(one, two):
-    _, y, x = place_in_slice()
-    return halve(one, 2, x, 2), halve(two, 1, y, 4)
-
-
-def over_other(one, two):
-    _, y, x = place_in_slice()
-    return halve(one, 1, y, 4), halve(two, 1, x, 2)
-
-
-def over_long(one, two):
-    z, _, _ = place_in_slice()
-    part = lambda step: jnp.concatenate([part_sum(one, 0, z ^ step), part_sum(two, 0, z ^ step)], axis=0)
+def over_cores(keep, send):
+    return keep, swap(send, 1, 32)
+
+
+def part_sum(pair, index):
+    return add(spot(pair[0], 0, index), spot(pair[1], 0, index))
+
+
+def halve(pair, index, bit):
+    return part_sum(pair, index), swap(part_sum(pair, 1 - index), bit, 32)
+
+
+def over_long(pair, z):
+    return [part_sum(pair, z)] + [swap(part_sum(pair, z ^ step), 8 * step, 32) for step in range(1, 4)]
+
+
+def over_long_both(one, two, z):
+    part = lambda step: jnp.concatenate([part_sum(one, z ^ step), part_sum(two, z ^ step)], axis=0)
     return [part(0)] + [swap(part(step), 8 * step, 32) for step in range(1, 4)]
 
 
@@ -726,35 +766,29 @@
         facts += [weight, take(all_gold, pair), take(lens, i).astype(f32), take(lens, other).astype(f32), own]
     meet = jnp.stack(holders), jnp.stack(facts + [count])
 
-    staged = (seq, devices) == (4, 32) and depth % 8 == 0
-    loss, dense, rest, d_xb, give_rows = run_forward_backward(
+    staged = (seq, devices) == (4, 32) and depth == 24
+    loss, dense_out, dense_in, rest, d_xb, give_rows = run_forward_backward(
         full, back, extra, slots, spots, plan, meet, staged, devices, depth, length, hidden
     )
 
-    def sum_up(parts):
-        if isinstance(parts, list | tuple):
-            keep, send = (jnp.concatenate([parts[i], parts[i + 2]], axis=1) for i in range(2))
-            both = jnp.stack([jnp.where(core == 0, keep, send), jnp.where(core == 0, send, keep)], axis=1)
-            parts = both.reshape((devices,) + keep.shape[1:])
-        return lax.psum_scatter(parts, AXES, scatter_dimension=0, tiled=True).astype(f32)[0]
-
     give_rows = exchange(give_rows.reshape(devices, room, width))
     if staged:
-        dense = over_other(*dense)
-        rest = over_wide(*over_cores(*rest))
-        dense, give_rows = lax.optimization_barrier((dense, give_rows))
-        dense = over_long(*dense)
-        rest = over_other(*rest)
-        dense, rest = lax.optimization_barrier((dense, rest))
-        rest = over_long(*rest)
-        dense, rest = total_of(dense), total_of(rest)
+        z, y, x = place_in_slice()
+        dense_in = halve(dense_in[0], y, 4), halve(dense_in[1], x, 2)
+        dense_out = total_of(dense_out).astype(bf)
+        dense_out = spot(dense_out, 0, x), swap(spot(dense_out, 0, 1 - x), 2, 32)
+        rest = halve(over_cores(*rest[:2]), x, 2), halve(over_cores(*rest[2:]), y, 4)
+        dense_in, give_rows = lax.optimization_barrier((dense_in, give_rows))
+        dense_in = over_long_both(*dense_in, z)
+        dense_out = halve(dense_out, y, 4)
+        rest = halve(rest[0], y, 4), halve(rest[1], x, 2)
+        dense_in, dense_out, rest = lax.optimization_barrier((dense_in, dense_out, rest))
+        rest = over_long_both(*rest, z)
+        dense_out, dense_in, rest = total_of(dense_out), total_of(dense_in), total_of(rest)
     else:
-        dense, rest = sum_up(dense), sum_up(rest)
-    beside = lambda v: jnp.concatenate(list(v), axis=1)
-    g_ff_out = dense[:turns].reshape(turns * depth, width)
-    g_ff_in = beside(dense[turns : 2 * turns])
-    g_attn_out = dense[2 * turns]
-    g_attn_in = beside(rest[:3])
+        sum_up = lambda parts: lax.psum_scatter(parts, AXES, scatter_dimension=0, tiled=True).astype(f32)
+        kinds = lambda v: v.reshape(depth, -1, width).transpose(1, 0, 2)
+        dense_out, dense_in, rest = sum_up(dense_out).reshape(turns, depth, width), kinds(sum_up(dense_in)), kinds(sum_up(rest))
     g_position = rest[3, :, :length].T
     g_vectors = rest[3, :, length : length + nvec].T
 
@@ -769,25 +803,32 @@
 
     _, g_embed = lax.while_loop(lambda state: state[0] < rounds, more_back, (jnp.int32(1), give(wanted_first, give_rows)))
 
-    grads = (g_embed, g_position, g_attn_in, g_attn_out, g_ff_in, g_ff_out, g_vectors)
-    squares = sum(jnp.sum(g * g) for g in (g_embed, dense, rest))
+    squares = sum(jnp.sum(g * g) for g in (g_embed, dense_out, dense_in, rest))
     sums = exchange(jnp.broadcast_to(jnp.stack([squares, loss])[None, :], (devices, 2)))
     sums = jnp.sum(sums, axis=0)
     norm = jnp.sqrt(sums[0])
     loss_sum = sums[1]
     scale = jnp.minimum(1.0, CLIP / (norm + 1e-06))
-    weights = (embed, position, attn_in, attn_out, ff_in, ff_out, vectors)
-    moms = (mom_embed, mom_position, mom_attn_in, mom_attn_out, mom_ff_in, mom_ff_out, mom_vectors)
-    avgs = (avg_embed, avg_position, avg_attn_in, avg_attn_out, avg_ff_in, avg_ff_out, avg_vectors)
-    news, next_moms, next_avgs = [], [], []
-    for weight, grad, mom, avg in zip(weights, grads, moms, avgs):
-        clipped = grad * scale
-        moment = MOMENT * mom + clipped
-        fresh = weight - RATE * (clipped + MOMENT * moment)
-        news.append(fresh)
-        next_moms.append(moment)
-        next_avgs.append(DECAY * avg + (1.0 - DECAY) * fresh)
-    return (loss_sum, count, norm, *news, *next_moms, *next_avgs)
+    state = (
+        embed, position, attn_in, attn_out, ff_in, ff_out, vectors,
+        mom_embed, mom_position, mom_attn_in, mom_attn_out, mom_ff_in, mom_ff_out, mom_vectors,
+        avg_embed, avg_position, avg_attn_in, avg_attn_out, avg_ff_in, avg_ff_out, avg_vectors,
+    )
+    steps = next(n for n in (8, 5, 4, 3, 2, 1) if per_owner % (8 * n) == 0 or n == 1)
+    strip = pl.BlockSpec((per_owner // steps, width), lambda i, *_: (i, 0))
+    whole = lambda v: strip if v.shape == embed.shape else fixed(v.shape, (0,) * v.ndim)
+    whole_out = lambda v: strip if v.shape == embed.shape else pl.BlockSpec(v.shape, lambda *_: (0,) * v.ndim)
+    inputs = (g_embed, dense_out, dense_in, rest, g_position, g_vectors) + state
+    done = pl.pallas_call(
+        functools.partial(update_kernel, turns),
+        grid_spec=pltpu.PrefetchScalarGridSpec(
+            num_scalar_prefetch=1, grid=(steps,), in_specs=[whole(v) for v in inputs], out_specs=[whole_out(v) for v in state]
+        ),
+        out_shape=[jax.ShapeDtypeStruct(v.shape, f32) for v in state],
+        compiler_params=params(60),
+        name="update",
+    )(scale[None], *inputs)
+    return (loss_sum, count, norm, *done)
 
 
 def solution(mesh):

time: 501 us -> 497 us (level)
  waiting for transfers between devices: 161 us -> 139 us
  other arithmetic: 73.9 us -> 55.8 us
  starting transfers between devices: 50.6 us -> 66 us
  Pallas kernels: 129 us -> 144 us
    ppermute x18 -> x24, waiting for transfers between devices: 61.9 us -> 44.6 us  [swap(): return lax.ppermute(v, AXES, [(i, i ^ bit) for i in range(devices)])]
    pallas_call x3 -> x5, Pallas kernels: 52.7 us -> 67.6 us  [the longest x1 24.2 us: run_forward_backward(): call(when_live(functools.partial(middle_kernel, staged, depth, turns)), 1...]
    add x7 -> x1, other arithmetic: 15.3 us -> 1.35 us  [total_of(): return sum((p.astype(f32) for p in parts))]
    ppermute x18 -> x24, starting transfers between devices: 19.3 us -> 28.4 us  [swap(): return lax.ppermute(v, AXES, [(i, i ^ bit) for i in range(devices)])]
    all_to_all x7, starting transfers between devices: 31.3 us -> 37.6 us  [exchange(): return lax.all_to_all(v, AXES, 0, 0, tiled=True)]
    reshape x2 -> x0, local copies, waits for them, and re-layouts: 5.36 us -> none  [over_cores(): view = lambda v: v.reshape((4, 2, 2) + v.shape[1:])]
    convert_element_type x11 -> x13, other arithmetic: 21.9 us -> 16.9 us  [add(): return (a.astype(f32) + b.astype(f32)).astype(bf)]
    unnamed x98 -> x68, local copies, waits for them, and re-layouts: 9.82 us -> 11.1 us
  transfers between devices with their start and end apart: 26 -> 32, of which waited for: 12 -> 14; matrix products, arithmetic and copies ran while one was open for 15% -> 15% of each run, Pallas kernels for 4% -> 11%
where the time goes in v6:
time: 497 us; the launch traced here: 489 us
  Pallas kernels  144 us (29%)
  waiting for transfers between devices  139 us (28%)
  starting transfers between devices  66 us (13%)
  other arithmetic  55.8 us (11%)
  between operations  38.7 us (8%)
  local copies, waits for them, and re-layouts  35.3 us (7%)
  matrix products  9.89 us (2%)
    all_to_all x7, waiting for transfers between devices, exchange(): return lax.all_to_all(v, AXES, 0, 0, tiled=True)  91.5 us
    ppermute x24, waiting for transfers between devices, swap(): return lax.ppermute(v, AXES, [(i, i ^ bit) for i in range(devices)])  44.6 us
    all_to_all x7, starting transfers between devices, exchange(): return lax.all_to_all(v, AXES, 0, 0, tiled=True)  37.6 us
    ppermute x24, starting transfers between devices, swap(): return lax.ppermute(v, AXES, [(i, i ^ bit) for i in range(devices)])  28.4 us
    pallas_call x1, Pallas kernels, run_forward_backward(): call(when_live(functools.partial(middle_kernel, staged, depth, turns)), 1...  24.2 us
    pallas_call x2, Pallas kernels, attend_back(): call(attend_back_kernel, 1, (count,), [block(0, start), block(1, start),...  21.8 us
    pallas_call x1, Pallas kernels, run_forward_backward(): call(when_live(back_kernel), 3, (BLOCKS,), [fixed((8, width), (0, 0)), fi...  19.8 us
    convert_element_type x13, other arithmetic, add(): return (a.astype(f32) + b.astype(f32)).astype(bf)  16.9 us
  transfers between devices with their start and end apart: 32, of which 14 were waited for; matrix products, arithmetic and copies ran while one was open for 15% of the time, Pallas kernels for 11%

profile of v6, /device:TPU:0, one launch (start us, length us, event | category | flops | bytes accessed | tf_op | source)
XLA Modules:
  0.0 489.1 jit_solution(8140096976218463885)
XLA Ops:
  14.8 7.3 %all-to-all-start.4 = ((s32[32,9,128]{2,1,0:T(8,128)}), s32[32,9,128]{2,1,0:T(8,128)S(1)}, u32[]{:S(2)}, u32[]{:S(2)}) async-start(s32[32,9,128]{2,1,0:T(8,128)} %broadcast_in_dim.172), calls=%async_computation.4 | async-start | bytes 524288 | tf_op jit(solution)/shard_map/all_to_all | solution.py:40
  22.2 12.6 %all-to-all-done.4 = s32[32,9,128]{2,1,0:T(8,128)S(1)} async-done(((s32[32,9,128]{2,1,0:T(8,128)}), s32[32,9,128]{2,1,0:T(8,128)S(1)}, u32[]{:S(2)}, u32[]{:S(2)}) %all-to-all-start.4) | async-done | bytes 147488 | tf_op jit(solution)/shard_map/all_to_all | solution.py:40
  40.3 2.0 fusion.89
  48.7 1.7 convert_reduce_fusion
  53.8 4.2 all-to-all-start.5
  59.3 5.9 %all-to-all-done.5 = s32[32,1,128]{2,1,0:T(1,128)S(1)} async-done(((s32[32,1,128]{2,1,0:T(1,128)}), s32[32,1,128]{2,1,0:T(1,128)S(1)}, u32[]{:S(2)}, u32[]{:S(2)}) %all-to-all-start.5) | async-done | bytes 16416 | tf_op jit(solution)/shard_map/all_to_all | solution.py:40
  65.3 4.5 fusion.32
  70.5 3.2 all-to-all-start.7
  75.1 5.7 %all-to-all-done.7 = f32[32,1,4]{2,1,0:T(1,128)} async-done(((f32[32,1,4]{2,1,0:T(1,128)}), f32[32,1,4]{2,1,0:T(1,128)}, u32[]{:S(2)}, u32[]{:S(2)}) %all-to-all-start.7) | async-done | bytes 544 | tf_op jit(solution)/shard_map/all_to_all | solution.py:40
  81.0 2.7 all-to-all-start.6
  87.6 1.9 stack.74.refs_0_.plan
  89.5 1.6 select_select_fusion.refs_2_.spot_in
  91.2 64.1 %all-to-all-done.6 = bf16[32,32,768]{2,1,0:T(8,128)(2,1)S(1)} async-done(((bf16[32,32,768]{2,1,0:T(8,128)(2,1)}), bf16[32,32,768]{2,1,0:T(8,128)(2,1)S(1)}, u32[]{:S(2)}, u32[]{:S(2)}) %all-to-all-start.6) | async-done | bytes 1572896 | tf_op jit(solution)/shard_map/all_to_all | solution.py:40
  155.3 2.8 all-gather.2.cloned.1.call-done.refs_5_.refs_6_.refs_7_.refs_3_.refs_4_.refs_8_.refs_9_
  158.1 10.4 %first.1 = (f32[1152,768]{1,0:T(8,128)}, bf16[1152,768]{1,0:T(8,128)(2,1)}, bf16[1152,2304]{1,0:T(8,128)(2,1)}, f32[16,768]{1,0:T(8,128)}) custom-call(s32[5]{0:T(128)} %stack.74.refs_0_.plan, s32[1152,1]{1,0:T(8,128)} %broadcast_in_dim.197.refs_1_, s32[1152,1]{1,0:T(8,128)} %select_select_fusion.refs_2_.spot_in, bf16[1024,768]{1,0:T(8,128)(2,1)} %bitcast.181, ...), custom_call_target="tpu_custom_call" | custom-call | tf_op jit(solution)/shard_map/first/pallas_call | solution.py:502
  168.4 12.6 %attend.1.refs_2_.mixed = bf16[1152,768]{1,0:T(8,128)(2,1)} custom-call(s32[5]{0:T(128)} %stack.74.refs_0_.plan, bf16[1152,2304]{1,0:T(8,128)(2,1)} %get-tuple-element.211.query.keys.values, bf16[1152,2304]{1,0:T(8,128)(2,1)} %get-tuple-element.211.query.keys.values, bf16[1152,2304]{1,0:T(8,128)(2,1)} %get-tuple-element.211.query.keys.values), custom_call_target="tpu_custom_call" | custom-call | tf_op jit(solution)/shard_map/attend/pallas_call | solution.py:514
  182.5 24.2 %middle.1 = (f32[1152,768]{1,0:T(8,128)}, bf16[1152,768]{1,0:T(8,128)(2,1)}, bf16[1152,3072]{1,0:T(8,128)(2,1)}, bf16[1152,3072]{1,0:T(8,128)(2,1)}, f32[1152,76...) custom-call(s32[5]{0:T(128)} %stack.74.refs_0_.plan, f32[1152,768]{1,0:T(8,128)} %get-tuple-element.212.refs_1_.refs_2_, ...), custom_call_target="tpu_custom_call" | custom-call | tf_op jit(solution)/shard_map/middle/pallas_call | solution.py:519
  208.2 3.2 all-to-all-start.8
  221.9 1.9 stack.86.refs_1_
  225.2 19.8 %back.1 = (bf16[1152,768]{1,0:T(8,128)(2,1)}, bf16[1152,3072]{1,0:T(8,128)(2,1)}, f32[1152,768]{1,0:T(8,128)}, bf16[1152,768]{1,0:T(8,128)(2,1)}, bf16[1152,768]...) custom-call(s32[5]{0:T(128)} %stack.74.refs_0_.plan, f32[11]{0:T(128)} %stack.86.refs_1_, ...), custom_call_target="tpu_custom_call" | custom-call | tf_op jit(solution)/shard_map/back/pallas_call | solution.py:532
  245.0 9.2 %out_grads.1 = (bf16[4,2,2,4,24,768]{5,4,3,2,1,0:T(8,128)(2,1)}, bf16[4,2,2,4,24,768]{5,4,3,2,1,0:T(8,128)(2,1)}) custom-call(s32[5]{0:T(128)} %stack.74.refs_0_.plan, bf16[1152,3072]{1,0:T(8,128)(2,1)} %get-tuple-element.220.act, bf16[1152,768]{1,0:T(8,128)(2,1)} %get-tuple-element.221.d_y), custom_call_target="tpu_custom_call" | custom-call | tf_op jit(solution)/shard_map/out_grads/pallas_call | solution.py:566
  254.5 11.7 %in_grads.1 = (bf16[2,2,4,2,24,768]{5,4,3,2,1,0:T(8,128)(2,1)}, bf16[2,2,4,2,24,768]{5,4,3,2,1,0:T(8,128)(2,1)}, bf16[2,2,4,3,24,768]{5,4,3,2,1,0:T(8,128)(2,1)}, bf16[2,2,4,3,24,768]{5,4,3,2,1,0:T(8,128)(2,1)}) custom-call(s32[5]{0:T(128)} %stack.74.refs_0_.plan, bf16[1152,768]{1,0:T(8,128)(2,1)} %get-tuple-element.224.h1, ...), custom_call_target="tpu_custom_call" | custom-call | tf_op jit(solution)/shard_map/in_grads/pallas_call | solution.py:570
  266.8 11.1 %attend_back.2.more_0_ = bf16[3,1152,768]{2,1,0:T(8,128)(2,1)} custom-call(s32[5]{0:T(128)} %stack.74.refs_0_.plan, bf16[1152,2304]{1,0:T(8,128)(2,1)} %get-tuple-element.211.query.keys.values, bf16[1152,2304]{1,0:T(8,128)(2,1)} %get-tuple-element.211.query.keys.values, bf16[1152,2304]{1,0:T(8,128)(2,1)} %get-tuple-element.211.query.keys.values, ...), custom_call_target="tpu_custom_call" | custom-call | flops 1006632960 | bytes 7077888 | tf_op jit(solution)/shard_map/attend_back/pallas_call | solution.py:585
  277.9 2.9 fusion.34
  280.8 1.7 collective-permute-start.4
  282.5 2.4 fusion.36
  284.9 1.5 collective-permute-start.3
  286.3 3.3 fusion.40
  289.6 1.5 collective-permute-start.7
  291.1 3.0 collective-permute-start.8
  294.1 10.6 %attend_back.3.refs_4_.d_proj = bf16[3,1152,768]{2,1,0:T(8,128)(2,1)} custom-call(s32[5]{0:T(128)} %stack.74.refs_0_.plan, bf16[1152,2304]{1,0:T(8,128)(2,1)} %get-tuple-element.211.query.keys.values, bf16[1152,2304]{1,0:T(8,128)(2,1)} %get-tuple-element.211.query.keys.values, ...), custom_call_target="tpu_custom_call", output_to_operand_aliasing={{}: (5, {})} | custom-call | flops 1006632960 | bytes 7077888 | tf_op jit(solution)/shard_map/attend_back/pallas_call | solution.py:585
  304.7 11.9 %last.1 = (bf16[1152,768]{1,0:T(8,128)(2,1)}, f32[8,768]{1,0:T(8,128)}, bf16[1024,768]{1,0:T(8,128)(2,1)}) custom-call(s32[5]{0:T(128)} %stack.74.refs_0_.plan, s32[1152,1]{1,0:T(8,128)} %broadcast_in_dim.197.refs_1_, f32[1152,768]{1,0:T(8,128)} %get-tuple-element.212.refs_1_.refs_2_, f32[1152,768]{1,0:T(8,128)} %get-tuple-element.245.refs_3_, ...), custom_call_target="tpu_custom_call" | custom-call | tf_op jit(solution)/shard_map/last/pallas_call | solution.py:603
  316.9 17.0 %collective-permute-done.8 = bf16[2,2,4,24,768]{4,3,2,1,0:T(8,128)(2,1)} collective-permute-done((bf16[2,2,4,24,768]{4,3,2,1,0:T(8,128)(2,1)}, bf16[2,2,4,24,768]{4,3,2,1,0:T(8,128)(2,1)}, u32[]{:S(2)}, u32[]{:S(2)}) %collective-permute-start.8) | collective-permute-done | bytes 589856 | tf_op jit(solution)/shard_map/ppermute | solution.py:633
  333.9 13.8 %all-to-all-start.9 = ((bf16[32,32,768]{2,1,0:T(8,128)(2,1)}), bf16[32,32,768]{2,1,0:T(8,128)(2,1)}, u32[]{:S(2)}, u32[]{:S(2)}) async-start(bf16[32,32,768]{2,1,0:T(8,128)(2,1)} %bitcast.183), calls=%async_computation.9 | async-start | bytes 3145728 | tf_op jit(solution)/shard_map/all_to_all | solution.py:40
  347.7 9.9 %rest_grads.1 = (bf16[2,2,4,2,24,768]{5,4,3,2,1,0:T(8,128)(2,1)}, bf16[2,2,4,2,24,768]{5,4,3,2,1,0:T(8,128)(2,1)}, bf16[2,2,4,2,24,768]{5,4,3,2,1,0:T(8,128)(2,1)}, bf16[2,2,4,2,24,768]{5,4,3,2,1,0:T(8,128)(2,1)}) custom-call(s32[5]{0:T(128)} %stack.74.refs_0_.plan, s32[1152,1]{1,0:T(8,128)} %select_select_fusion.refs_2_.spot_in, ...), custom_call_target="tpu_custom_call" | custom-call | tf_op jit(solution)/shard_map/rest_grads/pallas_call | solution.py:617
  361.9 1.5 add_convert_fusion.6
  363.5 1.9 collective-permute-start.13
  367.3 1.8 collective-permute-start.5
  369.1 1.7 add_convert_fusion.3
  371.1 1.7 add_convert_fusion.5
  372.8 1.8 collective-permute-start.16
  374.6 1.4 broadcast_select_fusion
  376.3 1.4 collective-permute-start.14
  377.7 15.9 %collective-permute-done.19 = bf16[2,4,2,24,768]{4,3,2,1,0:T(8,128)(2,1)S(1)} collective-permute-done((bf16[2,4,2,24,768]{4,3,2,1,0:T(8,128)(2,1)S(1)}, bf16[2,4,2,24,768]{4,3,2,1,0:T(8,128)(2,1)S(1)}, u32[]{:S(2)}, u32[]{:S(2)}) %collective-permute-start.19) | collective-permute-done | bytes 589856 | tf_op jit(solution)/shard_map/ppermute | solution.py:633
  394.5 1.8 collective-permute-start.20
  396.2 4.2 collective-permute-done.16
  403.0 4.0 collective-permute-start.12
  408.5 5.4 %fusion.28 = f32[960,768]{1,0:T(8,128)} fusion(bf16[1024,768]{1,0:T(8,128)(2,1)} %bitcast.44, s32[1024]{0:T(1024)S(1)} %copy-done.23), kind=kOutput, calls=%fused_computation.52 | convolution fusion | flops 1510932480 | bytes 4526080 | tf_op jit(solution)/shard_map/dot_general | solution.py:32
  416.1 3.3 multiply_reduce_fusion
  419.4 3.6 collective-permute-done.11
  423.0 1.9 collective-permute-done.10
  426.3 1.6 copy.153
  428.0 3.1 collective-permute-start.22
  431.0 1.4 collective-permute-start.23
  435.1 2.5 multiply_reduce_fusion.2
  439.5 1.6 collective-permute-done.22
  443.5 3.3 multiply_reduce_fusion.1
  450.6 3.1 all-to-all-start.10
  455.1 2.6 copy.157.rest
  457.6 3.2 all-to-all-done.10
  462.2 12.6 %update.1 = (f32[960,768]{1,0:T(8,128)}, f32[512,24]{1,0:T(8,128)}, f32[24,2304]{1,0:T(8,128)}, f32[24,768]{1,0:T(8,128)}, f32[24,3072]{1,0:T(8,128)}, /*index=5...) custom-call(f32[1]{0:T(128)} %bitcast.80.scale, ...), custom_call_target="tpu_custom_call" | custom-call | tf_op jit(solution)/shard_map/update/pallas_call | solution.py:822
  474.8 1.7 copy.161
  476.5 1.7 copy.162
  478.1 1.7 copy.163
  (186 shorter events, 53.5 us)
Async XLA Ops:
  7.2 6.6 %copy-start.26 = (s32[4,2]{0,1:T(2,128)S(1)}, s32[4,2]{0,1:T(2,128)}, u32[]{:S(2)}) copy-start(s32[4,2]{0,1:T(2,128)} %param.30) | copy-start | bytes 100
  7.2 6.8 %copy-start.28 = (s32[4]{0:T(128)S(1)}, s32[4]{0:T(128)}, u32[]{:S(2)}) copy-start(s32[4]{0:T(128)} %param.31) | copy-start | bytes 52
  7.2 6.8 %copy-start.21 = (s32[4,2,128]{2,1,0:T(2,128)S(1)}, s32[4,2,128]{2,1,0:T(2,128)}, u32[]{:S(2)}) copy-start(s32[4,2,128]{2,1,0:T(2,128)} %param.29) | copy-start | bytes 12292
  7.2 150.8 %all-gather.2.cloned.1.call-start = ((), (), s32[]{:S(2)}) async-start(), calls=%async_computation.11 | async-start | bytes 15611904 | tf_op jit(solution)/shard_map/all_gather | solution.py:699
  10.2 47.8 %copy-start = (f32[960,768]{1,0:T(8,128)S(1)}, f32[960,768]{1,0:T(8,128)}, u32[]{:S(2)}) copy-start(f32[960,768]{1,0:T(8,128)} %refs_0_.1) | copy-start | bytes 8847364
  14.8 20.0 %all-to-all-start.4 = ((s32[32,9,128]{2,1,0:T(8,128)}), s32[32,9,128]{2,1,0:T(8,128)S(1)}, u32[]{:S(2)}, u32[]{:S(2)}) async-start(s32[32,9,128]{2,1,0:T(8,128)} %broadcast_in_dim.172), calls=%async_computation.4 | async-start | bytes 524288 | tf_op jit(solution)/shard_map/all_to_all | solution.py:40
  35.5 4.7 copy-start.24
  53.8 11.4 %all-to-all-start.5 = ((s32[32,1,128]{2,1,0:T(1,128)}), s32[32,1,128]{2,1,0:T(1,128)S(1)}, u32[]{:S(2)}, u32[]{:S(2)}) async-start(s32[32,1,128]{2,1,0:T(1,128)} %bitcast.6), calls=%async_computation.5 | async-start | bytes 32768 | tf_op jit(solution)/shard_map/all_to_all | solution.py:40
  65.3 4.5 copy-start.22
  65.3 4.5 copy-start.27
  70.5 10.3 %all-to-all-start.7 = ((f32[32,1,4]{2,1,0:T(1,128)}), f32[32,1,4]{2,1,0:T(1,128)}, u32[]{:S(2)}, u32[]{:S(2)}) async-start(f32[32,1,4]{2,1,0:T(1,128)} %broadcast_in_dim.185), calls=%async_computation.7 | async-start | bytes 32768 | tf_op jit(solution)/shard_map/all_to_all | solution.py:40
  81.0 74.2 %all-to-all-start.6 = ((bf16[32,32,768]{2,1,0:T(8,128)(2,1)}), bf16[32,32,768]{2,1,0:T(8,128)(2,1)S(1)}, u32[]{:S(2)}, u32[]{:S(2)}) async-start(bf16[32,32,768]{2,1,0:T(8,128)(2,1)} %bitcast.182), calls=%async_computation.6 | async-start | bytes 3145728 | tf_op jit(solution)/shard_map/all_to_all | solution.py:40
  155.3 2.8 copy-start.4
  182.5 28.9 %copy-start.25 = (s32[64]{0:T(128)S(1)}, s32[64]{0:T(128)}, u32[]{:S(2)}) copy-start(s32[64]{0:T(128)} %copy-done.24) | copy-start | bytes 772
  208.2 16.2 %all-to-all-start.8 = ((f32[32,2,768]{2,1,0:T(2,128)}), f32[32,2,768]{2,1,0:T(2,128)S(1)}, u32[]{:S(2)}, u32[]{:S(2)}) async-start(f32[32,2,768]{2,1,0:T(2,128)} %broadcast_in_dim.187), calls=%async_computation.8 | async-start | bytes 393216 | tf_op jit(solution)/shard_map/all_to_all | solution.py:40
  254.2 11.9 %collective-permute-start = (bf16[4,2,2,4,24,768]{5,4,3,2,1,0:T(8,128)(2,1)}, bf16[4,2,2,4,24,768]{5,4,3,2,1,0:T(8,128)(2,1)}, u32[]{:S(2)}, u32[]{:S(2)}) collective-permute-start(bf16[4,2,2,4,24,768]{5,4,3,2,1,0:T(8,128)(2,1)} %get-tuple-element.223), channel_id=1, source_target_pairs={{0,1},{1,0},{2,3},{3,2},{4,5},{5,4},{6,7},{7,6},{8,9},{9,8},{10,11... | collective-permute-start | bytes 7077896 | tf_op jit(solution)/shard_map/ppermute | solution.py:633
  266.2 11.7 %collective-permute-start.2 = (bf16[2,2,4,3,24,768]{5,4,3,2,1,0:T(8,128)(2,1)}, bf16[2,2,4,3,24,768]{5,4,3,2,1,0:T(8,128)(2,1)}, u32[]{:S(2)}, u32[]{:S(2)}) collective-permute-start(bf16[2,2,4,3,24,768]{5,4,3,2,1,0:T(8,128)(2,1)} %get-tuple-element.235), channel_id=1, source_target_pairs={{0,1},{1,0},{2,3},{3,2},{4,5},{5,4},{6,7},{7,6},{8,9},{9,8},{10,11... | collective-permute-start | bytes 5308424 | tf_op jit(solution)/shard_map/ppermute | solution.py:633
  266.5 11.4 %collective-permute-start.1 = (bf16[2,2,4,2,24,768]{5,4,3,2,1,0:T(8,128)(2,1)}, bf16[2,2,4,2,24,768]{5,4,3,2,1,0:T(8,128)(2,1)}, u32[]{:S(2)}, u32[]{:S(2)}) collective-permute-start(bf16[2,2,4,2,24,768]{5,4,3,2,1,0:T(8,128)(2,1)} %get-tuple-element.233), channel_id=1, source_target_pairs={{0,1},{1,0},{2,3},{3,2},{4,5},{5,4},{6,7},{7,6},{8,9},{9,8},{10,11... | collective-permute-start | bytes 3538952 | tf_op jit(solution)/shard_map/ppermute | solution.py:633
  266.8 11.2 %copy-start.7 = (bf16[2,2,4,3,24,768]{5,4,3,2,1,0:T(8,128)(2,1)S(1)}, bf16[2,2,4,3,24,768]{5,4,3,2,1,0:T(8,128)(2,1)}, u32[]{:S(2)}) copy-start(bf16[2,2,4,3,24,768]{5,4,3,2,1,0:T(8,128)(2,1)} %get-tuple-element.239) | copy-start | bytes 5308420
  277.9 4.6 copy-start.8
  280.8 5.5 %copy-start.5 = (bf16[4,2,2,4,24,768]{5,4,3,2,1,0:T(8,128)(2,1)S(1)}, bf16[4,2,2,4,24,768]{5,4,3,2,1,0:T(8,128)(2,1)}, u32[]{:S(2)}) copy-start(bf16[4,2,2,4,24,768]{5,4,3,2,1,0:T(8,128)(2,1)} %get-tuple-element.248) | copy-start | bytes 7077892
  280.8 23.9 %collective-permute-start.4 = (bf16[2,4,3,24,768]{4,3,2,1,0:T(8,128)(2,1)}, bf16[2,4,3,24,768]{4,3,2,1,0:T(8,128)(2,1)}, u32[]{:S(2)}, u32[]{:S(2)}) collective-permute-start(bf16[2,4,3,24,768]{4,3,2,1,0:T(8,128)(2,1)} %get-tuple-element.580), channel_id=1, source_target_pairs={{0,4},{1,5},{2,6},{3,7},{4,0},{5,1},{6,2},{7,3},{8,12},{9,13},{10,... | collective-permute-start | bytes 2654216 | tf_op jit(solution)/shard_map/ppermute | solution.py:633
  284.9 19.9 %collective-permute-start.3 = (bf16[2,4,2,24,768]{4,3,2,1,0:T(8,128)(2,1)}, bf16[2,4,2,24,768]{4,3,2,1,0:T(8,128)(2,1)S(1)}, u32[]{:S(2)}, u32[]{:S(2)}) collective-permute-start(bf16[2,4,2,24,768]{4,3,2,1,0:T(8,128)(2,1)} %get-tuple-element.586), channel_id=1, source_target_pairs={{0,2},{1,3},{2,0},{3,1},{4,6},{5,7},{6,4},{7,5},{8,10},{9,11},{10,... | collective-permute-start | bytes 1769480 | tf_op jit(solution)/shard_map/ppermute | solution.py:633
  289.6 27.3 %collective-permute-start.7 = (bf16[2,2,4,24,768]{4,3,2,1,0:T(8,128)(2,1)}, bf16[2,2,4,24,768]{4,3,2,1,0:T(8,128)(2,1)S(1)}, u32[]{:S(2)}, u32[]{:S(2)}) collective-permute-start(bf16[2,2,4,24,768]{4,3,2,1,0:T(8,128)(2,1)} %get-tuple-element.578), channel_id=1, source_target_pairs={{0,8},{1,9},{2,10},{3,11},{4,12},{5,13},{6,14},{7,15},{8,0},{9,1},... | collective-permute-start | bytes 1769480 | tf_op jit(solution)/shard_map/ppermute | solution.py:633
  291.1 42.8 %collective-permute-start.8 = (bf16[2,2,4,24,768]{4,3,2,1,0:T(8,128)(2,1)}, bf16[2,2,4,24,768]{4,3,2,1,0:T(8,128)(2,1)}, u32[]{:S(2)}, u32[]{:S(2)}) collective-permute-start(bf16[2,2,4,24,768]{4,3,2,1,0:T(8,128)(2,1)} %get-tuple-element.577), channel_id=1, source_target_pairs={{0,16},{1,17},{2,18},{3,19},{4,20},{5,21},{6,22},{7,23},{8,24},{9,... | collective-permute-start | bytes 1769480 | tf_op jit(solution)/shard_map/ppermute | solution.py:633
  294.1 39.8 %collective-permute-start.9 = (bf16[2,2,4,24,768]{4,3,2,1,0:T(8,128)(2,1)}, bf16[2,2,4,24,768]{4,3,2,1,0:T(8,128)(2,1)}, u32[]{:S(2)}, u32[]{:S(2)}) collective-permute-start(bf16[2,2,4,24,768]{4,3,2,1,0:T(8,128)(2,1)} %get-tuple-element.576), channel_id=1, source_target_pairs={{0,24},{1,25},{2,26},{3,27},{4,28},{5,29},{6,30},{7,31},{8,16},{9,... | collective-permute-start | bytes 1769480 | tf_op jit(solution)/shard_map/ppermute | solution.py:633
  304.7 11.9 %copy-start.14 = (bf16[2,4,2,24,768]{4,3,2,1,0:T(8,128)(2,1)}, bf16[2,4,2,24,768]{4,3,2,1,0:T(8,128)(2,1)S(1)}, u32[]{:S(2)}) copy-start(bf16[2,4,2,24,768]{4,3,2,1,0:T(8,128)(2,1)S(1)} %collective-permute-done.3) | copy-start | bytes 1769476
  333.9 68.2 %all-to-all-start.9 = ((bf16[32,32,768]{2,1,0:T(8,128)(2,1)}), bf16[32,32,768]{2,1,0:T(8,128)(2,1)}, u32[]{:S(2)}, u32[]{:S(2)}) async-start(bf16[32,32,768]{2,1,0:T(8,128)(2,1)} %bitcast.183), calls=%async_computation.9 | async-start | bytes 3145728 | tf_op jit(solution)/shard_map/all_to_all | solution.py:40
  347.7 10.4 %copy-start.16 = (f32[512,24]{0,1:T(8,128)S(1)}, f32[512,24]{0,1:T(8,128)}, u32[]{:S(2)}) copy-start(f32[512,24]{0,1:T(8,128)} %param.34) | copy-start | bytes 147460
  347.7 11.3 %copy-start.19 = (f32[512,24]{0,1:T(8,128)S(1)}, f32[512,24]{0,1:T(8,128)}, u32[]{:S(2)}) copy-start(f32[512,24]{0,1:T(8,128)} %param.41) | copy-start | bytes 147460
  347.7 12.1 %copy-start.20 = (f32[512,24]{0,1:T(8,128)S(1)}, f32[512,24]{0,1:T(8,128)}, u32[]{:S(2)}) copy-start(f32[512,24]{0,1:T(8,128)} %param.48) | copy-start | bytes 147460
  357.6 11.5 %collective-permute-start.18 = (bf16[2,2,4,2,24,768]{5,4,3,2,1,0:T(8,128)(2,1)}, bf16[2,2,4,2,24,768]{5,4,3,2,1,0:T(8,128)(2,1)}, u32[]{:S(2)}, u32[]{:S(2)}) collective-permute-start(bf16[2,2,4,2,24,768]{5,4,3,2,1,0:T(8,128)(2,1)} %get-tuple-element.269), channel_id=1, source_target_pairs={{0,1},{1,0},{2,3},{3,2},{4,5},{5,4},{6,7},{7,6},{8,9},{9,8},{10,11... | collective-permute-start | bytes 3538952 | tf_op jit(solution)/shard_map/ppermute | solution.py:633
  358.0 13.1 %collective-permute-start.15 = (bf16[2,2,4,2,24,768]{5,4,3,2,1,0:T(8,128)(2,1)}, bf16[2,2,4,2,24,768]{5,4,3,2,1,0:T(8,128)(2,1)}, u32[]{:S(2)}, u32[]{:S(2)}) collective-permute-start(bf16[2,2,4,2,24,768]{5,4,3,2,1,0:T(8,128)(2,1)} %get-tuple-element.267), channel_id=1, source_target_pairs={{0,1},{1,0},{2,3},{3,2},{4,5},{5,4},{6,7},{7,6},{8,9},{9,8},{10,11... | collective-permute-start | bytes 3538952 | tf_op jit(solution)/shard_map/ppermute | solution.py:633
  363.4 3.7 copy-start.15
  363.5 5.6 %copy-start.10 = (bf16[2,2,4,2,24,768]{5,4,3,2,1,0:T(8,128)(2,1)S(1)}, bf16[2,2,4,2,24,768]{5,4,3,2,1,0:T(8,128)(2,1)}, u32[]{:S(2)}) copy-start(bf16[2,2,4,2,24,768]{5,4,3,2,1,0:T(8,128)(2,1)} %get-tuple-element.268) | copy-start | bytes 3538948
  363.5 12.7 %collective-permute-start.13 = (bf16[2,4,24,768]{3,2,1,0:T(8,128)(2,1)S(1)}, bf16[2,4,24,768]{3,2,1,0:T(8,128)(2,1)S(1)}, u32[]{:S(2)}, u32[]{:S(2)}) collective-permute-start(bf16[2,4,24,768]{3,2,1,0:T(8,128)(2,1)S(1)} %dynamic-slice_bitcast_fusion), channel_id=1, source_target_pairs={{0,2},{1,3},{2,0},{3,1},{4,6},{5,7},{6,4},{7,5},{8,10},{9,11},{10,... | collective-permute-start | bytes 884744 | tf_op jit(solution)/shard_map/ppermute | solution.py:633
  366.8 35.3 %collective-permute-start.6 = (bf16[4,3,24,768]{3,2,1,0:T(8,128)(2,1)S(1)}, bf16[4,3,24,768]{3,2,1,0:T(8,128)(2,1)S(1)}, u32[]{:S(2)}, u32[]{:S(2)}) collective-permute-start(bf16[4,3,24,768]{3,2,1,0:T(8,128)(2,1)S(1)} %get-tuple-element.588), channel_id=1, source_target_pairs={{0,2},{1,3},{2,0},{3,1},{4,6},{5,7},{6,4},{7,5},{8,10},{9,11},{10,... | collective-permute-start | bytes 1327112 | tf_op jit(solution)/shard_map/ppermute | solution.py:633
  367.3 34.8 %collective-permute-start.5 = (bf16[4,2,24,768]{3,2,1,0:T(8,128)(2,1)S(1)}, bf16[4,2,24,768]{3,2,1,0:T(8,128)(2,1)S(1)}, u32[]{:S(2)}, u32[]{:S(2)}) collective-permute-start(bf16[4,2,24,768]{3,2,1,0:T(8,128)(2,1)S(1)} %get-tuple-element.594), channel_id=1, source_target_pairs={{0,4},{1,5},{2,6},{3,7},{4,0},{5,1},{6,2},{7,3},{8,12},{9,13},{10,... | collective-permute-start | bytes 884744 | tf_op jit(solution)/shard_map/ppermute | solution.py:633
  369.1 2.0 copy-start.9
  370.8 22.8 %collective-permute-start.19 = (bf16[2,4,2,24,768]{4,3,2,1,0:T(8,128)(2,1)S(1)}, bf16[2,4,2,24,768]{4,3,2,1,0:T(8,128)(2,1)S(1)}, u32[]{:S(2)}, u32[]{:S(2)}) collective-permute-start(bf16[2,4,2,24,768]{4,3,2,1,0:T(8,128)(2,1)S(1)} %get-tuple-element.583), channel_id=1, source_target_pairs={{0,4},{1,5},{2,6},{3,7},{4,0},{5,1},{6,2},{7,3},{8,12},{9,13},{10,... | collective-permute-start | bytes 1769480 | tf_op jit(solution)/shard_map/ppermute | solution.py:633
  371.1 3.5 copy-start.3
  372.8 27.6 %collective-permute-start.16 = (bf16[2,4,2,24,768]{4,3,2,1,0:T(8,128)(2,1)S(1)}, bf16[2,4,2,24,768]{4,3,2,1,0:T(8,128)(2,1)S(1)}, u32[]{:S(2)}, u32[]{:S(2)}) collective-permute-start(bf16[2,4,2,24,768]{4,3,2,1,0:T(8,128)(2,1)S(1)} %get-tuple-element.585), channel_id=1, source_target_pairs={{0,2},{1,3},{2,0},{3,1},{4,6},{5,7},{6,4},{7,5},{8,10},{9,11},{10,... | collective-permute-start | bytes 1769480 | tf_op jit(solution)/shard_map/ppermute | solution.py:633
  376.3 38.9 %collective-permute-start.14 = (bf16[4,24,768]{2,1,0:T(8,128)(2,1)S(1)}, bf16[4,24,768]{2,1,0:T(8,128)(2,1)S(1)}, u32[]{:S(2)}, u32[]{:S(2)}) collective-permute-start(bf16[4,24,768]{2,1,0:T(8,128)(2,1)S(1)} %get-tuple-element.596), channel_id=1, source_target_pairs={{0,4},{1,5},{2,6},{3,7},{4,0},{5,1},{6,2},{7,3},{8,12},{9,13},{10,... | collective-permute-start | bytes 442376 | tf_op jit(solution)/shard_map/ppermute | solution.py:633
  394.5 24.9 %collective-permute-start.20 = (bf16[4,2,24,768]{3,2,1,0:T(8,128)(2,1)}, bf16[4,2,24,768]{3,2,1,0:T(8,128)(2,1)}, u32[]{:S(2)}, u32[]{:S(2)}) collective-permute-start(bf16[4,2,24,768]{3,2,1,0:T(8,128)(2,1)} %get-tuple-element.590), channel_id=1, source_target_pairs={{0,2},{1,3},{2,0},{3,1},{4,6},{5,7},{6,4},{7,5},{8,10},{9,11},{10,... | collective-permute-start | bytes 884744 | tf_op jit(solution)/shard_map/ppermute | solution.py:633
  401.4 7.1 %copy-start.23 = (s32[1024]{0:T(1024)S(1)}, s32[1024]{0:T(1024)}, u32[]{:S(2)}) copy-start(s32[1024]{0:T(1024)} %copy-done.22) | copy-start | bytes 12292
  401.4 18.0 %collective-permute-start.17 = (bf16[4,2,24,768]{3,2,1,0:T(8,128)(2,1)}, bf16[4,2,24,768]{3,2,1,0:T(8,128)(2,1)}, u32[]{:S(2)}, u32[]{:S(2)}) collective-permute-start(bf16[4,2,24,768]{3,2,1,0:T(8,128)(2,1)} %get-tuple-element.592), channel_id=1, source_target_pairs={{0,4},{1,5},{2,6},{3,7},{4,0},{5,1},{6,2},{7,3},{8,12},{9,13},{10,... | collective-permute-start | bytes 884744 | tf_op jit(solution)/shard_map/ppermute | solution.py:633
  403.0 16.4 %collective-permute-start.12 = (bf16[5,24,768]{2,1,0:T(8,128)(2,1)}, bf16[5,24,768]{2,1,0:T(8,128)(2,1)}, u32[]{:S(2)}, u32[]{:S(2)}) collective-permute-start(bf16[5,24,768]{2,1,0:T(8,128)(2,1)} %pad_maximum_fusion.3), channel_id=1, source_target_pairs={{0,24},{1,25},{2,26},{3,27},{4,28},{5,29},{6,30},{7,31},{8,16},{9,... | collective-permute-start | bytes 552968 | tf_op jit(solution)/shard_map/ppermute | solution.py:633
  407.7 15.3 %collective-permute-start.11 = (bf16[5,24,768]{2,1,0:T(8,128)(2,1)}, bf16[5,24,768]{2,1,0:T(8,128)(2,1)}, u32[]{:S(2)}, u32[]{:S(2)}) collective-permute-start(bf16[5,24,768]{2,1,0:T(8,128)(2,1)} %pad_maximum_fusion.2), channel_id=1, source_target_pairs={{0,16},{1,17},{2,18},{3,19},{4,20},{5,21},{6,22},{7,23},{8,24},{9,... | collective-permute-start | bytes 552968 | tf_op jit(solution)/shard_map/ppermute | solution.py:633
  408.5 6.8 %copy-start.6 = (bf16[1152,768]{1,0:T(8,128)(2,1)S(1)}, bf16[1152,768]{1,0:T(8,128)(2,1)}, u32[]{:S(2)}) copy-start(bf16[1152,768]{1,0:T(8,128)(2,1)} %broadcast_select_fusion) | copy-start | bytes 5308420
  415.3 0.7 copy-start.17
  415.3 9.6 %collective-permute-start.10 = (bf16[5,24,768]{2,1,0:T(8,128)(2,1)}, bf16[5,24,768]{2,1,0:T(8,128)(2,1)}, u32[]{:S(2)}, u32[]{:S(2)}) collective-permute-start(bf16[5,24,768]{2,1,0:T(8,128)(2,1)} %pad_maximum_fusion.1), channel_id=1, source_target_pairs={{0,8},{1,9},{2,10},{3,11},{4,12},{5,13},{6,14},{7,15},{8,0},{9,1},... | collective-permute-start | bytes 552968 | tf_op jit(solution)/shard_map/ppermute | solution.py:633
  416.1 8.7 %copy-start.11 = (bf16[4,2,24,768]{3,2,1,0:T(8,128)(2,1)S(1)}, bf16[4,2,24,768]{3,2,1,0:T(8,128)(2,1)}, u32[]{:S(2)}) copy-start(bf16[4,2,24,768]{3,2,1,0:T(8,128)(2,1)} %get-tuple-element.278) | copy-start | bytes 884740
  416.1 8.7 %copy-start.12 = (bf16[4,2,24,768]{3,2,1,0:T(8,128)(2,1)S(1)}, bf16[4,2,24,768]{3,2,1,0:T(8,128)(2,1)}, u32[]{:S(2)}) copy-start(bf16[4,2,24,768]{3,2,1,0:T(8,128)(2,1)} %get-tuple-element.276) | copy-start | bytes 884740
  426.2 6.3 %copy-start.18 = (bf16[4,24,768]{2,1,0:T(8,128)(2,1)S(1)}, bf16[4,24,768]{2,1,0:T(8,128)(2,1)}, u32[]{:S(2)}) copy-start(bf16[4,24,768]{2,1,0:T(8,128)(2,1)} %copy-done.17) | copy-start | bytes 442372
  426.2 8.9 %copy-start.13 = (bf16[5,24,768]{2,1,0:T(8,128)(2,1)S(1)}, bf16[5,24,768]{2,1,0:T(8,128)(2,1)}, u32[]{:S(2)}) copy-start(bf16[5,24,768]{2,1,0:T(8,128)(2,1)} %pad_maximum_fusion) | copy-start | bytes 552964
  426.2 12.1 %collective-permute-start.21 = (bf16[4,24,768]{2,1,0:T(8,128)(2,1)S(1)}, bf16[4,24,768]{2,1,0:T(8,128)(2,1)S(1)}, u32[]{:S(2)}, u32[]{:S(2)}) collective-permute-start(bf16[4,24,768]{2,1,0:T(8,128)(2,1)S(1)} %pad_maximum_fusion.4), channel_id=1, source_target_pairs={{0,8},{1,9},{2,10},{3,11},{4,12},{5,13},{6,14},{7,15},{8,0},{9,1},... | collective-permute-start | bytes 442376 | tf_op jit(solution)/shard_map/ppermute | solution.py:633
  428.0 13.2 %collective-permute-start.22 = (bf16[4,24,768]{2,1,0:T(8,128)(2,1)S(1)}, bf16[4,24,768]{2,1,0:T(8,128)(2,1)S(1)}, u32[]{:S(2)}, u32[]{:S(2)}) collective-permute-start(bf16[4,24,768]{2,1,0:T(8,128)(2,1)S(1)} %pad_maximum_fusion.5), channel_id=1, source_target_pairs={{0,16},{1,17},{2,18},{3,19},{4,20},{5,21},{6,22},{7,23},{8,24},{9,... | collective-permute-start | bytes 442376 | tf_op jit(solution)/shard_map/ppermute | solution.py:633
  431.0 11.3 %collective-permute-start.23 = (bf16[4,24,768]{2,1,0:T(8,128)(2,1)S(1)}, bf16[4,24,768]{2,1,0:T(8,128)(2,1)S(1)}, u32[]{:S(2)}, u32[]{:S(2)}) collective-permute-start(bf16[4,24,768]{2,1,0:T(8,128)(2,1)S(1)} %pad_maximum_fusion.6), channel_id=1, source_target_pairs={{0,24},{1,25},{2,26},{3,27},{4,28},{5,29},{6,30},{7,31},{8,16},{9,... | collective-permute-start | bytes 442376 | tf_op jit(solution)/shard_map/ppermute | solution.py:633
  443.5 18.7 %copy-start.1 = (f32[960,768]{1,0:T(8,128)S(1)}, f32[960,768]{1,0:T(8,128)}, u32[]{:S(2)}) copy-start(f32[960,768]{1,0:T(8,128)} %get-tuple-element.253.g_embed) | copy-start | bytes 8847364
  446.8 1.1 copy-start.2
  450.6 10.2 %all-to-all-start.10 = ((f32[32,1,2]{2,1,0:T(1,128)}), f32[32,1,2]{2,1,0:T(1,128)S(1)}, u32[]{:S(2)}, u32[]{:S(2)}) async-start(f32[32,1,2]{2,1,0:T(1,128)} %broadcast_in_dim.189), calls=%async_computation.10 | async-start | bytes 32768 | tf_op jit(solution)/shard_map/all_to_all | solution.py:40
Sparse Core Ops, SparseCore 0:
  13.9 144.1 all-gather.1

commit v7 on v6

--- a/solution.py
+++ b/solution.py
@@ -18,6 +18,8 @@
 GROUP = 128
 ROWS = 288
 BLOCKS = 4
+TIMES = dict(first=10, attend=12, middle=24, back=20, out_grads=9, in_grads=11, attend_back=11, last=12, rest_grads=6, query_key_grads=6)
+PACE = 1e+06
 SIZES = (128, 256, 384, 512)
 AXES = ("dp", "seq")
 bf = jnp.bfloat16
@@ -385,12 +387,16 @@
         pl.when(plan[3] == count)(functools.partial(run, count * ROWS))
 
 
-def out_grads_kernel(depth, turns, plan, act, d_y, *outs):
+def out_grads_kernel(depth, turns, plan, act, d_y, h1, d_f, *outs):
+    width = d_y.shape[1]
+
     def run(rows):
         g = dot_tn(act[:rows], d_y[:rows])
-        g = g.reshape(16, turns, depth, g.shape[1])
+        g = g.reshape(16, turns, depth, width)
         for j in range(turns):
-            put_split(outs, "zxy", j, g[:, j], plan[4])
+            put_split(outs, "xyz", j, g[:, j], plan[4])
+        for j in range(turns // 2):
+            put_split(outs, "xyz", turns + j, blocks(dot_tn(h1[:rows], d_f[:rows, j * width : (j + 1) * width]), depth), plan[4])
 
     by_blocks(plan, run)
 
@@ -399,32 +405,33 @@
     width = d_a.shape[1]
 
     def run(rows):
-        for j in range(turns):
-            g = blocks(dot_tn(h1[:rows], d_f[:rows, j * width : (j + 1) * width]), depth)
-            if j < 2:
-                put_split(outs[:2], "xyz", j, g, plan[4])
-            else:
-                put_split(outs[2:], "yxz", j - 2, g, plan[4])
-        put_split(outs[2:], "yxz", turns - 2, blocks(dot_tn(mixed[:rows], d_a[:rows]), depth), plan[4])
+        for j in range(turns // 2):
+            put_split(outs, "yxz", j, blocks(dot_tn(h1[:rows], d_f[:rows, j * width : (j + 1) * width]), depth), plan[4])
+        put_split(outs, "yxz", turns // 2, blocks(dot_tn(mixed[:rows], d_a[:rows]), depth), plan[4])
 
     by_blocks(plan, run)
 
 
-def rest_grads_kernel(depth, length, plan, spot_in, hin, d_proj, d_x, sums_0, sums, sums_ff, *outs):
-    width = d_proj.shape[2]
+def query_key_grads_kernel(depth, plan, hin, d_proj, *outs):
+    def run(rows):
+        for i in range(2):
+            put_split(outs, "xyz", i, blocks(dot_tn(hin[:rows], d_proj[i, :rows]), depth), plan[4])
+
+    by_blocks(plan, run)
+
+
+def rest_grads_kernel(depth, length, plan, spot_in, hin, d_value, d_x, sums_0, sums, sums_ff, *outs):
+    width = d_value.shape[2]
     part = hin.shape[1]
 
-    def put(kind, g):
-        put_split(outs[:2] if kind < 2 else outs[2:], "xyz" if kind < 2 else "yxz", kind % 2, blocks(g, depth), plan[4])
-
     def run(rows):
-        for i in range(3):
-            put(i, dot_tn(hin[:rows], d_proj[i, :rows]))
+        put_split(outs, "yxz", 0, blocks(dot_tn(hin[:rows], d_value[0, :rows]), depth), plan[4])
         line = jnp.where(spot_in[:rows] == iota((rows, length), 1), 1.0, 0.0).astype(bf)
         g_pos = dot_tn(d_x[:rows], line)
         vec = jnp.concatenate([sums_0[:4], sums[:3], sums_ff[...], sums[3:6]], axis=0)
         vec = jnp.concatenate([vec, jnp.zeros((128 - vec.shape[0], part), f32)], axis=0)
-        put(3, jnp.concatenate([g_pos, vec.T, jnp.zeros((part, width - length - 128), f32)], axis=1))
+        both = jnp.concatenate([g_pos, vec.T, jnp.zeros((part, width - length - 128), f32)], axis=1)
+        put_split(outs, "yxz", 1, blocks(both, depth), plan[4])
 
     by_blocks(plan, run)
 
@@ -458,8 +465,8 @@
         one(6, every, g_vectors[...])
 
 
-def cost(flops, nbytes):
-    return pl.CostEstimate(flops=int(flops), bytes_accessed=int(nbytes), transcendentals=0)
+def cost(micros):
+    return pl.CostEstimate(flops=0, bytes_accessed=int(micros * PACE), transcendentals=0)
 
 
 def run_forward_backward(full, back, extra, slots, spots, plan, meet, staged, devices, depth, length, hidden):
@@ -482,6 +489,7 @@
             ),
             out_shape=out_shape,
             compiler_params=params(60),
+            cost_estimate=cost(TIMES[name]),
             name=name,
             **more,
         )
@@ -564,18 +572,21 @@
     if staged:
         z, y, x_at = place_in_slice()
         dense_out = split_call(
-            functools.partial(out_grads_kernel, depth, turns), [halves(hidden // 2), fixed((rows, width), (0, 0))], [("zxy", turns)], "out_grads"
-        )(plan, act, d_y)
+            functools.partial(out_grads_kernel, depth, turns),
+            [halves(hidden // 2), fixed((rows, width), (0, 0)), halves(part), fixed((rows, hidden // 2), (0, 0))],
+            [("xyz", turns + turns // 2)],
+            "out_grads",
+        )(plan, act, d_y, h1, d_f)
         dense_out = over_cores(*dense_out)
         dense_in = split_call(
             functools.partial(in_grads_kernel, depth, turns),
-            [halves(part), fixed((rows, hidden), (0, 0)), halves(part), fixed((rows, width), (0, 0))],
-            [("xyz", 2), ("yxz", turns - 1)],
+            [halves(part), fixed((rows, hidden // 2), (0, 1)), halves(part), fixed((rows, width), (0, 0))],
+            [("yxz", turns // 2 + 1)],
             "in_grads",
         )(plan, h1, d_f, mixed, d_a)
         d_o, dense_out, dense_in = lax.optimization_barrier((d_o, dense_out, dense_in))
-        dense_in = over_cores(*dense_in[:2]), over_cores(*dense_in[2:])
-        dense_out = over_long(dense_out, z)
+        dense_in = over_cores(*dense_in)
+        dense_out = halve(dense_out, x_at, 2)
     else:
         dense_out = dot_tn(clean(act), clean(d_y)).astype(bf)
         dense_in = jnp.concatenate([dot_tn(clean(h1), clean(d_f)), dot_tn(clean(mixed), clean(d_a))], axis=1).astype(bf)
@@ -589,16 +600,23 @@
             shape((3, rows, width), bf),
             "attend_back",
             input_output_aliases={5: 0} if more else {},
-            cost_estimate=cost(10 * length * length * GROUP * count, 8 * rows * GROUP * count * 2),
         )(plan, qkv, qkv, qkv, d_o, *more)
 
-    d_proj = attend_back(0, pairs // 2, None)
+    d_proj = attend_back(0, pairs, None)
     if staged:
         d_proj, dense_in = lax.optimization_barrier((d_proj, dense_in))
-        dense_in = halve(dense_in[0], x_at, 2), halve(dense_in[1], y, 4)
-    d_proj = attend_back(pairs // 2, pairs - pairs // 2, d_proj)
+        in_sums = two_sums(dense_in, y)
+        d_proj, in_sums = lax.optimization_barrier((d_proj, in_sums))
+        dense_in = in_sums[0], swap(in_sums[1], 4, 32)
     if staged:
-        d_proj, dense_in = lax.optimization_barrier((d_proj, dense_in))
+        first_rest = split_call(
+            functools.partial(query_key_grads_kernel, depth),
+            [halves(part), pl.BlockSpec((2, rows, width), lambda i, *_: (0, 0, 0), pipeline_mode=pl.Buffered(1))],
+            [("xyz", 2)],
+            "query_key_grads",
+        )(plan, hin, d_proj)
+        d_proj, dense_out, first_rest = lax.optimization_barrier((d_proj, dense_out, first_rest))
+        first_rest = over_cores(*first_rest)
 
     d_xb, sums_0, give_rows = call(
         when_live(last_kernel), 1, (BLOCKS,),
@@ -612,14 +630,22 @@
     )(plan, slots[:, None], x, d_r1, d_proj, full, vec)
 
     if staged:
-        give_rows, dense_out = lax.optimization_barrier((give_rows, dense_out))
+        give_rows, dense_in = lax.optimization_barrier((give_rows, dense_in))
+        out_sums, in_sums = two_sums(dense_out, y), two_sums(dense_in, x_at)
+        d_xb, out_sums, in_sums = lax.optimization_barrier((d_xb, out_sums, in_sums))
+        dense_out = out_sums[0], swap(out_sums[1], 4, 32)
+        dense_in = in_sums[0], swap(in_sums[1], 2, 32)
         cols = lambda count: pl.BlockSpec((count, part), lambda i, *_: (0, i))
         rest = split_call(
             functools.partial(rest_grads_kernel, depth, length),
-            [fixed((rows, 1), (0, 0)), halves(part), fixed((3, rows, width), (0, 0, 0)), halves(part), cols(8), cols(8), cols(turns)],
-            [("xyz", 2), ("yxz", 2)],
+            [
+                fixed((rows, 1), (0, 0)), halves(part), pl.BlockSpec((1, rows, width), lambda i, *_: (2, 0, 0), pipeline_mode=pl.Buffered(1)),
+                halves(part), cols(8), cols(8), cols(turns),
+            ],
+            [("yxz", 2)],
             "rest_grads",
         )(plan, spots[:, None], hin, d_proj, d_xb, sums_0, sums, sums_ff)
+        rest = first_rest, over_cores(*rest)
     else:
         g_vec = jnp.concatenate([sums_0[:4], sums[:3], sums_ff, sums[3:6]], axis=0)
         g_pos = dot_tn(clean(d_xb), one_hot(spots, length))
@@ -654,12 +680,24 @@
     return add(spot(pair[0], 0, index), spot(pair[1], 0, index))
 
 
+def two_sums(pair, index):
+    return part_sum(pair, index), part_sum(pair, 1 - index)
+
+
 def halve(pair, index, bit):
     return part_sum(pair, index), swap(part_sum(pair, 1 - index), bit, 32)
 
 
 def over_long(pair, z):
     return [part_sum(pair, z)] + [swap(part_sum(pair, z ^ step), 8 * step, 32) for step in range(1, 4)]
+
+
+def z_parts(one, two, z):
+    return [jnp.concatenate([part_sum(one, z ^ step), part_sum(two, z ^ step)], axis=0) for step in range(4)]
+
+
+def z_swaps(parts):
+    return parts[:1] + [swap(parts[step], 8 * step, 32) for step in range(1, 4)]
 
 
 def over_long_both(one, two, z):
@@ -774,22 +812,20 @@
     give_rows = exchange(give_rows.reshape(devices, room, width))
     if staged:
         z, y, x = place_in_slice()
-        dense_in = halve(dense_in[0], y, 4), halve(dense_in[1], x, 2)
-        dense_out = total_of(dense_out).astype(bf)
-        dense_out = spot(dense_out, 0, x), swap(spot(dense_out, 0, 1 - x), 2, 32)
-        rest = halve(over_cores(*rest[:2]), x, 2), halve(over_cores(*rest[2:]), y, 4)
-        dense_in, give_rows = lax.optimization_barrier((dense_in, give_rows))
-        dense_in = over_long_both(*dense_in, z)
-        dense_out = halve(dense_out, y, 4)
+        parts = z_parts(dense_out, dense_in, z)
+        parts, rest = lax.optimization_barrier((parts, rest))
+        dense = z_swaps(parts)
+        rest = halve(rest[0], x, 2), halve(rest[1], y, 4)
         rest = halve(rest[0], y, 4), halve(rest[1], x, 2)
-        dense_in, dense_out, rest = lax.optimization_barrier((dense_in, dense_out, rest))
+        dense, rest, give_rows = lax.optimization_barrier((dense, rest, give_rows))
         rest = over_long_both(*rest, z)
-        dense_out, dense_in, rest = total_of(dense_out), total_of(dense_in), total_of(rest)
+        dense, rest = total_of(dense), total_of(rest)
+        dense_out, dense_in = dense[:turns], dense[turns:]
     else:
         sum_up = lambda parts: lax.psum_scatter(parts, AXES, scatter_dimension=0, tiled=True).astype(f32)
         kinds = lambda v: v.reshape(depth, -1, width).transpose(1, 0, 2)
         dense_out, dense_in, rest = sum_up(dense_out).reshape(turns, depth, width), kinds(sum_up(dense_in)), kinds(sum_up(rest))
-    g_position = rest[3, :, :length].T
+    g_position = rest[3, :, :length]
     g_vectors = rest[3, :, length : length + nvec].T
 
     def give(wanted, there):
@@ -810,9 +846,9 @@
     loss_sum = sums[1]
     scale = jnp.minimum(1.0, CLIP / (norm + 1e-06))
     state = (
-        embed, position, attn_in, attn_out, ff_in, ff_out, vectors,
-        mom_embed, mom_position, mom_attn_in, mom_attn_out, mom_ff_in, mom_ff_out, mom_vectors,
-        avg_embed, avg_position, avg_attn_in, avg_attn_out, avg_ff_in, avg_ff_out, avg_vectors,
+        embed, position.T, attn_in, attn_out, ff_in, ff_out, vectors,
+        mom_embed, mom_position.T, mom_attn_in, mom_attn_out, mom_ff_in, mom_ff_out, mom_vectors,
+        avg_embed, avg_position.T, avg_attn_in, avg_attn_out, avg_ff_in, avg_ff_out, avg_vectors,
     )
     steps = next(n for n in (8, 5, 4, 3, 2, 1) if per_owner % (8 * n) == 0 or n == 1)
     strip = pl.BlockSpec((per_owner // steps, width), lambda i, *_: (i, 0))
@@ -828,6 +864,7 @@
         compiler_params=params(60),
         name="update",
     )(scale[None], *inputs)
+    done = [v.T if i % 7 == 1 else v for i, v in enumerate(done)]
     return (loss_sum, count, norm, *done)
 
 

time: 497 us -> 476 us (0.958)
  starting transfers between devices: 66 us -> 51 us
  local copies, waits for them, and re-layouts: 35.3 us -> 27.2 us
    all_to_all x7, starting transfers between devices: 37.6 us -> 27.7 us  [exchange(): return lax.all_to_all(v, AXES, 0, 0, tiled=True)]
    unnamed x68 -> x38, local copies, waits for them, and re-layouts: 11.1 us -> 2.86 us
    pallas_call x0 -> x1, Pallas kernels: none -> 6.68 us  [run_forward_backward(): split_call(functools.partial(query_key_grads_kernel, depth), [halves(part...]
    ppermute x24 -> x18, starting transfers between devices: 28.4 us -> 23.3 us  [swap(): return lax.ppermute(v, AXES, [(i, i ^ bit) for i in range(devices)])]
    ppermute x24 -> x18, waiting for transfers between devices: 44.6 us -> 48.6 us  [swap(): return lax.ppermute(v, AXES, [(i, i ^ bit) for i in range(devices)])]
    pallas_call x2 -> x1, Pallas kernels: 21.8 us -> 18.3 us  [attend_back(): call(attend_back_kernel, 1, (count,), [block(0, start), block(1, start),...]
    convert_element_type x13 -> x11, other arithmetic: 16.9 us -> 18.3 us  [add(): return (a.astype(f32) + b.astype(f32)).astype(bf)]
  transfers between devices with their start and end apart: 32 -> 26, of which waited for: 14 -> 13; matrix products, arithmetic and copies ran while one was open for 15% -> 16% of each run, Pallas kernels for 11% -> 11%
where the time goes in v7:
time: 476 us; the launch traced here: 468 us
  Pallas kernels  144 us (30%)
  waiting for transfers between devices  141 us (30%)
  other arithmetic  56.5 us (12%)
  starting transfers between devices  51 us (11%)
  between operations  38.4 us (8%)
  local copies, waits for them, and re-layouts  27.2 us (6%)
  matrix products  9.77 us (2%)
    all_to_all x7, waiting for transfers between devices, exchange(): return lax.all_to_all(v, AXES, 0, 0, tiled=True)  89.7 us
    ppermute x18, waiting for transfers between devices, swap(): return lax.ppermute(v, AXES, [(i, i ^ bit) for i in range(devices)])  48.6 us
    all_to_all x7, starting transfers between devices, exchange(): return lax.all_to_all(v, AXES, 0, 0, tiled=True)  27.7 us
    pallas_call x1, Pallas kernels, run_forward_backward(): call(when_live(functools.partial(middle_kernel, staged, depth, turns)), 1...  24.5 us
    ppermute x18, starting transfers between devices, swap(): return lax.ppermute(v, AXES, [(i, i ^ bit) for i in range(devices)])  23.3 us
    pallas_call x1, Pallas kernels, run_forward_backward(): call(when_live(back_kernel), 3, (BLOCKS,), [fixed((8, width), (0, 0)), fi...  19.8 us
    pallas_call x1, Pallas kernels, attend_back(): call(attend_back_kernel, 1, (count,), [block(0, start), block(1, start),...  18.3 us
    convert_element_type x11, other arithmetic, add(): return (a.astype(f32) + b.astype(f32)).astype(bf)  18.3 us
  transfers between devices with their start and end apart: 26, of which 13 were waited for; matrix products, arithmetic and copies ran while one was open for 16% of the time, Pallas kernels for 11%

profile of v7, /device:TPU:0, one launch (start us, length us, event | category | flops | bytes accessed | tf_op | source)
XLA Modules:
  0.0 467.7 jit_solution(11997179719493603379)
XLA Ops:
  14.8 7.3 %all-to-all-start.4 = ((s32[32,9,128]{2,1,0:T(8,128)}), s32[32,9,128]{2,1,0:T(8,128)S(1)}, u32[]{:S(2)}, u32[]{:S(2)}) async-start(s32[32,9,128]{2,1,0:T(8,128)} %broadcast_in_dim.172), calls=%async_computation.4 | async-start | bytes 524288 | tf_op jit(solution)/shard_map/all_to_all | solution.py:42
  22.2 12.6 %all-to-all-done.4 = s32[32,9,128]{2,1,0:T(8,128)S(1)} async-done(((s32[32,9,128]{2,1,0:T(8,128)}), s32[32,9,128]{2,1,0:T(8,128)S(1)}, u32[]{:S(2)}, u32[]{:S(2)}) %all-to-all-start.4) | async-done | bytes 147488 | tf_op jit(solution)/shard_map/all_to_all | solution.py:42
  40.3 2.0 fusion.83
  48.7 1.7 convert_reduce_fusion
  50.4 1.9 and_select_fusion.3
  54.4 4.2 all-to-all-start.5
  58.6 1.3 convert_element_type.536
  59.9 5.9 %all-to-all-done.5 = s32[32,1,128]{2,1,0:T(1,128)S(1)} async-done(((s32[32,1,128]{2,1,0:T(1,128)}), s32[32,1,128]{2,1,0:T(1,128)S(1)}, u32[]{:S(2)}, u32[]{:S(2)}) %all-to-all-start.5) | async-done | bytes 16416 | tf_op jit(solution)/shard_map/all_to_all | solution.py:42
  65.9 4.5 fusion.34
  71.0 3.2 all-to-all-start.7
  75.6 5.7 %all-to-all-done.7 = f32[32,1,4]{2,1,0:T(1,128)} async-done(((f32[32,1,4]{2,1,0:T(1,128)}), f32[32,1,4]{2,1,0:T(1,128)}, u32[]{:S(2)}, u32[]{:S(2)}) %all-to-all-start.7) | async-done | bytes 544 | tf_op jit(solution)/shard_map/all_to_all | solution.py:42
  81.7 2.7 all-to-all-start.6
  86.6 1.3 and_select_fusion.2
  89.0 1.9 stack.74.refs_0_.plan
  90.9 1.6 select_select_fusion.refs_2_.spot_in
  92.5 63.0 %all-to-all-done.6 = bf16[32,32,768]{2,1,0:T(8,128)(2,1)S(1)} async-done(((bf16[32,32,768]{2,1,0:T(8,128)(2,1)}), bf16[32,32,768]{2,1,0:T(8,128)(2,1)S(1)}, u32[]{:S(2)}, u32[]{:S(2)}) %all-to-all-start.6) | async-done | bytes 1572896 | tf_op jit(solution)/shard_map/all_to_all | solution.py:42
  155.5 2.4 all-gather.2.cloned.1.call-done.refs_5_.refs_6_.refs_7_.refs_3_.refs_4_.refs_8_.refs_9_
  158.0 10.4 %first.1 = (f32[1152,768]{1,0:T(8,128)}, bf16[1152,768]{1,0:T(8,128)(2,1)}, bf16[1152,2304]{1,0:T(8,128)(2,1)}, f32[16,768]{1,0:T(8,128)}) custom-call(s32[5]{0:T(128)} %stack.74.refs_0_.plan, s32[1152,1]{1,0:T(8,128)} %broadcast_in_dim.197.refs_1_, s32[1152,1]{1,0:T(8,128)} %select_select_fusion.refs_2_.spot_in, bf16[1024,768]{1,0:T(8,128)(2,1)} %bitcast.162, ...), custom_call_target="tpu_custom_call" | custom-call | bytes 10000000 | tf_op jit(solution)/shard_map/first/pallas_call | solution.py:510
  168.3 12.6 %attend.1.refs_2_.mixed = bf16[1152,768]{1,0:T(8,128)(2,1)} custom-call(s32[5]{0:T(128)} %stack.74.refs_0_.plan, bf16[1152,2304]{1,0:T(8,128)(2,1)} %get-tuple-element.214.query.keys.values, bf16[1152,2304]{1,0:T(8,128)(2,1)} %get-tuple-element.214.query.keys.values, bf16[1152,2304]{1,0:T(8,128)(2,1)} %get-tuple-element.214.query.keys.values), custom_call_target="tpu_custom_call" | custom-call | bytes 12000000 | tf_op jit(solution)/shard_map/attend/pallas_call | solution.py:522
  182.4 24.5 %middle.1 = (f32[1152,768]{1,0:T(8,128)}, bf16[1152,768]{1,0:T(8,128)(2,1)}, bf16[1152,3072]{1,0:T(8,128)(2,1)}, bf16[1152,3072]{1,0:T(8,128)(2,1)}, f32[1152,76...) custom-call(s32[5]{0:T(128)} %stack.74.refs_0_.plan, f32[1152,768]{1,0:T(8,128)} %get-tuple-element.213.refs_1_.refs_2_, ...), custom_call_target="tpu_custom_call" | custom-call | bytes 24000000 | tf_op jit(solution)/shard_map/middle/pallas_call | solution.py:527
  208.4 2.8 all-to-all-start.8
  221.4 2.0 stack.86.refs_1_
  224.8 19.8 %back.1 = (bf16[1152,768]{1,0:T(8,128)(2,1)}, bf16[1152,3072]{1,0:T(8,128)(2,1)}, f32[1152,768]{1,0:T(8,128)}, bf16[1152,768]{1,0:T(8,128)(2,1)}, bf16[1152,768]...) custom-call(s32[5]{0:T(128)} %stack.74.refs_0_.plan, f32[11]{0:T(128)} %stack.86.refs_1_, ...), custom_call_target="tpu_custom_call" | custom-call | bytes 20000000 | tf_op jit(solution)/shard_map/back/pallas_call | solution.py:540
  244.6 12.5 %out_grads.1 = (bf16[2,2,4,6,24,768]{5,4,3,2,1,0:T(8,128)(2,1)}, bf16[2,2,4,6,24,768]{5,4,3,2,1,0:T(8,128)(2,1)}) custom-call(s32[5]{0:T(128)} %stack.74.refs_0_.plan, bf16[1152,3072]{1,0:T(8,128)(2,1)} %get-tuple-element.223.act, bf16[1152,768]{1,0:T(8,128)(2,1)} %get-tuple-element.224.d_y, bf16[1152,768]{1,0:T(8,128)(2,1)} %get-tuple-element.225.h1, ...), custom_call_target="tpu_custom_call" | custom-call | bytes 9000000 | tf_op jit(solution)/shard_map/out_grads/pallas_call | solution.py:574
  257.3 8.5 %in_grads.1 = (bf16[2,2,4,3,24,768]{5,4,3,2,1,0:T(8,128)(2,1)}, bf16[2,2,4,3,24,768]{5,4,3,2,1,0:T(8,128)(2,1)}) custom-call(s32[5]{0:T(128)} %stack.74.refs_0_.plan, bf16[1152,768]{1,0:T(8,128)(2,1)} %get-tuple-element.225.h1, bf16[1152,3072]{1,0:T(8,128)(2,1)} %get-tuple-element.226.d_f, bf16[1152,768]{1,0:T(8,128)(2,1)} %attend.1.refs_2_.mixed, ...), custom_call_target="tpu_custom_call" | custom-call | bytes 11000000 | tf_op jit(solution)/shard_map/in_grads/pallas_call | solution.py:581
  266.1 5.1 %fusion.33 = (bf16[2,4,6,24,768]{4,3,2,1,0:T(8,128)(2,1)}, bf16[2,4,6,24,768]{4,3,2,1,0:T(8,128)(2,1)S(1)}) fusion(bf16[2,2,4,6,24,768]{5,4,3,2,1,0:T(8,128)(2,1)} %collective-permute-done, s32[]{:T(128)S(6)} %select_n.352, bf16[2,2,4,6,24,768]{5,4,3,2,1,0:T(8,128)(2,1)} %get-tuple-element.239, s32[]{:T(128)S(6)} %select_n.351), kind=kLoop, calls=%fused_computation.60 | loop fusion | flops 7077888 | bytes 10616840 | tf_op jit(solution)/shard_map/convert_element_type | solution.py:663
  271.3 1.8 collective-permute-start.2
  273.1 18.3 %attend_back.1.d_proj.refs_4_.d_value = bf16[3,1152,768]{2,1,0:T(8,128)(2,1)} custom-call(s32[5]{0:T(128)} %stack.74.refs_0_.plan, bf16[1152,2304]{1,0:T(8,128)(2,1)} %get-tuple-element.214.query.keys.values, bf16[1152,2304]{1,0:T(8,128)(2,1)} %get-tuple-element.214.query.keys.values, bf16[1152,2304]{1,0:T(8,128)(2,1)} %get-tuple-element.214.query.keys.values, ...), custom_call_target="tpu_custom_call" | custom-call | bytes 11000000 | tf_op jit(solution)/shard_map/attend_back/pallas_call | solution.py:596
  291.4 3.3 fusion.36
  294.7 1.5 collective-permute-start.3
  296.2 6.7 %query_key_grads.1 = (bf16[2,2,4,2,24,768]{5,4,3,2,1,0:T(8,128)(2,1)}, bf16[2,2,4,2,24,768]{5,4,3,2,1,0:T(8,128)(2,1)}) custom-call(s32[5]{0:T(128)} %stack.74.refs_0_.plan, bf16[1152,768]{1,0:T(8,128)(2,1)} %get-tuple-element.241.hin, bf16[3,1152,768]{2,1,0:T(8,128)(2,1)} %attend_back.1.d_proj.refs_4_.d_value), custom_call_target="tpu_custom_call" | custom-call | bytes 6000000 | tf_op jit(solution)/shard_map/query_key_grads/pallas_call | solution.py:612
  302.9 9.5 %collective-permute-done.2 = bf16[2,4,6,24,768]{4,3,2,1,0:T(8,128)(2,1)} collective-permute-done((bf16[2,4,6,24,768]{4,3,2,1,0:T(8,128)(2,1)}, bf16[2,4,6,24,768]{4,3,2,1,0:T(8,128)(2,1)}, u32[]{:S(2)}, u32[]{:S(2)}) %collective-permute-start.2) | collective-permute-done | bytes 1769504 | tf_op jit(solution)/shard_map/ppermute | solution.py:659
  312.4 11.9 %last.1 = (bf16[1152,768]{1,0:T(8,128)(2,1)}, f32[8,768]{1,0:T(8,128)}, bf16[1024,768]{1,0:T(8,128)(2,1)}) custom-call(s32[5]{0:T(128)} %stack.74.refs_0_.plan, s32[1152,1]{1,0:T(8,128)} %broadcast_in_dim.197.refs_1_, f32[1152,768]{1,0:T(8,128)} %get-tuple-element.213.refs_1_.refs_2_, f32[1152,768]{1,0:T(8,128)} %get-tuple-element.221.refs_3_, ...), custom_call_target="tpu_custom_call" | custom-call | bytes 12000000 | tf_op jit(solution)/shard_map/last/pallas_call | solution.py:621
  324.2 2.8 fusion.38
  327.0 1.4 fusion.47
  328.3 1.8 collective-permute-start.4
  330.1 4.9 %all-to-all-start.9 = ((bf16[32,32,768]{2,1,0:T(8,128)(2,1)}), bf16[32,32,768]{2,1,0:T(8,128)(2,1)}, u32[]{:S(2)}, u32[]{:S(2)}) async-start(bf16[32,32,768]{2,1,0:T(8,128)(2,1)} %bitcast.163), calls=%async_computation.9 | async-start | bytes 3145728 | tf_op jit(solution)/shard_map/all_to_all | solution.py:42
  335.0 1.9 collective-permute-start.5
  336.9 6.4 %rest_grads.1 = (bf16[2,2,4,2,24,768]{5,4,3,2,1,0:T(8,128)(2,1)}, bf16[2,2,4,2,24,768]{5,4,3,2,1,0:T(8,128)(2,1)}) custom-call(s32[5]{0:T(128)} %stack.74.refs_0_.plan, s32[1152,1]{1,0:T(8,128)} %select_select_fusion.refs_2_.spot_in, bf16[1152,768]{1,0:T(8,128)(2,1)} %get-tuple-element.241.hin, bf16[3,1152,768]{2,1,0:T(8,128)(2,1)} %attend_back.1.d_proj.refs_4_.d_value, ...), custom_call_target="tpu_custom_call" | custom-call | bytes 6000000 | tf_op jit(solution)/shard_map/rest_grads/pallas_call | solution.py:639
  343.9 18.1 %collective-permute-done.5 = bf16[4,3,24,768]{3,2,1,0:T(8,128)(2,1)S(1)} collective-permute-done((bf16[4,3,24,768]{3,2,1,0:T(8,128)(2,1)S(1)}, bf16[4,3,24,768]{3,2,1,0:T(8,128)(2,1)S(1)}, u32[]{:S(2)}, u32[]{:S(2)}) %collective-permute-start.5) | collective-permute-done | bytes 442400 | tf_op jit(solution)/shard_map/ppermute | solution.py:659
  365.4 2.5 add_convert_fusion.7
  367.9 2.2 collective-permute-start.13
  370.0 2.4 add_convert_fusion.9
  372.4 1.7 collective-permute-start.11
  375.3 3.6 collective-permute-start.10
  379.7 3.1 collective-permute-done.13
  384.1 2.3 collective-permute-done.11
  387.8 1.4 broadcast_select_fusion
  389.2 4.6 collective-permute-done.8
  393.9 10.3 %collective-permute-done.9 = bf16[9,24,768]{2,1,0:T(8,128)(2,1)} collective-permute-done((bf16[9,24,768]{2,1,0:T(8,128)(2,1)}, bf16[9,24,768]{2,1,0:T(8,128)(2,1)}, u32[]{:S(2)}, u32[]{:S(2)}) %collective-permute-start.9) | collective-permute-done | bytes 331808 | tf_op jit(solution)/shard_map/ppermute | solution.py:659
  404.5 1.6 copy.127
  406.1 2.7 collective-permute-start.16
  408.9 1.8 collective-permute-start.17
  410.7 1.3 convert_add_fusion.1
  412.0 1.3 fusion.93
  413.3 5.2 %fusion.28 = f32[960,768]{1,0:T(8,128)} fusion(bf16[1024,768]{1,0:T(8,128)(2,1)} %bitcast.58, s32[1024]{0:T(1024)S(1)} %copy-done.11), kind=kOutput, calls=%fused_computation.52 | convolution fusion | flops 1510932480 | bytes 4526080 | tf_op jit(solution)/shard_map/dot_general | solution.py:34
  418.8 3.2 multiply_reduce_fusion
  423.3 1.4 fusion.92
  428.8 3.3 multiply_reduce_fusion.1
  435.2 2.6 all-to-all-start.10
  437.9 1.3 slice_bitcast_fusion.2.g_vectors
  439.2 2.6 copy.131.rest
  442.5 2.5 all-to-all-done.10
  446.3 12.0 %update.1 = (f32[960,768]{1,0:T(8,128)}, f32[24,512]{1,0:T(8,128)}, f32[24,2304]{1,0:T(8,128)}, f32[24,768]{1,0:T(8,128)}, f32[24,3072]{1,0:T(8,128)}, /*index=5...) custom-call(f32[1]{0:T(128)} %bitcast.71.scale, ...), custom_call_target="tpu_custom_call" | custom-call | tf_op jit(solution)/shard_map/update/pallas_call | solution.py:858
  (142 shorter events, 40.8 us)
Async XLA Ops:
  7.2 6.6 %copy-start.14 = (s32[4,2]{0,1:T(2,128)S(1)}, s32[4,2]{0,1:T(2,128)}, u32[]{:S(2)}) copy-start(s32[4,2]{0,1:T(2,128)} %param.30) | copy-start | bytes 100
  7.2 6.7 %copy-start.16 = (s32[4]{0:T(128)S(1)}, s32[4]{0:T(128)}, u32[]{:S(2)}) copy-start(s32[4]{0:T(128)} %param.31) | copy-start | bytes 52
  7.2 6.8 %copy-start.9 = (s32[4,2,128]{2,1,0:T(2,128)S(1)}, s32[4,2,128]{2,1,0:T(2,128)}, u32[]{:S(2)}) copy-start(s32[4,2,128]{2,1,0:T(2,128)} %param.29) | copy-start | bytes 12292
  7.2 150.7 %all-gather.2.cloned.1.call-start = ((), (), s32[]{:S(2)}) async-start(), calls=%async_computation.11 | async-start | bytes 15611904 | tf_op jit(solution)/shard_map/all_gather | solution.py:737
  10.2 48.4 %copy-start = (f32[960,768]{1,0:T(8,128)S(1)}, f32[960,768]{1,0:T(8,128)}, u32[]{:S(2)}) copy-start(f32[960,768]{1,0:T(8,128)} %refs_0_.1) | copy-start | bytes 8847364
  14.8 20.0 %all-to-all-start.4 = ((s32[32,9,128]{2,1,0:T(8,128)}), s32[32,9,128]{2,1,0:T(8,128)S(1)}, u32[]{:S(2)}, u32[]{:S(2)}) async-start(s32[32,9,128]{2,1,0:T(8,128)} %broadcast_in_dim.172), calls=%async_computation.4 | async-start | bytes 524288 | tf_op jit(solution)/shard_map/all_to_all | solution.py:42
  35.5 4.7 copy-start.12
  54.4 11.4 %all-to-all-start.5 = ((s32[32,1,128]{2,1,0:T(1,128)}), s32[32,1,128]{2,1,0:T(1,128)S(1)}, u32[]{:S(2)}, u32[]{:S(2)}) async-start(s32[32,1,128]{2,1,0:T(1,128)} %bitcast.6), calls=%async_computation.5 | async-start | bytes 32768 | tf_op jit(solution)/shard_map/all_to_all | solution.py:42
  65.9 4.5 copy-start.10
  65.9 4.5 copy-start.15
  71.0 10.2 %all-to-all-start.7 = ((f32[32,1,4]{2,1,0:T(1,128)}), f32[32,1,4]{2,1,0:T(1,128)}, u32[]{:S(2)}, u32[]{:S(2)}) async-start(f32[32,1,4]{2,1,0:T(1,128)} %broadcast_in_dim.185), calls=%async_computation.7 | async-start | bytes 32768 | tf_op jit(solution)/shard_map/all_to_all | solution.py:42
  81.7 7.3 %copy-start.7 = (pred[1152]{0:T(1024)(128)(4,1)}, pred[1152]{0:T(1024)(128)(4,1)S(1)}, u32[]{:S(2)}) copy-start(pred[1152]{0:T(1024)(128)(4,1)S(1)} %get-tuple-element.743) | copy-start | bytes 3460
  81.7 73.8 %all-to-all-start.6 = ((bf16[32,32,768]{2,1,0:T(8,128)(2,1)}), bf16[32,32,768]{2,1,0:T(8,128)(2,1)S(1)}, u32[]{:S(2)}, u32[]{:S(2)}) async-start(bf16[32,32,768]{2,1,0:T(8,128)(2,1)} %bitcast.164), calls=%async_computation.6 | async-start | bytes 3145728 | tf_op jit(solution)/shard_map/all_to_all | solution.py:42
  155.5 2.4 copy-start.4
  182.3 28.8 %copy-start.13 = (s32[64]{0:T(128)S(1)}, s32[64]{0:T(128)}, u32[]{:S(2)}) copy-start(s32[64]{0:T(128)} %copy-done.12) | copy-start | bytes 772
  208.4 15.6 %all-to-all-start.8 = ((f32[32,2,768]{2,1,0:T(2,128)}), f32[32,2,768]{2,1,0:T(2,128)S(1)}, u32[]{:S(2)}, u32[]{:S(2)}) async-start(f32[32,2,768]{2,1,0:T(2,128)} %broadcast_in_dim.187), calls=%async_computation.8 | async-start | bytes 393216 | tf_op jit(solution)/shard_map/all_to_all | solution.py:42
  257.1 8.8 %collective-permute-start = (bf16[2,2,4,6,24,768]{5,4,3,2,1,0:T(8,128)(2,1)}, bf16[2,2,4,6,24,768]{5,4,3,2,1,0:T(8,128)(2,1)}, u32[]{:S(2)}, u32[]{:S(2)}) collective-permute-start(bf16[2,2,4,6,24,768]{5,4,3,2,1,0:T(8,128)(2,1)} %get-tuple-element.228), channel_id=1, source_target_pairs={{0,1},{1,0},{2,3},{3,2},{4,5},{5,4},{6,7},{7,6},{8,9},{9,8},{10,11... | collective-permute-start | bytes 10616840 | tf_op jit(solution)/shard_map/ppermute | solution.py:659
  265.8 25.6 %collective-permute-start.1 = (bf16[2,2,4,3,24,768]{5,4,3,2,1,0:T(8,128)(2,1)}, bf16[2,2,4,3,24,768]{5,4,3,2,1,0:T(8,128)(2,1)}, u32[]{:S(2)}, u32[]{:S(2)}) collective-permute-start(bf16[2,2,4,3,24,768]{5,4,3,2,1,0:T(8,128)(2,1)} %get-tuple-element.234), channel_id=1, source_target_pairs={{0,1},{1,0},{2,3},{3,2},{4,5},{5,4},{6,7},{7,6},{8,9},{9,8},{10,11... | collective-permute-start | bytes 5308424 | tf_op jit(solution)/shard_map/ppermute | solution.py:659
  271.3 41.1 %collective-permute-start.2 = (bf16[2,4,6,24,768]{4,3,2,1,0:T(8,128)(2,1)}, bf16[2,4,6,24,768]{4,3,2,1,0:T(8,128)(2,1)}, u32[]{:S(2)}, u32[]{:S(2)}) collective-permute-start(bf16[2,4,6,24,768]{4,3,2,1,0:T(8,128)(2,1)} %get-tuple-element.434), channel_id=1, source_target_pairs={{0,2},{1,3},{2,0},{3,1},{4,6},{5,7},{6,4},{7,5},{8,10},{9,11},{10,... | collective-permute-start | bytes 5308424 | tf_op jit(solution)/shard_map/ppermute | solution.py:659
  294.7 32.3 %collective-permute-start.3 = (bf16[2,4,3,24,768]{4,3,2,1,0:T(8,128)(2,1)}, bf16[2,4,3,24,768]{4,3,2,1,0:T(8,128)(2,1)}, u32[]{:S(2)}, u32[]{:S(2)}) collective-permute-start(bf16[2,4,3,24,768]{4,3,2,1,0:T(8,128)(2,1)} %get-tuple-element.250), channel_id=1, source_target_pairs={{0,4},{1,5},{2,6},{3,7},{4,0},{5,1},{6,2},{7,3},{8,12},{9,13},{10,... | collective-permute-start | bytes 2654216 | tf_op jit(solution)/shard_map/ppermute | solution.py:659
  328.3 34.4 %collective-permute-start.4 = (bf16[4,6,24,768]{3,2,1,0:T(8,128)(2,1)}, bf16[4,6,24,768]{3,2,1,0:T(8,128)(2,1)S(1)}, u32[]{:S(2)}, u32[]{:S(2)}) collective-permute-start(bf16[4,6,24,768]{3,2,1,0:T(8,128)(2,1)} %get-tuple-element.254), channel_id=1, source_target_pairs={{0,4},{1,5},{2,6},{3,7},{4,0},{5,1},{6,2},{7,3},{8,12},{9,13},{10,... | collective-permute-start | bytes 2654216 | tf_op jit(solution)/shard_map/ppermute | solution.py:659
  330.1 74.1 %all-to-all-start.9 = ((bf16[32,32,768]{2,1,0:T(8,128)(2,1)}), bf16[32,32,768]{2,1,0:T(8,128)(2,1)}, u32[]{:S(2)}, u32[]{:S(2)}) async-start(bf16[32,32,768]{2,1,0:T(8,128)(2,1)} %bitcast.163), calls=%async_computation.9 | async-start | bytes 3145728 | tf_op jit(solution)/shard_map/all_to_all | solution.py:42
  335.0 27.0 %collective-permute-start.5 = (bf16[4,3,24,768]{3,2,1,0:T(8,128)(2,1)S(1)}, bf16[4,3,24,768]{3,2,1,0:T(8,128)(2,1)S(1)}, u32[]{:S(2)}, u32[]{:S(2)}) collective-permute-start(bf16[4,3,24,768]{3,2,1,0:T(8,128)(2,1)S(1)} %get-tuple-element.256), channel_id=1, source_target_pairs={{0,2},{1,3},{2,0},{3,1},{4,6},{5,7},{6,4},{7,5},{8,10},{9,11},{10,... | collective-permute-start | bytes 1327112 | tf_op jit(solution)/shard_map/ppermute | solution.py:659
  336.9 28.4 %collective-permute-start.6 = (bf16[2,2,4,2,24,768]{5,4,3,2,1,0:T(8,128)(2,1)}, bf16[2,2,4,2,24,768]{5,4,3,2,1,0:T(8,128)(2,1)}, u32[]{:S(2)}, u32[]{:S(2)}) collective-permute-start(bf16[2,2,4,2,24,768]{5,4,3,2,1,0:T(8,128)(2,1)} %get-tuple-element.258), channel_id=1, source_target_pairs={{0,1},{1,0},{2,3},{3,2},{4,5},{5,4},{6,7},{7,6},{8,9},{9,8},{10,11... | collective-permute-start | bytes 3538952 | tf_op jit(solution)/shard_map/ppermute | solution.py:659
  343.4 22.0 %collective-permute-start.7 = (bf16[2,2,4,2,24,768]{5,4,3,2,1,0:T(8,128)(2,1)}, bf16[2,2,4,2,24,768]{5,4,3,2,1,0:T(8,128)(2,1)}, u32[]{:S(2)}, u32[]{:S(2)}) collective-permute-start(bf16[2,2,4,2,24,768]{5,4,3,2,1,0:T(8,128)(2,1)} %get-tuple-element.264), channel_id=1, source_target_pairs={{0,1},{1,0},{2,3},{3,2},{4,5},{5,4},{6,7},{7,6},{8,9},{9,8},{10,11... | collective-permute-start | bytes 3538952 | tf_op jit(solution)/shard_map/ppermute | solution.py:659
  363.0 2.4 copy-start.6
  365.4 4.7 copy-start.5
  367.9 14.9 %collective-permute-start.13 = (bf16[2,4,2,24,768]{4,3,2,1,0:T(8,128)(2,1)}, bf16[2,4,2,24,768]{4,3,2,1,0:T(8,128)(2,1)S(1)}, u32[]{:S(2)}, u32[]{:S(2)}) collective-permute-start(bf16[2,4,2,24,768]{4,3,2,1,0:T(8,128)(2,1)} %get-tuple-element.441), channel_id=1, source_target_pairs={{0,4},{1,5},{2,6},{3,7},{4,0},{5,1},{6,2},{7,3},{8,12},{9,13},{10,... | collective-permute-start | bytes 1769480 | tf_op jit(solution)/shard_map/ppermute | solution.py:659
  372.4 14.0 %collective-permute-start.11 = (bf16[2,4,2,24,768]{4,3,2,1,0:T(8,128)(2,1)}, bf16[2,4,2,24,768]{4,3,2,1,0:T(8,128)(2,1)S(1)}, u32[]{:S(2)}, u32[]{:S(2)}) collective-permute-start(bf16[2,4,2,24,768]{4,3,2,1,0:T(8,128)(2,1)} %get-tuple-element.443), channel_id=1, source_target_pairs={{0,2},{1,3},{2,0},{3,1},{4,6},{5,7},{6,4},{7,5},{8,10},{9,11},{10,... | collective-permute-start | bytes 1769480 | tf_op jit(solution)/shard_map/ppermute | solution.py:659
  375.3 13.9 %collective-permute-start.10 = (bf16[9,24,768]{2,1,0:T(8,128)(2,1)}, bf16[9,24,768]{2,1,0:T(8,128)(2,1)}, u32[]{:S(2)}, u32[]{:S(2)}) collective-permute-start(bf16[9,24,768]{2,1,0:T(8,128)(2,1)} %pad_maximum_fusion.3), channel_id=1, source_target_pairs={{0,24},{1,25},{2,26},{3,27},{4,28},{5,29},{6,30},{7,31},{8,16},{9,... | collective-permute-start | bytes 995336 | tf_op jit(solution)/shard_map/ppermute | solution.py:659
  378.9 15.0 %collective-permute-start.8 = (bf16[9,24,768]{2,1,0:T(8,128)(2,1)}, bf16[9,24,768]{2,1,0:T(8,128)(2,1)}, u32[]{:S(2)}, u32[]{:S(2)}) collective-permute-start(bf16[9,24,768]{2,1,0:T(8,128)(2,1)} %pad_maximum_fusion.1), channel_id=1, source_target_pairs={{0,8},{1,9},{2,10},{3,11},{4,12},{5,13},{6,14},{7,15},{8,0},{9,1},... | collective-permute-start | bytes 995336 | tf_op jit(solution)/shard_map/ppermute | solution.py:659
  379.1 25.1 %collective-permute-start.9 = (bf16[9,24,768]{2,1,0:T(8,128)(2,1)}, bf16[9,24,768]{2,1,0:T(8,128)(2,1)}, u32[]{:S(2)}, u32[]{:S(2)}) collective-permute-start(bf16[9,24,768]{2,1,0:T(8,128)(2,1)} %pad_maximum_fusion.2), channel_id=1, source_target_pairs={{0,16},{1,17},{2,18},{3,19},{4,20},{5,21},{6,22},{7,23},{8,24},{9,... | collective-permute-start | bytes 995336 | tf_op jit(solution)/shard_map/ppermute | solution.py:659
  382.7 5.1 %copy-start.3 = (bf16[1152,768]{1,0:T(8,128)(2,1)S(1)}, bf16[1152,768]{1,0:T(8,128)(2,1)}, u32[]{:S(2)}) copy-start(bf16[1152,768]{1,0:T(8,128)(2,1)} %get-tuple-element.259.d_x) | copy-start | bytes 5308420
  382.9 21.3 %collective-permute-start.14 = (bf16[4,2,24,768]{3,2,1,0:T(8,128)(2,1)S(1)}, bf16[4,2,24,768]{3,2,1,0:T(8,128)(2,1)S(1)}, u32[]{:S(2)}, u32[]{:S(2)}) collective-permute-start(bf16[4,2,24,768]{3,2,1,0:T(8,128)(2,1)S(1)} %get-tuple-element.450), channel_id=1, source_target_pairs={{0,2},{1,3},{2,0},{3,1},{4,6},{5,7},{6,4},{7,5},{8,10},{9,11},{10,... | collective-permute-start | bytes 884744 | tf_op jit(solution)/shard_map/ppermute | solution.py:659
  386.5 17.6 %collective-permute-start.12 = (bf16[4,2,24,768]{3,2,1,0:T(8,128)(2,1)S(1)}, bf16[4,2,24,768]{3,2,1,0:T(8,128)(2,1)S(1)}, u32[]{:S(2)}, u32[]{:S(2)}) collective-permute-start(bf16[4,2,24,768]{3,2,1,0:T(8,128)(2,1)S(1)} %get-tuple-element.452), channel_id=1, source_target_pairs={{0,4},{1,5},{2,6},{3,7},{4,0},{5,1},{6,2},{7,3},{8,12},{9,13},{10,... | collective-permute-start | bytes 884744 | tf_op jit(solution)/shard_map/ppermute | solution.py:659
  404.4 20.9 %collective-permute-start.15 = (bf16[4,24,768]{2,1,0:T(8,128)(2,1)S(1)}, bf16[4,24,768]{2,1,0:T(8,128)(2,1)S(1)}, u32[]{:S(2)}, u32[]{:S(2)}) collective-permute-start(bf16[4,24,768]{2,1,0:T(8,128)(2,1)S(1)} %pad_maximum_fusion.4), channel_id=1, source_target_pairs={{0,8},{1,9},{2,10},{3,11},{4,12},{5,13},{6,14},{7,15},{8,0},{9,1},... | collective-permute-start | bytes 442376 | tf_op jit(solution)/shard_map/ppermute | solution.py:659
  406.1 7.2 %copy-start.11 = (s32[1024]{0:T(1024)S(1)}, s32[1024]{0:T(1024)}, u32[]{:S(2)}) copy-start(s32[1024]{0:T(1024)} %copy-done.10) | copy-start | bytes 12292
  406.1 20.3 %collective-permute-start.16 = (bf16[4,24,768]{2,1,0:T(8,128)(2,1)S(1)}, bf16[4,24,768]{2,1,0:T(8,128)(2,1)S(1)}, u32[]{:S(2)}, u32[]{:S(2)}) collective-permute-start(bf16[4,24,768]{2,1,0:T(8,128)(2,1)S(1)} %pad_maximum_fusion.5), channel_id=1, source_target_pairs={{0,16},{1,17},{2,18},{3,19},{4,20},{5,21},{6,22},{7,23},{8,24},{9,... | collective-permute-start | bytes 442376 | tf_op jit(solution)/shard_map/ppermute | solution.py:659
  408.9 18.7 %collective-permute-start.17 = (bf16[4,24,768]{2,1,0:T(8,128)(2,1)S(1)}, bf16[4,24,768]{2,1,0:T(8,128)(2,1)S(1)}, u32[]{:S(2)}, u32[]{:S(2)}) collective-permute-start(bf16[4,24,768]{2,1,0:T(8,128)(2,1)S(1)} %pad_maximum_fusion.6), channel_id=1, source_target_pairs={{0,24},{1,25},{2,26},{3,27},{4,28},{5,29},{6,30},{7,31},{8,16},{9,... | collective-permute-start | bytes 442376 | tf_op jit(solution)/shard_map/ppermute | solution.py:659
  413.3 5.3 %copy-start.8 = (pred[1152]{0:T(1024)(128)(4,1)S(1)}, pred[1152]{0:T(1024)(128)(4,1)}, u32[]{:S(2)}) copy-start(pred[1152]{0:T(1024)(128)(4,1)} %copy-done.7) | copy-start | bytes 3460
  428.8 17.5 %copy-start.1 = (f32[960,768]{1,0:T(8,128)S(1)}, f32[960,768]{1,0:T(8,128)}, u32[]{:S(2)}) copy-start(f32[960,768]{1,0:T(8,128)} %get-tuple-element.275.g_embed) | copy-start | bytes 8847364
  432.1 1.1 copy-start.2
  435.2 9.7 %all-to-all-start.10 = ((f32[32,1,2]{2,1,0:T(1,128)}), f32[32,1,2]{2,1,0:T(1,128)S(1)}, u32[]{:S(2)}, u32[]{:S(2)}) async-start(f32[32,1,2]{2,1,0:T(1,128)} %broadcast_in_dim.189), calls=%async_computation.10 | async-start | bytes 32768 | tf_op jit(solution)/shard_map/all_to_all | solution.py:42
Sparse Core Ops, SparseCore 0:
  13.9 144.0 all-gather.1

commit v8 on v7

--- a/solution.py
+++ b/solution.py
@@ -288,11 +288,14 @@
     rows, width = z1.shape
     step = pl.program_id(0)
     total = lambda a, b: jnp.sum(a * b, axis=1, keepdims=True)
-    count = facts[10]
+    count = facts[8]
     grads, losses = [], []
     for i in range(2):
-        labeled, gold, size, other_size, counts = (facts[5 * i + j] for j in range(5))
-        own, other = pooled[i : i + 1] / size, all_pooled[pl.ds(holders[i], 1), :] / other_size
+        labeled, size, other_size, counts = (facts[4 * i + j] for j in range(4))
+        holder, late, keeper, at = (holders[4 * i + j] for j in range(4))
+        own, other = pooled[i : i + 1] / size, all_pooled[holder, pl.ds(late, 1), :] / other_size
+        gold = all_pooled[keeper, 2:3, :]
+        gold = jnp.sum(jnp.where(iota(gold.shape, 1) == at, gold, 0.0), axis=1, keepdims=True)
         cross = total(own, other)
         root, other_root = lax.rsqrt(total(own, own) + EPS), lax.rsqrt(total(other, other) + EPS)
         miss = cross * root * other_root - gold
@@ -535,12 +538,12 @@
         "middle",
     )(plan, x, mixed, full, full, w_src, vec, vec_ff)
 
-    all_pooled = exchange(jnp.broadcast_to(pooled[None, :2], (devices, 2, width))).reshape(2 * devices, width)
-    holders, facts = meet
+    holders, facts, goal = meet
+    all_pooled = exchange(jnp.broadcast_to(jnp.concatenate([pooled[:2], goal], axis=0)[None], (devices, 3, width)))
     d_y, d_f, d_r1, d_a, d_o, sums, sums_ff, loss = call(
         when_live(back_kernel), 3, (BLOCKS,),
         [
-            fixed((8, width), (0, 0)), fixed((2 * devices, width), (0, 0)), row(width), row(hidden), row(width), w_out_spec, w_in_spec,
+            fixed((8, width), (0, 0)), fixed((devices, 3, width), (0, 0, 0)), row(width), row(hidden), row(width), w_out_spec, w_in_spec,
             w_back_spec, vec_spec,
         ],
         [
@@ -748,14 +751,15 @@
     ahead = (live[None, :] > live[:, None]) | ((live[None, :] == live[:, None]) & (index[None, :] < index[:, None]))
     order = jnp.sum(ahead.astype(jnp.int32), axis=1)
     me = lax.axis_index("dp") * seq + lax.axis_index("seq")
+    ranks = jnp.stack([me, 2 * devices - 1 - me])
+    picked = order[None, :] == ranks[:, None]
     take = lambda values, i: jnp.sum(jnp.where(index[: values.shape[0]] == i, values, 0))
-    chosen = [jnp.sum(jnp.where(order == rank, index, 0)) for rank in (me, 2 * devices - 1 - me)]
+    chosen = list(jnp.sum(jnp.where(picked, index[None, :], 0), axis=1))
     count = jnp.maximum(jnp.sum(lab).astype(f32), 1.0)
-    size = [take(live, i) for i in chosen]
+    size = list(jnp.sum(jnp.where(picked, live[None, :], 0), axis=1))
     start = (size[0] + 15) // 16 * 16
-    two_ids = [
-        lax.dynamic_slice(news, (i // group, 0, lax.rem(i, group), 0), (1, seq, 1, local)).reshape(length) for i in chosen
-    ]
+    among = picked.reshape(2, devices // seq, 1, group, 1)
+    two_ids = jnp.sum(jnp.where(among, news[None, :, :, :group, :], 0), axis=(1, 3)).reshape(2, length)
     ids = lax.dynamic_update_slice(jnp.pad(two_ids[0], (0, rows - length)), two_ids[1], (start,))
     line = jnp.arange(rows, dtype=jnp.int32)
     in_first, in_second = line < size[0], (line >= start) & (line < start + size[1])
@@ -792,17 +796,18 @@
 
     _, extra = lax.while_loop(lambda state: state[0] < rounds, more, (jnp.int32(1), jnp.zeros((rows, width), bf)))
 
-    all_gold = exchange(jnp.broadcast_to(gold[None], (devices, pairs_here))).reshape(devices // seq, seq, pairs_here)[:, 0]
-    all_gold = all_gold.reshape(devices)
     holders, facts = [], []
     for i in chosen:
         other, pair = i ^ 1, i // 2
         rank = take(order, other)
-        holders.append(jnp.where(rank < devices, 2 * rank, 2 * (2 * devices - 1 - rank) + 1))
+        late = rank >= devices
+        holders += [jnp.where(late, 2 * devices - 1 - rank, rank), late.astype(jnp.int32), pair // pairs_here * seq, lax.rem(pair, pairs_here)]
         weight = take(lab, pair).astype(f32)
         own = jnp.where(lax.rem(i, 2) == 0, weight, 0.0)
-        facts += [weight, take(all_gold, pair), take(lens, i).astype(f32), take(lens, other).astype(f32), own]
-    meet = jnp.stack(holders), jnp.stack(facts + [count])
+        facts += [weight, take(lens, i).astype(f32), take(lens, other).astype(f32), own]
+    goal = jnp.pad(gold[None, :], ((0, 0), (0, width - pairs_here)))
+    holders, facts, goal, plan, slots = lax.optimization_barrier((jnp.stack(holders), jnp.stack(facts + [count]), goal, plan, slots))
+    meet = holders, facts, goal
 
     staged = (seq, devices) == (4, 32) and depth == 24
     loss, dense_out, dense_in, rest, d_xb, give_rows = run_forward_backward(
@@ -850,7 +855,7 @@
         mom_embed, mom_position.T, mom_attn_in, mom_attn_out, mom_ff_in, mom_ff_out, mom_vectors,
         avg_embed, avg_position.T, avg_attn_in, avg_attn_out, avg_ff_in, avg_ff_out, avg_vectors,
     )
-    steps = next(n for n in (8, 5, 4, 3, 2, 1) if per_owner % (8 * n) == 0 or n == 1)
+    steps = next(n for n in (2, 5, 4, 3, 1) if per_owner % (8 * n) == 0 or n == 1)
     strip = pl.BlockSpec((per_owner // steps, width), lambda i, *_: (i, 0))
     whole = lambda v: strip if v.shape == embed.shape else fixed(v.shape, (0,) * v.ndim)
     whole_out = lambda v: strip if v.shape == embed.shape else pl.BlockSpec(v.shape, lambda *_: (0,) * v.ndim)

time: 476 us -> 463 us (0.973)
  blocking collectives: 0 us -> 15.6 us
  waiting for transfers between devices: 141 us -> 130 us
  starting transfers between devices: 51 us -> 42.3 us
    all_to_all x7 -> x5, waiting for transfers between devices: 89.7 us -> 64.8 us  [exchange(): return lax.all_to_all(v, AXES, 0, 0, tiled=True)]
    all_to_all x0 -> x1, blocking collectives: none -> 15.6 us  [exchange(): return lax.all_to_all(v, AXES, 0, 0, tiled=True)]
    all_gather x1, waiting for transfers between devices: 2.41 us -> 15.5 us  [body(): full = lax.all_gather(shard, AXES, axis=0, tiled=True)]
    all_to_all x7 -> x5, starting transfers between devices: 27.7 us -> 20.6 us  [exchange(): return lax.all_to_all(v, AXES, 0, 0, tiled=True)]
    convert_element_type x11 -> x12, other arithmetic: 18.3 us -> 18.3 us  [add(): return (a.astype(f32) + b.astype(f32)).astype(bf)]
  transfers between devices with their start and end apart: 26 -> 24, of which waited for: 13 -> 12; matrix products, arithmetic and copies ran while one was open for 16% -> 15% of each run, Pallas kernels for 11% -> 11%
where the time goes in v8:
time: 463 us; the launch traced here: 456 us
  Pallas kernels  141 us (30%)
  waiting for transfers between devices  130 us (28%)
  other arithmetic  54.9 us (12%)
  starting transfers between devices  42.3 us (9%)
  between operations  39.4 us (9%)
  local copies, waits for them, and re-layouts  22.8 us (5%)
  blocking collectives  15.6 us (3%)
  matrix products  9.75 us (2%)
    all_to_all x5, waiting for transfers between devices, exchange(): return lax.all_to_all(v, AXES, 0, 0, tiled=True)  64.8 us
    ppermute x18, waiting for transfers between devices, swap(): return lax.ppermute(v, AXES, [(i, i ^ bit) for i in range(devices)])  49.3 us
    pallas_call x1, Pallas kernels, run_forward_backward(): call(when_live(functools.partial(middle_kernel, staged, depth, turns)), 1...  24.4 us
    ppermute x18, starting transfers between devices, swap(): return lax.ppermute(v, AXES, [(i, i ^ bit) for i in range(devices)])  21.7 us
    all_to_all x5, starting transfers between devices, exchange(): return lax.all_to_all(v, AXES, 0, 0, tiled=True)  20.6 us
    pallas_call x1, Pallas kernels, run_forward_backward(): call(when_live(back_kernel), 3, (BLOCKS,), [fixed((8, width), (0, 0)), fi...  19.8 us
    pallas_call x1, Pallas kernels, attend_back(): call(attend_back_kernel, 1, (count,), [block(0, start), block(1, start),...  18.3 us
    convert_element_type x12, other arithmetic, add(): return (a.astype(f32) + b.astype(f32)).astype(bf)  18.3 us
  transfers between devices with their start and end apart: 24, of which 12 were waited for; matrix products, arithmetic and copies ran while one was open for 15% of the time, Pallas kernels for 11%

profile of v8, /device:TPU:0, one launch (start us, length us, event | category | flops | bytes accessed | tf_op | source)
XLA Modules:
  0.0 455.5 jit_solution(14928684991978442107)
XLA Ops:
  14.6 7.3 %all-to-all-start.4 = ((s32[32,9,128]{2,1,0:T(8,128)}), s32[32,9,128]{2,1,0:T(8,128)S(1)}, u32[]{:S(2)}, u32[]{:S(2)}) async-start(s32[32,9,128]{2,1,0:T(8,128)} %broadcast_in_dim.201), calls=%async_computation.4 | async-start | bytes 524288 | tf_op jit(solution)/shard_map/all_to_all | solution.py:42
  22.1 12.5 %all-to-all-done.4 = s32[32,9,128]{2,1,0:T(8,128)S(1)} async-done(((s32[32,9,128]{2,1,0:T(8,128)}), s32[32,9,128]{2,1,0:T(8,128)S(1)}, u32[]{:S(2)}, u32[]{:S(2)}) %all-to-all-start.4) | async-done | bytes 147488 | tf_op jit(solution)/shard_map/all_to_all | solution.py:42
  40.3 1.7 convert_reduce_fusion
  42.0 1.9 and_select_fusion.3
  46.0 4.2 all-to-all-start.5
  50.2 1.3 convert_element_type.544
  51.5 5.9 %all-to-all-done.5 = s32[32,1,128]{2,1,0:T(1,128)S(1)} async-done(((s32[32,1,128]{2,1,0:T(1,128)}), s32[32,1,128]{2,1,0:T(1,128)S(1)}, u32[]{:S(2)}, u32[]{:S(2)}) %all-to-all-start.5) | async-done | bytes 16416 | tf_op jit(solution)/shard_map/all_to_all | solution.py:42
  58.9 4.5 fusion.34
  63.9 2.7 all-to-all-start.6
  80.4 2.0 fusion.79
  90.0 1.6 select_select_fusion.refs_2_.spot_in
  91.6 43.8 %all-to-all-done.6 = bf16[32,32,768]{2,1,0:T(8,128)(2,1)S(1)} async-done(((bf16[32,32,768]{2,1,0:T(8,128)(2,1)}), bf16[32,32,768]{2,1,0:T(8,128)(2,1)S(1)}, u32[]{:S(2)}, u32[]{:S(2)}) %all-to-all-start.6) | async-done | bytes 1572896 | tf_op jit(solution)/shard_map/all_to_all | solution.py:42
  135.4 15.5 %all-gather.2.cloned.1.call-done.refs_5_.refs_6_.refs_7_.refs_3_.refs_4_.refs_8_.refs_9_ = bf16[768,9856]{1,0:T(8,128)(2,1)} async-done(((bf16[24,9856]{1,0:T(8,128)(2,1)}), bf16[768,9856]{1,0:T(8,128)(2,1)}) %all-gather.2.cloned.1.call-update) | async-done | bytes 15138832 | tf_op jit(solution)/shard_map/all_gather | solution.py:740
  150.9 10.4 %first.1 = (f32[1152,768]{1,0:T(8,128)}, bf16[1152,768]{1,0:T(8,128)(2,1)}, bf16[1152,2304]{1,0:T(8,128)(2,1)}, f32[16,768]{1,0:T(8,128)}) custom-call(s32[5]{0:T(128)} %pad_add_fusion.3.refs_0_.plan, s32[1152,1]{1,0:T(8,128)} %broadcast_in_dim.230.refs_1_, s32[1152,1]{1,0:T(8,128)} %select_select_fusion.refs_2_.spot_in, bf16[1024,768]{1,0:T(8,128)(2,1)} %bitcast.168, ...), custom_call_target="tpu_custom_call" | custom-call | bytes 10000000 | tf_op jit(solution)/shard_map/first/pallas_call | solution.py:513
  161.3 12.6 %attend.1.refs_2_.mixed = bf16[1152,768]{1,0:T(8,128)(2,1)} custom-call(s32[5]{0:T(128)} %pad_add_fusion.3.refs_0_.plan, bf16[1152,2304]{1,0:T(8,128)(2,1)} %get-tuple-element.223.query.keys.values, bf16[1152,2304]{1,0:T(8,128)(2,1)} %get-tuple-element.223.query.keys.values, bf16[1152,2304]{1,0:T(8,128)(2,1)} %get-tuple-element.223.query.keys.values), custom_call_target="tpu_custom_call" | custom-call | bytes 12000000 | tf_op jit(solution)/shard_map/attend/pallas_call | solution.py:525
  175.3 24.4 %middle.1 = (f32[1152,768]{1,0:T(8,128)}, bf16[1152,768]{1,0:T(8,128)(2,1)}, bf16[1152,3072]{1,0:T(8,128)(2,1)}, bf16[1152,3072]{1,0:T(8,128)(2,1)}, f32[1152,76...) custom-call(s32[5]{0:T(128)} %pad_add_fusion.3.refs_0_.plan, ...), custom_call_target="tpu_custom_call" | custom-call | bytes 24000000 | tf_op jit(solution)/shard_map/middle/pallas_call | solution.py:530
  200.5 15.6 %all_to_all.78.refs_4_ = f32[32,3,768]{2,1,0:T(4,128)} all-to-all(f32[32,3,768]{2,1,0:T(4,128)S(1)} %broadcast_in_dim.220), channel_id=1, replica_groups=mesh['dp'=8,'seq'=4] {'dp','seq'}, dimensions={0} | all-to-all | bytes 589824 | tf_op jit(solution)/shard_map/all_to_all | solution.py:42
  216.1 19.8 %back.1 = (bf16[1152,768]{1,0:T(8,128)(2,1)}, bf16[1152,3072]{1,0:T(8,128)(2,1)}, f32[1152,768]{1,0:T(8,128)}, bf16[1152,768]{1,0:T(8,128)(2,1)}, bf16[1152,768]...) custom-call(s32[5]{0:T(128)} %pad_add_fusion.3.refs_0_.plan, f32[9]{0:T(128)} %stack.114.refs_1_, ...), custom_call_target="tpu_custom_call" | custom-call | bytes 20000000 | tf_op jit(solution)/shard_map/back/pallas_call | solution.py:543
  235.9 12.6 %out_grads.1 = (bf16[2,2,4,6,24,768]{5,4,3,2,1,0:T(8,128)(2,1)}, bf16[2,2,4,6,24,768]{5,4,3,2,1,0:T(8,128)(2,1)}) custom-call(s32[5]{0:T(128)} %pad_add_fusion.3.refs_0_.plan, bf16[1152,3072]{1,0:T(8,128)(2,1)} %get-tuple-element.233.act, bf16[1152,768]{1,0:T(8,128)(2,1)} %get-tuple-element.234.d_y, bf16[1152,768]{1,0:T(8,128)(2,1)} %get-tuple-element.235.h1, ...), custom_call_target="tpu_custom_call" | custom-call | bytes 9000000 | tf_op jit(solution)/shard_map/out_grads/pallas_call | solution.py:577
  248.6 8.5 %in_grads.1 = (bf16[2,2,4,3,24,768]{5,4,3,2,1,0:T(8,128)(2,1)}, bf16[2,2,4,3,24,768]{5,4,3,2,1,0:T(8,128)(2,1)}) custom-call(s32[5]{0:T(128)} %pad_add_fusion.3.refs_0_.plan, bf16[1152,768]{1,0:T(8,128)(2,1)} %get-tuple-element.235.h1, bf16[1152,3072]{1,0:T(8,128)(2,1)} %get-tuple-element.236.d_f, bf16[1152,768]{1,0:T(8,128)(2,1)} %attend.1.refs_2_.mixed, ...), custom_call_target="tpu_custom_call" | custom-call | bytes 11000000 | tf_op jit(solution)/shard_map/in_grads/pallas_call | solution.py:584
  257.6 5.1 %fusion.33 = (bf16[2,4,6,24,768]{4,3,2,1,0:T(8,128)(2,1)}, bf16[2,4,6,24,768]{4,3,2,1,0:T(8,128)(2,1)S(1)}) fusion(bf16[2,2,4,6,24,768]{5,4,3,2,1,0:T(8,128)(2,1)} %collective-permute-done, s32[]{:T(128)S(6)} %select_n.316, bf16[2,2,4,6,24,768]{5,4,3,2,1,0:T(8,128)(2,1)} %get-tuple-element.249, s32[]{:T(128)S(6)} %select_n.315), kind=kLoop, calls=%fused_computation.60 | loop fusion | flops 7077888 | bytes 10616840 | tf_op jit(solution)/shard_map/convert_element_type | solution.py:666
  263.3 18.3 %attend_back.1.d_proj.refs_4_.d_value = bf16[3,1152,768]{2,1,0:T(8,128)(2,1)} custom-call(s32[5]{0:T(128)} %pad_add_fusion.3.refs_0_.plan, bf16[1152,2304]{1,0:T(8,128)(2,1)} %get-tuple-element.223.query.keys.values, bf16[1152,2304]{1,0:T(8,128)(2,1)} %get-tuple-element.223.query.keys.values, bf16[1152,2304]{1,0:T(8,128)(2,1)} %get-tuple-element.223.query.keys.values, ...), custom_call_target="tpu_custom_call" | custom-call | bytes 11000000 | tf_op jit(solution)/shard_map/attend_back/pallas_call | solution.py:599
  281.6 3.3 fusion.36
  284.9 1.5 collective-permute-start.3
  286.4 6.7 %query_key_grads.1 = (bf16[2,2,4,2,24,768]{5,4,3,2,1,0:T(8,128)(2,1)}, bf16[2,2,4,2,24,768]{5,4,3,2,1,0:T(8,128)(2,1)}) custom-call(s32[5]{0:T(128)} %pad_add_fusion.3.refs_0_.plan, bf16[1152,768]{1,0:T(8,128)(2,1)} %get-tuple-element.251.hin, bf16[3,1152,768]{2,1,0:T(8,128)(2,1)} %attend_back.1.d_proj.refs_4_.d_value), custom_call_target="tpu_custom_call" | custom-call | bytes 6000000 | tf_op jit(solution)/shard_map/query_key_grads/pallas_call | solution.py:615
  293.1 10.6 %collective-permute-done.2 = bf16[2,4,6,24,768]{4,3,2,1,0:T(8,128)(2,1)} collective-permute-done((bf16[2,4,6,24,768]{4,3,2,1,0:T(8,128)(2,1)}, bf16[2,4,6,24,768]{4,3,2,1,0:T(8,128)(2,1)}, u32[]{:S(2)}, u32[]{:S(2)}) %collective-permute-start.2) | collective-permute-done | bytes 1769504 | tf_op jit(solution)/shard_map/ppermute | solution.py:662
  303.6 11.9 %last.1 = (bf16[1152,768]{1,0:T(8,128)(2,1)}, f32[8,768]{1,0:T(8,128)}, bf16[1024,768]{1,0:T(8,128)(2,1)}) custom-call(s32[5]{0:T(128)} %pad_add_fusion.3.refs_0_.plan, s32[1152,1]{1,0:T(8,128)} %broadcast_in_dim.230.refs_1_, f32[1152,768]{1,0:T(8,128)} %get-tuple-element.220.refs_1_.refs_2_, f32[1152,768]{1,0:T(8,128)} %get-tuple-element.231.refs_3_, ...), custom_call_target="tpu_custom_call" | custom-call | bytes 12000000 | tf_op jit(solution)/shard_map/last/pallas_call | solution.py:624
  315.5 2.8 fusion.38
  318.3 1.4 fusion.47
  320.7 3.6 all-to-all-start.8
  324.3 1.8 collective-permute-start.5
  326.1 6.4 %rest_grads.1 = (bf16[2,2,4,2,24,768]{5,4,3,2,1,0:T(8,128)(2,1)}, bf16[2,2,4,2,24,768]{5,4,3,2,1,0:T(8,128)(2,1)}) custom-call(s32[5]{0:T(128)} %pad_add_fusion.3.refs_0_.plan, s32[1152,1]{1,0:T(8,128)} %select_select_fusion.refs_2_.spot_in, bf16[1152,768]{1,0:T(8,128)(2,1)} %get-tuple-element.251.hin, ...), custom_call_target="tpu_custom_call" | custom-call | bytes 6000000 | tf_op jit(solution)/shard_map/rest_grads/pallas_call | solution.py:642
  333.0 18.1 %collective-permute-done.5 = bf16[4,3,24,768]{3,2,1,0:T(8,128)(2,1)S(1)} collective-permute-done((bf16[4,3,24,768]{3,2,1,0:T(8,128)(2,1)S(1)}, bf16[4,3,24,768]{3,2,1,0:T(8,128)(2,1)S(1)}, u32[]{:S(2)}, u32[]{:S(2)}) %collective-permute-start.5) | collective-permute-done | bytes 442400 | tf_op jit(solution)/shard_map/ppermute | solution.py:662
  351.2 3.1 collective-permute-done.4
  357.0 2.5 add_convert_fusion.7
  360.4 2.4 add_convert_fusion.9
  362.8 1.3 collective-permute-start.11
  365.3 1.2 slice.108
  367.4 3.5 collective-permute-start.9
  370.9 1.2 collective-permute-done.13
  372.3 2.7 collective-permute-start.14
  374.9 2.3 collective-permute-done.11
  377.4 1.9 collective-permute-start.12
  379.3 1.4 broadcast_select_fusion
  380.7 2.8 collective-permute-done.8
  383.5 11.2 %collective-permute-done.9 = bf16[9,24,768]{2,1,0:T(8,128)(2,1)} collective-permute-done((bf16[9,24,768]{2,1,0:T(8,128)(2,1)}, bf16[9,24,768]{2,1,0:T(8,128)(2,1)}, u32[]{:S(2)}, u32[]{:S(2)}) %collective-permute-start.9) | collective-permute-done | bytes 331808 | tf_op jit(solution)/shard_map/ppermute | solution.py:662
  395.0 1.6 copy.117
  396.7 2.0 collective-permute-start.16
  398.7 2.5 collective-permute-start.17
  401.2 1.3 convert_add_fusion.1
  402.5 1.4 fusion.86
  403.9 5.2 %fusion.28 = f32[960,768]{1,0:T(8,128)} fusion(bf16[1024,768]{1,0:T(8,128)(2,1)} %bitcast.65, s32[1024]{0:T(1024)S(1)} %copy-done.17), kind=kOutput, calls=%fused_computation.52 | convolution fusion | flops 1510932480 | bytes 4526080 | tf_op jit(solution)/shard_map/dot_general | solution.py:34
  409.3 3.2 multiply_reduce_fusion
  413.8 1.4 fusion.85
  415.8 1.2 copy.116
  417.0 1.2 copy.118
  418.2 1.2 copy.119
  419.4 3.3 multiply_reduce_fusion.1
  422.7 1.1 copy-done.2
  425.8 2.8 all-to-all-start.9
  428.6 1.3 slice_bitcast_fusion.2.g_vectors
  429.9 2.6 copy.121.rest
  433.2 2.5 all-to-all-done.9
  437.0 9.2 %update.1 = (f32[960,768]{1,0:T(8,128)}, f32[24,512]{1,0:T(8,128)}, f32[24,2304]{1,0:T(8,128)}, f32[24,768]{1,0:T(8,128)}, f32[24,3072]{1,0:T(8,128)}, /*index=5...) custom-call(f32[1]{0:T(128)} %bitcast.79.scale, ...), custom_call_target="tpu_custom_call" | custom-call | tf_op jit(solution)/shard_map/update/pallas_call | solution.py:863
  (149 shorter events, 33.7 us)
Async XLA Ops:
  7.2 6.4 %copy-start.18 = (s32[4,2]{0,1:T(2,128)S(1)}, s32[4,2]{0,1:T(2,128)}, u32[]{:S(2)}) copy-start(s32[4,2]{0,1:T(2,128)} %param.30) | copy-start | bytes 100
  7.2 6.6 %copy-start.20 = (s32[4]{0:T(128)S(1)}, s32[4]{0:T(128)}, u32[]{:S(2)}) copy-start(s32[4]{0:T(128)} %param.31) | copy-start | bytes 52
  7.2 6.7 %copy-start.15 = (s32[4,2,128]{2,1,0:T(2,128)S(1)}, s32[4,2,128]{2,1,0:T(2,128)}, u32[]{:S(2)}) copy-start(s32[4,2,128]{2,1,0:T(2,128)} %param.29) | copy-start | bytes 12292
  7.2 143.7 %all-gather.2.cloned.1.call-start = ((), (), s32[]{:S(2)}) async-start(), calls=%async_computation.10 | async-start | bytes 15611904 | tf_op jit(solution)/shard_map/all_gather | solution.py:740
  12.7 37.5 %copy-start = (f32[960,768]{1,0:T(8,128)S(1)}, f32[960,768]{1,0:T(8,128)}, u32[]{:S(2)}) copy-start(f32[960,768]{1,0:T(8,128)} %refs_0_.1) | copy-start | bytes 8847364
  14.6 20.0 %all-to-all-start.4 = ((s32[32,9,128]{2,1,0:T(8,128)}), s32[32,9,128]{2,1,0:T(8,128)S(1)}, u32[]{:S(2)}, u32[]{:S(2)}) async-start(s32[32,9,128]{2,1,0:T(8,128)} %broadcast_in_dim.201), calls=%async_computation.4 | async-start | bytes 524288 | tf_op jit(solution)/shard_map/all_to_all | solution.py:42
  35.4 16.1 %copy-start.13 = (s32[64]{0:T(128)}, s32[64]{0:T(128)S(1)}, u32[]{:S(2)}) copy-start(s32[64]{0:T(128)S(1)} %convert_reduce_fusion.1) | copy-start | bytes 772
  35.6 1.3 copy-start.11
  46.0 11.5 %all-to-all-start.5 = ((s32[32,1,128]{2,1,0:T(1,128)}), s32[32,1,128]{2,1,0:T(1,128)S(1)}, u32[]{:S(2)}, u32[]{:S(2)}) async-start(s32[32,1,128]{2,1,0:T(1,128)} %bitcast.9), calls=%async_computation.5 | async-start | bytes 32768 | tf_op jit(solution)/shard_map/all_to_all | solution.py:42
  58.9 4.5 copy-start.16
  63.8 26.2 %copy-start.7 = (pred[1152]{0:T(1024)(128)(4,1)}, pred[1152]{0:T(1024)(128)(4,1)S(1)}, u32[]{:S(2)}) copy-start(pred[1152]{0:T(1024)(128)(4,1)S(1)} %get-tuple-element.746) | copy-start | bytes 3460
  63.8 2.8 copy-start.19
  63.8 10.6 %copy-start.14 = (s32[64]{0:T(128)S(1)}, s32[64]{0:T(128)}, u32[]{:S(2)}) copy-start(s32[64]{0:T(128)} %copy-done.13) | copy-start | bytes 772
  63.8 23.8 %copy-start.12 = (s32[2]{0:T(128)S(1)}, s32[2]{0:T(128)}, u32[]{:S(2)}) copy-start(s32[2]{0:T(128)} %copy-done.11) | copy-start | bytes 28
  63.8 24.4 %copy-start.10 = (pred[1152]{0:T(1024)(128)(4,1)S(1)}, pred[1152]{0:T(1024)(128)(4,1)}, u32[]{:S(2)}) copy-start(pred[1152]{0:T(1024)(128)(4,1)} %get-tuple-element.433) | copy-start | bytes 3460
  63.9 71.6 %all-to-all-start.6 = ((bf16[32,32,768]{2,1,0:T(8,128)(2,1)}), bf16[32,32,768]{2,1,0:T(8,128)(2,1)S(1)}, u32[]{:S(2)}, u32[]{:S(2)}) async-start(bf16[32,32,768]{2,1,0:T(8,128)(2,1)} %bitcast.169), calls=%async_computation.6 | async-start | bytes 3145728 | tf_op jit(solution)/shard_map/all_to_all | solution.py:42
  135.4 15.5 %copy-start.4 = (bf16[32,32,768]{2,1,0:T(8,128)(2,1)}, bf16[32,32,768]{2,1,0:T(8,128)(2,1)S(1)}, u32[]{:S(2)}) copy-start(bf16[32,32,768]{2,1,0:T(8,128)(2,1)S(1)} %all-to-all-done.6) | copy-start | bytes 4718596
  248.6 8.5 %collective-permute-start = (bf16[2,2,4,6,24,768]{5,4,3,2,1,0:T(8,128)(2,1)}, bf16[2,2,4,6,24,768]{5,4,3,2,1,0:T(8,128)(2,1)}, u32[]{:S(2)}, u32[]{:S(2)}) collective-permute-start(bf16[2,2,4,6,24,768]{5,4,3,2,1,0:T(8,128)(2,1)} %get-tuple-element.238), channel_id=1, source_target_pairs={{0,1},{1,0},{2,3},{3,2},{4,5},{5,4},{6,7},{7,6},{8,9},{9,8},{10,11... | collective-permute-start | bytes 10616840 | tf_op jit(solution)/shard_map/ppermute | solution.py:662
  257.1 24.6 %collective-permute-start.1 = (bf16[2,2,4,3,24,768]{5,4,3,2,1,0:T(8,128)(2,1)}, bf16[2,2,4,3,24,768]{5,4,3,2,1,0:T(8,128)(2,1)}, u32[]{:S(2)}, u32[]{:S(2)}) collective-permute-start(bf16[2,2,4,3,24,768]{5,4,3,2,1,0:T(8,128)(2,1)} %get-tuple-element.244), channel_id=1, source_target_pairs={{0,1},{1,0},{2,3},{3,2},{4,5},{5,4},{6,7},{7,6},{8,9},{9,8},{10,11... | collective-permute-start | bytes 5308424 | tf_op jit(solution)/shard_map/ppermute | solution.py:662
  262.8 40.9 %collective-permute-start.2 = (bf16[2,4,6,24,768]{4,3,2,1,0:T(8,128)(2,1)}, bf16[2,4,6,24,768]{4,3,2,1,0:T(8,128)(2,1)}, u32[]{:S(2)}, u32[]{:S(2)}) collective-permute-start(bf16[2,4,6,24,768]{4,3,2,1,0:T(8,128)(2,1)} %get-tuple-element.436), channel_id=1, source_target_pairs={{0,2},{1,3},{2,0},{3,1},{4,6},{5,7},{6,4},{7,5},{8,10},{9,11},{10,... | collective-permute-start | bytes 5308424 | tf_op jit(solution)/shard_map/ppermute | solution.py:662
  284.9 33.3 %collective-permute-start.3 = (bf16[2,4,3,24,768]{4,3,2,1,0:T(8,128)(2,1)}, bf16[2,4,3,24,768]{4,3,2,1,0:T(8,128)(2,1)}, u32[]{:S(2)}, u32[]{:S(2)}) collective-permute-start(bf16[2,4,3,24,768]{4,3,2,1,0:T(8,128)(2,1)} %get-tuple-element.260), channel_id=1, source_target_pairs={{0,4},{1,5},{2,6},{3,7},{4,0},{5,1},{6,2},{7,3},{8,12},{9,13},{10,... | collective-permute-start | bytes 2654216 | tf_op jit(solution)/shard_map/ppermute | solution.py:662
  319.6 34.7 %collective-permute-start.4 = (bf16[4,6,24,768]{3,2,1,0:T(8,128)(2,1)}, bf16[4,6,24,768]{3,2,1,0:T(8,128)(2,1)S(1)}, u32[]{:S(2)}, u32[]{:S(2)}) collective-permute-start(bf16[4,6,24,768]{3,2,1,0:T(8,128)(2,1)} %get-tuple-element.264), channel_id=1, source_target_pairs={{0,4},{1,5},{2,6},{3,7},{4,0},{5,1},{6,2},{7,3},{8,12},{9,13},{10,... | collective-permute-start | bytes 2654216 | tf_op jit(solution)/shard_map/ppermute | solution.py:662
  320.7 74.0 %all-to-all-start.8 = ((bf16[32,32,768]{2,1,0:T(8,128)(2,1)}), bf16[32,32,768]{2,1,0:T(8,128)(2,1)}, u32[]{:S(2)}, u32[]{:S(2)}) async-start(bf16[32,32,768]{2,1,0:T(8,128)(2,1)} %bitcast.170), calls=%async_computation.8 | async-start | bytes 3145728 | tf_op jit(solution)/shard_map/all_to_all | solution.py:42
  324.3 26.8 %collective-permute-start.5 = (bf16[4,3,24,768]{3,2,1,0:T(8,128)(2,1)S(1)}, bf16[4,3,24,768]{3,2,1,0:T(8,128)(2,1)S(1)}, u32[]{:S(2)}, u32[]{:S(2)}) collective-permute-start(bf16[4,3,24,768]{3,2,1,0:T(8,128)(2,1)S(1)} %get-tuple-element.266), channel_id=1, source_target_pairs={{0,2},{1,3},{2,0},{3,1},{4,6},{5,7},{6,4},{7,5},{8,10},{9,11},{10,... | collective-permute-start | bytes 1327112 | tf_op jit(solution)/shard_map/ppermute | solution.py:662
  326.1 30.8 %collective-permute-start.6 = (bf16[2,2,4,2,24,768]{5,4,3,2,1,0:T(8,128)(2,1)}, bf16[2,2,4,2,24,768]{5,4,3,2,1,0:T(8,128)(2,1)}, u32[]{:S(2)}, u32[]{:S(2)}) collective-permute-start(bf16[2,2,4,2,24,768]{5,4,3,2,1,0:T(8,128)(2,1)} %get-tuple-element.268), channel_id=1, source_target_pairs={{0,1},{1,0},{2,3},{3,2},{4,5},{5,4},{6,7},{7,6},{8,9},{9,8},{10,11... | collective-permute-start | bytes 3538952 | tf_op jit(solution)/shard_map/ppermute | solution.py:662
  332.5 24.4 %collective-permute-start.7 = (bf16[2,2,4,2,24,768]{5,4,3,2,1,0:T(8,128)(2,1)}, bf16[2,2,4,2,24,768]{5,4,3,2,1,0:T(8,128)(2,1)}, u32[]{:S(2)}, u32[]{:S(2)}) collective-permute-start(bf16[2,2,4,2,24,768]{5,4,3,2,1,0:T(8,128)(2,1)} %get-tuple-element.274), channel_id=1, source_target_pairs={{0,1},{1,0},{2,3},{3,2},{4,5},{5,4},{6,7},{7,6},{8,9},{9,8},{10,11... | collective-permute-start | bytes 3538952 | tf_op jit(solution)/shard_map/ppermute | solution.py:662
  354.6 2.4 copy-start.6
  357.0 3.5 copy-start.5
  359.4 4.7 %copy-start.9 = (s32[5]{0:T(128)S(1)}, s32[5]{0:T(128)}, u32[]{:S(2)}) copy-start(s32[5]{0:T(128)} %pad_add_fusion.3.refs_0_.plan) | copy-start | bytes 64
  359.4 12.7 %collective-permute-start.13 = (bf16[2,4,2,24,768]{4,3,2,1,0:T(8,128)(2,1)}, bf16[2,4,2,24,768]{4,3,2,1,0:T(8,128)(2,1)S(1)}, u32[]{:S(2)}, u32[]{:S(2)}) collective-permute-start(bf16[2,4,2,24,768]{4,3,2,1,0:T(8,128)(2,1)} %get-tuple-element.443), channel_id=1, source_target_pairs={{0,4},{1,5},{2,6},{3,7},{4,0},{5,1},{6,2},{7,3},{8,12},{9,13},{10,... | collective-permute-start | bytes 1769480 | tf_op jit(solution)/shard_map/ppermute | solution.py:662
  362.8 14.4 %collective-permute-start.11 = (bf16[2,4,2,24,768]{4,3,2,1,0:T(8,128)(2,1)}, bf16[2,4,2,24,768]{4,3,2,1,0:T(8,128)(2,1)S(1)}, u32[]{:S(2)}, u32[]{:S(2)}) collective-permute-start(bf16[2,4,2,24,768]{4,3,2,1,0:T(8,128)(2,1)} %get-tuple-element.445), channel_id=1, source_target_pairs={{0,2},{1,3},{2,0},{3,1},{4,6},{5,7},{6,4},{7,5},{8,10},{9,11},{10,... | collective-permute-start | bytes 1769480 | tf_op jit(solution)/shard_map/ppermute | solution.py:662
  366.5 14.1 %collective-permute-start.10 = (bf16[9,24,768]{2,1,0:T(8,128)(2,1)}, bf16[9,24,768]{2,1,0:T(8,128)(2,1)}, u32[]{:S(2)}, u32[]{:S(2)}) collective-permute-start(bf16[9,24,768]{2,1,0:T(8,128)(2,1)} %pad_maximum_fusion.3), channel_id=1, source_target_pairs={{0,24},{1,25},{2,26},{3,27},{4,28},{5,29},{6,30},{7,31},{8,16},{9,... | collective-permute-start | bytes 995336 | tf_op jit(solution)/shard_map/ppermute | solution.py:662
  367.3 16.2 %collective-permute-start.8 = (bf16[9,24,768]{2,1,0:T(8,128)(2,1)}, bf16[9,24,768]{2,1,0:T(8,128)(2,1)}, u32[]{:S(2)}, u32[]{:S(2)}) collective-permute-start(bf16[9,24,768]{2,1,0:T(8,128)(2,1)} %pad_maximum_fusion.1), channel_id=1, source_target_pairs={{0,8},{1,9},{2,10},{3,11},{4,12},{5,13},{6,14},{7,15},{8,0},{9,1},... | collective-permute-start | bytes 995336 | tf_op jit(solution)/shard_map/ppermute | solution.py:662
  367.4 27.2 %collective-permute-start.9 = (bf16[9,24,768]{2,1,0:T(8,128)(2,1)}, bf16[9,24,768]{2,1,0:T(8,128)(2,1)}, u32[]{:S(2)}, u32[]{:S(2)}) collective-permute-start(bf16[9,24,768]{2,1,0:T(8,128)(2,1)} %pad_maximum_fusion.2), channel_id=1, source_target_pairs={{0,16},{1,17},{2,18},{3,19},{4,20},{5,21},{6,22},{7,23},{8,24},{9,... | collective-permute-start | bytes 995336 | tf_op jit(solution)/shard_map/ppermute | solution.py:662
  372.1 7.2 %copy-start.3 = (bf16[1152,768]{1,0:T(8,128)(2,1)S(1)}, bf16[1152,768]{1,0:T(8,128)(2,1)}, u32[]{:S(2)}) copy-start(bf16[1152,768]{1,0:T(8,128)(2,1)} %get-tuple-element.269.d_x) | copy-start | bytes 5308420
  372.3 22.4 %collective-permute-start.14 = (bf16[4,2,24,768]{3,2,1,0:T(8,128)(2,1)S(1)}, bf16[4,2,24,768]{3,2,1,0:T(8,128)(2,1)S(1)}, u32[]{:S(2)}, u32[]{:S(2)}) collective-permute-start(bf16[4,2,24,768]{3,2,1,0:T(8,128)(2,1)S(1)} %get-tuple-element.452), channel_id=1, source_target_pairs={{0,2},{1,3},{2,0},{3,1},{4,6},{5,7},{6,4},{7,5},{8,10},{9,11},{10,... | collective-permute-start | bytes 884744 | tf_op jit(solution)/shard_map/ppermute | solution.py:662
  377.4 17.3 %collective-permute-start.12 = (bf16[4,2,24,768]{3,2,1,0:T(8,128)(2,1)S(1)}, bf16[4,2,24,768]{3,2,1,0:T(8,128)(2,1)S(1)}, u32[]{:S(2)}, u32[]{:S(2)}) collective-permute-start(bf16[4,2,24,768]{3,2,1,0:T(8,128)(2,1)S(1)} %get-tuple-element.454), channel_id=1, source_target_pairs={{0,4},{1,5},{2,6},{3,7},{4,0},{5,1},{6,2},{7,3},{8,12},{9,13},{10,... | collective-permute-start | bytes 884744 | tf_op jit(solution)/shard_map/ppermute | solution.py:662
  394.9 20.9 %collective-permute-start.15 = (bf16[4,24,768]{2,1,0:T(8,128)(2,1)S(1)}, bf16[4,24,768]{2,1,0:T(8,128)(2,1)S(1)}, u32[]{:S(2)}, u32[]{:S(2)}) collective-permute-start(bf16[4,24,768]{2,1,0:T(8,128)(2,1)S(1)} %pad_maximum_fusion.4), channel_id=1, source_target_pairs={{0,8},{1,9},{2,10},{3,11},{4,12},{5,13},{6,14},{7,15},{8,0},{9,1},... | collective-permute-start | bytes 442376 | tf_op jit(solution)/shard_map/ppermute | solution.py:662
  396.6 7.2 %copy-start.17 = (s32[1024]{0:T(1024)S(1)}, s32[1024]{0:T(1024)}, u32[]{:S(2)}) copy-start(s32[1024]{0:T(1024)} %copy-done.16) | copy-start | bytes 12292
  396.7 20.4 %collective-permute-start.16 = (bf16[4,24,768]{2,1,0:T(8,128)(2,1)S(1)}, bf16[4,24,768]{2,1,0:T(8,128)(2,1)S(1)}, u32[]{:S(2)}, u32[]{:S(2)}) collective-permute-start(bf16[4,24,768]{2,1,0:T(8,128)(2,1)S(1)} %pad_maximum_fusion.5), channel_id=1, source_target_pairs={{0,16},{1,17},{2,18},{3,19},{4,20},{5,21},{6,22},{7,23},{8,24},{9,... | collective-permute-start | bytes 442376 | tf_op jit(solution)/shard_map/ppermute | solution.py:662
  398.7 19.5 %collective-permute-start.17 = (bf16[4,24,768]{2,1,0:T(8,128)(2,1)S(1)}, bf16[4,24,768]{2,1,0:T(8,128)(2,1)S(1)}, u32[]{:S(2)}, u32[]{:S(2)}) collective-permute-start(bf16[4,24,768]{2,1,0:T(8,128)(2,1)S(1)} %pad_maximum_fusion.6), channel_id=1, source_target_pairs={{0,24},{1,25},{2,26},{3,27},{4,28},{5,29},{6,30},{7,31},{8,16},{9,... | collective-permute-start | bytes 442376 | tf_op jit(solution)/shard_map/ppermute | solution.py:662
  403.9 5.3 %copy-start.8 = (pred[1152]{0:T(1024)(128)(4,1)S(1)}, pred[1152]{0:T(1024)(128)(4,1)}, u32[]{:S(2)}) copy-start(pred[1152]{0:T(1024)(128)(4,1)} %copy-done.7) | copy-start | bytes 3460
  419.4 17.7 %copy-start.1 = (f32[960,768]{1,0:T(8,128)S(1)}, f32[960,768]{1,0:T(8,128)}, u32[]{:S(2)}) copy-start(f32[960,768]{1,0:T(8,128)} %get-tuple-element.285.g_embed) | copy-start | bytes 8847364
  422.7 1.1 copy-start.2
  425.8 9.9 %all-to-all-start.9 = ((f32[32,1,2]{2,1,0:T(1,128)}), f32[32,1,2]{2,1,0:T(1,128)S(1)}, u32[]{:S(2)}, u32[]{:S(2)}) async-start(f32[32,1,2]{2,1,0:T(1,128)} %broadcast_in_dim.222), calls=%async_computation.9 | async-start | bytes 32768 | tf_op jit(solution)/shard_map/all_to_all | solution.py:42
Sparse Core Ops, SparseCore 0:
  13.7 137.1 all-gather.1
